TPU v7x, 32 devices: a whole 2x2x4 slice. The times are simulated.
32 devices in a mesh: ctx: 8 (over y, x, core), batch: 4 (over z).
Axes of the slice: x: 2, y: 2, z: 4, core: 2. Of those that a mesh axis runs over, the one named last changes fastest.
Arguments:
- queries: bfloat16 [4, 2048, 2048], P('batch', 'ctx'), may hold values from -120 to 120
- keys: bfloat16 [4, 2048, 512], P('batch', 'ctx'), may hold values from -6 to 6
- values: bfloat16 [4, 2048, 512], P('batch', 'ctx'), may hold values from -6 to 6
- tau: float32 [16], replicated, may hold values from 0.5 to 2
- out_grad: bfloat16 [4, 2048, 2048], P('batch', 'ctx'), may hold values from -18 to 18
- key_blocks: int32 [4, 16, 13], replicated, may hold values from 0 to 15, as said below
Outputs:
- attended: bfloat16 [4, 2048, 2048], P('batch', 'ctx')
- query_grad: bfloat16 [4, 2048, 2048], P('batch', 'ctx')
- key_grad: bfloat16 [4, 2048, 512], P('batch', 'ctx')
- value_grad: bfloat16 [4, 2048, 512], P('batch', 'ctx')
- tau_grad: float32 [16], replicated
Inputs may be any that keep to these rules, and one draw needn't show every extreme that they name: `key_blocks`: row a of head group g lists a - 1, a, a + 1, then a + m s and a - m s for m = 1 to 5, all modulo 16, with a stride s of 2 or 3 drawn for each group and row.
All inputs are finite; a program needn't handle non-finite values.
Results may differ from a plain program's by a relative error of at most 0.0051.
Values may be sent and summed in bfloat16 or wider, within the bound.
No kernel may reach another device: no remote copies, remote signals or barrier semaphores. Data moves between devices by JAX's collectives and lax.ppermute only.
A program may use at most 192 MiB of HBM per device.

v0:
```python
import math

import jax
import jax.numpy as jnp
from jax import lax
from jax.sharding import PartitionSpec as P

HEADS = 16
KV_HEADS = 4
HD = 128
BLOCK = 128


def passed_along(block, axis, distance):
    devices = range(lax.axis_size(axis))
    route = [((i - distance) % len(devices), i) for i in devices]
    return lax.ppermute(block, axis, route)


def body(queries, keys, values, tau, out_grad, key_blocks):
    ctx_size = lax.axis_size("ctx")
    myself = lax.axis_index("ctx")
    tokens = queries.shape[1]
    local_blocks = tokens // BLOCK
    listed_count = key_blocks.shape[2]
    block_reach = 3 * ((listed_count - 3) // 2)
    reach_dev = min((local_blocks - 1 + block_reach) // local_blocks, ctx_size // 2)
    slot_count = 2 * reach_dev + 1
    per_group = HEADS // KV_HEADS
    root_hd = math.sqrt(HD)
    paired = jnp.stack([keys[0], values[0]])
    window = jnp.zeros((2, slot_count, tokens, KV_HEADS * HD), jnp.bfloat16)
    farthest = passed_along(paired, "ctx", -reach_dev)
    window = lax.dynamic_update_slice_in_dim(window, farthest[:, None], slot_count - 1, 1)

    def walk_turn(turn_no, state_in):
        current, filled = state_in
        current = passed_along(current, "ctx", 1)
        filled = lax.dynamic_update_slice_in_dim(
            filled, current[:, None], slot_count - 1 - turn_no, 1
        )
        return (current, filled)

    window = lax.fori_loop(1, slot_count, walk_turn, (farthest, window))[1]
    blocks_all = window.reshape(2, slot_count * local_blocks, BLOCK, KV_HEADS, HD)
    own_lists = lax.dynamic_slice_in_dim(key_blocks, myself * local_blocks, local_blocks, 1)
    window_index = (
        own_lists // local_blocks - myself + reach_dev
    ) % ctx_size * local_blocks + own_lists % local_blocks
    window_ids = jnp.arange(slot_count * local_blocks, dtype=jnp.int32)
    query_all = queries[0].reshape(local_blocks, BLOCK, KV_HEADS, per_group, HD)
    grad_all = out_grad[0].reshape(local_blocks, BLOCK, KV_HEADS, per_group, HD)
    factor = tau.reshape(KV_HEADS, per_group) / root_hd
    results = []
    query_parts = []
    placed_parts = []
    scale_parts = []
    for group_id in range(KV_HEADS):
        picks = window_index[group_id].reshape(-1)
        key_rows = jnp.take(blocks_all[0, :, :, group_id], picks, axis=0).reshape(
            local_blocks, listed_count * BLOCK, HD
        )
        value_rows = jnp.take(blocks_all[1, :, :, group_id], picks, axis=0).reshape(
            local_blocks, listed_count * BLOCK, HD
        )
        query_rows = query_all[:, :, group_id]
        grad_rows = grad_all[:, :, group_id]
        scale_row = factor[group_id]
        raw_scores = jnp.einsum(
            "nqhd,nkd->nhqk", query_rows, key_rows, preferred_element_type=jnp.float32
        )
        weights = jax.nn.softmax(raw_scores * scale_row[None, :, None, None], axis=-1)
        probs_low = weights.astype(jnp.bfloat16)
        result = jnp.einsum(
            "nhqk,nkd->nqhd", probs_low, value_rows, preferred_element_type=jnp.float32
        )
        row_dot = jnp.sum(grad_rows.astype(jnp.float32) * result, axis=-1)
        dweights = jnp.einsum(
            "nqhd,nkd->nhqk", grad_rows, value_rows, preferred_element_type=jnp.float32
        )
        dscores = weights * (dweights - row_dot.transpose(0, 2, 1)[..., None])
        scale_parts.append(jnp.sum(dscores * raw_scores, axis=(0, 2, 3)) / root_hd)
        scaled = (dscores * scale_row[None, :, None, None]).astype(jnp.bfloat16)
        query_part = jnp.einsum(
            "nhqk,nkd->nqhd", scaled, key_rows, preferred_element_type=jnp.float32
        )
        key_part = jnp.einsum(
            "nhqk,nqhd->nkd", scaled, query_rows, preferred_element_type=jnp.float32
        )
        value_part = jnp.einsum(
            "nhqk,nqhd->nkd", probs_low, grad_rows, preferred_element_type=jnp.float32
        )
        chooser = (picks[:, None] == window_ids[None, :]).astype(jnp.float32)
        both_parts = jnp.stack([key_part, value_part]).reshape(
            2, local_blocks * listed_count, BLOCK * HD
        )
        placed_parts.append(
            jnp.einsum("sw,csx->cwx", chooser, both_parts, precision=lax.Precision.HIGHEST)
        )
        results.append(result)
        query_parts.append(query_part)
    attended = jnp.stack(results, axis=2).reshape(1, tokens, HEADS * HD).astype(jnp.bfloat16)
    query_grad = jnp.stack(query_parts, axis=2).reshape(1, tokens, HEADS * HD).astype(jnp.bfloat16)
    stacked = jnp.stack(placed_parts).reshape(KV_HEADS, 2, slot_count, local_blocks, BLOCK, HD)
    grads_window = stacked.transpose(2, 1, 3, 4, 0, 5).reshape(slot_count, 2, tokens, KV_HEADS * HD)

    def chain_turn(turn_no, partial_sum):
        moved = passed_along(partial_sum, "ctx", -1)
        return moved + lax.dynamic_index_in_dim(grads_window, turn_no, 0, keepdims=False)

    partial_sum = lax.fori_loop(1, slot_count, chain_turn, grads_window[0])
    summed = passed_along(partial_sum.astype(jnp.bfloat16), "ctx", reach_dev).astype(
        partial_sum.dtype
    )
    key_grad = summed[0].reshape(1, tokens, KV_HEADS * HD).astype(jnp.bfloat16)
    value_grad = summed[1].reshape(1, tokens, KV_HEADS * HD).astype(jnp.bfloat16)
    scale_total = lax.psum(jnp.stack(scale_parts), ("ctx", "batch"))
    tau_grad = scale_total.reshape(HEADS) / math.sqrt(lax.axis_size("batch") * ctx_size * tokens)
    return (attended, query_grad, key_grad, value_grad, tau_grad)


def solution(mesh):
    return jax.shard_map(
        body,
        mesh=mesh,
        in_specs=(
            P("batch", "ctx", None),
            P("batch", "ctx", None),
            P("batch", "ctx", None),
            P(),
            P("batch", "ctx", None),
            P(),
        ),
        out_specs=(
            P("batch", "ctx", None),
            P("batch", "ctx", None),
            P("batch", "ctx", None),
            P("batch", "ctx", None),
            P(),
        ),
        check_vma=False,
    )
```

profile of v0, /device:TPU:0, one launch (start us, length us, event | category | flops | bytes accessed | tf_op | source)
XLA Modules:
  0.0 519.6 jit_solution(10780771625426360972)
XLA Ops:
  21.4 91.1 %while.30 = (s32[]{:T(128)}, bf16[2,256,512]{2,1,0:T(8,128)(2,1)}, bf16[2,9,256,512]{3,2,0,1:T(8,128)(2,1)}, s32[]{:T(128)}, s32[]{:T(128)}, /*index=5*/s32[]{:T(128)}, s32[]{:T(128)}) while((s32[]{:T(128)}, bf16[2,256,512]{2,1,0:T(8,128)(2,1)}, bf16[2,9,256,512]{3,2,0,1:T(8,128)(2,1)}, s32[]{:T(128)}, s32[]{:T(128)}, /*index=5*/s32[]{:T(128)}, ...), condition=%wide.region_1.0_spmd, body=%wide.region_0.0_spmd.sunk | while | flops 6 | bytes 4194471 | solution.py:44
  21.4 9.7 %collective-permute-done = bf16[2,256,512]{2,1,0:T(8,128)(2,1)S(1)} collective-permute-done((bf16[2,256,512]{2,1,0:T(8,128)(2,1)}, bf16[2,256,512]{2,1,0:T(8,128)(2,1)S(1)}, u32[]{:S(2)}, u32[]{:S(2)}) %collective-permute-start) | collective-permute-done | bytes 524320 | tf_op jit(solution)/shard_map/while/body/eval_jaxpr/ppermute | solution.py:17
  32.8 9.7 %collective-permute-done = bf16[2,256,512]{2,1,0:T(8,128)(2,1)S(1)} collective-permute-done((bf16[2,256,512]{2,1,0:T(8,128)(2,1)}, bf16[2,256,512]{2,1,0:T(8,128)(2,1)S(1)}, u32[]{:S(2)}, u32[]{:S(2)}) %collective-permute-start) | collective-permute-done | bytes 524320 | tf_op jit(solution)/shard_map/while/body/eval_jaxpr/ppermute | solution.py:17
  44.2 9.7 %collective-permute-done = bf16[2,256,512]{2,1,0:T(8,128)(2,1)S(1)} collective-permute-done((bf16[2,256,512]{2,1,0:T(8,128)(2,1)}, bf16[2,256,512]{2,1,0:T(8,128)(2,1)S(1)}, u32[]{:S(2)}, u32[]{:S(2)}) %collective-permute-start) | collective-permute-done | bytes 524320 | tf_op jit(solution)/shard_map/while/body/eval_jaxpr/ppermute | solution.py:17
  55.6 9.7 %collective-permute-done = bf16[2,256,512]{2,1,0:T(8,128)(2,1)S(1)} collective-permute-done((bf16[2,256,512]{2,1,0:T(8,128)(2,1)}, bf16[2,256,512]{2,1,0:T(8,128)(2,1)S(1)}, u32[]{:S(2)}, u32[]{:S(2)}) %collective-permute-start) | collective-permute-done | bytes 524320 | tf_op jit(solution)/shard_map/while/body/eval_jaxpr/ppermute | solution.py:17
  67.0 9.7 %collective-permute-done = bf16[2,256,512]{2,1,0:T(8,128)(2,1)S(1)} collective-permute-done((bf16[2,256,512]{2,1,0:T(8,128)(2,1)}, bf16[2,256,512]{2,1,0:T(8,128)(2,1)S(1)}, u32[]{:S(2)}, u32[]{:S(2)}) %collective-permute-start) | collective-permute-done | bytes 524320 | tf_op jit(solution)/shard_map/while/body/eval_jaxpr/ppermute | solution.py:17
  78.3 9.7 %collective-permute-done = bf16[2,256,512]{2,1,0:T(8,128)(2,1)S(1)} collective-permute-done((bf16[2,256,512]{2,1,0:T(8,128)(2,1)}, bf16[2,256,512]{2,1,0:T(8,128)(2,1)S(1)}, u32[]{:S(2)}, u32[]{:S(2)}) %collective-permute-start) | collective-permute-done | bytes 524320 | tf_op jit(solution)/shard_map/while/body/eval_jaxpr/ppermute | solution.py:17
  89.7 9.7 %collective-permute-done = bf16[2,256,512]{2,1,0:T(8,128)(2,1)S(1)} collective-permute-done((bf16[2,256,512]{2,1,0:T(8,128)(2,1)}, bf16[2,256,512]{2,1,0:T(8,128)(2,1)S(1)}, u32[]{:S(2)}, u32[]{:S(2)}) %collective-permute-start) | collective-permute-done | bytes 524320 | tf_op jit(solution)/shard_map/while/body/eval_jaxpr/ppermute | solution.py:17
  101.1 9.7 %collective-permute-done = bf16[2,256,512]{2,1,0:T(8,128)(2,1)S(1)} collective-permute-done((bf16[2,256,512]{2,1,0:T(8,128)(2,1)}, bf16[2,256,512]{2,1,0:T(8,128)(2,1)S(1)}, u32[]{:S(2)}, u32[]{:S(2)}) %collective-permute-start) | collective-permute-done | bytes 524320 | tf_op jit(solution)/shard_map/while/body/eval_jaxpr/ppermute | solution.py:17
  112.5 4.9 copy.85
  117.4 7.7 %reshape.174 = bf16[2,18,128,4,128]{4,3,2,1,0:T(4,128)(2,1)} reshape(bf16[2,9,256,512]{3,2,1,0:T(8,128)(2,1)} %copy.85) | data formatting | bytes 9437184 | tf_op jit(solution)/shard_map/reshape | solution.py:45
  125.1 16.8 %fusion.82 = (bf16[1,18,128,1,128]{4,3,2,1,0:T(2,128)(2,1)}, bf16[1,18,128,1,128]{4,3,2,1,0:T(2,128)(2,1)}, bf16[1,18,128,1,128]{4,3,2,1,0:T(2,128)(2,1)}, bf16[...) fusion(bf16[2,18,128,4,128]{4,3,2,1,0:T(4,128)(2,1)} %reshape.174), kind=kLoop, calls=%fused_computation.196 | loop fusion | bytes 9437184 | tf_op jit(solution)/shard_map/slice | solution.py:60
  148.6 4.7 fusion.90
  171.5 4.9 fusion.58
  176.5 4.7 fusion.89
  200.2 4.9 fusion.59
  205.1 4.8 fusion.88
  253.0 5.1 fusion.56
  258.1 4.7 fusion.91
  278.3 39.6 %psum.7 = f32[4,4]{1,0:T(4,128)S(1)} all-reduce(f32[4,4]{1,0:T(4,128)S(1)} %pad_maximum_fusion.3), channel_id=1, replica_groups=mesh['ctx'=8,'batch'=4] {'ctx','batch'}, use_global_device_ids=true, to_apply=%region_20.22 | all-reduce | flops 16 | bytes 128 | tf_op jit(solution)/shard_map/psum | solution.py:117
  337.5 4.8 copy.256
  343.9 15.6 %copy.128 = f32[9,2,2,128,4,128]{5,4,3,2,1,0:T(4,128)} copy(f32[9,2,2,128,4,128]{5,3,2,0,1,4:T(8,128)} %bitcast.371) | data formatting | bytes 18874368 | tf_op jit(solution)/shard_map/transpose | solution.py:105
  359.5 12.2 %reshape.183 = f32[9,2,256,512]{3,2,1,0:T(8,128)} reshape(f32[9,2,2,128,4,128]{5,4,3,2,1,0:T(4,128)} %copy.128) | data formatting | bytes 18874368 | tf_op jit(solution)/shard_map/reshape | solution.py:105
  374.2 131.3 %while.31 = (s32[]{:T(128)}, f32[2,256,512]{2,1,0:T(8,128)S(1)}, f32[9,2,256,512]{3,2,1,0:T(8,128)}, s32[]{:T(128)}, s32[]{:T(128)}, /*index=5*/s32[]{:T(128)}) while((s32[]{:T(128)}, f32[2,256,512]{2,1,0:T(8,128)S(1)}, f32[9,2,256,512]{3,2,1,0:T(8,128)}, s32[]{:T(128)}, s32[]{:T(128)}, /*index=5*/s32[]{:T(128)}) %tuple.109), condition=%wide.region_15.17_spmd, body=%wide.region_14.16_spmd.sunk | while | flops 262149 | bytes 7340179 | solution.py:111
  375.4 12.3 %collective-permute-done.1 = f32[2,256,512]{2,1,0:T(8,128)S(1)} collective-permute-done((f32[2,256,512]{2,1,0:T(8,128)S(1)}, f32[2,256,512]{2,1,0:T(8,128)S(1)}, u32[]{:S(2)}, u32[]{:S(2)}) %collective-permute-start.1) | collective-permute-done | bytes 1048608 | tf_op jit(solution)/shard_map/while/body/eval_jaxpr/ppermute | solution.py:17
  392.0 12.3 %collective-permute-done.1 = f32[2,256,512]{2,1,0:T(8,128)S(1)} collective-permute-done((f32[2,256,512]{2,1,0:T(8,128)S(1)}, f32[2,256,512]{2,1,0:T(8,128)S(1)}, u32[]{:S(2)}, u32[]{:S(2)}) %collective-permute-start.1) | collective-permute-done | bytes 1048608 | tf_op jit(solution)/shard_map/while/body/eval_jaxpr/ppermute | solution.py:17
  408.6 12.3 %collective-permute-done.1 = f32[2,256,512]{2,1,0:T(8,128)S(1)} collective-permute-done((f32[2,256,512]{2,1,0:T(8,128)S(1)}, f32[2,256,512]{2,1,0:T(8,128)S(1)}, u32[]{:S(2)}, u32[]{:S(2)}) %collective-permute-start.1) | collective-permute-done | bytes 1048608 | tf_op jit(solution)/shard_map/while/body/eval_jaxpr/ppermute | solution.py:17
  425.2 12.3 %collective-permute-done.1 = f32[2,256,512]{2,1,0:T(8,128)S(1)} collective-permute-done((f32[2,256,512]{2,1,0:T(8,128)S(1)}, f32[2,256,512]{2,1,0:T(8,128)S(1)}, u32[]{:S(2)}, u32[]{:S(2)}) %collective-permute-start.1) | collective-permute-done | bytes 1048608 | tf_op jit(solution)/shard_map/while/body/eval_jaxpr/ppermute | solution.py:17
  441.9 12.3 %collective-permute-done.1 = f32[2,256,512]{2,1,0:T(8,128)S(1)} collective-permute-done((f32[2,256,512]{2,1,0:T(8,128)S(1)}, f32[2,256,512]{2,1,0:T(8,128)S(1)}, u32[]{:S(2)}, u32[]{:S(2)}) %collective-permute-start.1) | collective-permute-done | bytes 1048608 | tf_op jit(solution)/shard_map/while/body/eval_jaxpr/ppermute | solution.py:17
  458.5 12.3 %collective-permute-done.1 = f32[2,256,512]{2,1,0:T(8,128)S(1)} collective-permute-done((f32[2,256,512]{2,1,0:T(8,128)S(1)}, f32[2,256,512]{2,1,0:T(8,128)S(1)}, u32[]{:S(2)}, u32[]{:S(2)}) %collective-permute-start.1) | collective-permute-done | bytes 1048608 | tf_op jit(solution)/shard_map/while/body/eval_jaxpr/ppermute | solution.py:17
  475.1 12.3 %collective-permute-done.1 = f32[2,256,512]{2,1,0:T(8,128)S(1)} collective-permute-done((f32[2,256,512]{2,1,0:T(8,128)S(1)}, f32[2,256,512]{2,1,0:T(8,128)S(1)}, u32[]{:S(2)}, u32[]{:S(2)}) %collective-permute-start.1) | collective-permute-done | bytes 1048608 | tf_op jit(solution)/shard_map/while/body/eval_jaxpr/ppermute | solution.py:17
  491.7 12.3 %collective-permute-done.1 = f32[2,256,512]{2,1,0:T(8,128)S(1)} collective-permute-done((f32[2,256,512]{2,1,0:T(8,128)S(1)}, f32[2,256,512]{2,1,0:T(8,128)S(1)}, u32[]{:S(2)}, u32[]{:S(2)}) %collective-permute-start.1) | collective-permute-done | bytes 1048608 | tf_op jit(solution)/shard_map/while/body/eval_jaxpr/ppermute | solution.py:17
  (265 shorter events, 205.6 us)
Async XLA Ops:
  0.6 9.5 %copy-start.27 = (bf16[1,256,2048]{2,1,0:T(8,128)(2,1)S(1)}, bf16[1,256,2048]{2,1,0:T(8,128)(2,1)}, u32[]{:S(2)}) copy-start(bf16[1,256,2048]{2,1,0:T(8,128)(2,1)} %param.12) | copy-start | bytes 3145732
  2.6 15.2 %collective-permute-start.2 = (bf16[2,256,512]{2,1,0:T(8,128)(2,1)}, bf16[2,256,512]{2,1,0:T(8,128)(2,1)}, u32[]{:S(2)}, u32[]{:S(2)}) collective-permute-start(bf16[2,256,512]{2,1,0:T(8,128)(2,1)} %pad_maximum_fusion.2), channel_id=1, source_target_pairs={{16,0},{20,4},{24,8},{28,12},{0,16},{4,20},{8,24},{12,28},{17,1},{... | collective-permute-start | bytes 1572872 | tf_op jit(solution)/shard_map/ppermute | solution.py:17
  21.4 9.7 %collective-permute-start = (bf16[2,256,512]{2,1,0:T(8,128)(2,1)}, bf16[2,256,512]{2,1,0:T(8,128)(2,1)S(1)}, u32[]{:S(2)}, u32[]{:S(2)}) collective-permute-start(bf16[2,256,512]{2,1,0:T(8,128)(2,1)} %get-tuple-element.288), channel_id=1, source_target_pairs={{28,0},{0,4},{4,8},{8,12},{12,16},{16,20},{20,24},{24,28},{29,1},{... | collective-permute-start | bytes 1572872 | tf_op jit(solution)/shard_map/while/body/eval_jaxpr/ppermute | solution.py:17
  32.8 9.7 %collective-permute-start = (bf16[2,256,512]{2,1,0:T(8,128)(2,1)}, bf16[2,256,512]{2,1,0:T(8,128)(2,1)S(1)}, u32[]{:S(2)}, u32[]{:S(2)}) collective-permute-start(bf16[2,256,512]{2,1,0:T(8,128)(2,1)} %get-tuple-element.288), channel_id=1, source_target_pairs={{28,0},{0,4},{4,8},{8,12},{12,16},{16,20},{20,24},{24,28},{29,1},{... | collective-permute-start | bytes 1572872 | tf_op jit(solution)/shard_map/while/body/eval_jaxpr/ppermute | solution.py:17
  44.2 9.7 %collective-permute-start = (bf16[2,256,512]{2,1,0:T(8,128)(2,1)}, bf16[2,256,512]{2,1,0:T(8,128)(2,1)S(1)}, u32[]{:S(2)}, u32[]{:S(2)}) collective-permute-start(bf16[2,256,512]{2,1,0:T(8,128)(2,1)} %get-tuple-element.288), channel_id=1, source_target_pairs={{28,0},{0,4},{4,8},{8,12},{12,16},{16,20},{20,24},{24,28},{29,1},{... | collective-permute-start | bytes 1572872 | tf_op jit(solution)/shard_map/while/body/eval_jaxpr/ppermute | solution.py:17
  55.6 9.7 %collective-permute-start = (bf16[2,256,512]{2,1,0:T(8,128)(2,1)}, bf16[2,256,512]{2,1,0:T(8,128)(2,1)S(1)}, u32[]{:S(2)}, u32[]{:S(2)}) collective-permute-start(bf16[2,256,512]{2,1,0:T(8,128)(2,1)} %get-tuple-element.288), channel_id=1, source_target_pairs={{28,0},{0,4},{4,8},{8,12},{12,16},{16,20},{20,24},{24,28},{29,1},{... | collective-permute-start | bytes 1572872 | tf_op jit(solution)/shard_map/while/body/eval_jaxpr/ppermute | solution.py:17
  67.0 9.7 %collective-permute-start = (bf16[2,256,512]{2,1,0:T(8,128)(2,1)}, bf16[2,256,512]{2,1,0:T(8,128)(2,1)S(1)}, u32[]{:S(2)}, u32[]{:S(2)}) collective-permute-start(bf16[2,256,512]{2,1,0:T(8,128)(2,1)} %get-tuple-element.288), channel_id=1, source_target_pairs={{28,0},{0,4},{4,8},{8,12},{12,16},{16,20},{20,24},{24,28},{29,1},{... | collective-permute-start | bytes 1572872 | tf_op jit(solution)/shard_map/while/body/eval_jaxpr/ppermute | solution.py:17
  78.3 9.7 %collective-permute-start = (bf16[2,256,512]{2,1,0:T(8,128)(2,1)}, bf16[2,256,512]{2,1,0:T(8,128)(2,1)S(1)}, u32[]{:S(2)}, u32[]{:S(2)}) collective-permute-start(bf16[2,256,512]{2,1,0:T(8,128)(2,1)} %get-tuple-element.288), channel_id=1, source_target_pairs={{28,0},{0,4},{4,8},{8,12},{12,16},{16,20},{20,24},{24,28},{29,1},{... | collective-permute-start | bytes 1572872 | tf_op jit(solution)/shard_map/while/body/eval_jaxpr/ppermute | solution.py:17
  89.7 9.7 %collective-permute-start = (bf16[2,256,512]{2,1,0:T(8,128)(2,1)}, bf16[2,256,512]{2,1,0:T(8,128)(2,1)S(1)}, u32[]{:S(2)}, u32[]{:S(2)}) collective-permute-start(bf16[2,256,512]{2,1,0:T(8,128)(2,1)} %get-tuple-element.288), channel_id=1, source_target_pairs={{28,0},{0,4},{4,8},{8,12},{12,16},{16,20},{20,24},{24,28},{29,1},{... | collective-permute-start | bytes 1572872 | tf_op jit(solution)/shard_map/while/body/eval_jaxpr/ppermute | solution.py:17
  101.1 9.7 %collective-permute-start = (bf16[2,256,512]{2,1,0:T(8,128)(2,1)}, bf16[2,256,512]{2,1,0:T(8,128)(2,1)S(1)}, u32[]{:S(2)}, u32[]{:S(2)}) collective-permute-start(bf16[2,256,512]{2,1,0:T(8,128)(2,1)} %get-tuple-element.288), channel_id=1, source_target_pairs={{28,0},{0,4},{4,8},{8,12},{12,16},{16,20},{20,24},{24,28},{29,1},{... | collective-permute-start | bytes 1572872 | tf_op jit(solution)/shard_map/while/body/eval_jaxpr/ppermute | solution.py:17
  153.4 7.9 %slice-start.9 = ((s8[6815744]{0:T(1024)(128)(4,1)}), s8[2621440]{0:T(1024)(128)(4,1)S(1)}, s32[]{:S(2)}) async-start(s8[6815744]{0:T(1024)(128)(4,1)} %bitcast.393), calls=%async_computation.9 | async-start | bytes 5242880
  176.5 8.4 %copy-start.26 = (bf16[2,128,1,4,128]{1,4,3,0,2:T(8,128)(2,1)S(1)}, bf16[2,128,1,4,128]{1,4,3,0,2:T(8,128)(2,1)}, u32[]{:S(2)}) copy-start(bf16[2,128,1,4,128]{1,4,3,0,2:T(8,128)(2,1)} %copy.205) | copy-start | bytes 786436
  181.2 7.9 %slice-start.11 = ((s8[6815744]{0:T(1024)(128)(4,1)}), s8[2621440]{0:T(1024)(128)(4,1)S(1)}, s32[]{:S(2)}) async-start(s8[6815744]{0:T(1024)(128)(4,1)} %bitcast.395), calls=%async_computation.11 | async-start | bytes 5242880
  205.1 8.5 %copy-start.25 = (bf16[2,128,1,4,128]{1,4,3,0,2:T(8,128)(2,1)S(1)}, bf16[2,128,1,4,128]{1,4,3,0,2:T(8,128)(2,1)}, u32[]{:S(2)}) copy-start(bf16[2,128,1,4,128]{1,4,3,0,2:T(8,128)(2,1)} %copy.206) | copy-start | bytes 786436
  209.9 7.4 %slice-start.6 = ((s8[6815744]{0:T(1024)(128)(4,1)}), s8[4194304]{0:T(1024)(128)(4,1)S(1)}, s32[]{:S(2)}) async-start(s8[6815744]{0:T(1024)(128)(4,1)} %bitcast.378), calls=%async_computation.6 | async-start | bytes 8388608
  209.9 7.4 %slice-start.12 = ((s8[6815744]{0:T(1024)(128)(4,1)}), s8[4194304]{0:T(1024)(128)(4,1)S(1)}, s32[]{:S(2)}) async-start(s8[6815744]{0:T(1024)(128)(4,1)} %bitcast.397), calls=%async_computation.12 | async-start | bytes 8388608
  209.9 7.4 %slice-start.7 = ((s8[6815744]{0:T(1024)(128)(4,1)}), s8[2621440]{0:T(1024)(128)(4,1)S(1)}, s32[]{:S(2)}) async-start(s8[6815744]{0:T(1024)(128)(4,1)} %bitcast.378), calls=%async_computation.7 | async-start | bytes 5242880
  209.9 7.9 %slice-start.13 = ((s8[6815744]{0:T(1024)(128)(4,1)}), s8[2621440]{0:T(1024)(128)(4,1)S(1)}, s32[]{:S(2)}) async-start(s8[6815744]{0:T(1024)(128)(4,1)} %bitcast.397), calls=%async_computation.13 | async-start | bytes 5242880
  258.1 8.4 %copy-start.24 = (bf16[2,128,1,4,128]{1,4,3,0,2:T(8,128)(2,1)S(1)}, bf16[2,128,1,4,128]{1,4,3,0,2:T(8,128)(2,1)}, u32[]{:S(2)}) copy-start(bf16[2,128,1,4,128]{1,4,3,0,2:T(8,128)(2,1)} %copy.203) | copy-start | bytes 786436
  262.9 7.4 %slice-start.14 = ((s8[6815744]{0:T(1024)(128)(4,1)}), s8[4194304]{0:T(1024)(128)(4,1)S(1)}, s32[]{:S(2)}) async-start(s8[6815744]{0:T(1024)(128)(4,1)} %bitcast.399), calls=%async_computation.14 | async-start | bytes 8388608
  262.9 7.4 %slice-start.1 = ((s8[6815744]{0:T(1024)(128)(4,1)}), s8[2621440]{0:T(1024)(128)(4,1)S(1)}, s32[]{:S(2)}) async-start(s8[6815744]{0:T(1024)(128)(4,1)} %bitcast.372), calls=%async_computation.1 | async-start | bytes 5242880
  262.9 7.5 %slice-start.15 = ((s8[6815744]{0:T(1024)(128)(4,1)}), s8[2621440]{0:T(1024)(128)(4,1)S(1)}, s32[]{:S(2)}) async-start(s8[6815744]{0:T(1024)(128)(4,1)} %bitcast.399), calls=%async_computation.15 | async-start | bytes 5242880
  374.1 133.9 %copy-start.7 = (bf16[26,128,128]{2,1,0:T(8,128)(2,1)S(1)}, bf16[26,128,128]{2,1,0:T(8,128)(2,1)}, u32[]{:S(2)}) copy-start(bf16[26,128,128]{2,1,0:T(8,128)(2,1)} %copy-done.6) | copy-start | bytes 2555908
  374.4 13.3 %collective-permute-start.1 = (f32[2,256,512]{2,1,0:T(8,128)S(1)}, f32[2,256,512]{2,1,0:T(8,128)S(1)}, u32[]{:S(2)}, u32[]{:S(2)}) collective-permute-start(f32[2,256,512]{2,1,0:T(8,128)S(1)} %get-tuple-element.308), channel_id=1, source_target_pairs={{4,0},{8,4},{12,8},{16,12},{20,16},{24,20},{28,24},{0,28},{5,1},{9... | collective-permute-start | bytes 3145736 | tf_op jit(solution)/shard_map/while/body/eval_jaxpr/ppermute | solution.py:17
  389.1 15.2 %collective-permute-start.1 = (f32[2,256,512]{2,1,0:T(8,128)S(1)}, f32[2,256,512]{2,1,0:T(8,128)S(1)}, u32[]{:S(2)}, u32[]{:S(2)}) collective-permute-start(f32[2,256,512]{2,1,0:T(8,128)S(1)} %get-tuple-element.308), channel_id=1, source_target_pairs={{4,0},{8,4},{12,8},{16,12},{20,16},{24,20},{28,24},{0,28},{5,1},{9... | collective-permute-start | bytes 3145736 | tf_op jit(solution)/shard_map/while/body/eval_jaxpr/ppermute | solution.py:17
  405.8 15.2 %collective-permute-start.1 = (f32[2,256,512]{2,1,0:T(8,128)S(1)}, f32[2,256,512]{2,1,0:T(8,128)S(1)}, u32[]{:S(2)}, u32[]{:S(2)}) collective-permute-start(f32[2,256,512]{2,1,0:T(8,128)S(1)} %get-tuple-element.308), channel_id=1, source_target_pairs={{4,0},{8,4},{12,8},{16,12},{20,16},{24,20},{28,24},{0,28},{5,1},{9... | collective-permute-start | bytes 3145736 | tf_op jit(solution)/shard_map/while/body/eval_jaxpr/ppermute | solution.py:17
  422.4 15.2 %collective-permute-start.1 = (f32[2,256,512]{2,1,0:T(8,128)S(1)}, f32[2,256,512]{2,1,0:T(8,128)S(1)}, u32[]{:S(2)}, u32[]{:S(2)}) collective-permute-start(f32[2,256,512]{2,1,0:T(8,128)S(1)} %get-tuple-element.308), channel_id=1, source_target_pairs={{4,0},{8,4},{12,8},{16,12},{20,16},{24,20},{28,24},{0,28},{5,1},{9... | collective-permute-start | bytes 3145736 | tf_op jit(solution)/shard_map/while/body/eval_jaxpr/ppermute | solution.py:17
  439.0 15.2 %collective-permute-start.1 = (f32[2,256,512]{2,1,0:T(8,128)S(1)}, f32[2,256,512]{2,1,0:T(8,128)S(1)}, u32[]{:S(2)}, u32[]{:S(2)}) collective-permute-start(f32[2,256,512]{2,1,0:T(8,128)S(1)} %get-tuple-element.308), channel_id=1, source_target_pairs={{4,0},{8,4},{12,8},{16,12},{20,16},{24,20},{28,24},{0,28},{5,1},{9... | collective-permute-start | bytes 3145736 | tf_op jit(solution)/shard_map/while/body/eval_jaxpr/ppermute | solution.py:17
  455.6 15.2 %collective-permute-start.1 = (f32[2,256,512]{2,1,0:T(8,128)S(1)}, f32[2,256,512]{2,1,0:T(8,128)S(1)}, u32[]{:S(2)}, u32[]{:S(2)}) collective-permute-start(f32[2,256,512]{2,1,0:T(8,128)S(1)} %get-tuple-element.308), channel_id=1, source_target_pairs={{4,0},{8,4},{12,8},{16,12},{20,16},{24,20},{28,24},{0,28},{5,1},{9... | collective-permute-start | bytes 3145736 | tf_op jit(solution)/shard_map/while/body/eval_jaxpr/ppermute | solution.py:17
  472.2 15.2 %collective-permute-start.1 = (f32[2,256,512]{2,1,0:T(8,128)S(1)}, f32[2,256,512]{2,1,0:T(8,128)S(1)}, u32[]{:S(2)}, u32[]{:S(2)}) collective-permute-start(f32[2,256,512]{2,1,0:T(8,128)S(1)} %get-tuple-element.308), channel_id=1, source_target_pairs={{4,0},{8,4},{12,8},{16,12},{20,16},{24,20},{28,24},{0,28},{5,1},{9... | collective-permute-start | bytes 3145736 | tf_op jit(solution)/shard_map/while/body/eval_jaxpr/ppermute | solution.py:17
  488.9 15.2 %collective-permute-start.1 = (f32[2,256,512]{2,1,0:T(8,128)S(1)}, f32[2,256,512]{2,1,0:T(8,128)S(1)}, u32[]{:S(2)}, u32[]{:S(2)}) collective-permute-start(f32[2,256,512]{2,1,0:T(8,128)S(1)} %get-tuple-element.308), channel_id=1, source_target_pairs={{4,0},{8,4},{12,8},{16,12},{20,16},{24,20},{28,24},{0,28},{5,1},{9... | collective-permute-start | bytes 3145736 | tf_op jit(solution)/shard_map/while/body/eval_jaxpr/ppermute | solution.py:17
  506.4 10.9 %collective-permute-start.3 = (bf16[2,256,512]{2,1,0:T(8,128)(2,1)}, bf16[2,256,512]{2,1,0:T(8,128)(2,1)}, u32[]{:S(2)}, u32[]{:S(2)}) collective-permute-start(bf16[2,256,512]{2,1,0:T(8,128)(2,1)} %convert_element_type.84), channel_id=1, source_target_pairs={{16,0},{20,4},{24,8},{28,12},{0,16},{4,20},{8,24},{12,28},{17,1},{... | collective-permute-start | bytes 1572872 | tf_op jit(solution)/shard_map/ppermute | solution.py:17
  (37 other events, 157.7 us)
where the time goes:
time: 526 us; the launch traced here: 520 us
  waiting for transfers between devices  179 us (34%)
  local copies, waits for them, and re-layouts  139 us (26%)
  matrix products  97 us (18%)
  blocking collectives  39.6 us (8%)
  other arithmetic  36.7 us (7%)
  starting transfers between devices  25.6 us (5%)
    ppermute x18, waiting for transfers between devices, passed_along(): return lax.ppermute(block, axis, route)  179 us
    psum x1, blocking collectives, body(): scale_total = lax.psum(jnp.stack(scale_parts), ('ctx', 'batch'))  39.6 us
    ppermute x18, starting transfers between devices, passed_along(): return lax.ppermute(block, axis, route)  25.6 us
    sub x4, matrix products, body(): jax.nn.softmax(raw_scores * scale_row[None, :, None, None], axis=-1)  19 us
    dot_general x4, matrix products, body(): jnp.einsum('nqhd,nkd->nhqk', query_rows, key_rows, preferred_element_type...  18.9 us
    another operation x8, local copies, waits for them, and re-layouts, body(): jnp.stack([key_part, value_part])  18.1 us
    slice x1, local copies, waits for them, and re-layouts, body(): blocks_all[0, :, :, group_id]  16.8 us
    transpose x1, local copies, waits for them, and re-layouts, body(): stacked.transpose(2, 1, 3, 4, 0, 5)  15.6 us
  transfers between devices with their start and end apart: 18, of which 17 were waited for; matrix products, arithmetic and copies ran while one was open for 4% of the time, Pallas kernels for 0%

commit v1 on v0

v1 whole, which is shorter than its diff:
```python
import functools
import math

import jax
import jax.numpy as jnp
from jax import lax
from jax.experimental import pallas as pl
from jax.experimental.pallas import tpu as pltpu
from jax.sharding import PartitionSpec as P

HEADS = 16
KV_HEADS = 4
HD = 128
BLOCK = 128
QPG = HEADS // KV_HEADS
ROWS = QPG * BLOCK
STRIDES = (2, 3)
CHUNK = 3
LOG2E = math.log2(math.e)
NEVER = -1e30


def distinct_bound(block_count, listed_count):
    most = 0
    for stride in STRIDES:
        steps = range(1, (listed_count - 3) // 2 + 1)
        offsets = [-1, 0, 1] + [stride * m for m in steps] + [-stride * m for m in steps]
        most = max(most, len({o % block_count for o in offsets}))
    return most


def nt(a, b):
    return jnp.dot(a, b, preferred_element_type=jnp.float32)


def group_kernel(listed, pieces, *refs):
    slots, bias, _ = refs[:3]
    q_own, q_sib, g_own, g_sib, coef = refs[3:8]
    kv_in = refs[8 : 8 + pieces]
    att_own, dq_own, sib_out, tau_out = refs[8 + pieces : 12 + pieces]
    kv_out = refs[12 + pieces : 12 + 2 * pieces]
    k_s, v_s, kt_s, vt_s, dk_s, dv_s, e_s, dp_s, p_s, ds_s = refs[12 + 2 * pieces :]
    unit = pl.program_id(0)

    @pl.when(unit == 0)
    def _():
        for i in range(pieces):
            for half in range(2):
                rows = slice(half * BLOCK, (half + 1) * BLOCK)
                k_block = kv_in[i][0, rows, :]
                v_block = kv_in[i][1, rows, :]
                k_s[2 * i + half] = k_block
                v_s[2 * i + half] = v_block
                kt_s[2 * i + half] = k_block.T
                vt_s[2 * i + half] = v_block.T
        dk_s[...] = jnp.zeros_like(dk_s)
        dv_s[...] = jnp.zeros_like(dv_s)
        tau_out[...] = jnp.zeros_like(tau_out)

    own = unit < 2
    q_here = jnp.where(own, q_own[...], q_sib[0])
    g_here = jnp.where(own, g_own[...], g_sib[0])

    def per_head(x):
        return [x[:, h * HD : (h + 1) * HD] for h in range(QPG)]

    q_rows = jnp.concatenate(per_head(q_here), axis=0)
    g_rows = jnp.concatenate(per_head(g_here), axis=0)
    q_t = jnp.concatenate([x.T for x in per_head(q_here)], axis=1)
    g_t = jnp.concatenate([x.T for x in per_head(g_here)], axis=1)
    factor = coef[0:1, :]
    scale = coef[1:2, :]
    ids = [slots[unit, j] for j in range(listed)]
    chunks = [range(c, min(c + CHUNK, listed)) for c in range(0, listed, CHUNK)]

    def rows_of(c):
        return slice(c[0] * BLOCK, (c[-1] + 1) * BLOCK)

    most = None
    for c in chunks:
        raw = nt(jnp.concatenate([k_s[ids[j]] for j in c], axis=0), q_t)
        e_s[rows_of(c), :] = raw
        top = jnp.max(raw.reshape(-1, 8, ROWS), axis=0)
        most = top if most is None else jnp.maximum(most, top)
    top_row = jnp.max(most, axis=0, keepdims=True) * factor

    total = jnp.zeros((8, ROWS), jnp.float32)
    for c in chunks:
        dp_s[rows_of(c), :] = nt(jnp.concatenate([v_s[ids[j]] for j in c], axis=0), g_t)
        for j in c:
            rows = slice(j * BLOCK, (j + 1) * BLOCK)
            e = jnp.exp2(e_s[rows, :] * factor - (top_row - bias[unit, j]))
            e_s[rows, :] = e
            total = total + jnp.sum(e.reshape(-1, 8, ROWS), axis=0)
    inverse = 1.0 / jnp.sum(total, axis=0, keepdims=True)

    for c in chunks:
        probs = (e_s[rows_of(c), :] * inverse).astype(jnp.bfloat16)
        p_s[rows_of(c), :] = probs
        part = nt(probs, g_rows)
        for n, j in enumerate(c):
            dv_s[ids[j]] += part[n * BLOCK : (n + 1) * BLOCK, :]
    o_t = nt(jnp.concatenate([vt_s[s] for s in ids], axis=1), p_s[...])
    row_dot = jnp.sum(g_t.astype(jnp.float32) * o_t, axis=0, keepdims=True)

    weight_scale = inverse * scale
    for c in chunks:
        scaled = (e_s[rows_of(c), :] * weight_scale * (dp_s[rows_of(c), :] - row_dot)).astype(
            jnp.bfloat16
        )
        ds_s[rows_of(c), :] = scaled
        part = nt(scaled, q_rows)
        for n, j in enumerate(c):
            dk_s[ids[j]] += part[n * BLOCK : (n + 1) * BLOCK, :]
    dq_t = nt(jnp.concatenate([kt_s[s] for s in ids], axis=1), ds_s[...])
    tau_out[...] += jnp.sum(q_t.astype(jnp.float32) * dq_t, axis=0, keepdims=True)

    def back(x):
        low = x.astype(jnp.bfloat16)
        return jnp.concatenate([y.T for y in per_head(low)], axis=1)

    att = back(o_t)
    dq = back(dq_t)

    @pl.when(own)
    def _():
        att_own[...] = att
        dq_own[...] = dq

    @pl.when(jnp.logical_not(own))
    def _():
        sib_out[0] = att
        sib_out[1] = dq

    @pl.when(unit == 3)
    def _():
        for i in range(pieces):
            for half in range(2):
                rows = slice(half * BLOCK, (half + 1) * BLOCK)
                kv_out[i][0, rows, :] = dk_s[2 * i + half].astype(jnp.bfloat16)
                kv_out[i][1, rows, :] = dv_s[2 * i + half].astype(jnp.bfloat16)


def run_group(gi, slots, bias, column, queries, q_sib, out_grad, g_sib, coef, pieces_in):
    listed = slots.shape[1]
    pieces = len(pieces_in)
    tokens = queries.shape[0]
    width = QPG * HD
    own_map = lambda u, s, b, c: (jnp.minimum(u, 1), c[0])
    sib_map = lambda u, s, b, c: (0, jnp.maximum(u - 2, 0), 0)
    whole3 = pl.BlockSpec((2, tokens, HD), lambda u, s, b, c: (0, 0, 0))
    block_own = pl.BlockSpec((BLOCK, width), own_map)
    out_own = pl.BlockSpec((BLOCK, width), lambda u, s, b, c: (jnp.minimum(u, 1), 0))
    bf = lambda *shape: jax.ShapeDtypeStruct(shape, jnp.bfloat16)
    slot_count = 2 * pieces
    keys_wide = listed * BLOCK
    qs = pl.BlockSpec((1, BLOCK, width), lambda u, s, b, c: (0, jnp.maximum(u - 2, 0), 0))
    gs = pl.BlockSpec((1, BLOCK, width), lambda u, s, b, c: (1, jnp.maximum(u - 2, 0), 0))
    macs = 4 * ROWS * keys_wide * HD * 6
    return pl.pallas_call(
        functools.partial(group_kernel, listed, pieces),
        grid_spec=pltpu.PrefetchScalarGridSpec(
            num_scalar_prefetch=3,
            grid=(4,),
            in_specs=[block_own, qs, block_own, gs, pl.BlockSpec((8, ROWS), lambda u, s, b, c: (0, 0))]
            + [whole3] * pieces,
            out_specs=[
                out_own,
                out_own,
                pl.BlockSpec((2, BLOCK, width), sib_map),
                pl.BlockSpec((1, ROWS), lambda u, s, b, c: (0, 0)),
            ]
            + [whole3] * pieces,
            scratch_shapes=[pltpu.VMEM((slot_count, BLOCK, HD), jnp.bfloat16)] * 4
            + [pltpu.VMEM((slot_count, BLOCK, HD), jnp.float32)] * 2
            + [pltpu.VMEM((keys_wide, ROWS), jnp.float32)] * 2
            + [pltpu.VMEM((keys_wide, ROWS), jnp.bfloat16)] * 2,
        ),
        out_shape=[bf(tokens, width), bf(tokens, width), bf(2, tokens, width)]
        + [jax.ShapeDtypeStruct((1, ROWS), jnp.float32)]
        + [bf(2, tokens, HD)] * pieces,
        compiler_params=pltpu.CompilerParams(
            dimension_semantics=("arbitrary",), vmem_limit_bytes=48 * 2**20
        ),
        cost_estimate=pl.CostEstimate(
            flops=2 * macs, bytes_accessed=6 * 2**20, transcendentals=4 * ROWS * keys_wide
        ),
        name="group_attention",
    )(slots, bias, column, queries, q_sib, out_grad, g_sib, coef, *pieces_in)


def body(queries, keys, values, tau, out_grad, key_blocks):
    ctx = lax.axis_size("ctx")
    me = lax.axis_index("ctx")
    pair, core = me // 2, me % 2
    pairs = ctx // 2
    tokens = queries.shape[1]
    local_blocks = tokens // BLOCK
    pair_blocks = 2 * local_blocks
    block_count = ctx * local_blocks
    listed_count = key_blocks.shape[2]
    block_reach = max(STRIDES) * ((listed_count - 3) // 2)
    reach = (block_reach + pair_blocks - 1) // pair_blocks
    everyone = 2 * reach + 1 >= pairs
    by_xor = everyone and pairs & (pairs - 1) == 0
    if everyone:
        offsets = list(range(pairs))
    else:
        offsets = [o % pairs for o in range(-reach, reach + 1)]
        offsets.remove(0)
        offsets.insert(0, 0)

    def moved(p, r, sign):
        return p ^ r if by_xor else (p + sign * r) % pairs

    def route(r, cx, sign):
        return [
            (2 * p + k, 2 * moved(p, r, sign) + (k ^ cx)) for p in range(pairs) for k in range(2)
        ]

    def send(x, r, cx, sign):
        return lax.ppermute(x, "ctx", route(r, cx, sign))

    def columns(x, group, width):
        return lax.dynamic_slice_in_dim(x, group * width, width, 1)

    q0, k0, v0, g0 = queries[0], keys[0], values[0], out_grad[0]
    wide = QPG * HD
    order = [(r, cx) for r in offsets for cx in range(2)]

    units = jnp.arange(4)
    unit_block = pair * pair_blocks + (core ^ (units // 2)) * local_blocks + units % 2
    rel_of = jnp.array([offsets.index(r) if r in offsets else 0 for r in range(pairs)], jnp.int32)
    block_pair = key_blocks // pair_blocks
    relative = block_pair ^ pair if by_xor else (pair - block_pair) % pairs
    rel_index = jnp.sum(
        jnp.where(relative[..., None] == jnp.arange(pairs), rel_of, 0), axis=-1
    )
    slot = (
        rel_index * pair_blocks
        + ((key_blocks // local_blocks) % 2 ^ core) * local_blocks
        + key_blocks % local_blocks
    )
    listed = distinct_bound(block_count, listed_count)

    def lists(group):
        rows = jnp.take(lax.dynamic_index_in_dim(slot, group, 0, keepdims=False), unit_block, axis=0)
        same = rows[:, :, None] == rows[:, None, :]
        times = jnp.sum(same, axis=2)
        earlier = jnp.tril(jnp.ones((listed_count, listed_count), bool), -1)
        first = jnp.logical_not(jnp.any(same & earlier, axis=2))
        rank = jnp.sum(
            first[:, None, :] & jnp.tril(jnp.ones((listed_count, listed_count), bool)), axis=2
        ) - 1
        place = (rank[:, None, :] == jnp.arange(listed)[:, None]) & first[:, None, :]
        used = jnp.any(place, axis=2)
        chosen = jnp.where(used, jnp.sum(jnp.where(place, rows[:, None, :], 0), axis=2), rows[:, :1])
        count = jnp.sum(jnp.where(place, times[:, None, :], 0), axis=2)
        bias = jnp.where(
            count == 0,
            NEVER,
            jnp.where(count == 1, 0.0, jnp.where(count == 2, 1.0, jnp.log2(count.astype(jnp.float32)))),
        )
        return chosen.astype(jnp.int32), bias.astype(jnp.float32)

    att_parts, dq_parts, grads, tau_parts = [], [], [], []
    for gi in range(2):
        mine = 2 * core + gi
        theirs = 2 * (1 - core) + gi
        kv_same = jnp.stack([columns(k0, mine, HD), columns(v0, mine, HD)])
        kv_other = jnp.stack([columns(k0, theirs, HD), columns(v0, theirs, HD)])
        pieces = [
            kv_same if (r, cx) == (0, 0) else send((kv_same, kv_other)[cx], r, cx, 1)
            for r, cx in order
        ]
        qg_sib = send(jnp.stack([columns(q0, theirs, wide), columns(g0, theirs, wide)]), 0, 1, 1)
        tau_group = lax.dynamic_slice_in_dim(tau, mine * QPG, QPG, 0)
        scale = jnp.repeat(tau_group / math.sqrt(HD), BLOCK)[None]
        coef = jnp.concatenate([scale * LOG2E, scale, jnp.zeros((6, ROWS), jnp.float32)], axis=0)
        slots, bias = lists(mine)
        out = run_group(
            gi, slots, bias, mine[None].astype(jnp.int32), q0, qg_sib, g0, qg_sib, coef, pieces
        )
        att_own, dq_own, sib, tau_rows = out[:4]
        kv_grads = out[4:]
        sib = send(sib, 0, 1, 1)
        att_parts.append((att_own, sib[0]))
        dq_parts.append((dq_own, sib[1]))
        received = [
            x if (r, cx) == (0, 0) else send(x, r, cx, -1) for (r, cx), x in zip(order, kv_grads)
        ]
        grads.append([[x for (r, c), x in zip(order, received) if c == cx] for cx in range(2)])
        tau_parts.append(jnp.sum(tau_rows.reshape(QPG, BLOCK), axis=1) / tau_group)

    def by_group(parts):
        return jnp.concatenate(
            [jnp.where(core == c // 2, parts[c % 2][0], parts[c % 2][1]) for c in range(4)], axis=1
        )

    attended = by_group(att_parts)[None]
    query_grad = by_group(dq_parts)[None]

    def summed(which):
        cols = []
        for c in range(4):
            total = None
            for a, b in zip(*grads[c % 2]):
                term = jnp.where(core == c // 2, a[which], b[which]).astype(jnp.float32)
                total = term if total is None else total + term
            cols.append(total.astype(jnp.bfloat16))
        return jnp.concatenate(cols, axis=1)[None]

    key_grad, value_grad = summed(0), summed(1)
    mine = jnp.concatenate(tau_parts)
    placed = lax.dynamic_update_slice_in_dim(
        jnp.zeros((HEADS,), jnp.float32), mine, core * 2 * QPG, 0
    )
    scale_total = jnp.sum(lax.all_gather(placed, ("ctx", "batch")), axis=0)
    tau_grad = scale_total / math.sqrt(lax.axis_size("batch") * ctx * tokens)
    return (attended, query_grad, key_grad, value_grad, tau_grad)


def solution(mesh):
    rows = P("batch", "ctx", None)
    return jax.shard_map(
        body,
        mesh=mesh,
        in_specs=(rows, rows, rows, P(), rows, P()),
        out_specs=(rows, rows, rows, rows, P()),
        check_vma=False,
    )
```

time: 526 us -> 182 us (0.35); the launches traced: 520 us -> 181 us
  waiting for transfers between devices: 179 us -> 7.22 us
  local copies, waits for them, and re-layouts: 139 us -> 22.9 us
  matrix products: 97 us -> 0 us
  Pallas kernels: 0 us -> 32.4 us
  blocking collectives: 39.6 us -> 67.5 us
  other arithmetic: 36.7 us -> 19.3 us
    ppermute x18 -> x32, waiting for transfers between devices: 179 us -> 7.22 us  [send(): return lax.ppermute(x, 'ctx', route(r, cx, sign))]
    dot_general x28 -> x0, matrix products: 78 us -> none  [the longest x4 18.9 us: body(): jnp.einsum('nqhd,nkd->nhqk', query_rows, key_rows, preferred_element_type...]
    all_gather x0 -> x1, blocking collectives: none -> 67.5 us  [body(): scale_total = jnp.sum(lax.all_gather(placed, ('ctx', 'batch')), axis=0)]
    psum x1 -> x0, blocking collectives: 39.6 us -> none  [body(): scale_total = lax.psum(jnp.stack(scale_parts), ('ctx', 'batch'))]
    another operation x22 -> x1, local copies, waits for them, and re-layouts: 34.5 us -> 0.01 us  [the longest x8 18.1 us: body(): jnp.stack([key_part, value_part])]
    pallas_call x0 -> x2, Pallas kernels: none -> 32.4 us  [run_group(): pl.pallas_call(functools.partial(group_kernel, listed, pieces), grid_spec...]
    slice x12 -> x2, local copies, waits for them, and re-layouts: 22.6 us -> 0.23 us  [lists(): rows[:, :1]]
    reshape x2 -> x0, local copies, waits for them, and re-layouts: 19.9 us -> none  [the longest x1 12.2 us: body(): stacked.transpose(2, 1, 3, 4, 0, 5)]
  transfers between devices with their start and end apart: 18 -> 32, of which waited for: 17 -> 6; matrix products, arithmetic and copies ran while one was open for 4% -> 12% of each run, Pallas kernels for 0% -> 18%
where the time goes in v1:
time: 182 us; the launch traced here: 181 us
  blocking collectives  67.5 us (37%)
  Pallas kernels  32.4 us (18%)
  starting transfers between devices  30.6 us (17%)
  local copies, waits for them, and re-layouts  22.9 us (13%)
  other arithmetic  19.3 us (11%)
  waiting for transfers between devices  7.22 us (4%)
    all_gather x1, blocking collectives, body(): scale_total = jnp.sum(lax.all_gather(placed, ('ctx', 'batch')), axis=0)  67.5 us
    pallas_call x2, Pallas kernels, run_group(): pl.pallas_call(functools.partial(group_kernel, listed, pieces), grid_spec...  32.4 us
    ppermute x32, starting transfers between devices, send(): return lax.ppermute(x, 'ctx', route(r, cx, sign))  30.6 us
    unnamed x71, local copies, waits for them, and re-layouts  17 us
    ppermute x32, waiting for transfers between devices, send(): return lax.ppermute(x, 'ctx', route(r, cx, sign))  7.22 us
  transfers between devices with their start and end apart: 32, of which 6 were waited for; matrix products, arithmetic and copies ran while one was open for 12% of the time, Pallas kernels for 18%

profile of v1, /device:TPU:0, one launch (start us, length us, event | category | flops | bytes accessed | tf_op | source)
XLA Modules:
  0.0 181.1 jit_solution(9510634405849517132)
XLA Ops:
  0.7 1.9 %constant_dynamic-slice_fusion.7 = (bf16[1,256,128]{2,1,0:T(8,128)(2,1)S(1)}, bf16[1,256,128]{2,1,0:T(8,128)(2,1)}, bf16[1,256,128]{2,1,0:T(8,128)(2,1)S(1)}, bf...) fusion(bf16[1,256,512]{2,1,0:T(8,128)(2,1)} %param.11, ...), kind=kLoop, calls=%fused_computation.95 | loop fusion | bytes 1048592 | tf_op jit(solution)/shard_map/dynamic_slice | solution.py:225
  2.7 4.0 %collective-permute-start.15 = (bf16[2,256,128]{2,1,0:T(8,128)(2,1)S(1)}, bf16[2,256,128]{2,1,0:T(8,128)(2,1)S(1)}, u32[]{:S(2)}, u32[]{:S(2)}) collective-permute-start(bf16[2,256,128]{2,1,0:T(8,128)(2,1)S(1)} %pad_maximum_fusion.4.refs_8_), channel_id=1, source_target_pairs={{0,24},{4,28},{8,16},{12,20},{16,8},{20,12},{24,0},{28,4},{1,25},{... | collective-permute-start | bytes 393224 | tf_op jit(solution)/shard_map/ppermute | solution.py:222
  7.9 1.4 collective-permute-start.16
  9.4 1.6 collective-permute-start.14
  19.0 0.9 constant_dynamic-slice_fusion.11
  20.0 0.8 pad_maximum_fusion.1
  21.5 0.9 pad_maximum_fusion.2.refs_8_
  22.4 2.6 %collective-permute-start.6 = (bf16[2,256,128]{2,1,0:T(8,128)(2,1)S(1)}, bf16[2,256,128]{2,1,0:T(8,128)(2,1)}, u32[]{:S(2)}, u32[]{:S(2)}) collective-permute-start(bf16[2,256,128]{2,1,0:T(8,128)(2,1)S(1)} %pad_maximum_fusion.2.refs_8_), channel_id=1, source_target_pairs={{0,24},{4,28},{8,16},{12,20},{16,8},{20,12},{24,0},{28,4},{1,25},{... | collective-permute-start | bytes 393224 | tf_op jit(solution)/shard_map/ppermute | solution.py:222
  25.5 1.2 collective-permute-done.12.refs_11_
  27.5 0.8 pad_maximum_fusion
  28.4 1.5 pad_maximum_fusion.3
  30.0 2.1 %collective-permute-start.7 = (bf16[2,256,128]{2,1,0:T(8,128)(2,1)}, bf16[2,256,128]{2,1,0:T(8,128)(2,1)}, u32[]{:S(2)}, u32[]{:S(2)}) collective-permute-start(bf16[2,256,128]{2,1,0:T(8,128)(2,1)} %pad_maximum_fusion.3), channel_id=1, source_target_pairs={{0,28},{4,24},{8,20},{12,16},{16,12},{20,8},{24,4},{28,0},{1,29},{... | collective-permute-start | bytes 393224 | tf_op jit(solution)/shard_map/ppermute | solution.py:222
  32.7 0.9 collective-permute-start.5
  35.0 1.0 copy-done.10
  36.1 0.9 copy-done.12
  37.0 0.9 copy-done.29
  37.9 16.1 %group_attention.3 = (bf16[256,512]{1,0:T(8,128)(2,1)S(1)}, bf16[256,512]{1,0:T(8,128)(2,1)S(1)}, bf16[2,256,512]{2,1,0:T(8,128)(2,1)S(1)}, f32[1,512]{1,0:T(1,1...) custom-call(s32[4,11]{1,0:T(4,128)S(1)} %broadcast_select_fusion.10., ...), custom_call_target="tpu_custom_call" | custom-call | flops 4429185024 | bytes 6291456 | tf_op jit(solution)/shard_map/group_attention/pallas_call | solution.py:160
  60.5 1.6 collective-permute-start.26
  62.1 1.5 collective-permute-start.28
  65.4 16.3 %group_attention.2 = (bf16[256,512]{1,0:T(8,128)(2,1)S(1)}, bf16[256,512]{1,0:T(8,128)(2,1)S(1)}, bf16[2,256,512]{2,1,0:T(8,128)(2,1)S(1)}, f32[1,512]{1,0:T(1,1...) custom-call(s32[4,11]{1,0:T(4,128)S(1)} %copy-done.4, ...), custom_call_target="tpu_custom_call" | custom-call | flops 4429185024 | bytes 6291456 | tf_op jit(solution)/shard_map/group_attention/pallas_call | solution.py:160
  89.4 67.5 %all-gather = f32[32,1,16]{2,1,0:T(1,128)S(1)} all-gather(f32[1,1,16]{2,1,0:T(1,128)S(1)} %dynamic_update_slice.5), channel_id=1, replica_groups=mesh['ctx'=8,'batch'=4] {'ctx','batch'}, dimensions={0}, use_global_device_ids=true | all-gather | bytes 2112 | tf_op jit(solution)/shard_map/all_gather | solution.py:318
  157.6 2.9 %collective-permute-start.18 = (bf16[2,256,128]{2,1,0:T(8,128)(2,1)}, bf16[2,256,128]{2,1,0:T(8,128)(2,1)S(1)}, u32[]{:S(2)}, u32[]{:S(2)}) collective-permute-start(bf16[2,256,128]{2,1,0:T(8,128)(2,1)} %copy-done.30), channel_id=1, source_target_pairs={{0,4},{4,0},{8,12},{12,8},{16,20},{20,16},{24,28},{28,24},{1,5},{5... | collective-permute-start | bytes 393224 | tf_op jit(solution)/shard_map/ppermute | solution.py:222
  160.6 1.4 collective-permute-start.20
  162.0 2.0 %collective-permute-done.30 = bf16[2,256,128]{2,1,0:T(8,128)(2,1)S(1)} collective-permute-done((bf16[2,256,128]{2,1,0:T(8,128)(2,1)}, bf16[2,256,128]{2,1,0:T(8,128)(2,1)S(1)}, u32[]{:S(2)}, u32[]{:S(2)}) %collective-permute-start.30) | collective-permute-done | bytes 131104 | tf_op jit(solution)/shard_map/ppermute | solution.py:222
  164.0 1.6 collective-permute-start.21
  165.7 2.2 %collective-permute-start.22 = (bf16[2,256,128]{2,1,0:T(8,128)(2,1)}, bf16[2,256,128]{2,1,0:T(8,128)(2,1)S(1)}, u32[]{:S(2)}, u32[]{:S(2)}) collective-permute-start(bf16[2,256,128]{2,1,0:T(8,128)(2,1)} %copy-done.19), channel_id=1, source_target_pairs={{0,20},{4,16},{8,28},{12,24},{16,4},{20,0},{24,12},{28,8},{1,21},{... | collective-permute-start | bytes 393224 | tf_op jit(solution)/shard_map/ppermute | solution.py:222
  167.9 1.3 fusion.6
  170.1 1.3 fusion.8
  171.4 2.3 %collective-permute-start.17 = (bf16[2,256,512]{2,1,0:T(8,128)(2,1)S(1)}, bf16[2,256,512]{2,1,0:T(8,128)(2,1)S(1)}, u32[]{:S(2)}, u32[]{:S(2)}) collective-permute-start(bf16[2,256,512]{2,1,0:T(8,128)(2,1)S(1)} %copy-done.6), channel_id=1, source_target_pairs={{0,4},{4,0},{8,12},{12,8},{16,20},{20,16},{24,28},{28,24},{1,5},{5... | collective-permute-start | bytes 1572872 | tf_op jit(solution)/shard_map/ppermute | solution.py:222
  173.8 3.1 %collective-permute-done.22 = bf16[2,256,128]{2,1,0:T(8,128)(2,1)S(1)} collective-permute-done((bf16[2,256,128]{2,1,0:T(8,128)(2,1)}, bf16[2,256,128]{2,1,0:T(8,128)(2,1)S(1)}, u32[]{:S(2)}, u32[]{:S(2)}) %collective-permute-start.22) | collective-permute-done | bytes 131104 | tf_op jit(solution)/shard_map/ppermute | solution.py:222
  178.9 1.1 maximum_bitcast_fusion.1
  180.0 1.1 maximum_bitcast_fusion
  (182 shorter events, 33.0 us)
Async XLA Ops:
  2.7 18.2 %collective-permute-start.15 = (bf16[2,256,128]{2,1,0:T(8,128)(2,1)S(1)}, bf16[2,256,128]{2,1,0:T(8,128)(2,1)S(1)}, u32[]{:S(2)}, u32[]{:S(2)}) collective-permute-start(bf16[2,256,128]{2,1,0:T(8,128)(2,1)S(1)} %pad_maximum_fusion.4.refs_8_), channel_id=1, source_target_pairs={{0,24},{4,28},{8,16},{12,20},{16,8},{20,12},{24,0},{28,4},{1,25},{... | collective-permute-start | bytes 393224 | tf_op jit(solution)/shard_map/ppermute | solution.py:222
  6.6 14.3 %collective-permute-start.13 = (bf16[2,256,128]{2,1,0:T(8,128)(2,1)S(1)}, bf16[2,256,128]{2,1,0:T(8,128)(2,1)S(1)}, u32[]{:S(2)}, u32[]{:S(2)}) collective-permute-start(bf16[2,256,128]{2,1,0:T(8,128)(2,1)S(1)} %pad_maximum_fusion.4.refs_8_), channel_id=1, source_target_pairs={{0,16},{4,20},{8,24},{12,28},{16,0},{20,4},{24,8},{28,12},{1,17},{... | collective-permute-start | bytes 393224 | tf_op jit(solution)/shard_map/ppermute | solution.py:222
  7.1 14.0 %collective-permute-start.11 = (bf16[2,256,128]{2,1,0:T(8,128)(2,1)S(1)}, bf16[2,256,128]{2,1,0:T(8,128)(2,1)S(1)}, u32[]{:S(2)}, u32[]{:S(2)}) collective-permute-start(bf16[2,256,128]{2,1,0:T(8,128)(2,1)S(1)} %pad_maximum_fusion.4.refs_8_), channel_id=1, source_target_pairs={{0,8},{4,12},{8,0},{12,4},{16,24},{20,28},{24,16},{28,20},{1,9},{5... | collective-permute-start | bytes 393224 | tf_op jit(solution)/shard_map/ppermute | solution.py:222
  7.9 14.5 %collective-permute-start.16 = (bf16[2,256,128]{2,1,0:T(8,128)(2,1)}, bf16[2,256,128]{2,1,0:T(8,128)(2,1)S(1)}, u32[]{:S(2)}, u32[]{:S(2)}) collective-permute-start(bf16[2,256,128]{2,1,0:T(8,128)(2,1)} %pad_maximum_fusion.5), channel_id=1, source_target_pairs={{0,28},{4,24},{8,20},{12,16},{16,12},{20,8},{24,4},{28,0},{1,29},{... | collective-permute-start | bytes 393224 | tf_op jit(solution)/shard_map/ppermute | solution.py:222
  9.4 15.7 %collective-permute-start.14 = (bf16[2,256,128]{2,1,0:T(8,128)(2,1)}, bf16[2,256,128]{2,1,0:T(8,128)(2,1)}, u32[]{:S(2)}, u32[]{:S(2)}) collective-permute-start(bf16[2,256,128]{2,1,0:T(8,128)(2,1)} %pad_maximum_fusion.5), channel_id=1, source_target_pairs={{0,20},{4,16},{8,28},{12,24},{16,4},{20,0},{24,12},{28,8},{1,21},{... | collective-permute-start | bytes 393224 | tf_op jit(solution)/shard_map/ppermute | solution.py:222
  20.9 5.9 %collective-permute-start.12 = (bf16[2,256,128]{2,1,0:T(8,128)(2,1)}, bf16[2,256,128]{2,1,0:T(8,128)(2,1)S(1)}, u32[]{:S(2)}, u32[]{:S(2)}) collective-permute-start(bf16[2,256,128]{2,1,0:T(8,128)(2,1)} %pad_maximum_fusion.5), channel_id=1, source_target_pairs={{0,12},{4,8},{8,4},{12,0},{16,28},{20,24},{24,20},{28,16},{1,13},{... | collective-permute-start | bytes 393224 | tf_op jit(solution)/shard_map/ppermute | solution.py:222
  20.9 13.3 %collective-permute-start.9 = (bf16[2,256,512]{2,1,0:T(8,128)(2,1)}, bf16[2,256,512]{2,1,0:T(8,128)(2,1)S(1)}, u32[]{:S(2)}, u32[]{:S(2)}) collective-permute-start(bf16[2,256,512]{2,1,0:T(8,128)(2,1)} %pad_maximum_fusion.1), channel_id=1, source_target_pairs={{0,4},{4,0},{8,12},{12,8},{16,20},{20,16},{24,28},{28,24},{1,5},{5... | collective-permute-start | bytes 1572872 | tf_op jit(solution)/shard_map/ppermute | solution.py:222
  21.1 7.2 %collective-permute-start.10 = (bf16[2,256,128]{2,1,0:T(8,128)(2,1)}, bf16[2,256,128]{2,1,0:T(8,128)(2,1)}, u32[]{:S(2)}, u32[]{:S(2)}) collective-permute-start(bf16[2,256,128]{2,1,0:T(8,128)(2,1)} %pad_maximum_fusion.5), channel_id=1, source_target_pairs={{0,4},{4,0},{8,12},{12,8},{16,20},{20,16},{24,28},{28,24},{1,5},{5... | collective-permute-start | bytes 393224 | tf_op jit(solution)/shard_map/ppermute | solution.py:222
  22.4 7.6 %collective-permute-start.6 = (bf16[2,256,128]{2,1,0:T(8,128)(2,1)S(1)}, bf16[2,256,128]{2,1,0:T(8,128)(2,1)}, u32[]{:S(2)}, u32[]{:S(2)}) collective-permute-start(bf16[2,256,128]{2,1,0:T(8,128)(2,1)S(1)} %pad_maximum_fusion.2.refs_8_), channel_id=1, source_target_pairs={{0,24},{4,28},{8,16},{12,20},{16,8},{20,12},{24,0},{28,4},{1,25},{... | collective-permute-start | bytes 393224 | tf_op jit(solution)/shard_map/ppermute | solution.py:222
  25.0 7.7 %collective-permute-start.4 = (bf16[2,256,128]{2,1,0:T(8,128)(2,1)S(1)}, bf16[2,256,128]{2,1,0:T(8,128)(2,1)}, u32[]{:S(2)}, u32[]{:S(2)}) collective-permute-start(bf16[2,256,128]{2,1,0:T(8,128)(2,1)S(1)} %pad_maximum_fusion.2.refs_8_), channel_id=1, source_target_pairs={{0,16},{4,20},{8,24},{12,28},{16,0},{20,4},{24,8},{28,12},{1,17},{... | collective-permute-start | bytes 393224 | tf_op jit(solution)/shard_map/ppermute | solution.py:222
  27.4 6.2 %collective-permute-start.2 = (bf16[2,256,128]{2,1,0:T(8,128)(2,1)S(1)}, bf16[2,256,128]{2,1,0:T(8,128)(2,1)}, u32[]{:S(2)}, u32[]{:S(2)}) collective-permute-start(bf16[2,256,128]{2,1,0:T(8,128)(2,1)S(1)} %pad_maximum_fusion.2.refs_8_), channel_id=1, source_target_pairs={{0,8},{4,12},{8,0},{12,4},{16,24},{20,28},{24,16},{28,20},{1,9},{5... | collective-permute-start | bytes 393224 | tf_op jit(solution)/shard_map/ppermute | solution.py:222
  28.3 35.3 %collective-permute-start = (bf16[2,256,512]{2,1,0:T(8,128)(2,1)}, bf16[2,256,512]{2,1,0:T(8,128)(2,1)}, u32[]{:S(2)}, u32[]{:S(2)}) collective-permute-start(bf16[2,256,512]{2,1,0:T(8,128)(2,1)} %pad_maximum_fusion), channel_id=1, source_target_pairs={{0,4},{4,0},{8,12},{12,8},{16,20},{20,16},{24,28},{28,24},{1,5},{5... | collective-permute-start | bytes 1572872 | tf_op jit(solution)/shard_map/ppermute | solution.py:222
  30.0 30.0 %collective-permute-start.7 = (bf16[2,256,128]{2,1,0:T(8,128)(2,1)}, bf16[2,256,128]{2,1,0:T(8,128)(2,1)}, u32[]{:S(2)}, u32[]{:S(2)}) collective-permute-start(bf16[2,256,128]{2,1,0:T(8,128)(2,1)} %pad_maximum_fusion.3), channel_id=1, source_target_pairs={{0,28},{4,24},{8,20},{12,16},{16,12},{20,8},{24,4},{28,0},{1,29},{... | collective-permute-start | bytes 393224 | tf_op jit(solution)/shard_map/ppermute | solution.py:222
  32.7 27.8 %collective-permute-start.5 = (bf16[2,256,128]{2,1,0:T(8,128)(2,1)}, bf16[2,256,128]{2,1,0:T(8,128)(2,1)}, u32[]{:S(2)}, u32[]{:S(2)}) collective-permute-start(bf16[2,256,128]{2,1,0:T(8,128)(2,1)} %pad_maximum_fusion.3), channel_id=1, source_target_pairs={{0,20},{4,16},{8,28},{12,24},{16,4},{20,0},{24,12},{28,8},{1,21},{... | collective-permute-start | bytes 393224 | tf_op jit(solution)/shard_map/ppermute | solution.py:222
  33.6 28.5 %collective-permute-start.3 = (bf16[2,256,128]{2,1,0:T(8,128)(2,1)}, bf16[2,256,128]{2,1,0:T(8,128)(2,1)}, u32[]{:S(2)}, u32[]{:S(2)}) collective-permute-start(bf16[2,256,128]{2,1,0:T(8,128)(2,1)} %pad_maximum_fusion.3), channel_id=1, source_target_pairs={{0,12},{4,8},{8,4},{12,0},{16,28},{20,24},{24,20},{28,16},{1,13},{... | collective-permute-start | bytes 393224 | tf_op jit(solution)/shard_map/ppermute | solution.py:222
  35.0 27.1 %collective-permute-start.1 = (bf16[2,256,128]{2,1,0:T(8,128)(2,1)}, bf16[2,256,128]{2,1,0:T(8,128)(2,1)}, u32[]{:S(2)}, u32[]{:S(2)}) collective-permute-start(bf16[2,256,128]{2,1,0:T(8,128)(2,1)} %pad_maximum_fusion.3), channel_id=1, source_target_pairs={{0,4},{4,0},{8,12},{12,8},{16,20},{20,16},{24,28},{28,24},{1,5},{5... | collective-permute-start | bytes 393224 | tf_op jit(solution)/shard_map/ppermute | solution.py:222
  60.0 97.0 %collective-permute-start.25 = (bf16[2,256,128]{2,1,0:T(8,128)(2,1)}, bf16[2,256,128]{2,1,0:T(8,128)(2,1)}, u32[]{:S(2)}, u32[]{:S(2)}) collective-permute-start(bf16[2,256,128]{2,1,0:T(8,128)(2,1)} %copy-done.27), channel_id=1, source_target_pairs={{0,4},{4,0},{8,12},{12,8},{16,20},{20,16},{24,28},{28,24},{1,5},{5... | collective-permute-start | bytes 393224 | tf_op jit(solution)/shard_map/ppermute | solution.py:222
  60.5 96.5 %collective-permute-start.26 = (bf16[2,256,128]{2,1,0:T(8,128)(2,1)}, bf16[2,256,128]{2,1,0:T(8,128)(2,1)}, u32[]{:S(2)}, u32[]{:S(2)}) collective-permute-start(bf16[2,256,128]{2,1,0:T(8,128)(2,1)} %copy-done.25), channel_id=1, source_target_pairs={{0,8},{4,12},{8,0},{12,4},{16,24},{20,28},{24,16},{28,20},{1,9},{5... | collective-permute-start | bytes 393224 | tf_op jit(solution)/shard_map/ppermute | solution.py:222
  62.1 95.6 %collective-permute-start.27 = (bf16[2,256,128]{2,1,0:T(8,128)(2,1)}, bf16[2,256,128]{2,1,0:T(8,128)(2,1)}, u32[]{:S(2)}, u32[]{:S(2)}) collective-permute-start(bf16[2,256,128]{2,1,0:T(8,128)(2,1)} %copy-done.24), channel_id=1, source_target_pairs={{0,12},{4,8},{8,4},{12,0},{16,28},{20,24},{24,20},{28,16},{1,13},{... | collective-permute-start | bytes 393224 | tf_op jit(solution)/shard_map/ppermute | solution.py:222
  62.1 98.5 %collective-permute-start.28 = (bf16[2,256,128]{2,1,0:T(8,128)(2,1)}, bf16[2,256,128]{2,1,0:T(8,128)(2,1)}, u32[]{:S(2)}, u32[]{:S(2)}) collective-permute-start(bf16[2,256,128]{2,1,0:T(8,128)(2,1)} %copy-done.22), channel_id=1, source_target_pairs={{0,16},{4,20},{8,24},{12,28},{16,0},{20,4},{24,8},{28,12},{1,17},{... | collective-permute-start | bytes 393224 | tf_op jit(solution)/shard_map/ppermute | solution.py:222
  63.6 97.0 %collective-permute-start.29 = (bf16[2,256,128]{2,1,0:T(8,128)(2,1)}, bf16[2,256,128]{2,1,0:T(8,128)(2,1)}, u32[]{:S(2)}, u32[]{:S(2)}) collective-permute-start(bf16[2,256,128]{2,1,0:T(8,128)(2,1)} %copy-done.20), channel_id=1, source_target_pairs={{0,20},{4,16},{8,28},{12,24},{16,4},{20,0},{24,12},{28,8},{1,21},{... | collective-permute-start | bytes 393224 | tf_op jit(solution)/shard_map/ppermute | solution.py:222
  157.0 7.1 %collective-permute-start.30 = (bf16[2,256,128]{2,1,0:T(8,128)(2,1)}, bf16[2,256,128]{2,1,0:T(8,128)(2,1)S(1)}, u32[]{:S(2)}, u32[]{:S(2)}) collective-permute-start(bf16[2,256,128]{2,1,0:T(8,128)(2,1)} %copy-done.16), channel_id=1, source_target_pairs={{0,24},{4,28},{8,16},{12,20},{16,8},{20,12},{24,0},{28,4},{1,25},{... | collective-permute-start | bytes 393224 | tf_op jit(solution)/shard_map/ppermute | solution.py:222
  157.1 8.6 %collective-permute-start.31 = (bf16[2,256,128]{2,1,0:T(8,128)(2,1)}, bf16[2,256,128]{2,1,0:T(8,128)(2,1)S(1)}, u32[]{:S(2)}, u32[]{:S(2)}) collective-permute-start(bf16[2,256,128]{2,1,0:T(8,128)(2,1)} %copy-done.13), channel_id=1, source_target_pairs={{0,28},{4,24},{8,20},{12,16},{16,12},{20,8},{24,4},{28,0},{1,29},{... | collective-permute-start | bytes 393224 | tf_op jit(solution)/shard_map/ppermute | solution.py:222
  157.6 11.6 %collective-permute-start.18 = (bf16[2,256,128]{2,1,0:T(8,128)(2,1)}, bf16[2,256,128]{2,1,0:T(8,128)(2,1)S(1)}, u32[]{:S(2)}, u32[]{:S(2)}) collective-permute-start(bf16[2,256,128]{2,1,0:T(8,128)(2,1)} %copy-done.30), channel_id=1, source_target_pairs={{0,4},{4,0},{8,12},{12,8},{16,20},{20,16},{24,28},{28,24},{1,5},{5... | collective-permute-start | bytes 393224 | tf_op jit(solution)/shard_map/ppermute | solution.py:222
  160.6 8.9 %collective-permute-start.19 = (bf16[2,256,128]{2,1,0:T(8,128)(2,1)}, bf16[2,256,128]{2,1,0:T(8,128)(2,1)S(1)}, u32[]{:S(2)}, u32[]{:S(2)}) collective-permute-start(bf16[2,256,128]{2,1,0:T(8,128)(2,1)} %copy-done.26), channel_id=1, source_target_pairs={{0,8},{4,12},{8,0},{12,4},{16,24},{20,28},{24,16},{28,20},{1,9},{5... | collective-permute-start | bytes 393224 | tf_op jit(solution)/shard_map/ppermute | solution.py:222
  160.6 10.8 %collective-permute-start.20 = (bf16[2,256,128]{2,1,0:T(8,128)(2,1)}, bf16[2,256,128]{2,1,0:T(8,128)(2,1)S(1)}, u32[]{:S(2)}, u32[]{:S(2)}) collective-permute-start(bf16[2,256,128]{2,1,0:T(8,128)(2,1)} %copy-done.23), channel_id=1, source_target_pairs={{0,12},{4,8},{8,4},{12,0},{16,28},{20,24},{24,20},{28,16},{1,13},{... | collective-permute-start | bytes 393224 | tf_op jit(solution)/shard_map/ppermute | solution.py:222
  164.0 9.7 %collective-permute-start.21 = (bf16[2,256,128]{2,1,0:T(8,128)(2,1)}, bf16[2,256,128]{2,1,0:T(8,128)(2,1)S(1)}, u32[]{:S(2)}, u32[]{:S(2)}) collective-permute-start(bf16[2,256,128]{2,1,0:T(8,128)(2,1)} %copy-done.21), channel_id=1, source_target_pairs={{0,16},{4,20},{8,24},{12,28},{16,0},{20,4},{24,8},{28,12},{1,17},{... | collective-permute-start | bytes 393224 | tf_op jit(solution)/shard_map/ppermute | solution.py:222
  165.7 11.3 %collective-permute-start.22 = (bf16[2,256,128]{2,1,0:T(8,128)(2,1)}, bf16[2,256,128]{2,1,0:T(8,128)(2,1)S(1)}, u32[]{:S(2)}, u32[]{:S(2)}) collective-permute-start(bf16[2,256,128]{2,1,0:T(8,128)(2,1)} %copy-done.19), channel_id=1, source_target_pairs={{0,20},{4,16},{8,28},{12,24},{16,4},{20,0},{24,12},{28,8},{1,21},{... | collective-permute-start | bytes 393224 | tf_op jit(solution)/shard_map/ppermute | solution.py:222
  169.3 7.7 %collective-permute-start.23 = (bf16[2,256,128]{2,1,0:T(8,128)(2,1)S(1)}, bf16[2,256,128]{2,1,0:T(8,128)(2,1)S(1)}, u32[]{:S(2)}, u32[]{:S(2)}) collective-permute-start(bf16[2,256,128]{2,1,0:T(8,128)(2,1)S(1)} %copy-done.18), channel_id=1, source_target_pairs={{0,24},{4,28},{8,16},{12,20},{16,8},{20,12},{24,0},{28,4},{1,25},{... | collective-permute-start | bytes 393224 | tf_op jit(solution)/shard_map/ppermute | solution.py:222
  169.5 7.4 %collective-permute-start.24 = (bf16[2,256,128]{2,1,0:T(8,128)(2,1)S(1)}, bf16[2,256,128]{2,1,0:T(8,128)(2,1)S(1)}, u32[]{:S(2)}, u32[]{:S(2)}) collective-permute-start(bf16[2,256,128]{2,1,0:T(8,128)(2,1)S(1)} %copy-done.15), channel_id=1, source_target_pairs={{0,28},{4,24},{8,20},{12,16},{16,12},{20,8},{24,4},{28,0},{1,29},{... | collective-permute-start | bytes 393224 | tf_op jit(solution)/shard_map/ppermute | solution.py:222
  171.4 7.3 %collective-permute-start.17 = (bf16[2,256,512]{2,1,0:T(8,128)(2,1)S(1)}, bf16[2,256,512]{2,1,0:T(8,128)(2,1)S(1)}, u32[]{:S(2)}, u32[]{:S(2)}) collective-permute-start(bf16[2,256,512]{2,1,0:T(8,128)(2,1)S(1)} %copy-done.6), channel_id=1, source_target_pairs={{0,4},{4,0},{8,12},{12,8},{16,20},{20,16},{24,28},{28,24},{1,5},{5... | collective-permute-start | bytes 1572872 | tf_op jit(solution)/shard_map/ppermute | solution.py:222
  173.7 5.1 %collective-permute-start.8 = (bf16[2,256,512]{2,1,0:T(8,128)(2,1)S(1)}, bf16[2,256,512]{2,1,0:T(8,128)(2,1)S(1)}, u32[]{:S(2)}, u32[]{:S(2)}) collective-permute-start(bf16[2,256,512]{2,1,0:T(8,128)(2,1)S(1)} %copy-done.8), channel_id=1, source_target_pairs={{0,4},{4,0},{8,12},{12,8},{16,20},{20,16},{24,28},{28,24},{1,5},{5... | collective-permute-start | bytes 1572872 | tf_op jit(solution)/shard_map/ppermute | solution.py:222
  (35 other events, 281.6 us)

commit v2 on v1

v2 whole, which is shorter than its diff:
```python
import functools
import math

import jax
import jax.numpy as jnp
from jax import lax
from jax.experimental import pallas as pl
from jax.experimental.pallas import tpu as pltpu
from jax.sharding import PartitionSpec as P

HEADS = 16
KV_HEADS = 4
HD = 128
BLOCK = 128
QPG = HEADS // KV_HEADS
ROWS = QPG * BLOCK
STRIDES = (2, 3)
CHUNK = 3
LOG2E = math.log2(math.e)
NEVER = -1e30


def distinct_offsets(block_count, listed_count):
    tables = []
    for stride in STRIDES:
        steps = range(1, (listed_count - 3) // 2 + 1)
        listed = [-1, 0, 1] + [stride * m for m in steps] + [-stride * m for m in steps]
        times = {}
        for o in listed:
            times[o % block_count] = times.get(o % block_count, 0) + 1
        tables.append(sorted(times.items()))
    most = max(len(t) for t in tables)
    return [t + [(0, 0)] * (most - len(t)) for t in tables]


def nt(a, b):
    return jnp.dot(a, b, preferred_element_type=jnp.float32)


def group_kernel(gi, devices, local_blocks, listed, offsets, *refs):
    place, strides, taus = refs[:3]
    q_own, q_sib, g_own, g_sib, kv_in, tau_in = refs[3:9]
    att_own, dq_own, sib_out, tau_out, kv_out = refs[9:14]
    k_s, v_s, kt_s, vt_s, dk_s, dv_s, s_s, e_s, dp_s, p_s, ds_s, tau_s = refs[14:]
    unit = pl.program_id(0)
    blocks = devices * local_blocks
    me = place[0]
    core = me % 2
    group = 2 * core + gi

    @pl.when(unit == 0)
    def _():
        def fill(b, carry):
            for half in range(local_blocks):
                rows = slice(half * BLOCK, (half + 1) * BLOCK)
                k_block = kv_in[b, 0, rows, :]
                v_block = kv_in[b, 1, rows, :]
                at = b * local_blocks + half
                k_s[at] = k_block
                v_s[at] = v_block
                kt_s[at] = k_block.T
                vt_s[at] = v_block.T
            return carry

        lax.fori_loop(0, devices, fill, 0, unroll=2)
        dk_s[...] = jnp.zeros_like(dk_s)
        dv_s[...] = jnp.zeros_like(dv_s)
        tau_s[...] = jnp.zeros_like(tau_s)

    own = unit < local_blocks
    q_here = jnp.where(own, q_own[...], q_sib[0])
    g_here = jnp.where(own, g_own[...], g_sib[0])

    def per_head(x):
        return [x[:, h * HD : (h + 1) * HD] for h in range(QPG)]

    q_rows = jnp.concatenate(per_head(q_here), axis=0)
    g_rows = jnp.concatenate(per_head(g_here), axis=0)
    q_t = jnp.concatenate([x.T for x in per_head(q_here)], axis=1)
    g_t = jnp.concatenate([x.T for x in per_head(g_here)], axis=1)
    scale = jnp.concatenate(
        [jnp.full((1, BLOCK), taus[group * QPG + h], jnp.float32) for h in range(QPG)], axis=1
    ) / math.sqrt(HD)
    factor = scale * LOG2E

    query_block = (me ^ (unit // local_blocks)) * local_blocks + unit % local_blocks
    wide = strides[group * blocks + query_block] == STRIDES[1]
    ids, bias = [], []
    for (narrow_off, narrow_times), (wide_off, wide_times) in zip(*offsets):
        ids.append((query_block + jnp.where(wide, wide_off, narrow_off)) % blocks)
        bias.append(
            times_bias(narrow_times)
            if narrow_times == wide_times
            else jnp.where(wide, times_bias(wide_times), times_bias(narrow_times))
        )
    chunks = [range(c, min(c + CHUNK, listed)) for c in range(0, listed, CHUNK)]

    def rows_of(c):
        return slice(c[0] * BLOCK, (c[-1] + 1) * BLOCK)

    most = None
    for c in chunks:
        raw = nt(jnp.concatenate([k_s[ids[j]] for j in c], axis=0), q_t)
        s_s[rows_of(c), :] = raw
        top = jnp.max(raw.reshape(-1, 8, ROWS), axis=0)
        most = top if most is None else jnp.maximum(most, top)
    top_row = jnp.max(most, axis=0, keepdims=True) * factor

    total = jnp.zeros((8, ROWS), jnp.float32)
    for c in chunks:
        dp_s[rows_of(c), :] = nt(jnp.concatenate([v_s[ids[j]] for j in c], axis=0), g_t)
        for j in c:
            rows = slice(j * BLOCK, (j + 1) * BLOCK)
            e = jnp.exp2(s_s[rows, :] * factor - (top_row - bias[j]))
            e_s[rows, :] = e
            total = total + jnp.sum(e.reshape(-1, 8, ROWS), axis=0)
    inverse = 1.0 / jnp.sum(total, axis=0, keepdims=True)

    for c in chunks:
        probs = (e_s[rows_of(c), :] * inverse).astype(jnp.bfloat16)
        p_s[rows_of(c), :] = probs
        part = nt(probs, g_rows)
        for n, j in enumerate(c):
            dv_s[ids[j]] += part[n * BLOCK : (n + 1) * BLOCK, :]
    o_t = nt(jnp.concatenate([vt_s[s] for s in ids], axis=1), p_s[...])
    row_dot = jnp.sum(g_t.astype(jnp.float32) * o_t, axis=0, keepdims=True)

    weight_scale = inverse * scale
    tau_rows = jnp.zeros((8, ROWS), jnp.float32)
    for c in chunks:
        scaled = e_s[rows_of(c), :] * weight_scale * (dp_s[rows_of(c), :] - row_dot)
        tau_rows = tau_rows + jnp.sum((scaled * s_s[rows_of(c), :]).reshape(-1, 8, ROWS), axis=0)
        low = scaled.astype(jnp.bfloat16)
        ds_s[rows_of(c), :] = low
        part = nt(low, q_rows)
        for n, j in enumerate(c):
            dk_s[ids[j]] += part[n * BLOCK : (n + 1) * BLOCK, :]
    dq_t = nt(jnp.concatenate([kt_s[s] for s in ids], axis=1), ds_s[...])
    tau_s[...] += tau_rows

    def back(x):
        low = x.astype(jnp.bfloat16)
        return jnp.concatenate([y.T for y in per_head(low)], axis=1)

    att = back(o_t)
    dq = back(dq_t)

    @pl.when(own)
    def _():
        att_own[...] = att
        dq_own[...] = dq

    @pl.when(jnp.logical_not(own))
    def _():
        sib_out[0] = att
        sib_out[1] = dq

    @pl.when(unit == 2 * local_blocks - 1)
    def _():
        def drain(b, carry):
            for half in range(local_blocks):
                rows = slice(half * BLOCK, (half + 1) * BLOCK)
                at = b * local_blocks + half
                kv_out[b, 0, rows, :] = dk_s[at].astype(jnp.bfloat16)
                kv_out[b, 1, rows, :] = dv_s[at].astype(jnp.bfloat16)
            return carry

        lax.fori_loop(0, devices, drain, 0, unroll=2)
        lane = lax.broadcasted_iota(jnp.int32, (8, HD), 1)
        sums = tau_in[...]
        for h in range(QPG):
            head = group * QPG + h
            share = jnp.sum(tau_s[:, h * BLOCK : (h + 1) * BLOCK]) / taus[head]
            sums = sums + jnp.where(lane == head, share, 0.0)
        tau_out[...] = sums


def times_bias(times):
    return math.log2(times) if times else NEVER


def run_group(gi, devices, place, strides, tau, queries, out_grad, qg_sib, kv_in, tau_in, offsets):
    listed = len(offsets[0])
    tokens = queries.shape[0]
    local_blocks = tokens // BLOCK
    units = 2 * local_blocks
    blocks = devices * local_blocks
    width = QPG * HD
    last = local_blocks - 1
    mine = lambda u, p, s, t: (jnp.minimum(u, last), 2 * (p[0] % 2) + gi)
    qs = pl.BlockSpec((1, BLOCK, width), lambda u, p, s, t: (0, jnp.maximum(u - local_blocks, 0), gi))
    gs = pl.BlockSpec((1, BLOCK, width), lambda u, p, s, t: (1, jnp.maximum(u - local_blocks, 0), gi))
    block_own = pl.BlockSpec((BLOCK, width), mine)
    out_own = pl.BlockSpec((BLOCK, width), lambda u, p, s, t: (jnp.minimum(u, last), 0))
    out_sib = pl.BlockSpec((2, BLOCK, width), lambda u, p, s, t: (0, jnp.maximum(u - local_blocks, 0), 0))
    kv_all = pl.BlockSpec((devices, 2, tokens, HD), lambda u, p, s, t: (0, 0, 0, 0))
    small = pl.BlockSpec((8, HD), lambda u, p, s, t: (0, 0))
    bf = lambda *shape: jax.ShapeDtypeStruct(shape, jnp.bfloat16)
    keys_wide = listed * BLOCK
    macs = units * ROWS * keys_wide * HD * 6
    return pl.pallas_call(
        functools.partial(group_kernel, gi, devices, local_blocks, listed, offsets),
        grid_spec=pltpu.PrefetchScalarGridSpec(
            num_scalar_prefetch=3,
            grid=(units,),
            in_specs=[block_own, qs, block_own, gs, kv_all, small],
            out_specs=[out_own, out_own, out_sib, small, kv_all],
            scratch_shapes=[pltpu.VMEM((blocks, BLOCK, HD), jnp.bfloat16)] * 4
            + [pltpu.VMEM((blocks, BLOCK, HD), jnp.float32)] * 2
            + [pltpu.VMEM((keys_wide, ROWS), jnp.float32)] * 3
            + [pltpu.VMEM((keys_wide, ROWS), jnp.bfloat16)] * 2
            + [pltpu.VMEM((8, ROWS), jnp.float32)],
        ),
        out_shape=[bf(tokens, width), bf(tokens, width), bf(2, tokens, width)]
        + [jax.ShapeDtypeStruct((8, HD), jnp.float32), bf(devices, 2, tokens, HD)],
        compiler_params=pltpu.CompilerParams(
            dimension_semantics=("arbitrary",), vmem_limit_bytes=60 * 2**20
        ),
        cost_estimate=pl.CostEstimate(
            flops=2 * macs, bytes_accessed=6 * 2**20, transcendentals=units * ROWS * keys_wide
        ),
        name="group_attention",
    )(place, strides, tau, queries, qg_sib, out_grad, qg_sib, kv_in, tau_in)


def total_over(x, axis):
    size = lax.axis_size(axis)
    if size & (size - 1):
        return lax.psum(x, axis)

    def partner(distance):
        return lax.ppermute(x, axis, [(i, i ^ distance) for i in range(size)])

    step = 1
    while step < size:
        if size // step % 4 == 0 and size // step != 8:
            x = (x + partner(step)) + (partner(2 * step) + partner(3 * step))
            step *= 4
        else:
            x = x + partner(step)
            step *= 2
    return x


def body(queries, keys, values, tau, out_grad, key_blocks):
    ctx = lax.axis_size("ctx")
    me = lax.axis_index("ctx").astype(jnp.int32)
    core = me % 2
    tokens = queries.shape[1]
    local_blocks = tokens // BLOCK
    block_count = ctx * local_blocks
    listed_count = key_blocks.shape[2]
    offsets = distinct_offsets(block_count, listed_count)
    swap = [(d, d ^ 1) for d in range(ctx)]
    wide = 2 * QPG * HD

    q0, k0, v0, g0 = queries[0], keys[0], values[0], out_grad[0]
    place = me[None]
    strides = ((key_blocks[:, :, 3] - jnp.arange(block_count, dtype=jnp.int32)) % block_count).reshape(-1)

    def kv_for(gi):
        halves = [
            jnp.stack([x[:, g * HD : (g + 1) * HD] for x in (k0, v0)]) for g in (gi, 2 + gi)
        ]
        return lax.all_to_all(jnp.stack(halves * (ctx // 2)), "ctx", 0, 0)

    def theirs(x):
        return lax.dynamic_slice_in_dim(x, (1 - core) * wide, wide, 1)

    kv_in = [kv_for(gi) for gi in range(2)]
    qg_sib = lax.ppermute(jnp.stack([theirs(q0), theirs(g0)]), "ctx", swap)

    att_parts, dq_parts, grads = [], [], []
    tau_rows = jnp.zeros((8, HD), jnp.float32)
    for gi in range(2):
        att_own, dq_own, sib, tau_rows, kv_grads = run_group(
            gi, ctx, place, strides, tau, q0, g0, qg_sib, kv_in[gi], tau_rows, offsets
        )
        sib = lax.ppermute(sib, "ctx", swap)
        att_parts.append((att_own, sib[0]))
        dq_parts.append((dq_own, sib[1]))
        grads.append(lax.all_to_all(kv_grads, "ctx", 0, 0))

    def by_group(parts):
        return jnp.concatenate(
            [jnp.where(core == c // 2, parts[c % 2][0], parts[c % 2][1]) for c in range(4)], axis=1
        )

    attended = by_group(att_parts)[None]
    query_grad = by_group(dq_parts)[None]

    def summed(which):
        cols = []
        for c in range(4):
            total = None
            for src in range(c // 2, ctx, 2):
                term = grads[c % 2][src, which].astype(jnp.float32)
                total = term if total is None else total + term
            cols.append(total.astype(jnp.bfloat16))
        return jnp.concatenate(cols, axis=1)[None]

    key_grad, value_grad = summed(0), summed(1)
    scale_total = total_over(total_over(tau_rows, "ctx"), "batch")[0, :HEADS]
    tau_grad = scale_total / math.sqrt(lax.axis_size("batch") * ctx * tokens)
    return (attended, query_grad, key_grad, value_grad, tau_grad)


def solution(mesh):
    rows = P("batch", "ctx", None)
    return jax.shard_map(
        body,
        mesh=mesh,
        in_specs=(rows, rows, rows, P(), rows, P()),
        out_specs=(rows, rows, rows, rows, P()),
        check_vma=False,
    )
```

time: 182 us -> 119 us (0.65)
  blocking collectives: 67.5 us -> 0 us
  waiting for transfers between devices: 7.22 us -> 31.9 us
  local copies, waits for them, and re-layouts: 22.9 us -> 2.97 us
  Pallas kernels: 32.4 us -> 38.8 us
  starting transfers between devices: 30.6 us -> 26.2 us
    all_gather x1 -> x0, blocking collectives: 67.5 us -> none  [body(): scale_total = jnp.sum(lax.all_gather(placed, ('ctx', 'batch')), axis=0)]
    all_to_all x0 -> x4, waiting for transfers between devices: none -> 25.7 us  [the longest x2 16.4 us: body(): grads.append(lax.all_to_all(kv_grads, 'ctx', 0, 0))]
    ppermute x32 -> x10, starting transfers between devices: 30.6 us -> 9.47 us  [the longest x7 8.4 us: partner(): return lax.ppermute(x, axis, [(i, i ^ distance) for i in range(size)])]
    all_to_all x0 -> x4, starting transfers between devices: none -> 16.7 us  [the longest x2 8.86 us: kv_for(): return lax.all_to_all(jnp.stack(halves * (ctx // 2)), 'ctx', 0, 0)]
    unnamed x71 -> x16, local copies, waits for them, and re-layouts: 17 us -> 0.99 us
    unnamed x1 -> x14, other arithmetic: 0.08 us -> 9.29 us
    pallas_call x2, Pallas kernels: 32.4 us -> 38.8 us  [run_group(): pl.pallas_call(functools.partial(group_kernel, gi, devices, local_blocks,...]
    reduce_sum x8 -> x0, other arithmetic: 3.62 us -> none  [the longest x2 1.48 us: body(): tau_parts.append(jnp.sum(tau_rows.reshape(QPG, BLOCK), axis=1) / tau_group)]
  transfers between devices with their start and end apart: 32 -> 14, of which waited for: 6 -> 6; matrix products, arithmetic and copies ran while one was open for 12% -> 9% of each run, Pallas kernels for 18% -> 16%
where the time goes in v2:
time: 119 us; the launch traced here: 118 us
  Pallas kernels  38.8 us (33%)
  waiting for transfers between devices  31.9 us (27%)
  starting transfers between devices  26.2 us (22%)
  other arithmetic  17.7 us (15%)
  local copies, waits for them, and re-layouts  2.97 us (2%)
    pallas_call x2, Pallas kernels, run_group(): pl.pallas_call(functools.partial(group_kernel, gi, devices, local_blocks,...  38.8 us
    all_to_all x2, waiting for transfers between devices, body(): grads.append(lax.all_to_all(kv_grads, 'ctx', 0, 0))  16.4 us
    all_to_all x2, waiting for transfers between devices, kv_for(): return lax.all_to_all(jnp.stack(halves * (ctx // 2)), 'ctx', 0, 0)  9.31 us
    unnamed x14, other arithmetic  9.29 us
    all_to_all x2, starting transfers between devices, kv_for(): return lax.all_to_all(jnp.stack(halves * (ctx // 2)), 'ctx', 0, 0)  8.86 us
    ppermute x7, starting transfers between devices, partner(): return lax.ppermute(x, axis, [(i, i ^ distance) for i in range(size)])  8.4 us
    all_to_all x2, starting transfers between devices, body(): grads.append(lax.all_to_all(kv_grads, 'ctx', 0, 0))  7.89 us
    ppermute x7, waiting for transfers between devices, partner(): return lax.ppermute(x, axis, [(i, i ^ distance) for i in range(size)])  6.22 us
  transfers between devices with their start and end apart: 14, of which 6 were waited for; matrix products, arithmetic and copies ran while one was open for 9% of the time, Pallas kernels for 16%

profile of v2, /device:TPU:0, one launch (start us, length us, event | category | flops | bytes accessed | tf_op | source)
XLA Modules:
  0.0 118.4 jit_solution(11635435260030469810)
XLA Ops:
  0.6 1.1 slice_bitcast_fusion.8
  1.8 0.7 constant_dynamic-update-slice_fusion.7
  2.4 0.7 constant_dynamic-update-slice_fusion.6
  3.1 0.7 constant_dynamic-update-slice_fusion.5
  3.7 0.7 constant_dynamic-update-slice_fusion.4
  4.4 0.7 constant_dynamic-update-slice_fusion.3
  5.1 0.7 constant_dynamic-update-slice_fusion.2
  5.7 0.7 constant_dynamic-update-slice_fusion.1
  6.4 0.7 constant_dynamic-update-slice_fusion
  7.1 5.3 %all-to-all-start = ((bf16[8,2,256,128]{3,2,1,0:T(8,128)(2,1)}), bf16[8,2,256,128]{3,2,1,0:T(8,128)(2,1)S(1)}, u32[]{:S(2)}, u32[]{:S(2)}) async-start(bf16[8,2,256,128]{3,2,1,0:T(8,128)(2,1)} %constant_dynamic-update-slice_fusion), calls=%async_computation | async-start | bytes 2097152 | tf_op jit(solution)/shard_map/all_to_all | solution.py:265
  18.5 9.3 %all-to-all-done.refs_7_ = bf16[8,2,256,128]{3,2,1,0:T(8,128)(2,1)S(1)} async-done(((bf16[8,2,256,128]{3,2,1,0:T(8,128)(2,1)}), bf16[8,2,256,128]{3,2,1,0:T(8,128)(2,1)S(1)}, u32[]{:S(2)}, u32[]{:S(2)}) %all-to-all-start) | async-done | bytes 1048608 | tf_op jit(solution)/shard_map/all_to_all | solution.py:265
  27.8 3.6 %all-to-all-start.1 = ((bf16[8,2,256,128]{3,2,1,0:T(8,128)(2,1)}), bf16[8,2,256,128]{3,2,1,0:T(8,128)(2,1)S(1)}, u32[]{:S(2)}, u32[]{:S(2)}) async-start(bf16[8,2,256,128]{3,2,1,0:T(8,128)(2,1)} %constant_dynamic-update-slice_fusion.8), calls=%async_computation.1 | async-start | bytes 2097152 | tf_op jit(solution)/shard_map/all_to_all | solution.py:265
  32.7 19.4 %group_attention.2 = (bf16[256,512]{1,0:T(8,128)(2,1)}, bf16[256,512]{1,0:T(8,128)(2,1)}, bf16[2,256,512]{2,1,0:T(8,128)(2,1)}, f32[8,128]{1,0:T(8,128)}, bf16[8,2,256,128]{3,2,1,0:T(8,128)(2,1)}) custom-call(s32[1]{0:T(128)} %bitcast.refs_0_, s32[64]{0:T(128)} %and_select_fusion.refs_1_, f32[16]{0:T(128)} %refs_2_.3, bf16[256,2048]{1,0:T(8,128)(2,1)} %bitcast.113, ...), custom_call_target="tpu_custom_call" | custom-call | flops 4429185024 | bytes 6291456 | tf_op jit(solution)/shard_map/group_attention/pallas_call | solution.py:201
  52.1 1.0 copy-done.1
  53.1 19.4 %group_attention.3 = (bf16[256,512]{1,0:T(8,128)(2,1)}, bf16[256,512]{1,0:T(8,128)(2,1)}, bf16[2,256,512]{2,1,0:T(8,128)(2,1)}, f32[8,128]{1,0:T(8,128)}, bf16[8,2,256,128]{3,2,1,0:T(8,128)(2,1)}) custom-call(s32[1]{0:T(128)} %bitcast.refs_0_, s32[64]{0:T(128)} %and_select_fusion.refs_1_, f32[16]{0:T(128)} %refs_2_.3, bf16[256,2048]{1,0:T(8,128)(2,1)} %bitcast.114, ...), custom_call_target="tpu_custom_call" | custom-call | flops 4429185024 | bytes 6291456 | tf_op jit(solution)/shard_map/group_attention/pallas_call | solution.py:201
  72.9 1.0 collective-permute-done.3
  74.0 0.7 add.183
  74.7 1.9 %collective-permute-start.4 = (f32[8,128]{1,0:T(8,128)S(1)}, f32[8,128]{1,0:T(8,128)S(1)}, u32[]{:S(2)}, u32[]{:S(2)}) collective-permute-start(f32[8,128]{1,0:T(8,128)S(1)} %add.183), channel_id=1, source_target_pairs={{0,8},{4,12},{8,0},{12,4},{16,24},{20,28},{24,16},{28,20},{1,9},{5... | collective-permute-start | bytes 12296 | tf_op jit(solution)/shard_map/ppermute | solution.py:232
  76.5 1.5 %collective-permute-start.5 = (f32[8,128]{1,0:T(8,128)S(1)}, f32[8,128]{1,0:T(8,128)S(1)}, u32[]{:S(2)}, u32[]{:S(2)}) collective-permute-start(f32[8,128]{1,0:T(8,128)S(1)} %add.183), channel_id=1, source_target_pairs={{0,16},{4,20},{8,24},{12,28},{16,0},{20,4},{24,8},{28,12},{1,17},{... | collective-permute-start | bytes 12296 | tf_op jit(solution)/shard_map/ppermute | solution.py:232
  78.2 4.2 %all-to-all-start.3 = ((bf16[8,2,256,128]{3,2,1,0:T(8,128)(2,1)}), bf16[8,2,256,128]{3,2,1,0:T(8,128)(2,1)S(1)}, u32[]{:S(2)}, u32[]{:S(2)}) async-start(bf16[8,2,256,128]{3,2,1,0:T(8,128)(2,1)} %get-tuple-element.23), calls=%async_computation.3 | async-start | bytes 2097152 | tf_op jit(solution)/shard_map/all_to_all | solution.py:282
  82.9 1.6 %collective-permute-start.7 = (f32[8,128]{1,0:T(8,128)S(1)}, f32[8,128]{1,0:T(8,128)S(1)}, u32[]{:S(2)}, u32[]{:S(2)}) collective-permute-start(f32[8,128]{1,0:T(8,128)S(1)} %add_add_fusion.1), channel_id=1, source_target_pairs={{0,1},{1,0},{2,3},{3,2},{4,5},{5,4},{6,7},{7,6},{8,9},{9,8},{10,11... | collective-permute-start | bytes 12296 | tf_op jit(solution)/shard_map/ppermute | solution.py:232
  84.5 2.6 %collective-permute-start.8 = (f32[8,128]{1,0:T(8,128)S(1)}, f32[8,128]{1,0:T(8,128)S(1)}, u32[]{:S(2)}, u32[]{:S(2)}) collective-permute-start(f32[8,128]{1,0:T(8,128)S(1)} %add_add_fusion.1), channel_id=1, source_target_pairs={{0,2},{1,3},{2,0},{3,1},{4,6},{5,7},{6,4},{7,5},{8,10},{9,11},{10,... | collective-permute-start | bytes 12296 | tf_op jit(solution)/shard_map/ppermute | solution.py:232
  87.3 1.7 %collective-permute-done.8 = f32[8,128]{1,0:T(8,128)S(1)} collective-permute-done((f32[8,128]{1,0:T(8,128)S(1)}, f32[8,128]{1,0:T(8,128)S(1)}, u32[]{:S(2)}, u32[]{:S(2)}) %collective-permute-start.8) | collective-permute-done | bytes 4128 | tf_op jit(solution)/shard_map/ppermute | solution.py:232
  89.0 3.5 %collective-permute-done.9 = f32[8,128]{1,0:T(8,128)S(1)} collective-permute-done((f32[8,128]{1,0:T(8,128)S(1)}, f32[8,128]{1,0:T(8,128)S(1)}, u32[]{:S(2)}, u32[]{:S(2)}) %collective-permute-start.9) | collective-permute-done | bytes 4128 | tf_op jit(solution)/shard_map/ppermute | solution.py:232
  93.1 4.6 %all-to-all-done.3 = bf16[8,2,256,128]{3,2,1,0:T(8,128)(2,1)S(1)} async-done(((bf16[8,2,256,128]{3,2,1,0:T(8,128)(2,1)}), bf16[8,2,256,128]{3,2,1,0:T(8,128)(2,1)S(1)}, u32[]{:S(2)}, u32[]{:S(2)}) %all-to-all-start.3) | async-done | bytes 1048608 | tf_op jit(solution)/shard_map/all_to_all | solution.py:282
  97.8 3.7 %all-to-all-start.2 = ((bf16[8,2,256,128]{3,2,1,0:T(8,128)(2,1)}), bf16[8,2,256,128]{3,2,1,0:T(8,128)(2,1)S(1)}, u32[]{:S(2)}, u32[]{:S(2)}) async-start(bf16[8,2,256,128]{3,2,1,0:T(8,128)(2,1)} %get-tuple-element.22), calls=%async_computation.2 | async-start | bytes 2097152 | tf_op jit(solution)/shard_map/all_to_all | solution.py:282
  101.5 1.2 %broadcast_select_fusion.4 = (bf16[256,512]{1,0:T(8,128)(2,1)S(1)}, bf16[256,512]{1,0:T(8,128)(2,1)S(1)}, bf16[256,512]{1,0:T(8,128)(2,1)S(1)}, bf16[256,512]{1,0:T(8,128)(2,1)S(1)}) fusion(bf16[256,512]{1,0:T(8,128)(2,1)} %get-tuple-element.21, pred[]{:T(512)S(6)} %eq.8, bf16[2,256,512]{2,1,0:T(8,128)(2,1)} %collective-permute-done.2, pred[]{:T(512)S(6)} %eq.9, ...), kind=kLoop, calls=%fused_computation.13 | loop fusion | flops 524288 | bytes 2097154 | tf_op jit(solution)/shard_map/jit(_where)/select_n | solution.py:286
  102.7 1.1 maximum_bitcast_fusion.1
  103.8 1.1 maximum_bitcast_fusion
  105.0 11.8 %all-to-all-done.2 = bf16[8,2,256,128]{3,2,1,0:T(8,128)(2,1)S(1)} async-done(((bf16[8,2,256,128]{3,2,1,0:T(8,128)(2,1)}), bf16[8,2,256,128]{3,2,1,0:T(8,128)(2,1)S(1)}, u32[]{:S(2)}, u32[]{:S(2)}) %all-to-all-start.2) | async-done | bytes 1048608 | tf_op jit(solution)/shard_map/all_to_all | solution.py:282
  116.9 0.7 maximum_bitcast_fusion.3
  117.7 0.7 maximum_bitcast_fusion.2
  (52 shorter events, 9.6 us)
Async XLA Ops:
  7.1 5.3 %copy-start.2 = (bf16[1,256,2048]{2,1,0:T(8,128)(2,1)S(1)}, bf16[1,256,2048]{2,1,0:T(8,128)(2,1)}, u32[]{:S(2)}) copy-start(bf16[1,256,2048]{2,1,0:T(8,128)(2,1)} %param.6) | copy-start | bytes 3145732
  7.1 5.3 %copy-start.3 = (bf16[1,256,2048]{2,1,0:T(8,128)(2,1)S(1)}, bf16[1,256,2048]{2,1,0:T(8,128)(2,1)}, u32[]{:S(2)}) copy-start(bf16[1,256,2048]{2,1,0:T(8,128)(2,1)} %param.10) | copy-start | bytes 3145732
  7.1 20.7 %all-to-all-start = ((bf16[8,2,256,128]{3,2,1,0:T(8,128)(2,1)}), bf16[8,2,256,128]{3,2,1,0:T(8,128)(2,1)S(1)}, u32[]{:S(2)}, u32[]{:S(2)}) async-start(bf16[8,2,256,128]{3,2,1,0:T(8,128)(2,1)} %constant_dynamic-update-slice_fusion), calls=%async_computation | async-start | bytes 2097152 | tf_op jit(solution)/shard_map/all_to_all | solution.py:265
  12.6 19.5 %collective-permute-start = (bf16[2,256,1024]{2,1,0:T(8,128)(2,1)S(1)}, bf16[2,256,1024]{2,1,0:T(8,128)(2,1)}, u32[]{:S(2)}, u32[]{:S(2)}) collective-permute-start(bf16[2,256,1024]{2,1,0:T(8,128)(2,1)S(1)} %pad_maximum_fusion), channel_id=1, source_target_pairs={{0,4},{4,0},{8,12},{12,8},{16,20},{20,16},{24,28},{28,24},{1,5},{5... | collective-permute-start | bytes 3145736 | tf_op jit(solution)/shard_map/ppermute | solution.py:271
  18.5 12.9 %slice-start = ((s32[4,16,13]{1,0,2:T(4,128)}), s32[4,16,1]{1,0,2:T(4,128)S(1)}, s32[]{:S(2)}) async-start(s32[4,16,13]{1,0,2:T(4,128)} %param.11), calls=%async_computation.4 | async-start | bytes 4096 | tf_op jit(solution)/shard_map/slice | solution.py:259
  27.8 3.6 %copy-start = (bf16[8,2,256,128]{3,2,1,0:T(8,128)(2,1)}, bf16[8,2,256,128]{3,2,1,0:T(8,128)(2,1)S(1)}, u32[]{:S(2)}) copy-start(bf16[8,2,256,128]{3,2,1,0:T(8,128)(2,1)S(1)} %all-to-all-done.refs_7_) | copy-start | bytes 3145732
  27.8 24.3 %all-to-all-start.1 = ((bf16[8,2,256,128]{3,2,1,0:T(8,128)(2,1)}), bf16[8,2,256,128]{3,2,1,0:T(8,128)(2,1)S(1)}, u32[]{:S(2)}, u32[]{:S(2)}) async-start(bf16[8,2,256,128]{3,2,1,0:T(8,128)(2,1)} %constant_dynamic-update-slice_fusion.8), calls=%async_computation.1 | async-start | bytes 2097152 | tf_op jit(solution)/shard_map/all_to_all | solution.py:265
  52.1 1.0 copy-start.1
  72.5 1.5 %collective-permute-start.3 = (f32[8,128]{1,0:T(8,128)}, f32[8,128]{1,0:T(8,128)S(1)}, u32[]{:S(2)}, u32[]{:S(2)}) collective-permute-start(f32[8,128]{1,0:T(8,128)} %get-tuple-element.24), channel_id=1, source_target_pairs={{0,4},{4,0},{8,12},{12,8},{16,20},{20,16},{24,28},{28,24},{1,5},{5... | collective-permute-start | bytes 12296 | tf_op jit(solution)/shard_map/ppermute | solution.py:232
  74.7 8.2 %collective-permute-start.4 = (f32[8,128]{1,0:T(8,128)S(1)}, f32[8,128]{1,0:T(8,128)S(1)}, u32[]{:S(2)}, u32[]{:S(2)}) collective-permute-start(f32[8,128]{1,0:T(8,128)S(1)} %add.183), channel_id=1, source_target_pairs={{0,8},{4,12},{8,0},{12,4},{16,24},{20,28},{24,16},{28,20},{1,9},{5... | collective-permute-start | bytes 12296 | tf_op jit(solution)/shard_map/ppermute | solution.py:232
  76.5 6.3 %collective-permute-start.5 = (f32[8,128]{1,0:T(8,128)S(1)}, f32[8,128]{1,0:T(8,128)S(1)}, u32[]{:S(2)}, u32[]{:S(2)}) collective-permute-start(f32[8,128]{1,0:T(8,128)S(1)} %add.183), channel_id=1, source_target_pairs={{0,16},{4,20},{8,24},{12,28},{16,0},{20,4},{24,8},{28,12},{1,17},{... | collective-permute-start | bytes 12296 | tf_op jit(solution)/shard_map/ppermute | solution.py:232
  78.0 4.9 %collective-permute-start.6 = (f32[8,128]{1,0:T(8,128)S(1)}, f32[8,128]{1,0:T(8,128)S(1)}, u32[]{:S(2)}, u32[]{:S(2)}) collective-permute-start(f32[8,128]{1,0:T(8,128)S(1)} %add.183), channel_id=1, source_target_pairs={{0,24},{4,28},{8,16},{12,20},{16,8},{20,12},{24,0},{28,4},{1,25},{... | collective-permute-start | bytes 12296 | tf_op jit(solution)/shard_map/ppermute | solution.py:232
  78.1 4.2 %copy-start.7 = (bf16[2,256,512]{2,1,0:T(8,128)(2,1)S(1)}, bf16[2,256,512]{2,1,0:T(8,128)(2,1)}, u32[]{:S(2)}) copy-start(bf16[2,256,512]{2,1,0:T(8,128)(2,1)} %get-tuple-element.16) | copy-start | bytes 1572868
  78.1 14.9 %copy-start.5 = (bf16[256,512]{1,0:T(8,128)(2,1)S(1)}, bf16[256,512]{1,0:T(8,128)(2,1)}, u32[]{:S(2)}) copy-start(bf16[256,512]{1,0:T(8,128)(2,1)} %get-tuple-element.15) | copy-start | bytes 786436
  78.1 14.9 %copy-start.6 = (bf16[256,512]{1,0:T(8,128)(2,1)S(1)}, bf16[256,512]{1,0:T(8,128)(2,1)}, u32[]{:S(2)}) copy-start(bf16[256,512]{1,0:T(8,128)(2,1)} %get-tuple-element.20) | copy-start | bytes 786436
  78.2 19.6 %all-to-all-start.3 = ((bf16[8,2,256,128]{3,2,1,0:T(8,128)(2,1)}), bf16[8,2,256,128]{3,2,1,0:T(8,128)(2,1)S(1)}, u32[]{:S(2)}, u32[]{:S(2)}) async-start(bf16[8,2,256,128]{3,2,1,0:T(8,128)(2,1)} %get-tuple-element.23), calls=%async_computation.3 | async-start | bytes 2097152 | tf_op jit(solution)/shard_map/all_to_all | solution.py:282
  82.4 10.7 %collective-permute-start.1 = (bf16[2,256,512]{2,1,0:T(8,128)(2,1)S(1)}, bf16[2,256,512]{2,1,0:T(8,128)(2,1)S(1)}, u32[]{:S(2)}, u32[]{:S(2)}) collective-permute-start(bf16[2,256,512]{2,1,0:T(8,128)(2,1)S(1)} %copy-done.7), channel_id=1, source_target_pairs={{0,4},{4,0},{8,12},{12,8},{16,20},{20,16},{24,28},{28,24},{1,5},{5... | collective-permute-start | bytes 1572872 | tf_op jit(solution)/shard_map/ppermute | solution.py:279
  82.9 4.5 %collective-permute-start.7 = (f32[8,128]{1,0:T(8,128)S(1)}, f32[8,128]{1,0:T(8,128)S(1)}, u32[]{:S(2)}, u32[]{:S(2)}) collective-permute-start(f32[8,128]{1,0:T(8,128)S(1)} %add_add_fusion.1), channel_id=1, source_target_pairs={{0,1},{1,0},{2,3},{3,2},{4,5},{5,4},{6,7},{7,6},{8,9},{9,8},{10,11... | collective-permute-start | bytes 12296 | tf_op jit(solution)/shard_map/ppermute | solution.py:232
  84.5 4.5 %collective-permute-start.8 = (f32[8,128]{1,0:T(8,128)S(1)}, f32[8,128]{1,0:T(8,128)S(1)}, u32[]{:S(2)}, u32[]{:S(2)}) collective-permute-start(f32[8,128]{1,0:T(8,128)S(1)} %add_add_fusion.1), channel_id=1, source_target_pairs={{0,2},{1,3},{2,0},{3,1},{4,6},{5,7},{6,4},{7,5},{8,10},{9,11},{10,... | collective-permute-start | bytes 12296 | tf_op jit(solution)/shard_map/ppermute | solution.py:232
  87.1 5.4 %collective-permute-start.9 = (f32[8,128]{1,0:T(8,128)S(1)}, f32[8,128]{1,0:T(8,128)S(1)}, u32[]{:S(2)}, u32[]{:S(2)}) collective-permute-start(f32[8,128]{1,0:T(8,128)S(1)} %add_add_fusion.1), channel_id=1, source_target_pairs={{0,3},{1,2},{2,1},{3,0},{4,7},{5,6},{6,5},{7,4},{8,11},{9,10},{10,... | collective-permute-start | bytes 12296 | tf_op jit(solution)/shard_map/ppermute | solution.py:232
  87.3 14.1 %collective-permute-start.2 = (bf16[2,256,512]{2,1,0:T(8,128)(2,1)}, bf16[2,256,512]{2,1,0:T(8,128)(2,1)}, u32[]{:S(2)}, u32[]{:S(2)}) collective-permute-start(bf16[2,256,512]{2,1,0:T(8,128)(2,1)} %get-tuple-element.19), channel_id=1, source_target_pairs={{0,4},{4,0},{8,12},{12,8},{16,20},{20,16},{24,28},{28,24},{1,5},{5... | collective-permute-start | bytes 1572872 | tf_op jit(solution)/shard_map/ppermute | solution.py:279
  97.8 3.7 %copy-start.4 = (bf16[256,512]{1,0:T(8,128)(2,1)S(1)}, bf16[256,512]{1,0:T(8,128)(2,1)}, u32[]{:S(2)}) copy-start(bf16[256,512]{1,0:T(8,128)(2,1)} %get-tuple-element.18) | copy-start | bytes 786436
  97.8 19.0 %all-to-all-start.2 = ((bf16[8,2,256,128]{3,2,1,0:T(8,128)(2,1)}), bf16[8,2,256,128]{3,2,1,0:T(8,128)(2,1)S(1)}, u32[]{:S(2)}, u32[]{:S(2)}) async-start(bf16[8,2,256,128]{3,2,1,0:T(8,128)(2,1)} %get-tuple-element.22), calls=%async_computation.2 | async-start | bytes 2097152 | tf_op jit(solution)/shard_map/all_to_all | solution.py:282

commit v3 on v2

v3 whole, which is shorter than its diff:
```python
import functools
import math

import jax
import jax.numpy as jnp
from jax import lax
from jax.experimental import pallas as pl
from jax.experimental.pallas import tpu as pltpu
from jax.sharding import PartitionSpec as P

HEADS = 16
KV_HEADS = 4
HD = 128
BLOCK = 128
QPG = HEADS // KV_HEADS
SPLIT = 2
HEADS_EACH = QPG // SPLIT
ROWS = HEADS_EACH * BLOCK
TAIL = 16
STRIDES = (2, 3)
LOG2E = math.log2(math.e)
NEVER = -1e30


def distinct_offsets(block_count, listed_count):
    tables = []
    for stride in STRIDES:
        steps = range(1, (listed_count - 3) // 2 + 1)
        listed = [-1, 0, 1] + [stride * m for m in steps] + [-stride * m for m in steps]
        times = {}
        for o in listed:
            times[o % block_count] = times.get(o % block_count, 0) + 1
        tables.append(sorted(times.items()))
    most = max(len(t) for t in tables)
    return [t + [(0, 0)] * (most - len(t)) for t in tables]


def nt(a, b):
    return jnp.dot(a, b, preferred_element_type=jnp.float32)


def group_kernel(gi, devices, local_blocks, listed, offsets, *refs):
    place, strides, taus = refs[:3]
    q_own, q_sib, g_own, g_sib, kv_in, tau_in = refs[3:9]
    att_own, dq_own, sib_out, tau_out, kv_out = refs[9:14]
    k_s, v_s, kt_s, vt_s, dk_s, dv_s, s_s, e_s, dp_s, p_s, ds_s, tau_s = refs[14:]
    unit = pl.program_id(0)
    blocks = devices * local_blocks
    tokens = local_blocks * BLOCK
    me = place[0]
    core = me % 2
    group = 2 * core + gi

    @pl.when(unit == 0)
    def _():
        def fill(b, carry):
            for half in range(local_blocks):
                rows = slice(half * BLOCK, (half + 1) * BLOCK)
                k_block = kv_in[b, 0, rows, :]
                v_block = kv_in[b, 1, rows, :]
                at = b * local_blocks + half
                k_s[at] = k_block
                v_s[at] = v_block
                kt_s[at] = k_block.T
                vt_s[at] = v_block.T
            return carry

        lax.fori_loop(0, devices, fill, 0, unroll=2)
        dk_s[...] = jnp.zeros_like(dk_s)
        dv_s[...] = jnp.zeros_like(dv_s)
        tau_s[...] = jnp.zeros_like(tau_s)

    own = unit < local_blocks
    query_block = (me ^ (unit // local_blocks)) * local_blocks + unit % local_blocks
    wide = strides[group * blocks + query_block] == STRIDES[1]
    ids, bias = [], []
    for (narrow_off, narrow_times), (wide_off, wide_times) in zip(*offsets):
        ids.append((query_block + jnp.where(wide, wide_off, narrow_off)) % blocks)
        bias.append(
            times_bias(narrow_times)
            if narrow_times == wide_times
            else jnp.where(wide, times_bias(wide_times), times_bias(narrow_times))
        )
    keys_all = jnp.concatenate([k_s[i] for i in ids], axis=0)
    values_all = jnp.concatenate([v_s[i] for i in ids], axis=0)
    keys_t = jnp.concatenate([kt_s[i] for i in ids], axis=1)
    values_t = jnp.concatenate([vt_s[i] for i in ids], axis=1)
    span = [slice(j * BLOCK, (j + 1) * BLOCK) for j in range(listed)]

    def in_rows(x):
        return x.reshape(-1, 8, ROWS)

    def part(n):
        cols = slice(n * HEADS_EACH * HD, (n + 1) * HEADS_EACH * HD)
        s_n, e_n, dp_n, p_n, ds_n = (x.at[n] for x in (s_s, e_s, dp_s, p_s, ds_s))
        q_here = jnp.where(own, q_own[:, cols], q_sib[0, :, cols])
        g_here = jnp.where(own, g_own[:, cols], g_sib[0, :, cols])

        def per_head(x):
            return [x[:, h * HD : (h + 1) * HD] for h in range(HEADS_EACH)]

        q_rows = jnp.concatenate(per_head(q_here), axis=0)
        g_rows = jnp.concatenate(per_head(g_here), axis=0)
        q_t = jnp.concatenate([x.T for x in per_head(q_here)], axis=1)
        g_t = jnp.concatenate([x.T for x in per_head(g_here)], axis=1)
        first = group * QPG + n * HEADS_EACH
        scale = jnp.concatenate(
            [jnp.full((1, BLOCK), taus[first + h], jnp.float32) for h in range(HEADS_EACH)], axis=1
        ) / math.sqrt(HD)
        factor = scale * LOG2E

        s_n[...] = nt(keys_all, q_t)
        yield
        dp_n[...] = nt(values_all, g_t)
        most = jnp.max(in_rows(s_n[span[0], :]), axis=0)
        for j in range(1, listed):
            most = jnp.maximum(most, jnp.max(in_rows(s_n[span[j], :]), axis=0))
        top_row = jnp.max(most, axis=0, keepdims=True) * factor
        total = jnp.zeros((8, ROWS), jnp.float32)
        for j in range(listed):
            e = jnp.exp2(s_n[span[j], :] * factor - (top_row - bias[j]))
            e_n[span[j], :] = e
            total = total + jnp.sum(in_rows(e), axis=0)
        inverse = 1.0 / jnp.sum(total, axis=0, keepdims=True)
        yield
        for j in range(listed):
            p_n[span[j], :] = (e_n[span[j], :] * inverse).astype(jnp.bfloat16)
        o_t = nt(values_t, p_n[...])
        dv = nt(p_n[...], g_rows)
        for j in range(listed):
            dv_s[ids[j]] += dv[span[j], :]
        row_dot = jnp.sum(g_t.astype(jnp.float32) * o_t, axis=0, keepdims=True)
        write(n, 0, o_t)
        yield
        weight_scale = inverse * scale
        tau_rows = jnp.zeros((8, ROWS), jnp.float32)
        for j in range(listed):
            scaled = e_n[span[j], :] * weight_scale * (dp_n[span[j], :] - row_dot)
            tau_rows = tau_rows + jnp.sum(in_rows(scaled * s_n[span[j], :]), axis=0)
            ds_n[span[j], :] = scaled.astype(jnp.bfloat16)
        tau_s[n] += tau_rows
        yield
        dq_t = nt(keys_t, ds_n[...])
        dk = nt(ds_n[...], q_rows)
        for j in range(listed):
            dk_s[ids[j]] += dk[span[j], :]
        write(n, 1, dq_t)

    def write(n, which, x_t):
        low = x_t.astype(jnp.bfloat16)
        out = jnp.concatenate([low[:, h * HD : (h + 1) * HD].T for h in range(HEADS_EACH)], axis=1)
        cols = slice(n * HEADS_EACH * HD, (n + 1) * HEADS_EACH * HD)
        (att_own, dq_own)[which][:, cols] = out
        sib_out[which, :, cols] = out

    shares = [part(n) for n in range(SPLIT)]
    live = []
    while shares or live:
        if shares:
            live.append(shares.pop(0))
        for share in list(live):
            if next(share, 1) == 1:
                live.remove(share)

    @pl.when(unit == 2 * local_blocks - 1)
    def _():
        lane = lax.broadcasted_iota(jnp.int32, (TAIL, HD), 1)
        row = lax.broadcasted_iota(jnp.int32, (TAIL, HD), 0)
        sums = tau_in[...]
        for h in range(QPG):
            head = group * QPG + h
            rows = tau_s[h // HEADS_EACH, :, (h % HEADS_EACH) * BLOCK : (h % HEADS_EACH + 1) * BLOCK]
            sums = sums + jnp.where(lane == head, jnp.sum(rows) / taus[head], 0.0)
        tau_out[...] = sums
        high = sums.astype(jnp.bfloat16).astype(jnp.float32)
        mid = (sums - high).astype(jnp.bfloat16).astype(jnp.float32)
        low = sums - high - mid
        tail = jnp.where(
            row == 0, high, jnp.where(row == 1, mid, jnp.where(row == 2, low, 0.0))
        ).astype(jnp.bfloat16)

        def drain(b, carry):
            for half in range(local_blocks):
                at = b * local_blocks + half
                low, high = half * BLOCK, (half + 1) * BLOCK
                kv_out[b, low:high, :] = dk_s[at].astype(jnp.bfloat16)
                kv_out[b, tokens + low : tokens + high, :] = dv_s[at].astype(jnp.bfloat16)
            kv_out[b, 2 * tokens :, :] = tail
            return carry

        lax.fori_loop(0, devices, drain, 0, unroll=2)


def times_bias(times):
    return math.log2(times) if times else NEVER


def run_group(gi, devices, place, strides, tau, queries, out_grad, qg_sib, kv_in, tau_in, offsets):
    listed = len(offsets[0])
    tokens = queries.shape[0]
    local_blocks = tokens // BLOCK
    units = 2 * local_blocks
    blocks = devices * local_blocks
    width = QPG * HD
    last = local_blocks - 1
    mine = lambda u, p, s, t: (jnp.minimum(u, last), 2 * (p[0] % 2) + gi)
    qs = pl.BlockSpec((1, BLOCK, width), lambda u, p, s, t: (0, jnp.maximum(u - local_blocks, 0), gi))
    gs = pl.BlockSpec((1, BLOCK, width), lambda u, p, s, t: (1, jnp.maximum(u - local_blocks, 0), gi))
    block_own = pl.BlockSpec((BLOCK, width), mine)
    out_own = pl.BlockSpec((BLOCK, width), lambda u, p, s, t: (jnp.minimum(u, local_blocks), 0))
    out_sib = pl.BlockSpec((2, BLOCK, width), lambda u, p, s, t: (0, jnp.maximum(u - local_blocks, 0), 0))
    kv_back = pl.BlockSpec((devices, 2 * tokens + TAIL, HD), lambda u, p, s, t: (0, 0, 0))
    kv_all = pl.BlockSpec((devices, 2, tokens, HD), lambda u, p, s, t: (0, 0, 0, 0))
    small = pl.BlockSpec((TAIL, HD), lambda u, p, s, t: (0, 0))
    bf = lambda *shape: jax.ShapeDtypeStruct(shape, jnp.bfloat16)
    keys_wide = listed * BLOCK
    macs = units * QPG * BLOCK * keys_wide * HD * 6
    return pl.pallas_call(
        functools.partial(group_kernel, gi, devices, local_blocks, listed, offsets),
        grid_spec=pltpu.PrefetchScalarGridSpec(
            num_scalar_prefetch=3,
            grid=(units,),
            in_specs=[block_own, qs, block_own, gs, kv_all, small],
            out_specs=[out_own, out_own, out_sib, small, kv_back],
            scratch_shapes=[pltpu.VMEM((blocks, BLOCK, HD), jnp.bfloat16)] * 4
            + [pltpu.VMEM((blocks, BLOCK, HD), jnp.float32)] * 2
            + [pltpu.VMEM((SPLIT, keys_wide, ROWS), jnp.float32)] * 3
            + [pltpu.VMEM((SPLIT, keys_wide, ROWS), jnp.bfloat16)] * 2
            + [pltpu.VMEM((SPLIT, 8, ROWS), jnp.float32)],
        ),
        out_shape=[bf(tokens + BLOCK, width), bf(tokens + BLOCK, width), bf(2, tokens, width)]
        + [jax.ShapeDtypeStruct((TAIL, HD), jnp.float32), bf(devices, 2 * tokens + TAIL, HD)],
        compiler_params=pltpu.CompilerParams(
            dimension_semantics=("arbitrary",), vmem_limit_bytes=60 * 2**20
        ),
        cost_estimate=pl.CostEstimate(
            flops=2 * macs, bytes_accessed=6 * 2**20, transcendentals=units * QPG * BLOCK * keys_wide
        ),
        name="group_attention",
    )(place, strides, tau, queries, qg_sib, out_grad, qg_sib, kv_in, tau_in)


def spread_kernel(k_ref, v_ref, out):
    for parity in range(2):
        cols = slice(parity * 2 * HD, parity * 2 * HD + HD)
        out[parity, 0] = k_ref[:, cols]
        out[parity, 1] = v_ref[:, cols]


def spread(gi, devices, keys, values):
    tokens, width = keys.shape
    cols = width - HD
    taken = pl.BlockSpec((tokens, width), lambda d: (0, 0))

    def kernel(k_ref, v_ref, out):
        at = gi * HD
        spread_kernel(k_ref.at[:, at : at + cols], v_ref.at[:, at : at + cols], out)

    return pl.pallas_call(
        kernel,
        grid=(devices // 2,),
        in_specs=[taken, taken],
        out_specs=pl.BlockSpec((2, 2, tokens, HD), lambda d: (d, 0, 0, 0)),
        out_shape=jax.ShapeDtypeStruct((devices, 2, tokens, HD), jnp.bfloat16),
        compiler_params=pltpu.CompilerParams(vmem_limit_bytes=60 * 2**20),
        name="spread_keys_values",
    )(keys, values)


def total_over(x, axis):
    size = lax.axis_size(axis)
    if size & (size - 1):
        return lax.psum(x, axis)

    def partner(distance):
        return lax.ppermute(x, axis, [(i, i ^ distance) for i in range(size)])

    step = 1
    while step < size:
        if size // step % 4 == 0 and size // step != 8:
            x = (x + partner(step)) + (partner(2 * step) + partner(3 * step))
            step *= 4
        else:
            x = x + partner(step)
            step *= 2
    return x


def body(queries, keys, values, tau, out_grad, key_blocks):
    ctx = lax.axis_size("ctx")
    me = lax.axis_index("ctx").astype(jnp.int32)
    core = me % 2
    tokens = queries.shape[1]
    local_blocks = tokens // BLOCK
    block_count = ctx * local_blocks
    listed_count = key_blocks.shape[2]
    offsets = distinct_offsets(block_count, listed_count)
    swap = [(d, d ^ 1) for d in range(ctx)]
    wide = 2 * QPG * HD

    q0, k0, v0, g0 = queries[0], keys[0], values[0], out_grad[0]
    place = me[None]
    strides = ((key_blocks[:, :, 3] - jnp.arange(block_count, dtype=jnp.int32)) % block_count).reshape(-1)

    def kv_for(gi):
        return lax.all_to_all(spread(gi, ctx, k0, v0), "ctx", 0, 0)

    def theirs(x):
        return lax.dynamic_slice_in_dim(x, (1 - core) * wide, wide, 1)

    kv_in = [kv_for(gi) for gi in range(2)]
    qg_sib = lax.ppermute(jnp.stack([theirs(q0), theirs(g0)]), "ctx", swap)

    att_parts, dq_parts, grads = [], [], []
    tau_rows = jnp.zeros((TAIL, HD), jnp.float32)
    for gi in range(2):
        att_own, dq_own, sib, tau_rows, kv_grads = run_group(
            gi, ctx, place, strides, tau, q0, g0, qg_sib, kv_in[gi], tau_rows, offsets
        )
        sib = lax.ppermute(sib, "ctx", swap)
        att_parts.append((att_own[:tokens], sib[0]))
        dq_parts.append((dq_own[:tokens], sib[1]))
        grads.append(lax.all_to_all(kv_grads, "ctx", 0, 0))

    def by_group(parts):
        return jnp.concatenate(
            [jnp.where(core == c // 2, parts[c % 2][0], parts[c % 2][1]) for c in range(4)], axis=1
        )

    attended = by_group(att_parts)[None]
    query_grad = by_group(dq_parts)[None]

    def summed(which):
        cols = []
        for c in range(4):
            total = None
            for src in range(c // 2, ctx, 2):
                term = grads[c % 2][src, which * tokens : (which + 1) * tokens].astype(jnp.float32)
                total = term if total is None else total + term
            cols.append(total.astype(jnp.bfloat16))
        return jnp.concatenate(cols, axis=1)[None]

    key_grad, value_grad = summed(0), summed(1)
    tails = grads[1][:, 2 * tokens : 2 * tokens + 3, :HEADS].astype(jnp.float32)
    scale_total = total_over(jnp.sum(tails, axis=(0, 1))[None], "batch")[0]
    tau_grad = scale_total / math.sqrt(lax.axis_size("batch") * ctx * tokens)
    return (attended, query_grad, key_grad, value_grad, tau_grad)


def solution(mesh):
    rows = P("batch", "ctx", None)
    return jax.shard_map(
        body,
        mesh=mesh,
        in_specs=(rows, rows, rows, P(), rows, P()),
        out_specs=(rows, rows, rows, rows, P()),
        check_vma=False,
    )
```

time: 119 us -> 109 us (0.916)
  other arithmetic: 17.7 us -> 7.44 us
  starting transfers between devices: 26.2 us -> 22.1 us
  Pallas kernels: 38.8 us -> 42.5 us
  waiting for transfers between devices: 31.9 us -> 33.9 us
    unnamed x14 -> x0, other arithmetic: 9.29 us -> none
    ppermute x7 -> x3, waiting for transfers between devices: 6.22 us -> 0.01 us  [partner(): return lax.ppermute(x, axis, [(i, i ^ distance) for i in range(size)])]
    pallas_call x0 -> x2, Pallas kernels: none -> 5.25 us  [spread(): pl.pallas_call(kernel, grid=(devices // 2,), in_specs=[taken, taken], out...]
    ppermute x7 -> x3, starting transfers between devices: 8.4 us -> 4.27 us  [partner(): return lax.ppermute(x, axis, [(i, i ^ distance) for i in range(size)])]
    all_to_all x2, waiting for transfers between devices: 16.4 us -> 20.4 us  [body(): grads.append(lax.all_to_all(kv_grads, 'ctx', 0, 0))]
    all_to_all x2, waiting for transfers between devices: 9.31 us -> 12 us  [kv_for(): return lax.all_to_all(spread(gi, ctx, k0, v0), 'ctx', 0, 0)]
    pallas_call x2, Pallas kernels: 38.8 us -> 37.2 us  [run_group(): pl.pallas_call(functools.partial(group_kernel, gi, devices, local_blocks,...]
    ppermute x2, waiting for transfers between devices: 0.01 us -> 1.52 us  [body(): sib = lax.ppermute(sib, 'ctx', swap)]
  transfers between devices with their start and end apart: 14 -> 10, of which waited for: 6 -> 4; matrix products, arithmetic and copies ran while one was open for 9% -> 7% of each run, Pallas kernels for 16% -> 20%
where the time goes in v3:
time: 109 us
  Pallas kernels  42.5 us (39%)
  waiting for transfers between devices  33.9 us (31%)
  starting transfers between devices  22.1 us (20%)
  other arithmetic  7.44 us (7%)
  local copies, waits for them, and re-layouts  1.86 us (2%)
    pallas_call x2, Pallas kernels, run_group(): pl.pallas_call(functools.partial(group_kernel, gi, devices, local_blocks,...  37.2 us
    all_to_all x2, waiting for transfers between devices, body(): grads.append(lax.all_to_all(kv_grads, 'ctx', 0, 0))  20.4 us
    all_to_all x2, waiting for transfers between devices, kv_for(): return lax.all_to_all(spread(gi, ctx, k0, v0), 'ctx', 0, 0)  12 us
    all_to_all x2, starting transfers between devices, kv_for(): return lax.all_to_all(spread(gi, ctx, k0, v0), 'ctx', 0, 0)  8.86 us
    all_to_all x2, starting transfers between devices, body(): grads.append(lax.all_to_all(kv_grads, 'ctx', 0, 0))  7.8 us
    pallas_call x2, Pallas kernels, spread(): pl.pallas_call(kernel, grid=(devices // 2,), in_specs=[taken, taken], out...  5.25 us
    ppermute x3, starting transfers between devices, partner(): return lax.ppermute(x, axis, [(i, i ^ distance) for i in range(size)])  4.27 us
    select_n x2, other arithmetic, by_group(): jnp.where(core == c // 2, parts[c % 2][0], parts[c % 2][1])  2.29 us
  transfers between devices with their start and end apart: 10, of which 4 were waited for; matrix products, arithmetic and copies ran while one was open for 7% of the time, Pallas kernels for 20%

profile of v3, /device:TPU:0, one launch (start us, length us, event | category | flops | bytes accessed | tf_op | source)
XLA Modules:
  0.0 108.5 jit_solution(13738551949591951093)
XLA Ops:
  0.6 2.6 %spread_keys_values.2 = bf16[8,2,256,128]{3,2,1,0:T(8,128)(2,1)} custom-call(bf16[256,512]{1,0:T(8,128)(2,1)} %bitcast.59, bf16[256,512]{1,0:T(8,128)(2,1)} %bitcast.61), custom_call_target="tpu_custom_call" | custom-call | tf_op jit(solution)/shard_map/spread_keys_values/pallas_call | solution.py:259
  3.3 5.3 %all-to-all-start = ((bf16[8,2,256,128]{3,2,1,0:T(8,128)(2,1)}), bf16[8,2,256,128]{3,2,1,0:T(8,128)(2,1)S(1)}, u32[]{:S(2)}, u32[]{:S(2)}) async-start(bf16[8,2,256,128]{3,2,1,0:T(8,128)(2,1)} %spread_keys_values.2), calls=%async_computation | async-start | bytes 2097152 | tf_op jit(solution)/shard_map/all_to_all | solution.py:306
  8.6 0.1 constant_dynamic-slice_fusion
  8.7 0.1 pad_maximum_fusion
  8.8 0.6 collective-permute-start
  9.4 2.6 %spread_keys_values.3 = bf16[8,2,256,128]{3,2,1,0:T(8,128)(2,1)} custom-call(bf16[256,512]{1,0:T(8,128)(2,1)} %bitcast.60, bf16[256,512]{1,0:T(8,128)(2,1)} %bitcast.62), custom_call_target="tpu_custom_call" | custom-call | tf_op jit(solution)/shard_map/spread_keys_values/pallas_call | solution.py:259
  12.0 12.0 %all-to-all-done.refs_7_ = bf16[8,2,256,128]{3,2,1,0:T(8,128)(2,1)S(1)} async-done(((bf16[8,2,256,128]{3,2,1,0:T(8,128)(2,1)}), bf16[8,2,256,128]{3,2,1,0:T(8,128)(2,1)S(1)}, u32[]{:S(2)}, u32[]{:S(2)}) %all-to-all-start) | async-done | bytes 1048608 | tf_op jit(solution)/shard_map/all_to_all | solution.py:306
  24.0 3.6 %all-to-all-start.1 = ((bf16[8,2,256,128]{3,2,1,0:T(8,128)(2,1)}), bf16[8,2,256,128]{3,2,1,0:T(8,128)(2,1)S(1)}, u32[]{:S(2)}, u32[]{:S(2)}) async-start(bf16[8,2,256,128]{3,2,1,0:T(8,128)(2,1)} %spread_keys_values.3), calls=%async_computation.1 | async-start | bytes 2097152 | tf_op jit(solution)/shard_map/all_to_all | solution.py:306
  27.7 0.1 sub.16
  27.7 0.6 and_select_fusion.refs_1_
  28.3 0.6 broadcast_in_dim.23.refs_8_
  28.9 18.6 %group_attention.2 = (bf16[384,512]{1,0:T(8,128)(2,1)}, bf16[384,512]{1,0:T(8,128)(2,1)}, bf16[2,256,512]{2,1,0:T(8,128)(2,1)}, f32[16,128]{1,0:T(8,128)}, bf16[8,528,128]{2,1,0:T(8,128)(2,1)}) custom-call(s32[1]{0:T(128)} %bitcast.refs_0_, s32[64]{0:T(128)} %and_select_fusion.refs_1_, f32[16]{0:T(128)} %refs_2_.3, bf16[256,2048]{1,0:T(8,128)(2,1)} %bitcast.63, ...), custom_call_target="tpu_custom_call" | custom-call | flops 4429185024 | bytes 6291456 | tf_op jit(solution)/shard_map/group_attention/pallas_call | solution.py:218
  47.5 1.0 copy-done.1
  48.5 18.6 %group_attention.3 = (bf16[384,512]{1,0:T(8,128)(2,1)}, bf16[384,512]{1,0:T(8,128)(2,1)}, bf16[2,256,512]{2,1,0:T(8,128)(2,1)}, f32[16,128]{1,0:T(8,128)}, bf16[8,528,128]{2,1,0:T(8,128)(2,1)}) custom-call(s32[1]{0:T(128)} %bitcast.refs_0_, s32[64]{0:T(128)} %and_select_fusion.refs_1_, f32[16]{0:T(128)} %refs_2_.3, bf16[256,2048]{1,0:T(8,128)(2,1)} %bitcast.64, ...), custom_call_target="tpu_custom_call" | custom-call | flops 4429185024 | bytes 6291456 | tf_op jit(solution)/shard_map/group_attention/pallas_call | solution.py:218
  67.1 4.2 %all-to-all-start.3 = ((bf16[8,528,128]{2,1,0:T(8,128)(2,1)}), bf16[8,528,128]{2,1,0:T(8,128)(2,1)S(1)}, u32[]{:S(2)}, u32[]{:S(2)}) async-start(bf16[8,528,128]{2,1,0:T(8,128)(2,1)} %get-tuple-element.22), calls=%async_computation.3 | async-start | bytes 2162688 | tf_op jit(solution)/shard_map/all_to_all | solution.py:323
  71.4 0.5 collective-permute-start.2
  72.0 1.5 %collective-permute-done.2 = bf16[2,256,512]{2,1,0:T(8,128)(2,1)S(1)} collective-permute-done((bf16[2,256,512]{2,1,0:T(8,128)(2,1)S(1)}, bf16[2,256,512]{2,1,0:T(8,128)(2,1)S(1)}, u32[]{:S(2)}, u32[]{:S(2)}) %collective-permute-start.2) | collective-permute-done | bytes 524320 | tf_op jit(solution)/shard_map/ppermute | solution.py:320
  73.5 1.0 broadcast_select_fusion.4
  74.5 12.6 %all-to-all-done.3 = bf16[8,528,128]{2,1,0:T(8,128)(2,1)S(1)} async-done(((bf16[8,528,128]{2,1,0:T(8,128)(2,1)}), bf16[8,528,128]{2,1,0:T(8,128)(2,1)S(1)}, u32[]{:S(2)}, u32[]{:S(2)}) %all-to-all-start.3) | async-done | bytes 1081376 | tf_op jit(solution)/shard_map/all_to_all | solution.py:323
  87.1 3.6 %all-to-all-start.2 = ((bf16[8,528,128]{2,1,0:T(8,128)(2,1)}), bf16[8,528,128]{2,1,0:T(8,128)(2,1)S(1)}, u32[]{:S(2)}, u32[]{:S(2)}) async-start(bf16[8,528,128]{2,1,0:T(8,128)(2,1)} %get-tuple-element.21), calls=%async_computation.2 | async-start | bytes 2162688 | tf_op jit(solution)/shard_map/all_to_all | solution.py:323
  90.7 1.3 %broadcast_select_fusion.5 = (bf16[256,512]{1,0:T(8,128)(2,1)S(1)}, bf16[256,512]{1,0:T(8,128)(2,1)S(1)}, bf16[256,512]{1,0:T(8,128)(2,1)S(1)}, bf16[256,512]{1,0:T(8,128)(2,1)S(1)}) fusion(pred[]{:T(512)S(6)} %eq.8, bf16[2,256,512]{2,1,0:T(8,128)(2,1)} %collective-permute-done.1, bf16[384,512]{1,0:T(8,128)(2,1)} %get-tuple-element.19, pred[]{:T(512)S(6)} %eq.9, ...), kind=kLoop, calls=%fused_computation.14 | loop fusion | flops 524288 | bytes 2097154 | tf_op jit(solution)/shard_map/jit(_where)/select_n | solution.py:327
  92.0 1.1 %maximum_bitcast_fusion.1 = bf16[1,256,2048]{2,1,0:T(8,128)(2,1)} fusion(bf16[256,512]{1,0:T(8,128)(2,1)S(1)} %get-tuple-element.34, bf16[256,512]{1,0:T(8,128)(2,1)S(1)} %get-tuple-element.32, bf16[256,512]{1,0:T(8,128)(2,1)S(1)} %get-tuple-element.33, bf16[256,512]{1,0:T(8,128)(2,1)S(1)} %get-tuple-element.31), kind=kLoop, calls=%fused_computation.2 | loop fusion | flops 4194304 | bytes 2097152 | tf_op jit(solution)/shard_map/broadcast_in_dim | solution.py:331
  93.1 1.1 %maximum_bitcast_fusion = bf16[1,256,2048]{2,1,0:T(8,128)(2,1)} fusion(bf16[256,512]{1,0:T(8,128)(2,1)S(1)} %get-tuple-element.41, bf16[256,512]{1,0:T(8,128)(2,1)S(1)} %get-tuple-element.39, bf16[256,512]{1,0:T(8,128)(2,1)S(1)} %get-tuple-element.42, bf16[256,512]{1,0:T(8,128)(2,1)S(1)} %get-tuple-element.40), kind=kLoop, calls=%fused_computation.1 | loop fusion | flops 4194304 | bytes 2097152 | tf_op jit(solution)/shard_map/broadcast_in_dim | solution.py:330
  94.2 2.7 %collective-permute-start.4 = (f32[1,16]{1,0:T(1,128)S(1)}, f32[1,16]{1,0:T(1,128)S(1)}, u32[]{:S(2)}, u32[]{:S(2)}) collective-permute-start(f32[1,16]{1,0:T(1,128)S(1)} %bitcast.67), channel_id=1, source_target_pairs={{0,2},{1,3},{2,0},{3,1},{4,6},{5,7},{6,4},{7,5},{8,10},{9,11},{10,... | collective-permute-start | bytes 200 | tf_op jit(solution)/shard_map/ppermute | solution.py:276
  96.9 1.4 %collective-permute-start.5 = (f32[1,16]{1,0:T(1,128)S(1)}, f32[1,16]{1,0:T(1,128)S(1)}, u32[]{:S(2)}, u32[]{:S(2)}) collective-permute-start(f32[1,16]{1,0:T(1,128)S(1)} %bitcast.68), channel_id=1, source_target_pairs={{0,3},{1,2},{2,1},{3,0},{4,7},{5,6},{6,5},{7,4},{8,11},{9,10},{10,... | collective-permute-start | bytes 200 | tf_op jit(solution)/shard_map/ppermute | solution.py:276
  98.3 0.2 collective-permute-start.3
  98.5 0.1 fusion.5
  98.6 7.8 %all-to-all-done.2 = bf16[8,528,128]{2,1,0:T(8,128)(2,1)S(1)} async-done(((bf16[8,528,128]{2,1,0:T(8,128)(2,1)}), bf16[8,528,128]{2,1,0:T(8,128)(2,1)S(1)}, u32[]{:S(2)}, u32[]{:S(2)}) %all-to-all-start.2) | async-done | bytes 1081376 | tf_op jit(solution)/shard_map/all_to_all | solution.py:323
  106.4 0.1 fusion.4
  106.5 0.7 maximum_bitcast_fusion.3
  107.3 0.7 maximum_bitcast_fusion.2
  108.0 0.5 multiply_bitcast_fusion
  (23 shorter events, 0.2 us)
Async XLA Ops:
  3.3 5.3 %copy-start.2 = (bf16[1,256,2048]{2,1,0:T(8,128)(2,1)S(1)}, bf16[1,256,2048]{2,1,0:T(8,128)(2,1)}, u32[]{:S(2)}) copy-start(bf16[1,256,2048]{2,1,0:T(8,128)(2,1)} %param.6) | copy-start | bytes 3145732
  3.3 5.3 %copy-start.3 = (bf16[1,256,2048]{2,1,0:T(8,128)(2,1)S(1)}, bf16[1,256,2048]{2,1,0:T(8,128)(2,1)}, u32[]{:S(2)}) copy-start(bf16[1,256,2048]{2,1,0:T(8,128)(2,1)} %param.10) | copy-start | bytes 3145732
  3.3 20.7 %all-to-all-start = ((bf16[8,2,256,128]{3,2,1,0:T(8,128)(2,1)}), bf16[8,2,256,128]{3,2,1,0:T(8,128)(2,1)S(1)}, u32[]{:S(2)}, u32[]{:S(2)}) async-start(bf16[8,2,256,128]{3,2,1,0:T(8,128)(2,1)} %spread_keys_values.2), calls=%async_computation | async-start | bytes 2097152 | tf_op jit(solution)/shard_map/all_to_all | solution.py:306
  8.8 19.5 %collective-permute-start = (bf16[2,256,1024]{2,1,0:T(8,128)(2,1)S(1)}, bf16[2,256,1024]{2,1,0:T(8,128)(2,1)}, u32[]{:S(2)}, u32[]{:S(2)}) collective-permute-start(bf16[2,256,1024]{2,1,0:T(8,128)(2,1)S(1)} %pad_maximum_fusion), channel_id=1, source_target_pairs={{0,4},{4,0},{8,12},{12,8},{16,20},{20,16},{24,28},{28,24},{1,5},{5... | collective-permute-start | bytes 3145736 | tf_op jit(solution)/shard_map/ppermute | solution.py:312
  12.0 15.6 %slice-start = ((s32[4,16,13]{1,0,2:T(4,128)}), s32[4,16,1]{1,0,2:T(4,128)S(1)}, s32[]{:S(2)}) async-start(s32[4,16,13]{1,0,2:T(4,128)} %param.11), calls=%async_computation.4 | async-start | bytes 4096 | tf_op jit(solution)/shard_map/slice | solution.py:303
  24.0 4.9 %copy-start = (bf16[8,2,256,128]{3,2,1,0:T(8,128)(2,1)}, bf16[8,2,256,128]{3,2,1,0:T(8,128)(2,1)S(1)}, u32[]{:S(2)}) copy-start(bf16[8,2,256,128]{3,2,1,0:T(8,128)(2,1)S(1)} %all-to-all-done.refs_7_) | copy-start | bytes 3145732
  24.0 23.5 %all-to-all-start.1 = ((bf16[8,2,256,128]{3,2,1,0:T(8,128)(2,1)}), bf16[8,2,256,128]{3,2,1,0:T(8,128)(2,1)S(1)}, u32[]{:S(2)}, u32[]{:S(2)}) async-start(bf16[8,2,256,128]{3,2,1,0:T(8,128)(2,1)} %spread_keys_values.3), calls=%async_computation.1 | async-start | bytes 2097152 | tf_op jit(solution)/shard_map/all_to_all | solution.py:306
  47.5 1.0 copy-start.1
  67.1 4.3 %copy-start.5 = (bf16[2,256,512]{2,1,0:T(8,128)(2,1)S(1)}, bf16[2,256,512]{2,1,0:T(8,128)(2,1)}, u32[]{:S(2)}) copy-start(bf16[2,256,512]{2,1,0:T(8,128)(2,1)} %get-tuple-element.18) | copy-start | bytes 1572868
  67.1 6.4 %copy-start.4 = (bf16[384,512]{1,0:T(8,128)(2,1)S(1)}, bf16[384,512]{1,0:T(8,128)(2,1)}, u32[]{:S(2)}) copy-start(bf16[384,512]{1,0:T(8,128)(2,1)} %get-tuple-element.17) | copy-start | bytes 1179652
  67.1 20.0 %all-to-all-start.3 = ((bf16[8,528,128]{2,1,0:T(8,128)(2,1)}), bf16[8,528,128]{2,1,0:T(8,128)(2,1)S(1)}, u32[]{:S(2)}, u32[]{:S(2)}) async-start(bf16[8,528,128]{2,1,0:T(8,128)(2,1)} %get-tuple-element.22), calls=%async_computation.3 | async-start | bytes 2162688 | tf_op jit(solution)/shard_map/all_to_all | solution.py:323
  71.4 2.1 %collective-permute-start.2 = (bf16[2,256,512]{2,1,0:T(8,128)(2,1)S(1)}, bf16[2,256,512]{2,1,0:T(8,128)(2,1)S(1)}, u32[]{:S(2)}, u32[]{:S(2)}) collective-permute-start(bf16[2,256,512]{2,1,0:T(8,128)(2,1)S(1)} %copy-done.5), channel_id=1, source_target_pairs={{0,4},{4,0},{8,12},{12,8},{16,20},{20,16},{24,28},{28,24},{1,5},{5... | collective-permute-start | bytes 1572872 | tf_op jit(solution)/shard_map/ppermute | solution.py:320
  71.9 18.8 %collective-permute-start.1 = (bf16[2,256,512]{2,1,0:T(8,128)(2,1)}, bf16[2,256,512]{2,1,0:T(8,128)(2,1)}, u32[]{:S(2)}, u32[]{:S(2)}) collective-permute-start(bf16[2,256,512]{2,1,0:T(8,128)(2,1)} %get-tuple-element.15), channel_id=1, source_target_pairs={{0,4},{4,0},{8,12},{12,8},{16,20},{20,16},{24,28},{28,24},{1,5},{5... | collective-permute-start | bytes 1572872 | tf_op jit(solution)/shard_map/ppermute | solution.py:320
  87.1 19.3 %all-to-all-start.2 = ((bf16[8,528,128]{2,1,0:T(8,128)(2,1)}), bf16[8,528,128]{2,1,0:T(8,128)(2,1)S(1)}, u32[]{:S(2)}, u32[]{:S(2)}) async-start(bf16[8,528,128]{2,1,0:T(8,128)(2,1)} %get-tuple-element.21), calls=%async_computation.2 | async-start | bytes 2162688 | tf_op jit(solution)/shard_map/all_to_all | solution.py:323
  94.2 13.8 %collective-permute-start.4 = (f32[1,16]{1,0:T(1,128)S(1)}, f32[1,16]{1,0:T(1,128)S(1)}, u32[]{:S(2)}, u32[]{:S(2)}) collective-permute-start(f32[1,16]{1,0:T(1,128)S(1)} %bitcast.67), channel_id=1, source_target_pairs={{0,2},{1,3},{2,0},{3,1},{4,6},{5,7},{6,4},{7,5},{8,10},{9,11},{10,... | collective-permute-start | bytes 200 | tf_op jit(solution)/shard_map/ppermute | solution.py:276
  96.9 11.1 %collective-permute-start.5 = (f32[1,16]{1,0:T(1,128)S(1)}, f32[1,16]{1,0:T(1,128)S(1)}, u32[]{:S(2)}, u32[]{:S(2)}) collective-permute-start(f32[1,16]{1,0:T(1,128)S(1)} %bitcast.68), channel_id=1, source_target_pairs={{0,3},{1,2},{2,1},{3,0},{4,7},{5,6},{6,5},{7,4},{8,11},{9,10},{10,... | collective-permute-start | bytes 200 | tf_op jit(solution)/shard_map/ppermute | solution.py:276
  98.3 9.8 %collective-permute-start.3 = (f32[1,16]{1,0:T(1,128)S(1)}, f32[1,16]{1,0:T(1,128)S(1)}, u32[]{:S(2)}, u32[]{:S(2)}) collective-permute-start(f32[1,16]{1,0:T(1,128)S(1)} %bitcast.69), channel_id=1, source_target_pairs={{0,1},{1,0},{2,3},{3,2},{4,5},{5,4},{6,7},{7,6},{8,9},{9,8},{10,11... | collective-permute-start | bytes 200 | tf_op jit(solution)/shard_map/ppermute | solution.py:276

commit v4 on v3

--- a/solution.py
+++ b/solution.py
@@ -14,6 +14,7 @@
 BLOCK = 128
 QPG = HEADS // KV_HEADS
 SPLIT = 2
+CHUNK = 4
 HEADS_EACH = QPG // SPLIT
 ROWS = HEADS_EACH * BLOCK
 TAIL = 16
@@ -43,7 +44,7 @@
     place, strides, taus = refs[:3]
     q_own, q_sib, g_own, g_sib, kv_in, tau_in = refs[3:9]
     att_own, dq_own, sib_out, tau_out, kv_out = refs[9:14]
-    k_s, v_s, kt_s, vt_s, dk_s, dv_s, s_s, e_s, dp_s, p_s, ds_s, tau_s = refs[14:]
+    k_s, v_s, kt_s, vt_s, dk_s, dv_s, s_s, e_s, tau_s = refs[14:]
     unit = pl.program_id(0)
     blocks = devices * local_blocks
     tokens = local_blocks * BLOCK
@@ -81,18 +82,20 @@
             if narrow_times == wide_times
             else jnp.where(wide, times_bias(wide_times), times_bias(narrow_times))
         )
-    keys_all = jnp.concatenate([k_s[i] for i in ids], axis=0)
-    values_all = jnp.concatenate([v_s[i] for i in ids], axis=0)
-    keys_t = jnp.concatenate([kt_s[i] for i in ids], axis=1)
-    values_t = jnp.concatenate([vt_s[i] for i in ids], axis=1)
-    span = [slice(j * BLOCK, (j + 1) * BLOCK) for j in range(listed)]
+    chunks = [range(c, min(c + CHUNK, listed)) for c in range(0, listed, CHUNK)]
+
+    def rows_of(c):
+        return slice(c[0] * BLOCK, (c[-1] + 1) * BLOCK)
+
+    def picked(ref, c, axis):
+        return jnp.concatenate([ref[ids[j]] for j in c], axis=axis)
 
     def in_rows(x):
         return x.reshape(-1, 8, ROWS)
 
     def part(n):
         cols = slice(n * HEADS_EACH * HD, (n + 1) * HEADS_EACH * HD)
-        s_n, e_n, dp_n, p_n, ds_n = (x.at[n] for x in (s_s, e_s, dp_s, p_s, ds_s))
+        s_n, e_n = s_s.at[n], e_s.at[n]
         q_here = jnp.where(own, q_own[:, cols], q_sib[0, :, cols])
         g_here = jnp.where(own, g_own[:, cols], g_sib[0, :, cols])
 
@@ -109,42 +112,48 @@
         ) / math.sqrt(HD)
         factor = scale * LOG2E
 
-        s_n[...] = nt(keys_all, q_t)
-        yield
-        dp_n[...] = nt(values_all, g_t)
-        most = jnp.max(in_rows(s_n[span[0], :]), axis=0)
-        for j in range(1, listed):
-            most = jnp.maximum(most, jnp.max(in_rows(s_n[span[j], :]), axis=0))
+        most = None
+        for c in chunks:
+            raw = nt(picked(k_s, c, 0), q_t)
+            s_n[rows_of(c), :] = raw
+            top = jnp.max(in_rows(raw), axis=0)
+            most = top if most is None else jnp.maximum(most, top)
+            yield
         top_row = jnp.max(most, axis=0, keepdims=True) * factor
         total = jnp.zeros((8, ROWS), jnp.float32)
-        for j in range(listed):
-            e = jnp.exp2(s_n[span[j], :] * factor - (top_row - bias[j]))
-            e_n[span[j], :] = e
-            total = total + jnp.sum(in_rows(e), axis=0)
+        for c in chunks:
+            for j in c:
+                rows = slice(j * BLOCK, (j + 1) * BLOCK)
+                e = jnp.exp2(s_n[rows, :] * factor - (top_row - bias[j]))
+                e_n[rows, :] = e
+                total = total + jnp.sum(in_rows(e), axis=0)
+            yield
         inverse = 1.0 / jnp.sum(total, axis=0, keepdims=True)
-        yield
-        for j in range(listed):
-            p_n[span[j], :] = (e_n[span[j], :] * inverse).astype(jnp.bfloat16)
-        o_t = nt(values_t, p_n[...])
-        dv = nt(p_n[...], g_rows)
-        for j in range(listed):
-            dv_s[ids[j]] += dv[span[j], :]
+        o_t = jnp.zeros((HD, ROWS), jnp.float32)
+        for c in chunks:
+            probs = (e_n[rows_of(c), :] * inverse).astype(jnp.bfloat16)
+            o_t = o_t + nt(picked(vt_s, c, 1), probs)
+            add_blocks(dv_s, c, nt(probs, g_rows))
+            yield
         row_dot = jnp.sum(g_t.astype(jnp.float32) * o_t, axis=0, keepdims=True)
         write(n, 0, o_t)
-        yield
         weight_scale = inverse * scale
         tau_rows = jnp.zeros((8, ROWS), jnp.float32)
-        for j in range(listed):
-            scaled = e_n[span[j], :] * weight_scale * (dp_n[span[j], :] - row_dot)
-            tau_rows = tau_rows + jnp.sum(in_rows(scaled * s_n[span[j], :]), axis=0)
-            ds_n[span[j], :] = scaled.astype(jnp.bfloat16)
+        dq_t = jnp.zeros((HD, ROWS), jnp.float32)
+        for c in chunks:
+            dweights = nt(picked(v_s, c, 0), g_t)
+            scaled = e_n[rows_of(c), :] * weight_scale * (dweights - row_dot)
+            tau_rows = tau_rows + jnp.sum(in_rows(scaled * s_n[rows_of(c), :]), axis=0)
+            low = scaled.astype(jnp.bfloat16)
+            dq_t = dq_t + nt(picked(kt_s, c, 1), low)
+            add_blocks(dk_s, c, nt(low, q_rows))
+            yield
         tau_s[n] += tau_rows
-        yield
-        dq_t = nt(keys_t, ds_n[...])
-        dk = nt(ds_n[...], q_rows)
-        for j in range(listed):
-            dk_s[ids[j]] += dk[span[j], :]
         write(n, 1, dq_t)
+
+    def add_blocks(ref, c, x):
+        for n, j in enumerate(c):
+            ref[ids[j]] += x[n * BLOCK : (n + 1) * BLOCK, :]
 
     def write(n, which, x_t):
         low = x_t.astype(jnp.bfloat16)
@@ -154,13 +163,10 @@
         sib_out[which, :, cols] = out
 
     shares = [part(n) for n in range(SPLIT)]
-    live = []
-    while shares or live:
-        if shares:
-            live.append(shares.pop(0))
-        for share in list(live):
-            if next(share, 1) == 1:
-                live.remove(share)
+    for turn in range((4 + SPLIT) * len(chunks)):
+        for n, share in enumerate(shares):
+            if turn >= n * len(chunks):
+                next(share, None)
 
     @pl.when(unit == 2 * local_blocks - 1)
     def _():
@@ -224,8 +230,7 @@
             out_specs=[out_own, out_own, out_sib, small, kv_back],
             scratch_shapes=[pltpu.VMEM((blocks, BLOCK, HD), jnp.bfloat16)] * 4
             + [pltpu.VMEM((blocks, BLOCK, HD), jnp.float32)] * 2
-            + [pltpu.VMEM((SPLIT, keys_wide, ROWS), jnp.float32)] * 3
-            + [pltpu.VMEM((SPLIT, keys_wide, ROWS), jnp.bfloat16)] * 2
+            + [pltpu.VMEM((SPLIT, keys_wide, ROWS), jnp.float32)] * 2
             + [pltpu.VMEM((SPLIT, 8, ROWS), jnp.float32)],
         ),
         out_shape=[bf(tokens + BLOCK, width), bf(tokens + BLOCK, width), bf(2, tokens, width)]
@@ -317,6 +322,8 @@
         att_own, dq_own, sib, tau_rows, kv_grads = run_group(
             gi, ctx, place, strides, tau, q0, g0, qg_sib, kv_in[gi], tau_rows, offsets
         )
+        if grads:
+            kv_grads, grads[0] = lax.optimization_barrier((kv_grads, grads[0]))
         sib = lax.ppermute(sib, "ctx", swap)
         att_parts.append((att_own[:tokens], sib[0]))
         dq_parts.append((dq_own[:tokens], sib[1]))

time: 109 us -> 101 us (0.927)
  waiting for transfers between devices: 33.9 us -> 27.7 us
  Pallas kernels: 42.5 us -> 40 us
    all_to_all x2, waiting for transfers between devices: 20.4 us -> 12.1 us  [body(): grads.append(lax.all_to_all(kv_grads, 'ctx', 0, 0))]
    ppermute x3, waiting for transfers between devices: 0.01 us -> 3.51 us  [partner(): return lax.ppermute(x, axis, [(i, i ^ distance) for i in range(size)])]
    pallas_call x2, Pallas kernels: 37.2 us -> 34.8 us  [run_group(): pl.pallas_call(functools.partial(group_kernel, gi, devices, local_blocks,...]
    ppermute x2, waiting for transfers between devices: 1.52 us -> 0.01 us  [body(): sib = lax.ppermute(sib, 'ctx', swap)]
  transfers between devices with their start and end apart: 10 -> 10, of which waited for: 4 -> 3; matrix products, arithmetic and copies ran while one was open for 7% -> 8% of each run, Pallas kernels for 20% -> 37%
where the time goes in v4:
time: 101 us; the launch traced here: 100 us
  Pallas kernels  40 us (40%)
  waiting for transfers between devices  27.7 us (27%)
  starting transfers between devices  22.8 us (23%)
  other arithmetic  7.43 us (7%)
  local copies, waits for them, and re-layouts  1.84 us (2%)
    pallas_call x2, Pallas kernels, run_group(): pl.pallas_call(functools.partial(group_kernel, gi, devices, local_blocks,...  34.8 us
    all_to_all x2, waiting for transfers between devices, body(): grads.append(lax.all_to_all(kv_grads, 'ctx', 0, 0))  12.1 us
    all_to_all x2, waiting for transfers between devices, kv_for(): return lax.all_to_all(spread(gi, ctx, k0, v0), 'ctx', 0, 0)  12 us
    all_to_all x2, starting transfers between devices, kv_for(): return lax.all_to_all(spread(gi, ctx, k0, v0), 'ctx', 0, 0)  8.86 us
    all_to_all x2, starting transfers between devices, body(): grads.append(lax.all_to_all(kv_grads, 'ctx', 0, 0))  8.23 us
    pallas_call x2, Pallas kernels, spread(): pl.pallas_call(kernel, grid=(devices // 2,), in_specs=[taken, taken], out...  5.25 us
    ppermute x3, starting transfers between devices, partner(): return lax.ppermute(x, axis, [(i, i ^ distance) for i in range(size)])  4.44 us
    ppermute x3, waiting for transfers between devices, partner(): return lax.ppermute(x, axis, [(i, i ^ distance) for i in range(size)])  3.51 us
  transfers between devices with their start and end apart: 10, of which 3 were waited for; matrix products, arithmetic and copies ran while one was open for 8% of the time, Pallas kernels for 37%

profile of v4, /device:TPU:0, one launch (start us, length us, event | category | flops | bytes accessed | tf_op | source)
XLA Modules:
  0.0 100.5 jit_solution(12094064347598631616)
XLA Ops:
  0.6 2.6 %spread_keys_values.2 = bf16[8,2,256,128]{3,2,1,0:T(8,128)(2,1)} custom-call(bf16[256,512]{1,0:T(8,128)(2,1)} %bitcast.59, bf16[256,512]{1,0:T(8,128)(2,1)} %bitcast.61), custom_call_target="tpu_custom_call" | custom-call | tf_op jit(solution)/shard_map/spread_keys_values/pallas_call | solution.py:264
  3.3 5.3 %all-to-all-start = ((bf16[8,2,256,128]{3,2,1,0:T(8,128)(2,1)}), bf16[8,2,256,128]{3,2,1,0:T(8,128)(2,1)S(1)}, u32[]{:S(2)}, u32[]{:S(2)}) async-start(bf16[8,2,256,128]{3,2,1,0:T(8,128)(2,1)} %spread_keys_values.2), calls=%async_computation | async-start | bytes 2097152 | tf_op jit(solution)/shard_map/all_to_all | solution.py:311
  8.6 0.1 constant_dynamic-slice_fusion
  8.7 0.1 pad_maximum_fusion
  8.8 0.6 collective-permute-start
  9.4 2.6 %spread_keys_values.3 = bf16[8,2,256,128]{3,2,1,0:T(8,128)(2,1)} custom-call(bf16[256,512]{1,0:T(8,128)(2,1)} %bitcast.60, bf16[256,512]{1,0:T(8,128)(2,1)} %bitcast.62), custom_call_target="tpu_custom_call" | custom-call | tf_op jit(solution)/shard_map/spread_keys_values/pallas_call | solution.py:264
  12.0 12.0 %all-to-all-done.refs_7_ = bf16[8,2,256,128]{3,2,1,0:T(8,128)(2,1)S(1)} async-done(((bf16[8,2,256,128]{3,2,1,0:T(8,128)(2,1)}), bf16[8,2,256,128]{3,2,1,0:T(8,128)(2,1)S(1)}, u32[]{:S(2)}, u32[]{:S(2)}) %all-to-all-start) | async-done | bytes 1048608 | tf_op jit(solution)/shard_map/all_to_all | solution.py:311
  24.0 3.6 %all-to-all-start.1 = ((bf16[8,2,256,128]{3,2,1,0:T(8,128)(2,1)}), bf16[8,2,256,128]{3,2,1,0:T(8,128)(2,1)S(1)}, u32[]{:S(2)}, u32[]{:S(2)}) async-start(bf16[8,2,256,128]{3,2,1,0:T(8,128)(2,1)} %spread_keys_values.3), calls=%async_computation.1 | async-start | bytes 2097152 | tf_op jit(solution)/shard_map/all_to_all | solution.py:311
  27.7 0.1 sub.16
  27.7 0.5 and_select_fusion.refs_1_
  28.3 0.6 broadcast_in_dim.23.refs_8_
  28.9 17.3 %group_attention.2 = (bf16[384,512]{1,0:T(8,128)(2,1)}, bf16[384,512]{1,0:T(8,128)(2,1)}, bf16[2,256,512]{2,1,0:T(8,128)(2,1)}, f32[16,128]{1,0:T(8,128)}, bf16[8,528,128]{2,1,0:T(8,128)(2,1)}) custom-call(s32[1]{0:T(128)} %bitcast.refs_0_, s32[64]{0:T(128)} %and_select_fusion.refs_1_, f32[16]{0:T(128)} %refs_2_.3, bf16[256,2048]{1,0:T(8,128)(2,1)} %bitcast.63, ...), custom_call_target="tpu_custom_call" | custom-call | flops 4429185024 | bytes 6291456 | tf_op jit(solution)/shard_map/group_attention/pallas_call | solution.py:224
  46.3 1.0 copy-done.1
  47.2 4.1 %all-to-all-start.2 = ((bf16[8,528,128]{2,1,0:T(8,128)(2,1)}), bf16[8,528,128]{2,1,0:T(8,128)(2,1)S(1)}, u32[]{:S(2)}, u32[]{:S(2)}) async-start(bf16[8,528,128]{2,1,0:T(8,128)(2,1)} %get-tuple-element.24), calls=%async_computation.2 | async-start | bytes 2162688 | tf_op jit(solution)/shard_map/all_to_all | solution.py:330
  51.3 0.5 collective-permute-start.1
  51.8 17.4 %group_attention.3 = (bf16[384,512]{1,0:T(8,128)(2,1)}, bf16[384,512]{1,0:T(8,128)(2,1)}, bf16[2,256,512]{2,1,0:T(8,128)(2,1)}, f32[16,128]{1,0:T(8,128)}, bf16[8,528,128]{2,1,0:T(8,128)(2,1)}) custom-call(s32[1]{0:T(128)} %bitcast.refs_0_, s32[64]{0:T(128)} %and_select_fusion.refs_1_, f32[16]{0:T(128)} %refs_2_.3, bf16[256,2048]{1,0:T(8,128)(2,1)} %bitcast.64, ...), custom_call_target="tpu_custom_call" | custom-call | flops 4429185024 | bytes 6291456 | tf_op jit(solution)/shard_map/group_attention/pallas_call | solution.py:224
  69.3 0.2 collective-permute-start.2
  69.4 1.0 %broadcast_select_fusion.5 = (bf16[256,512]{1,0:T(8,128)(2,1)S(1)}, bf16[256,512]{1,0:T(8,128)(2,1)S(1)}, bf16[256,512]{1,0:T(8,128)(2,1)S(1)}, bf16[256,512]{1,0:T(8,128)(2,1)S(1)}) fusion(pred[]{:T(512)S(6)} %eq.8, bf16[2,256,512]{2,1,0:T(8,128)(2,1)S(1)} %collective-permute-done.1, bf16[384,512]{1,0:T(8,128)(2,1)} %get-tuple-element.21, pred[]{:T(512)S(6)} %eq.9, ...), kind=kLoop, calls=%fused_computation.14 | loop fusion | flops 524288 | bytes 2097154 | tf_op jit(solution)/shard_map/jit(_where)/select_n | solution.py:334
  70.5 4.1 %all-to-all-start.3 = ((bf16[8,528,128]{2,1,0:T(8,128)(2,1)}), bf16[8,528,128]{2,1,0:T(8,128)(2,1)S(1)}, u32[]{:S(2)}, u32[]{:S(2)}) async-start(bf16[8,528,128]{2,1,0:T(8,128)(2,1)} %get-tuple-element.26), calls=%async_computation.3 | async-start | bytes 2162688 | tf_op jit(solution)/shard_map/all_to_all | solution.py:330
  74.6 1.3 %broadcast_select_fusion.4 = (bf16[256,512]{1,0:T(8,128)(2,1)S(1)}, bf16[256,512]{1,0:T(8,128)(2,1)S(1)}, bf16[256,512]{1,0:T(8,128)(2,1)S(1)}, bf16[256,512]{1,0:T(8,128)(2,1)S(1)}) fusion(pred[]{:T(512)S(6)} %eq.8, bf16[2,256,512]{2,1,0:T(8,128)(2,1)} %collective-permute-done.2, bf16[384,512]{1,0:T(8,128)(2,1)} %get-tuple-element.22, pred[]{:T(512)S(6)} %eq.9, ...), kind=kLoop, calls=%fused_computation.13 | loop fusion | flops 524288 | bytes 2097154 | tf_op jit(solution)/shard_map/jit(_where)/select_n | solution.py:334
  75.9 1.1 %maximum_bitcast_fusion.1 = bf16[1,256,2048]{2,1,0:T(8,128)(2,1)} fusion(bf16[256,512]{1,0:T(8,128)(2,1)S(1)} %get-tuple-element.38, bf16[256,512]{1,0:T(8,128)(2,1)S(1)} %get-tuple-element.36, bf16[256,512]{1,0:T(8,128)(2,1)S(1)} %get-tuple-element.37, bf16[256,512]{1,0:T(8,128)(2,1)S(1)} %get-tuple-element.35), kind=kLoop, calls=%fused_computation.2 | loop fusion | flops 4194304 | bytes 2097152 | tf_op jit(solution)/shard_map/broadcast_in_dim | solution.py:338
  77.0 1.1 %maximum_bitcast_fusion = bf16[1,256,2048]{2,1,0:T(8,128)(2,1)} fusion(bf16[256,512]{1,0:T(8,128)(2,1)S(1)} %get-tuple-element.45, bf16[256,512]{1,0:T(8,128)(2,1)S(1)} %get-tuple-element.43, bf16[256,512]{1,0:T(8,128)(2,1)S(1)} %get-tuple-element.46, bf16[256,512]{1,0:T(8,128)(2,1)S(1)} %get-tuple-element.44), kind=kLoop, calls=%fused_computation.1 | loop fusion | flops 4194304 | bytes 2097152 | tf_op jit(solution)/shard_map/broadcast_in_dim | solution.py:337
  78.1 0.1 fusion.4
  78.2 12.1 %all-to-all-done.3 = bf16[8,528,128]{2,1,0:T(8,128)(2,1)S(1)} async-done(((bf16[8,528,128]{2,1,0:T(8,128)(2,1)}), bf16[8,528,128]{2,1,0:T(8,128)(2,1)S(1)}, u32[]{:S(2)}, u32[]{:S(2)}) %all-to-all-start.3) | async-done | bytes 1081376 | tf_op jit(solution)/shard_map/all_to_all | solution.py:330
  90.4 1.6 %collective-permute-start.3 = (f32[1,16]{1,0:T(1,128)S(1)}, f32[1,16]{1,0:T(1,128)S(1)}, u32[]{:S(2)}, u32[]{:S(2)}) collective-permute-start(f32[1,16]{1,0:T(1,128)S(1)} %bitcast.67), channel_id=1, source_target_pairs={{0,1},{1,0},{2,3},{3,2},{4,5},{5,4},{6,7},{7,6},{8,9},{9,8},{10,11... | collective-permute-start | bytes 200 | tf_op jit(solution)/shard_map/ppermute | solution.py:281
  92.0 2.6 %collective-permute-start.4 = (f32[1,16]{1,0:T(1,128)S(1)}, f32[1,16]{1,0:T(1,128)S(1)}, u32[]{:S(2)}, u32[]{:S(2)}) collective-permute-start(f32[1,16]{1,0:T(1,128)S(1)} %bitcast.68), channel_id=1, source_target_pairs={{0,2},{1,3},{2,0},{3,1},{4,6},{5,7},{6,4},{7,5},{8,10},{9,11},{10,... | collective-permute-start | bytes 200 | tf_op jit(solution)/shard_map/ppermute | solution.py:281
  94.6 0.2 collective-permute-start.5
  94.8 0.1 fusion.5
  95.0 0.7 maximum_bitcast_fusion.3
  95.7 0.7 maximum_bitcast_fusion.2
  96.4 3.5 %collective-permute-done.5 = f32[1,16]{1,0:T(1,128)S(1)} collective-permute-done((f32[1,16]{1,0:T(1,128)S(1)}, f32[1,16]{1,0:T(1,128)S(1)}, u32[]{:S(2)}, u32[]{:S(2)}) %collective-permute-start.5) | collective-permute-done | bytes 96 | tf_op jit(solution)/shard_map/ppermute | solution.py:281
  99.9 0.5 multiply_bitcast_fusion
  (23 shorter events, 0.2 us)
Async XLA Ops:
  3.3 5.3 %copy-start.2 = (bf16[1,256,2048]{2,1,0:T(8,128)(2,1)S(1)}, bf16[1,256,2048]{2,1,0:T(8,128)(2,1)}, u32[]{:S(2)}) copy-start(bf16[1,256,2048]{2,1,0:T(8,128)(2,1)} %param.6) | copy-start | bytes 3145732
  3.3 5.3 %copy-start.3 = (bf16[1,256,2048]{2,1,0:T(8,128)(2,1)S(1)}, bf16[1,256,2048]{2,1,0:T(8,128)(2,1)}, u32[]{:S(2)}) copy-start(bf16[1,256,2048]{2,1,0:T(8,128)(2,1)} %param.10) | copy-start | bytes 3145732
  3.3 20.7 %all-to-all-start = ((bf16[8,2,256,128]{3,2,1,0:T(8,128)(2,1)}), bf16[8,2,256,128]{3,2,1,0:T(8,128)(2,1)S(1)}, u32[]{:S(2)}, u32[]{:S(2)}) async-start(bf16[8,2,256,128]{3,2,1,0:T(8,128)(2,1)} %spread_keys_values.2), calls=%async_computation | async-start | bytes 2097152 | tf_op jit(solution)/shard_map/all_to_all | solution.py:311
  8.8 19.5 %collective-permute-start = (bf16[2,256,1024]{2,1,0:T(8,128)(2,1)S(1)}, bf16[2,256,1024]{2,1,0:T(8,128)(2,1)}, u32[]{:S(2)}, u32[]{:S(2)}) collective-permute-start(bf16[2,256,1024]{2,1,0:T(8,128)(2,1)S(1)} %pad_maximum_fusion), channel_id=1, source_target_pairs={{0,4},{4,0},{8,12},{12,8},{16,20},{20,16},{24,28},{28,24},{1,5},{5... | collective-permute-start | bytes 3145736 | tf_op jit(solution)/shard_map/ppermute | solution.py:317
  12.0 15.6 %slice-start = ((s32[4,16,13]{1,0,2:T(4,128)}), s32[4,16,1]{1,0,2:T(4,128)S(1)}, s32[]{:S(2)}) async-start(s32[4,16,13]{1,0,2:T(4,128)} %param.11), calls=%async_computation.4 | async-start | bytes 4096 | tf_op jit(solution)/shard_map/slice | solution.py:308
  24.0 4.9 %copy-start = (bf16[8,2,256,128]{3,2,1,0:T(8,128)(2,1)}, bf16[8,2,256,128]{3,2,1,0:T(8,128)(2,1)S(1)}, u32[]{:S(2)}) copy-start(bf16[8,2,256,128]{3,2,1,0:T(8,128)(2,1)S(1)} %all-to-all-done.refs_7_) | copy-start | bytes 3145732
  24.0 22.2 %all-to-all-start.1 = ((bf16[8,2,256,128]{3,2,1,0:T(8,128)(2,1)}), bf16[8,2,256,128]{3,2,1,0:T(8,128)(2,1)S(1)}, u32[]{:S(2)}, u32[]{:S(2)}) async-start(bf16[8,2,256,128]{3,2,1,0:T(8,128)(2,1)} %spread_keys_values.3), calls=%async_computation.1 | async-start | bytes 2097152 | tf_op jit(solution)/shard_map/all_to_all | solution.py:311
  46.2 1.0 copy-start.1
  46.2 5.1 %copy-start.5 = (bf16[2,256,512]{2,1,0:T(8,128)(2,1)S(1)}, bf16[2,256,512]{2,1,0:T(8,128)(2,1)}, u32[]{:S(2)}) copy-start(bf16[2,256,512]{2,1,0:T(8,128)(2,1)} %get-tuple-element.17) | copy-start | bytes 1572868
  47.2 23.2 %all-to-all-start.2 = ((bf16[8,528,128]{2,1,0:T(8,128)(2,1)}), bf16[8,528,128]{2,1,0:T(8,128)(2,1)S(1)}, u32[]{:S(2)}, u32[]{:S(2)}) async-start(bf16[8,528,128]{2,1,0:T(8,128)(2,1)} %get-tuple-element.24), calls=%async_computation.2 | async-start | bytes 2162688 | tf_op jit(solution)/shard_map/all_to_all | solution.py:330
  51.3 18.1 %collective-permute-start.1 = (bf16[2,256,512]{2,1,0:T(8,128)(2,1)S(1)}, bf16[2,256,512]{2,1,0:T(8,128)(2,1)S(1)}, u32[]{:S(2)}, u32[]{:S(2)}) collective-permute-start(bf16[2,256,512]{2,1,0:T(8,128)(2,1)S(1)} %copy-done.5), channel_id=1, source_target_pairs={{0,4},{4,0},{8,12},{12,8},{16,20},{20,16},{24,28},{28,24},{1,5},{5... | collective-permute-start | bytes 1572872 | tf_op jit(solution)/shard_map/ppermute | solution.py:327
  51.8 17.6 %copy-start.4 = (bf16[384,512]{1,0:T(8,128)(2,1)S(1)}, bf16[384,512]{1,0:T(8,128)(2,1)}, u32[]{:S(2)}) copy-start(bf16[384,512]{1,0:T(8,128)(2,1)} %get-tuple-element.16) | copy-start | bytes 1179652
  69.3 5.3 %collective-permute-start.2 = (bf16[2,256,512]{2,1,0:T(8,128)(2,1)}, bf16[2,256,512]{2,1,0:T(8,128)(2,1)}, u32[]{:S(2)}, u32[]{:S(2)}) collective-permute-start(bf16[2,256,512]{2,1,0:T(8,128)(2,1)} %get-tuple-element.20), channel_id=1, source_target_pairs={{0,4},{4,0},{8,12},{12,8},{16,20},{20,16},{24,28},{28,24},{1,5},{5... | collective-permute-start | bytes 1572872 | tf_op jit(solution)/shard_map/ppermute | solution.py:327
  70.5 19.9 %all-to-all-start.3 = ((bf16[8,528,128]{2,1,0:T(8,128)(2,1)}), bf16[8,528,128]{2,1,0:T(8,128)(2,1)S(1)}, u32[]{:S(2)}, u32[]{:S(2)}) async-start(bf16[8,528,128]{2,1,0:T(8,128)(2,1)} %get-tuple-element.26), calls=%async_computation.3 | async-start | bytes 2162688 | tf_op jit(solution)/shard_map/all_to_all | solution.py:330
  90.4 6.1 %collective-permute-start.3 = (f32[1,16]{1,0:T(1,128)S(1)}, f32[1,16]{1,0:T(1,128)S(1)}, u32[]{:S(2)}, u32[]{:S(2)}) collective-permute-start(f32[1,16]{1,0:T(1,128)S(1)} %bitcast.67), channel_id=1, source_target_pairs={{0,1},{1,0},{2,3},{3,2},{4,5},{5,4},{6,7},{7,6},{8,9},{9,8},{10,11... | collective-permute-start | bytes 200 | tf_op jit(solution)/shard_map/ppermute | solution.py:281
  92.0 4.4 %collective-permute-start.4 = (f32[1,16]{1,0:T(1,128)S(1)}, f32[1,16]{1,0:T(1,128)S(1)}, u32[]{:S(2)}, u32[]{:S(2)}) collective-permute-start(f32[1,16]{1,0:T(1,128)S(1)} %bitcast.68), channel_id=1, source_target_pairs={{0,2},{1,3},{2,0},{3,1},{4,6},{5,7},{6,4},{7,5},{8,10},{9,11},{10,... | collective-permute-start | bytes 200 | tf_op jit(solution)/shard_map/ppermute | solution.py:281
  94.6 5.3 %collective-permute-start.5 = (f32[1,16]{1,0:T(1,128)S(1)}, f32[1,16]{1,0:T(1,128)S(1)}, u32[]{:S(2)}, u32[]{:S(2)}) collective-permute-start(f32[1,16]{1,0:T(1,128)S(1)} %bitcast.69), channel_id=1, source_target_pairs={{0,3},{1,2},{2,1},{3,0},{4,7},{5,6},{6,5},{7,4},{8,11},{9,10},{10,... | collective-permute-start | bytes 200 | tf_op jit(solution)/shard_map/ppermute | solution.py:281

commit v5 on v4

v5 whole, which is shorter than its diff:
```python
import functools
import math

import jax
import jax.numpy as jnp
from jax import lax
from jax.experimental import pallas as pl
from jax.experimental.pallas import tpu as pltpu
from jax.sharding import PartitionSpec as P

HEADS = 16
KV_HEADS = 4
HD = 128
BLOCK = 128
QPG = HEADS // KV_HEADS
CHUNK = 4
ROWS = QPG * BLOCK
TAIL = 8
STRIDES = (2, 3)
LOG2E = math.log2(math.e)
NEVER = -1e30


def distinct_offsets(block_count, listed_count):
    tables = []
    for stride in STRIDES:
        steps = range(1, (listed_count - 3) // 2 + 1)
        listed = [-1, 0, 1] + [stride * m for m in steps] + [-stride * m for m in steps]
        times = {}
        for o in listed:
            times[o % block_count] = times.get(o % block_count, 0) + 1
        tables.append(sorted(times.items()))
    most = max(len(t) for t in tables)
    return [t + [(0, 0)] * (most - len(t)) for t in tables]


def nt(a, b):
    return jnp.dot(a, b, preferred_element_type=jnp.float32)


def group_kernel(gi, devices, local_blocks, listed, offsets, *refs):
    place, key_blocks, taus = refs[:3]
    inputs, rest = refs[3 : 8 + gi], refs[8 + gi :]
    q_own, q_sib, g_own, g_sib, kv_in = inputs[:5]
    att_own, dq_own, sib_out, tau_out, kv_out = rest[:5]
    k_s, v_s, kt_s, vt_s, dk_s, dv_s, s_s, e_s, tau_s = rest[5:]
    step = pl.program_id(0)
    blocks = devices * local_blocks
    me = place[0]
    group = 2 * (me % 2) + gi

    @pl.when(step == 0)
    def _():
        def fill(b, carry):
            for half in range(local_blocks):
                rows = slice(half * BLOCK, (half + 1) * BLOCK)
                k_block = kv_in[b, 0, rows, :]
                v_block = kv_in[b, 1, rows, :]
                at = b * local_blocks + half
                k_s[at] = k_block
                v_s[at] = v_block
                kt_s[at] = k_block.T
                vt_s[at] = v_block.T
            return carry

        lax.fori_loop(0, devices, fill, 0, unroll=2)
        dk_s[...] = jnp.zeros_like(dk_s)
        dv_s[...] = jnp.zeros_like(dv_s)
        tau_s[...] = jnp.zeros_like(tau_s)

    chunks = [range(c, min(c + CHUNK, listed)) for c in range(0, listed, CHUNK)]
    scale = jnp.concatenate(
        [jnp.full((1, BLOCK), taus[group * QPG + h], jnp.float32) for h in range(QPG)], axis=1
    ) / math.sqrt(HD)
    factor = scale * LOG2E

    def rows_of(c):
        return slice(c[0] * BLOCK, (c[-1] + 1) * BLOCK)

    def per_head(x):
        return [x[:, h * HD : (h + 1) * HD] for h in range(QPG)]

    def in_rows(x):
        return x.reshape(-1, 8, ROWS)

    def part(n):
        s_n, e_n = s_s.at[n], e_s.at[n]
        query_block = (me ^ n) * local_blocks + step
        wide = (key_blocks[group, query_block, 3] - query_block) % blocks == STRIDES[1]
        ids, bias = [], []
        for (narrow_off, narrow_times), (wide_off, wide_times) in zip(*offsets):
            ids.append((query_block + jnp.where(wide, wide_off, narrow_off)) % blocks)
            bias.append(
                times_bias(narrow_times)
                if narrow_times == wide_times
                else jnp.where(wide, times_bias(wide_times), times_bias(narrow_times))
            )

        def picked(ref, c, axis):
            return jnp.concatenate([ref[ids[j]] for j in c], axis=axis)

        def add_blocks(ref, c, x):
            for n, j in enumerate(c):
                ref[ids[j]] += x[n * BLOCK : (n + 1) * BLOCK, :]

        q_here = q_sib[0] if n else q_own[...]
        g_here = g_sib[0] if n else g_own[...]
        q_rows = jnp.concatenate(per_head(q_here), axis=0)
        g_rows = jnp.concatenate(per_head(g_here), axis=0)
        q_t = jnp.concatenate([x.T for x in per_head(q_here)], axis=1)
        g_t = jnp.concatenate([x.T for x in per_head(g_here)], axis=1)
        most = None
        for c in chunks:
            raw = nt(picked(k_s, c, 0), q_t)
            s_n[rows_of(c), :] = raw
            top = jnp.max(in_rows(raw), axis=0)
            most = top if most is None else jnp.maximum(most, top)
            yield
        top_row = jnp.max(most, axis=0, keepdims=True) * factor
        total = jnp.zeros((8, ROWS), jnp.float32)
        for c in chunks:
            for j in c:
                rows = slice(j * BLOCK, (j + 1) * BLOCK)
                e = jnp.exp2(s_n[rows, :] * factor - (top_row - bias[j]))
                e_n[rows, :] = e
                total = total + jnp.sum(in_rows(e), axis=0)
            yield
        inverse = 1.0 / jnp.sum(total, axis=0, keepdims=True)
        o_t = jnp.zeros((HD, ROWS), jnp.float32)
        for c in chunks:
            probs = (e_n[rows_of(c), :] * inverse).astype(jnp.bfloat16)
            o_t = o_t + nt(picked(vt_s, c, 1), probs)
            add_blocks(dv_s, c, nt(probs, g_rows))
            yield
        row_dot = jnp.sum(g_t.astype(jnp.float32) * o_t, axis=0, keepdims=True)
        write(n, 0, o_t)
        weight_scale = inverse * scale
        tau_rows = jnp.zeros((8, ROWS), jnp.float32)
        dq_t = jnp.zeros((HD, ROWS), jnp.float32)
        for c in chunks:
            dweights = nt(picked(v_s, c, 0), g_t)
            scaled = e_n[rows_of(c), :] * weight_scale * (dweights - row_dot)
            tau_rows = tau_rows + jnp.sum(in_rows(scaled * s_n[rows_of(c), :]), axis=0)
            low = scaled.astype(jnp.bfloat16)
            dq_t = dq_t + nt(picked(kt_s, c, 1), low)
            add_blocks(dk_s, c, nt(low, q_rows))
            yield
        tau_s[n] += tau_rows
        write(n, 1, dq_t)

    def write(n, which, x_t):
        low = x_t.astype(jnp.bfloat16)
        out = jnp.concatenate([x.T for x in per_head(low)], axis=1)
        if n:
            sib_out[which] = out
        else:
            (att_own, dq_own)[which][...] = out

    shares = [part(n) for n in range(2)]
    for turn in range(6 * len(chunks)):
        for n, share in enumerate(shares):
            if turn >= n * len(chunks):
                next(share, None)

    @pl.when(step == local_blocks - 1)
    def _():
        lane = lax.broadcasted_iota(jnp.int32, (TAIL, HD), 1)
        sums = inputs[5][...] if gi else jnp.zeros((TAIL, HD), jnp.float32)
        for h in range(QPG):
            head = group * QPG + h
            rows = tau_s[:, :, h * BLOCK : (h + 1) * BLOCK]
            sums = sums + jnp.where(lane == head, jnp.sum(rows) / taus[head], 0.0)
        tau_out[...] = sums

        def drain(b, carry):
            for half in range(local_blocks):
                at = b * local_blocks + half
                rows = slice(half * BLOCK, (half + 1) * BLOCK)
                kv_out[b, 0, rows, :] = dk_s[at].astype(jnp.bfloat16)
                kv_out[b, 1, rows, :] = dv_s[at].astype(jnp.bfloat16)
            return carry

        lax.fori_loop(0, devices, drain, 0, unroll=2)


def times_bias(times):
    return math.log2(times) if times else NEVER


def run_group(gi, devices, place, key_blocks, tau, queries, out_grad, qg_sib, kv_in, tau_in, offsets):
    listed = len(offsets[0])
    tokens = queries.shape[0]
    local_blocks = tokens // BLOCK
    blocks = devices * local_blocks
    width = QPG * HD
    block_own = pl.BlockSpec((BLOCK, width), lambda u, p, s, t: (u, 2 * (p[0] % 2) + gi))
    qs = pl.BlockSpec((1, BLOCK, width), lambda u, p, s, t: (0, u, gi))
    gs = pl.BlockSpec((1, BLOCK, width), lambda u, p, s, t: (1, u, gi))
    out_own = pl.BlockSpec((BLOCK, width), lambda u, p, s, t: (u, 0))
    out_sib = pl.BlockSpec((2, BLOCK, width), lambda u, p, s, t: (0, u, 0))
    kv_all = pl.BlockSpec((devices, 2, tokens, HD), lambda u, p, s, t: (0, 0, 0, 0))
    small = pl.BlockSpec((TAIL, HD), lambda u, p, s, t: (0, 0))
    bf = lambda *shape: jax.ShapeDtypeStruct(shape, jnp.bfloat16)
    keys_wide = listed * BLOCK
    cells = 2 * local_blocks * ROWS * keys_wide
    return pl.pallas_call(
        functools.partial(group_kernel, gi, devices, local_blocks, listed, offsets),
        grid_spec=pltpu.PrefetchScalarGridSpec(
            num_scalar_prefetch=3,
            grid=(local_blocks,),
            in_specs=[block_own, qs, block_own, gs, kv_all] + [small] * gi,
            out_specs=[out_own, out_own, out_sib, small, kv_all],
            scratch_shapes=[pltpu.VMEM((blocks, BLOCK, HD), jnp.bfloat16)] * 4
            + [pltpu.VMEM((blocks, BLOCK, HD), jnp.float32)] * 2
            + [pltpu.VMEM((2, keys_wide, ROWS), jnp.float32)] * 2
            + [pltpu.VMEM((2, 8, ROWS), jnp.float32)],
        ),
        out_shape=[bf(tokens, width), bf(tokens, width), bf(2, tokens, width)]
        + [jax.ShapeDtypeStruct((TAIL, HD), jnp.float32), bf(devices, 2, tokens, HD)],
        compiler_params=pltpu.CompilerParams(
            dimension_semantics=("arbitrary",), vmem_limit_bytes=60 * 2**20
        ),
        cost_estimate=pl.CostEstimate(
            flops=12 * HD * cells, bytes_accessed=6 * 2**20, transcendentals=cells
        ),
        name="group_attention",
    )(place, key_blocks, tau, queries, qg_sib, out_grad, qg_sib, kv_in, *tau_in[:gi])


def total_over(x, axis):
    size = lax.axis_size(axis)
    if size & (size - 1):
        return lax.psum(x, axis)
    step = 1
    while step < size:
        radix = min(8, size // step)
        terms = [x] + [
            lax.ppermute(x, axis, [(i, i ^ (step * d)) for i in range(size)]) for d in range(1, radix)
        ]
        while len(terms) > 1:
            terms = [a + b for a, b in zip(terms[::2], terms[1::2])]
        x = terms[0]
        step *= radix
    return x


def spread(gi, devices, keys, values):
    tokens = keys.shape[0]

    def kernel(k_ref, v_ref, out, sems):
        copies = []
        for d in range(devices):
            group = 2 * (d % 2) + gi
            for which, ref in enumerate((k_ref, v_ref)):
                source = ref.at[:, group * HD : (group + 1) * HD]
                copies.append(pltpu.make_async_copy(source, out.at[d, which], sems.at[d, which]))
        for copy in copies:
            copy.start()
        for copy in copies:
            copy.wait()

    anywhere = pl.BlockSpec(memory_space=pl.ANY)
    return pl.pallas_call(
        kernel,
        in_specs=[anywhere, anywhere],
        out_specs=anywhere,
        out_shape=jax.ShapeDtypeStruct((devices, 2, tokens, HD), jnp.bfloat16),
        scratch_shapes=[pltpu.SemaphoreType.DMA((devices, 2))],
        compiler_params=pltpu.CompilerParams(vmem_limit_bytes=60 * 2**20),
        name="spread_keys_values",
    )(keys, values)


def body(queries, keys, values, tau, out_grad, key_blocks):
    ctx = lax.axis_size("ctx")
    me = lax.axis_index("ctx").astype(jnp.int32)
    core = me % 2
    tokens = queries.shape[1]
    local_blocks = tokens // BLOCK
    block_count = ctx * local_blocks
    listed_count = key_blocks.shape[2]
    offsets = distinct_offsets(block_count, listed_count)
    swap = [(d, d ^ 1) for d in range(ctx)]
    wide = 2 * QPG * HD

    q0, k0, v0, g0 = queries[0], keys[0], values[0], out_grad[0]
    place = me[None]

    def kv_for(gi):
        return lax.all_to_all(spread(gi, ctx, k0, v0), "ctx", 0, 0)

    def theirs(x):
        return lax.dynamic_slice_in_dim(x, (1 - core) * wide, wide, 1)

    kv_in = [kv_for(gi) for gi in range(2)]
    qg_sib = lax.ppermute(jnp.stack([theirs(q0), theirs(g0)]), "ctx", swap)

    sibs, owns, grads, tau_rows = [], [], [], []
    for gi in range(2):
        att_own, dq_own, sib, tau_here, kv_grads = run_group(
            gi, ctx, place, key_blocks, tau, q0, g0, qg_sib, kv_in[gi], tau_rows, offsets
        )
        tau_rows.append(tau_here)
        if gi:
            kv_grads, grads[0] = lax.optimization_barrier((kv_grads, grads[0]))
        owns.append((att_own, dq_own))
        sibs.append(lax.ppermute(sib, "ctx", swap))
        grads.append(lax.all_to_all(kv_grads, "ctx", 0, 0))
    tau_all, sibs = lax.optimization_barrier((tau_rows[1], sibs))
    att_parts, dq_parts = (
        [(own[which], sib[which]) for own, sib in zip(owns, sibs)] for which in range(2)
    )

    def by_group(parts):
        return jnp.concatenate(
            [jnp.where(core == c // 2, parts[c % 2][0], parts[c % 2][1]) for c in range(4)], axis=1
        )

    attended = by_group(att_parts)[None]
    query_grad = by_group(dq_parts)[None]

    def summed(which):
        cols = []
        for c in range(4):
            total = None
            for src in range(c // 2, ctx, 2):
                term = grads[c % 2][src, which].astype(jnp.float32)
                total = term if total is None else total + term
            cols.append(total.astype(jnp.bfloat16))
        return jnp.concatenate(cols, axis=1)[None]

    key_grad, value_grad = summed(0), summed(1)
    scale_total = total_over(total_over(tau_all[:1], "batch"), "ctx")[0, :HEADS]
    tau_grad = scale_total / math.sqrt(lax.axis_size("batch") * ctx * tokens)
    return (attended, query_grad, key_grad, value_grad, tau_grad)


def solution(mesh):
    rows = P("batch", "ctx", None)
    return jax.shard_map(
        body,
        mesh=mesh,
        in_specs=(rows, rows, rows, P(), rows, P()),
        out_specs=(rows, rows, rows, rows, P()),
        check_vma=False,
    )
```

time: 101 us -> 154 us (1.52)
  Pallas kernels: 40 us -> 98.9 us
  waiting for transfers between devices: 27.7 us -> 13.1 us
  starting transfers between devices: 22.8 us -> 31.6 us
  other arithmetic: 7.43 us -> 5.42 us
  local copies, waits for them, and re-layouts: 1.84 us -> 3.58 us
    pallas_call x2, Pallas kernels: 5.25 us -> 66 us  [spread(): pl.pallas_call(kernel, in_specs=[anywhere, anywhere], out_specs=anywhere,...]
    all_to_all x2, waiting for transfers between devices: 12 us -> 0.01 us  [kv_for(): return lax.all_to_all(spread(gi, ctx, k0, v0), 'ctx', 0, 0)]
    all_to_all x2, waiting for transfers between devices: 12.1 us -> 0.75 us  [body(): grads.append(lax.all_to_all(kv_grads, 'ctx', 0, 0))]
    ppermute x5 -> x12, starting transfers between devices: 5.1 us -> 14 us  [the longest x10 13.4 us: total_over(): lax.ppermute(x, axis, [(i, i ^ step * d) for i in range(size)])]
    ppermute x5 -> x12, waiting for transfers between devices: 3.51 us -> 12.4 us  [the longest x10 12.3 us: total_over(): lax.ppermute(x, axis, [(i, i ^ step * d) for i in range(size)])]
    select_n x2, other arithmetic: 2.29 us -> 0.15 us  [by_group(): jnp.where(core == c // 2, parts[c % 2][0], parts[c % 2][1])]
    pallas_call x2, Pallas kernels: 34.8 us -> 32.9 us  [run_group(): pl.pallas_call(functools.partial(group_kernel, gi, devices, local_blocks,...]
    unnamed x12 -> x25, local copies, waits for them, and re-layouts: 0.97 us -> 2.79 us
  transfers between devices with their start and end apart: 10 -> 17, of which waited for: 3 -> 3; matrix products, arithmetic and copies ran while one was open for 8% -> 3% of each run, Pallas kernels for 37% -> 32%
where the time goes in v5:
time: 154 us; the launch traced here: 153 us
  Pallas kernels  98.9 us (64%)
  starting transfers between devices  31.6 us (21%)
  waiting for transfers between devices  13.1 us (9%)
  other arithmetic  5.42 us (4%)
  local copies, waits for them, and re-layouts  3.58 us (2%)
    pallas_call x2, Pallas kernels, spread(): pl.pallas_call(kernel, in_specs=[anywhere, anywhere], out_specs=anywhere,...  66 us
    pallas_call x2, Pallas kernels, run_group(): pl.pallas_call(functools.partial(group_kernel, gi, devices, local_blocks,...  32.9 us
    ppermute x10, starting transfers between devices, total_over(): lax.ppermute(x, axis, [(i, i ^ step * d) for i in range(size)])  13.4 us
    ppermute x10, waiting for transfers between devices, total_over(): lax.ppermute(x, axis, [(i, i ^ step * d) for i in range(size)])  12.3 us
    all_to_all x2, starting transfers between devices, kv_for(): return lax.all_to_all(spread(gi, ctx, k0, v0), 'ctx', 0, 0)  9.18 us
    all_to_all x2, starting transfers between devices, body(): grads.append(lax.all_to_all(kv_grads, 'ctx', 0, 0))  7.81 us
  transfers between devices with their start and end apart: 17, of which 3 were waited for; matrix products, arithmetic and copies ran while one was open for 3% of the time, Pallas kernels for 32%

profile of v5, /device:TPU:0, one launch (start us, length us, event | category | flops | bytes accessed | tf_op | source)
XLA Modules:
  0.0 153.5 jit_solution(16840711925429354382)
XLA Ops:
  0.6 33.0 %spread_keys_values.2 = bf16[8,2,256,128]{3,2,1,0:T(8,128)(2,1)} custom-call(bf16[256,512]{1,0:T(8,128)(2,1)} %bitcast.43, bf16[256,512]{1,0:T(8,128)(2,1)} %bitcast.45), custom_call_target="tpu_custom_call" | custom-call | tf_op jit(solution)/shard_map/spread_keys_values/pallas_call | solution.py:263
  33.7 5.3 %all-to-all-start = ((bf16[8,2,256,128]{3,2,1,0:T(8,128)(2,1)}), bf16[8,2,256,128]{3,2,1,0:T(8,128)(2,1)S(1)}, u32[]{:S(2)}, u32[]{:S(2)}) async-start(bf16[8,2,256,128]{3,2,1,0:T(8,128)(2,1)} %spread_keys_values.2), calls=%async_computation | async-start | bytes 2097152 | tf_op jit(solution)/shard_map/all_to_all | solution.py:290
  39.2 0.6 collective-permute-start
  39.8 33.0 %spread_keys_values.3 = bf16[8,2,256,128]{3,2,1,0:T(8,128)(2,1)} custom-call(bf16[256,512]{1,0:T(8,128)(2,1)} %bitcast.44, bf16[256,512]{1,0:T(8,128)(2,1)} %bitcast.46), custom_call_target="tpu_custom_call" | custom-call | tf_op jit(solution)/shard_map/spread_keys_values/pallas_call | solution.py:263
  72.8 3.9 %all-to-all-start.1 = ((bf16[8,2,256,128]{3,2,1,0:T(8,128)(2,1)}), bf16[8,2,256,128]{3,2,1,0:T(8,128)(2,1)S(1)}, u32[]{:S(2)}, u32[]{:S(2)}) async-start(bf16[8,2,256,128]{3,2,1,0:T(8,128)(2,1)} %spread_keys_values.3), calls=%async_computation.1 | async-start | bytes 2097152 | tf_op jit(solution)/shard_map/all_to_all | solution.py:290
  76.7 0.7 copy.11.refs_1_
  77.4 16.4 %group_attention.2 = (bf16[256,512]{1,0:T(8,128)(2,1)}, bf16[256,512]{1,0:T(8,128)(2,1)}, bf16[2,256,512]{2,1,0:T(8,128)(2,1)}, f32[8,128]{1,0:T(8,128)}, bf16[8,2,256,128]{3,2,1,0:T(8,128)(2,1)}) custom-call(s32[1]{0:T(128)} %bitcast.refs_0_, s32[4,16,13]{2,1,0:T(8,128)} %copy.11.refs_1_, f32[16]{0:T(128)} %refs_2_.3, bf16[256,2048]{1,0:T(8,128)(2,1)} %bitcast.47, ...), custom_call_target="tpu_custom_call" | custom-call | flops 4429185024 | bytes 6291456 | tf_op jit(solution)/shard_map/group_attention/pallas_call | solution.py:206
  93.8 1.0 copy-done.1
  94.8 16.5 %group_attention.3 = (bf16[256,512]{1,0:T(8,128)(2,1)}, bf16[256,512]{1,0:T(8,128)(2,1)}, bf16[2,256,512]{2,1,0:T(8,128)(2,1)}, f32[8,128]{1,0:T(8,128)}, bf16[8,2,256,128]{3,2,1,0:T(8,128)(2,1)}) custom-call(s32[1]{0:T(128)} %bitcast.refs_0_, s32[4,16,13]{2,1,0:T(8,128)} %copy.11.refs_1_, f32[16]{0:T(128)} %refs_2_.3, bf16[256,2048]{1,0:T(8,128)(2,1)} %bitcast.48, ...), custom_call_target="tpu_custom_call" | custom-call | flops 4429185024 | bytes 6291456 | tf_op jit(solution)/shard_map/group_attention/pallas_call | solution.py:206
  111.3 0.6 collective-permute-start.2
  112.0 4.3 %all-to-all-start.2 = ((bf16[8,2,256,128]{3,2,1,0:T(8,128)(2,1)}), bf16[8,2,256,128]{3,2,1,0:T(8,128)(2,1)S(1)}, u32[]{:S(2)}, u32[]{:S(2)}) async-start(bf16[8,2,256,128]{3,2,1,0:T(8,128)(2,1)} %get-tuple-element.31), calls=%async_computation.2 | async-start | bytes 2097152 | tf_op jit(solution)/shard_map/all_to_all | solution.py:308
  116.2 0.7 slice.150
  116.9 1.6 %collective-permute-start.3 = (f32[1,128]{1,0:T(1,128)S(1)}, f32[1,128]{1,0:T(1,128)S(1)}, u32[]{:S(2)}, u32[]{:S(2)}) collective-permute-start(f32[1,128]{1,0:T(1,128)S(1)} %slice.150), channel_id=1, source_target_pairs={{0,1},{1,0},{2,3},{3,2},{4,5},{5,4},{6,7},{7,6},{8,9},{9,8},{10,11... | collective-permute-start | bytes 1544 | tf_op jit(solution)/shard_map/ppermute | solution.py:238
  118.5 2.6 %collective-permute-start.4 = (f32[1,128]{1,0:T(1,128)S(1)}, f32[1,128]{1,0:T(1,128)S(1)}, u32[]{:S(2)}, u32[]{:S(2)}) collective-permute-start(f32[1,128]{1,0:T(1,128)S(1)} %slice.150), channel_id=1, source_target_pairs={{0,2},{1,3},{2,0},{3,1},{4,6},{5,7},{6,4},{7,5},{8,10},{9,11},{10,... | collective-permute-start | bytes 1544 | tf_op jit(solution)/shard_map/ppermute | solution.py:238
  121.1 0.2 collective-permute-start.5
  121.5 0.9 copy-done.3
  122.6 1.1 maximum_bitcast_fusion.1
  123.7 2.7 %collective-permute-done.5 = f32[1,128]{1,0:T(1,128)S(1)} collective-permute-done((f32[1,128]{1,0:T(1,128)S(1)}, f32[1,128]{1,0:T(1,128)S(1)}, u32[]{:S(2)}, u32[]{:S(2)}) %collective-permute-start.5) | collective-permute-done | bytes 544 | tf_op jit(solution)/shard_map/ppermute | solution.py:238
  126.4 0.7 add_add_fusion.1
  127.2 2.9 %collective-permute-start.11 = (f32[1,128]{1,0:T(1,128)S(1)}, f32[1,128]{1,0:T(1,128)S(1)}, u32[]{:S(2)}, u32[]{:S(2)}) collective-permute-start(f32[1,128]{1,0:T(1,128)S(1)} %add_add_fusion.1), channel_id=1, source_target_pairs={{0,24},{4,28},{8,16},{12,20},{16,8},{20,12},{24,0},{28,4},{1,25},{... | collective-permute-start | bytes 1544 | tf_op jit(solution)/shard_map/ppermute | solution.py:238
  130.0 1.5 collective-permute-start.12
  131.5 1.5 collective-permute-start.7
  132.9 3.6 %all-to-all-start.3 = ((bf16[8,2,256,128]{3,2,1,0:T(8,128)(2,1)}), bf16[8,2,256,128]{3,2,1,0:T(8,128)(2,1)S(1)}, u32[]{:S(2)}, u32[]{:S(2)}) async-start(bf16[8,2,256,128]{3,2,1,0:T(8,128)(2,1)} %get-tuple-element.33), calls=%async_computation.3 | async-start | bytes 2097152 | tf_op jit(solution)/shard_map/all_to_all | solution.py:308
  136.5 1.7 %collective-permute-start.8 = (f32[1,128]{1,0:T(1,128)S(1)}, f32[1,128]{1,0:T(1,128)S(1)}, u32[]{:S(2)}, u32[]{:S(2)}) collective-permute-start(f32[1,128]{1,0:T(1,128)S(1)} %add_add_fusion.1), channel_id=1, source_target_pairs={{0,12},{4,8},{8,4},{12,0},{16,28},{20,24},{24,20},{28,16},{1,13},{... | collective-permute-start | bytes 1544 | tf_op jit(solution)/shard_map/ppermute | solution.py:238
  138.2 1.5 collective-permute-start.9
  139.7 1.1 maximum_bitcast_fusion
  140.8 9.6 %collective-permute-done.8 = f32[1,128]{1,0:T(1,128)S(1)} collective-permute-done((f32[1,128]{1,0:T(1,128)S(1)}, f32[1,128]{1,0:T(1,128)S(1)}, u32[]{:S(2)}, u32[]{:S(2)}) %collective-permute-start.8) | collective-permute-done | bytes 544 | tf_op jit(solution)/shard_map/ppermute | solution.py:238
  150.4 0.5 multiply_bitcast_fusion
  151.0 0.1 fusion.4
  151.1 0.8 all-to-all-done.3
  152.0 0.7 maximum_bitcast_fusion.3
  152.7 0.7 maximum_bitcast_fusion.2
  (45 shorter events, 0.8 us)
Async XLA Ops:
  33.6 5.3 %copy-start.4 = (bf16[1,256,2048]{2,1,0:T(8,128)(2,1)S(1)}, bf16[1,256,2048]{2,1,0:T(8,128)(2,1)}, u32[]{:S(2)}) copy-start(bf16[1,256,2048]{2,1,0:T(8,128)(2,1)} %param.6) | copy-start | bytes 3145732
  33.7 5.3 %copy-start.5 = (bf16[1,256,2048]{2,1,0:T(8,128)(2,1)S(1)}, bf16[1,256,2048]{2,1,0:T(8,128)(2,1)}, u32[]{:S(2)}) copy-start(bf16[1,256,2048]{2,1,0:T(8,128)(2,1)} %param.10) | copy-start | bytes 3145732
  33.7 39.1 %all-to-all-start = ((bf16[8,2,256,128]{3,2,1,0:T(8,128)(2,1)}), bf16[8,2,256,128]{3,2,1,0:T(8,128)(2,1)S(1)}, u32[]{:S(2)}, u32[]{:S(2)}) async-start(bf16[8,2,256,128]{3,2,1,0:T(8,128)(2,1)} %spread_keys_values.2), calls=%async_computation | async-start | bytes 2097152 | tf_op jit(solution)/shard_map/all_to_all | solution.py:290
  39.2 38.2 %collective-permute-start = (bf16[2,256,1024]{2,1,0:T(8,128)(2,1)S(1)}, bf16[2,256,1024]{2,1,0:T(8,128)(2,1)}, u32[]{:S(2)}, u32[]{:S(2)}) collective-permute-start(bf16[2,256,1024]{2,1,0:T(8,128)(2,1)S(1)} %pad_maximum_fusion), channel_id=1, source_target_pairs={{0,4},{4,0},{8,12},{12,8},{16,20},{20,16},{24,28},{28,24},{1,5},{5... | collective-permute-start | bytes 3145736 | tf_op jit(solution)/shard_map/ppermute | solution.py:296
  72.8 3.9 %copy-start.10 = (s32[4,16,13]{1,0,2:T(4,128)S(1)}, s32[4,16,13]{1,0,2:T(4,128)}, u32[]{:S(2)}) copy-start(s32[4,16,13]{1,0,2:T(4,128)} %param.11) | copy-start | bytes 9988
  72.8 4.6 %copy-start = (bf16[8,2,256,128]{3,2,1,0:T(8,128)(2,1)}, bf16[8,2,256,128]{3,2,1,0:T(8,128)(2,1)S(1)}, u32[]{:S(2)}) copy-start(bf16[8,2,256,128]{3,2,1,0:T(8,128)(2,1)S(1)} %all-to-all-done.refs_7_) | copy-start | bytes 3145732
  72.8 21.0 %all-to-all-start.1 = ((bf16[8,2,256,128]{3,2,1,0:T(8,128)(2,1)}), bf16[8,2,256,128]{3,2,1,0:T(8,128)(2,1)S(1)}, u32[]{:S(2)}, u32[]{:S(2)}) async-start(bf16[8,2,256,128]{3,2,1,0:T(8,128)(2,1)} %spread_keys_values.3), calls=%async_computation.1 | async-start | bytes 2097152 | tf_op jit(solution)/shard_map/all_to_all | solution.py:290
  93.8 1.0 copy-start.1
  94.8 17.1 %copy-start.11 = (bf16[2,256,512]{2,1,0:T(8,128)(2,1)S(1)}, bf16[2,256,512]{2,1,0:T(8,128)(2,1)}, u32[]{:S(2)}) copy-start(bf16[2,256,512]{2,1,0:T(8,128)(2,1)} %get-tuple-element.23) | copy-start | bytes 1572868
  111.3 4.9 %collective-permute-start.2 = (bf16[2,256,512]{2,1,0:T(8,128)(2,1)}, bf16[2,256,512]{2,1,0:T(8,128)(2,1)S(1)}, u32[]{:S(2)}, u32[]{:S(2)}) collective-permute-start(bf16[2,256,512]{2,1,0:T(8,128)(2,1)} %get-tuple-element.24), channel_id=1, source_target_pairs={{0,4},{4,0},{8,12},{12,8},{16,20},{20,16},{24,28},{28,24},{1,5},{5... | collective-permute-start | bytes 1572872 | tf_op jit(solution)/shard_map/ppermute | solution.py:307
  111.9 4.4 %collective-permute-start.1 = (bf16[2,256,512]{2,1,0:T(8,128)(2,1)S(1)}, bf16[2,256,512]{2,1,0:T(8,128)(2,1)S(1)}, u32[]{:S(2)}, u32[]{:S(2)}) collective-permute-start(bf16[2,256,512]{2,1,0:T(8,128)(2,1)S(1)} %copy-done.11), channel_id=1, source_target_pairs={{0,4},{4,0},{8,12},{12,8},{16,20},{20,16},{24,28},{28,24},{1,5},{5... | collective-permute-start | bytes 1572872 | tf_op jit(solution)/shard_map/ppermute | solution.py:307
  112.0 9.4 %copy-start.6 = (bf16[256,512]{1,0:T(8,128)(2,1)S(1)}, bf16[256,512]{1,0:T(8,128)(2,1)}, u32[]{:S(2)}) copy-start(bf16[256,512]{1,0:T(8,128)(2,1)} %get-tuple-element.20) | copy-start | bytes 786436
  112.0 9.4 %copy-start.7 = (bf16[256,512]{1,0:T(8,128)(2,1)S(1)}, bf16[256,512]{1,0:T(8,128)(2,1)}, u32[]{:S(2)}) copy-start(bf16[256,512]{1,0:T(8,128)(2,1)} %get-tuple-element.28) | copy-start | bytes 786436
  112.0 21.0 %all-to-all-start.2 = ((bf16[8,2,256,128]{3,2,1,0:T(8,128)(2,1)}), bf16[8,2,256,128]{3,2,1,0:T(8,128)(2,1)S(1)}, u32[]{:S(2)}, u32[]{:S(2)}) async-start(bf16[8,2,256,128]{3,2,1,0:T(8,128)(2,1)} %get-tuple-element.31), calls=%async_computation.2 | async-start | bytes 2097152 | tf_op jit(solution)/shard_map/all_to_all | solution.py:308
  116.2 5.1 %copy-start.2 = (bf16[2,256,512]{2,1,0:T(8,128)(2,1)}, bf16[2,256,512]{2,1,0:T(8,128)(2,1)S(1)}, u32[]{:S(2)}) copy-start(bf16[2,256,512]{2,1,0:T(8,128)(2,1)S(1)} %collective-permute-done.2) | copy-start | bytes 1572868
  116.9 6.8 %collective-permute-start.3 = (f32[1,128]{1,0:T(1,128)S(1)}, f32[1,128]{1,0:T(1,128)S(1)}, u32[]{:S(2)}, u32[]{:S(2)}) collective-permute-start(f32[1,128]{1,0:T(1,128)S(1)} %slice.150), channel_id=1, source_target_pairs={{0,1},{1,0},{2,3},{3,2},{4,5},{5,4},{6,7},{7,6},{8,9},{9,8},{10,11... | collective-permute-start | bytes 1544 | tf_op jit(solution)/shard_map/ppermute | solution.py:238
  118.5 5.2 %collective-permute-start.4 = (f32[1,128]{1,0:T(1,128)S(1)}, f32[1,128]{1,0:T(1,128)S(1)}, u32[]{:S(2)}, u32[]{:S(2)}) collective-permute-start(f32[1,128]{1,0:T(1,128)S(1)} %slice.150), channel_id=1, source_target_pairs={{0,2},{1,3},{2,0},{3,1},{4,6},{5,7},{6,4},{7,5},{8,10},{9,11},{10,... | collective-permute-start | bytes 1544 | tf_op jit(solution)/shard_map/ppermute | solution.py:238
  121.1 5.3 %collective-permute-start.5 = (f32[1,128]{1,0:T(1,128)S(1)}, f32[1,128]{1,0:T(1,128)S(1)}, u32[]{:S(2)}, u32[]{:S(2)}) collective-permute-start(f32[1,128]{1,0:T(1,128)S(1)} %slice.150), channel_id=1, source_target_pairs={{0,3},{1,2},{2,1},{3,0},{4,7},{5,6},{6,5},{7,4},{8,11},{9,10},{10,... | collective-permute-start | bytes 1544 | tf_op jit(solution)/shard_map/ppermute | solution.py:238
  121.3 1.0 copy-start.3
  121.3 1.1 copy-start.8
  121.4 1.2 copy-start.9
  127.1 9.4 %collective-permute-start.10 = (f32[1,128]{1,0:T(1,128)S(1)}, f32[1,128]{1,0:T(1,128)S(1)}, u32[]{:S(2)}, u32[]{:S(2)}) collective-permute-start(f32[1,128]{1,0:T(1,128)S(1)} %add_add_fusion.1), channel_id=1, source_target_pairs={{0,20},{4,16},{8,28},{12,24},{16,4},{20,0},{24,12},{28,8},{1,21},{... | collective-permute-start | bytes 1544 | tf_op jit(solution)/shard_map/ppermute | solution.py:238
  127.2 11.0 %collective-permute-start.11 = (f32[1,128]{1,0:T(1,128)S(1)}, f32[1,128]{1,0:T(1,128)S(1)}, u32[]{:S(2)}, u32[]{:S(2)}) collective-permute-start(f32[1,128]{1,0:T(1,128)S(1)} %add_add_fusion.1), channel_id=1, source_target_pairs={{0,24},{4,28},{8,16},{12,20},{16,8},{20,12},{24,0},{28,4},{1,25},{... | collective-permute-start | bytes 1544 | tf_op jit(solution)/shard_map/ppermute | solution.py:238
  130.0 10.8 %collective-permute-start.12 = (f32[1,128]{1,0:T(1,128)S(1)}, f32[1,128]{1,0:T(1,128)S(1)}, u32[]{:S(2)}, u32[]{:S(2)}) collective-permute-start(f32[1,128]{1,0:T(1,128)S(1)} %add_add_fusion.1), channel_id=1, source_target_pairs={{0,28},{4,24},{8,20},{12,16},{16,12},{20,8},{24,4},{28,0},{1,29},{... | collective-permute-start | bytes 1544 | tf_op jit(solution)/shard_map/ppermute | solution.py:238
  131.5 9.3 %collective-permute-start.6 = (f32[1,128]{1,0:T(1,128)S(1)}, f32[1,128]{1,0:T(1,128)S(1)}, u32[]{:S(2)}, u32[]{:S(2)}) collective-permute-start(f32[1,128]{1,0:T(1,128)S(1)} %add_add_fusion.1), channel_id=1, source_target_pairs={{0,4},{4,0},{8,12},{12,8},{16,20},{20,16},{24,28},{28,24},{1,5},{5... | collective-permute-start | bytes 1544 | tf_op jit(solution)/shard_map/ppermute | solution.py:238
  131.5 9.3 %collective-permute-start.7 = (f32[1,128]{1,0:T(1,128)S(1)}, f32[1,128]{1,0:T(1,128)S(1)}, u32[]{:S(2)}, u32[]{:S(2)}) collective-permute-start(f32[1,128]{1,0:T(1,128)S(1)} %add_add_fusion.1), channel_id=1, source_target_pairs={{0,8},{4,12},{8,0},{12,4},{16,24},{20,28},{24,16},{28,20},{1,9},{5... | collective-permute-start | bytes 1544 | tf_op jit(solution)/shard_map/ppermute | solution.py:238
  132.9 18.9 %all-to-all-start.3 = ((bf16[8,2,256,128]{3,2,1,0:T(8,128)(2,1)}), bf16[8,2,256,128]{3,2,1,0:T(8,128)(2,1)S(1)}, u32[]{:S(2)}, u32[]{:S(2)}) async-start(bf16[8,2,256,128]{3,2,1,0:T(8,128)(2,1)} %get-tuple-element.33), calls=%async_computation.3 | async-start | bytes 2097152 | tf_op jit(solution)/shard_map/all_to_all | solution.py:308
  136.5 13.9 %collective-permute-start.8 = (f32[1,128]{1,0:T(1,128)S(1)}, f32[1,128]{1,0:T(1,128)S(1)}, u32[]{:S(2)}, u32[]{:S(2)}) collective-permute-start(f32[1,128]{1,0:T(1,128)S(1)} %add_add_fusion.1), channel_id=1, source_target_pairs={{0,12},{4,8},{8,4},{12,0},{16,28},{20,24},{24,20},{28,16},{1,13},{... | collective-permute-start | bytes 1544 | tf_op jit(solution)/shard_map/ppermute | solution.py:238
  138.2 12.2 %collective-permute-start.9 = (f32[1,128]{1,0:T(1,128)S(1)}, f32[1,128]{1,0:T(1,128)S(1)}, u32[]{:S(2)}, u32[]{:S(2)}) collective-permute-start(f32[1,128]{1,0:T(1,128)S(1)} %add_add_fusion.1), channel_id=1, source_target_pairs={{0,16},{4,20},{8,24},{12,28},{16,0},{20,4},{24,8},{28,12},{1,17},{... | collective-permute-start | bytes 1544 | tf_op jit(solution)/shard_map/ppermute | solution.py:238

commit v6 on v5

v6 whole, which is shorter than its diff:
```python
import functools
import math

import jax
import jax.numpy as jnp
from jax import lax
from jax.experimental import pallas as pl
from jax.experimental.pallas import tpu as pltpu
from jax.sharding import PartitionSpec as P

HEADS = 16
KV_HEADS = 4
HD = 128
BLOCK = 128
QPG = HEADS // KV_HEADS
CHUNK = 4
ROWS = QPG * BLOCK
TAIL = 16
STRIDES = (2, 3)
LOG2E = math.log2(math.e)
NEVER = -1e30


def distinct_offsets(block_count, listed_count):
    tables = []
    for stride in STRIDES:
        steps = range(1, (listed_count - 3) // 2 + 1)
        listed = [-1, 0, 1] + [stride * m for m in steps] + [-stride * m for m in steps]
        times = {}
        for o in listed:
            times[o % block_count] = times.get(o % block_count, 0) + 1
        tables.append(sorted(times.items()))
    most = max(len(t) for t in tables)
    return [t + [(0, 0)] * (most - len(t)) for t in tables]


def nt(a, b):
    return jnp.dot(a, b, preferred_element_type=jnp.float32)


def group_kernel(gi, devices, local_blocks, listed, offsets, *refs):
    place, key_blocks, taus = refs[:3]
    inputs, rest = refs[3 : 8 + gi], refs[8 + gi :]
    q_own, q_sib, g_own, g_sib, kv_in = inputs[:5]
    att_own, dq_own, sib_out, tau_out, kv_out = rest[:5]
    kt_s, vt_s, dk_s, dv_s, s_s, e_s = rest[5:]
    blocks = devices * local_blocks
    me = place[0]
    group = 2 * (me % 2) + gi
    units = 2 * local_blocks

    chunks = [range(c, min(c + CHUNK, listed)) for c in range(0, listed, CHUNK)]
    scale = jnp.concatenate(
        [jnp.full((1, BLOCK), taus[group * QPG + h], jnp.float32) for h in range(QPG)], axis=1
    ) / math.sqrt(HD)
    factor = scale * LOG2E

    def rows_of(c):
        return slice(c[0] * BLOCK, (c[-1] + 1) * BLOCK)

    def per_head(x):
        return [x[:, h * HD : (h + 1) * HD] for h in range(QPG)]

    def in_rows(x):
        return x.reshape(-1, 8, ROWS)

    tau_totals = []

    def part(n):
        s_n, e_n = s_s.at[n], e_s.at[n]
        side, at = n // local_blocks, n % local_blocks
        here = slice(at * BLOCK, (at + 1) * BLOCK)
        query_block = (me ^ side) * local_blocks + at
        wide = (key_blocks[group, query_block, 3] - query_block) % blocks == STRIDES[1]
        ids, bias = [], []
        for (narrow_off, narrow_times), (wide_off, wide_times) in zip(*offsets):
            ids.append((query_block + jnp.where(wide, wide_off, narrow_off)) % blocks)
            bias.append(
                times_bias(narrow_times)
                if narrow_times == wide_times
                else jnp.where(wide, times_bias(wide_times), times_bias(narrow_times))
            )

        def taken(which, c):
            return jnp.concatenate([kv_in[ids[j], which] for j in c], axis=0)

        def picked(ref, c, axis):
            return jnp.concatenate([ref[ids[j]] for j in c], axis=axis)

        def add_blocks(ref, c, x):
            for n, j in enumerate(c):
                ref[ids[j]] += x[n * BLOCK : (n + 1) * BLOCK, :]

        q_here = q_sib[0, here, :] if side else q_own[here, :]
        g_here = g_sib[0, here, :] if side else g_own[here, :]
        q_rows = jnp.concatenate(per_head(q_here), axis=0)
        g_rows = jnp.concatenate(per_head(g_here), axis=0)
        q_t = jnp.concatenate([x.T for x in per_head(q_here)], axis=1)
        g_t = jnp.concatenate([x.T for x in per_head(g_here)], axis=1)
        most = None
        for c in chunks:
            raw = nt(taken(0, c), q_t)
            s_n[rows_of(c), :] = raw
            top = jnp.max(in_rows(raw), axis=0)
            most = top if most is None else jnp.maximum(most, top)
            yield
        top_row = jnp.max(most, axis=0, keepdims=True) * factor
        total = jnp.zeros((8, ROWS), jnp.float32)
        for c in chunks:
            for j in c:
                rows = slice(j * BLOCK, (j + 1) * BLOCK)
                e = jnp.exp2(s_n[rows, :] * factor - (top_row - bias[j]))
                e_n[rows, :] = e
                total = total + jnp.sum(in_rows(e), axis=0)
            yield
        inverse = 1.0 / jnp.sum(total, axis=0, keepdims=True)
        o_t = jnp.zeros((HD, ROWS), jnp.float32)
        for c in chunks:
            probs = (e_n[rows_of(c), :] * inverse).astype(jnp.bfloat16)
            o_t = o_t + nt(picked(vt_s, c, 1), probs)
            add_blocks(dv_s, c, nt(probs, g_rows))
            yield
        row_dot = jnp.sum(g_t.astype(jnp.float32) * o_t, axis=0, keepdims=True)
        write(side, here, 0, o_t)
        weight_scale = inverse * scale
        tau_rows = jnp.zeros((8, ROWS), jnp.float32)
        dq_t = jnp.zeros((HD, ROWS), jnp.float32)
        for c in chunks:
            dweights = nt(taken(1, c), g_t)
            scaled = e_n[rows_of(c), :] * weight_scale * (dweights - row_dot)
            tau_rows = tau_rows + jnp.sum(in_rows(scaled * s_n[rows_of(c), :]), axis=0)
            low = scaled.astype(jnp.bfloat16)
            dq_t = dq_t + nt(picked(kt_s, c, 1), low)
            add_blocks(dk_s, c, nt(low, q_rows))
            yield
        tau_totals.append(tau_rows)
        write(side, here, 1, dq_t)

    def write(side, here, which, x_t):
        low = x_t.astype(jnp.bfloat16)
        out = jnp.concatenate([x.T for x in per_head(low)], axis=1)
        if side:
            sib_out[which, here, :] = out
        else:
            (att_own, dq_own)[which][here, :] = out

    def turned(which, ref, wait):
        turns = 2 * len(chunks)
        for turn in range(wait):
            yield
        for turn in range(turns):
            for b in range(blocks * turn // turns, blocks * (turn + 1) // turns):
                ref[b] = kv_in[b, which].T
            yield

    dk_s[...] = jnp.zeros_like(dk_s)
    dv_s[...] = jnp.zeros_like(dv_s)
    shares = [(0, turned(1, vt_s, 0)), (0, turned(0, kt_s, len(chunks)))]
    shares += [(n * len(chunks), part(n)) for n in range(units)]
    for turn in range((4 + units) * len(chunks)):
        for begin, share in shares:
            if turn >= begin:
                next(share, None)

    lane = lax.broadcasted_iota(jnp.int32, (TAIL, HD), 1)
    row = lax.broadcasted_iota(jnp.int32, (TAIL, HD), 0)
    sums = inputs[5][...] if gi else jnp.zeros((TAIL, HD), jnp.float32)
    tau_rows = functools.reduce(jnp.add, tau_totals)
    for h in range(QPG):
        head = group * QPG + h
        total = jnp.sum(tau_rows[:, h * BLOCK : (h + 1) * BLOCK])
        sums = sums + jnp.where(lane == head, total / taus[head], 0.0)
    tau_out[...] = sums
    high = sums.astype(jnp.bfloat16).astype(jnp.float32)
    mid = (sums - high).astype(jnp.bfloat16).astype(jnp.float32)
    low = sums - high - mid
    tail = jnp.where(row == 0, high, jnp.where(row == 1, mid, jnp.where(row == 2, low, 0.0)))

    def drain(d, carry):
        for half in range(local_blocks):
            for which, ref in enumerate((dk_s, dv_s)):
                at = (2 * half + which) * BLOCK
                kv_out[d, at : at + BLOCK, :] = ref[d * local_blocks + half].astype(jnp.bfloat16)
        kv_out[d, 2 * local_blocks * BLOCK :, :] = tail.astype(jnp.bfloat16)
        return carry

    lax.fori_loop(0, devices, drain, 0, unroll=2)


def times_bias(times):
    return math.log2(times) if times else NEVER


def run_group(gi, devices, place, key_blocks, tau, queries, out_grad, qg_sib, kv_in, tau_in, offsets):
    listed = len(offsets[0])
    tokens = queries.shape[0]
    local_blocks = tokens // BLOCK
    blocks = devices * local_blocks
    width = QPG * HD
    block_own = pl.BlockSpec((tokens, width), lambda u, p, s, t: (0, 2 * (p[0] % 2) + gi))
    qs = pl.BlockSpec((1, tokens, width), lambda u, p, s, t: (0, 0, gi))
    gs = pl.BlockSpec((1, tokens, width), lambda u, p, s, t: (1, 0, gi))
    out_own = pl.BlockSpec((tokens, width), lambda u, p, s, t: (0, 0))
    out_sib = pl.BlockSpec((2, tokens, width), lambda u, p, s, t: (0, 0, 0))
    kv_all = pl.BlockSpec((blocks, 2, BLOCK, HD), lambda u, p, s, t: (0, 0, 0, 0))
    kv_back = pl.BlockSpec((devices, 2 * tokens + TAIL, HD), lambda u, p, s, t: (0, 0, 0))
    small = pl.BlockSpec((TAIL, HD), lambda u, p, s, t: (0, 0))
    bf = lambda *shape: jax.ShapeDtypeStruct(shape, jnp.bfloat16)
    keys_wide = listed * BLOCK
    cells = 2 * local_blocks * ROWS * keys_wide
    return pl.pallas_call(
        functools.partial(group_kernel, gi, devices, local_blocks, listed, offsets),
        grid_spec=pltpu.PrefetchScalarGridSpec(
            num_scalar_prefetch=3,
            grid=(1,),
            in_specs=[block_own, qs, block_own, gs, kv_all] + [small] * gi,
            out_specs=[out_own, out_own, out_sib, small, kv_back],
            scratch_shapes=[pltpu.VMEM((blocks, HD, BLOCK), jnp.bfloat16)] * 2
            + [pltpu.VMEM((blocks, BLOCK, HD), jnp.float32)] * 2
            + [pltpu.VMEM((2 * local_blocks, keys_wide, ROWS), jnp.float32)] * 2,
        ),
        out_shape=[bf(tokens, width), bf(tokens, width), bf(2, tokens, width)]
        + [jax.ShapeDtypeStruct((TAIL, HD), jnp.float32), bf(devices, 2 * tokens + TAIL, HD)],
        compiler_params=pltpu.CompilerParams(
            dimension_semantics=("arbitrary",), vmem_limit_bytes=60 * 2**20
        ),
        cost_estimate=pl.CostEstimate(
            flops=12 * HD * cells, bytes_accessed=6 * 2**20, transcendentals=cells
        ),
        name="group_attention",
    )(place, key_blocks, tau, queries, qg_sib, out_grad, qg_sib, kv_in, *tau_in[:gi])


def spread(gi, devices, keys, values):
    tokens, width = keys.shape
    local_blocks = tokens // BLOCK

    def kernel(k_ref, v_ref, out):
        for parity in range(2):
            cols = slice((2 * parity + gi) * HD, (2 * parity + gi + 1) * HD)
            for half in range(local_blocks):
                rows = slice(half * BLOCK, (half + 1) * BLOCK)
                out[parity, half, 0] = k_ref[rows, cols]
                out[parity, half, 1] = v_ref[rows, cols]

    taken = pl.BlockSpec((tokens, width), lambda d: (0, 0))
    block = (2, local_blocks, 2, BLOCK, HD)
    return pl.pallas_call(
        kernel,
        grid=(devices // 2,),
        in_specs=[taken, taken],
        out_specs=pl.BlockSpec(block, lambda d: (d, 0, 0, 0, 0)),
        out_shape=jax.ShapeDtypeStruct((devices, *block[1:]), jnp.bfloat16),
        compiler_params=pltpu.CompilerParams(vmem_limit_bytes=60 * 2**20),
        name="spread_keys_values",
    )(keys, values)


def body(queries, keys, values, tau, out_grad, key_blocks):
    ctx = lax.axis_size("ctx")
    me = lax.axis_index("ctx").astype(jnp.int32)
    core = me % 2
    tokens = queries.shape[1]
    local_blocks = tokens // BLOCK
    block_count = ctx * local_blocks
    listed_count = key_blocks.shape[2]
    offsets = distinct_offsets(block_count, listed_count)
    swap = [(d, d ^ 1) for d in range(ctx)]
    wide = 2 * QPG * HD

    q0, k0, v0, g0 = queries[0], keys[0], values[0], out_grad[0]
    place = me[None]

    def kv_for(gi):
        arrived = lax.all_to_all(spread(gi, ctx, k0, v0), "ctx", 0, 0)
        return arrived.reshape(block_count, 2, BLOCK, HD)

    def theirs(x):
        return lax.dynamic_slice_in_dim(x, (1 - core) * wide, wide, 1)

    kv_in = [kv_for(gi) for gi in range(2)]
    qg_sib = lax.ppermute(jnp.stack([theirs(q0), theirs(g0)]), "ctx", swap)

    sibs, owns, grads, tau_rows = [], [], [], []
    for gi in range(2):
        att_own, dq_own, sib, tau_here, kv_grads = run_group(
            gi, ctx, place, key_blocks, tau, q0, g0, qg_sib, kv_in[gi], tau_rows, offsets
        )
        tau_rows.append(tau_here)
        if gi:
            kv_grads, grads[0] = lax.optimization_barrier((kv_grads, grads[0]))
        owns.append((att_own, dq_own))
        sibs.append(lax.ppermute(sib, "ctx", swap))
        grads.append(lax.all_to_all(kv_grads, "ctx", 0, 0))
    sibs = lax.optimization_barrier(sibs)
    att_parts, dq_parts = (
        [(own[which], sib[which]) for own, sib in zip(owns, sibs)] for which in range(2)
    )

    def by_group(parts):
        return jnp.concatenate(
            [jnp.where(core == c // 2, parts[c % 2][0], parts[c % 2][1]) for c in range(4)], axis=1
        )

    attended = by_group(att_parts)[None]
    query_grad = by_group(dq_parts)[None]

    def summed(which):
        cols = []
        for c in range(4):
            total = None
            for src in range(c // 2, ctx, 2):
                term = grads[c % 2][src, : 2 * tokens].reshape(local_blocks, 2, BLOCK, HD)[:, which]
                term = term.astype(jnp.float32)
                total = term if total is None else total + term
            cols.append(total.reshape(tokens, HD).astype(jnp.bfloat16))
        return jnp.concatenate(cols, axis=1)[None]

    key_grad, value_grad = summed(0), summed(1)
    tails = grads[1][:, 2 * tokens : 2 * tokens + 3].astype(jnp.float32)
    here = jnp.sum(tails, axis=(0, 1))
    batch = lax.axis_size("batch")
    over_batch = lax.all_to_all(jnp.broadcast_to(here, (batch, 1, HD)), "batch", 0, 0)
    scale_total = jnp.sum(over_batch, axis=(0, 1))[:HEADS]
    tau_grad = scale_total / math.sqrt(lax.axis_size("batch") * ctx * tokens)
    return (attended, query_grad, key_grad, value_grad, tau_grad)


def solution(mesh):
    rows = P("batch", "ctx", None)
    return jax.shard_map(
        body,
        mesh=mesh,
        in_specs=(rows, rows, rows, P(), rows, P()),
        out_specs=(rows, rows, rows, rows, P()),
        check_vma=False,
    )
```

time: 154 us -> 113 us (0.73)
  Pallas kernels: 98.9 us -> 36.9 us
  waiting for transfers between devices: 13.1 us -> 42.8 us
  starting transfers between devices: 31.6 us -> 22.6 us
    pallas_call x2, Pallas kernels: 66 us -> 5.25 us  [spread(): pl.pallas_call(kernel, grid=(devices // 2,), in_specs=[taken, taken], out...]
    all_to_all x2, waiting for transfers between devices: 0.75 us -> 27 us  [body(): grads.append(lax.all_to_all(kv_grads, 'ctx', 0, 0))]
    all_to_all x2 -> x3, waiting for transfers between devices: 0.01 us -> 15.8 us  [the longest x2 12 us: kv_for(): arrived = lax.all_to_all(spread(gi, ctx, k0, v0), 'ctx', 0, 0)]
    ppermute x10 -> x0, starting transfers between devices: 13.4 us -> none  [total_over(): lax.ppermute(x, axis, [(i, i ^ step * d) for i in range(size)])]
    ppermute x10 -> x0, waiting for transfers between devices: 12.3 us -> none  [total_over(): lax.ppermute(x, axis, [(i, i ^ step * d) for i in range(size)])]
    all_to_all x2 -> x3, starting transfers between devices: 9.18 us -> 13.7 us  [the longest x2 8.86 us: kv_for(): arrived = lax.all_to_all(spread(gi, ctx, k0, v0), 'ctx', 0, 0)]
  transfers between devices with their start and end apart: 17 -> 8, of which waited for: 3 -> 4; matrix products, arithmetic and copies ran while one was open for 3% -> 5% of each run, Pallas kernels for 32% -> 17%
where the time goes in v6:
time: 113 us; the launch traced here: 112 us
  waiting for transfers between devices  42.8 us (38%)
  Pallas kernels  36.9 us (33%)
  starting transfers between devices  22.6 us (20%)
  other arithmetic  5.75 us (5%)
  local copies, waits for them, and re-layouts  3.35 us (3%)
    pallas_call x2, Pallas kernels, run_group(): pl.pallas_call(functools.partial(group_kernel, gi, devices, local_blocks,...  31.6 us
    all_to_all x2, waiting for transfers between devices, body(): grads.append(lax.all_to_all(kv_grads, 'ctx', 0, 0))  27 us
    all_to_all x2, waiting for transfers between devices, kv_for(): arrived = lax.all_to_all(spread(gi, ctx, k0, v0), 'ctx', 0, 0)  12 us
    all_to_all x2, starting transfers between devices, kv_for(): arrived = lax.all_to_all(spread(gi, ctx, k0, v0), 'ctx', 0, 0)  8.86 us
    all_to_all x2, starting transfers between devices, body(): grads.append(lax.all_to_all(kv_grads, 'ctx', 0, 0))  7.82 us
    pallas_call x2, Pallas kernels, spread(): pl.pallas_call(kernel, grid=(devices // 2,), in_specs=[taken, taken], out...  5.25 us
    all_to_all x1, starting transfers between devices, body(): lax.all_to_all(jnp.broadcast_to(here, (batch, 1, HD)), 'batch', 0, 0)  4.87 us
    all_to_all x1, waiting for transfers between devices, body(): lax.all_to_all(jnp.broadcast_to(here, (batch, 1, HD)), 'batch', 0, 0)  3.82 us
  transfers between devices with their start and end apart: 8, of which 4 were waited for; matrix products, arithmetic and copies ran while one was open for 5% of the time, Pallas kernels for 17%

profile of v6, /device:TPU:0, one launch (start us, length us, event | category | flops | bytes accessed | tf_op | source)
XLA Modules:
  0.0 112.2 jit_solution(2584241847998036499)
XLA Ops:
  0.6 2.6 %spread_keys_values.2 = bf16[8,2,2,128,128]{4,3,2,1,0:T(8,128)(2,1)} custom-call(bf16[256,512]{1,0:T(8,128)(2,1)} %bitcast.54, bf16[256,512]{1,0:T(8,128)(2,1)} %bitcast.56), custom_call_target="tpu_custom_call" | custom-call | tf_op jit(solution)/shard_map/spread_keys_values/pallas_call | solution.py:248
  3.3 5.3 %all-to-all-start = ((bf16[8,2,2,128,128]{4,3,2,1,0:T(8,128)(2,1)}), bf16[8,2,2,128,128]{4,3,2,1,0:T(8,128)(2,1)S(1)}, u32[]{:S(2)}, u32[]{:S(2)}) async-start(bf16[8,2,2,128,128]{4,3,2,1,0:T(8,128)(2,1)} %spread_keys_values.2), calls=%async_computation | async-start | bytes 2097152 | tf_op jit(solution)/shard_map/all_to_all | solution.py:275
  8.6 0.1 constant_dynamic-slice_fusion
  8.7 0.1 pad_maximum_fusion
  8.8 0.6 collective-permute-start
  9.4 2.6 %spread_keys_values.3 = bf16[8,2,2,128,128]{4,3,2,1,0:T(8,128)(2,1)} custom-call(bf16[256,512]{1,0:T(8,128)(2,1)} %bitcast.55, bf16[256,512]{1,0:T(8,128)(2,1)} %bitcast.57), custom_call_target="tpu_custom_call" | custom-call | tf_op jit(solution)/shard_map/spread_keys_values/pallas_call | solution.py:248
  12.0 12.0 %all-to-all-done = bf16[8,2,2,128,128]{4,3,2,1,0:T(8,128)(2,1)S(1)} async-done(((bf16[8,2,2,128,128]{4,3,2,1,0:T(8,128)(2,1)}), bf16[8,2,2,128,128]{4,3,2,1,0:T(8,128)(2,1)S(1)}, u32[]{:S(2)}, u32[]{:S(2)}) %all-to-all-start) | async-done | bytes 1048608 | tf_op jit(solution)/shard_map/all_to_all | solution.py:275
  24.0 3.6 %all-to-all-start.1 = ((bf16[8,2,2,128,128]{4,3,2,1,0:T(8,128)(2,1)}), bf16[8,2,2,128,128]{4,3,2,1,0:T(8,128)(2,1)S(1)}, u32[]{:S(2)}, u32[]{:S(2)}) async-start(bf16[8,2,2,128,128]{4,3,2,1,0:T(8,128)(2,1)} %spread_keys_values.3), calls=%async_computation.1 | async-start | bytes 2097152 | tf_op jit(solution)/shard_map/all_to_all | solution.py:275
  27.6 0.7 copy.15.refs_1_
  28.3 15.9 %group_attention.2 = (bf16[256,512]{1,0:T(8,128)(2,1)}, bf16[256,512]{1,0:T(8,128)(2,1)}, bf16[2,256,512]{2,1,0:T(8,128)(2,1)}, f32[16,128]{1,0:T(8,128)}, bf16[8,528,128]{2,1,0:T(8,128)(2,1)}) custom-call(s32[1]{0:T(128)} %bitcast.refs_0_, s32[4,16,13]{2,1,0:T(8,128)} %copy.15.refs_1_, f32[16]{0:T(128)} %refs_2_.3, bf16[256,2048]{1,0:T(8,128)(2,1)} %bitcast.74, ...), custom_call_target="tpu_custom_call" | custom-call | flops 4429185024 | bytes 6291456 | tf_op jit(solution)/shard_map/group_attention/pallas_call | solution.py:211
  44.2 1.0 copy-done.1
  45.2 15.7 %group_attention.3 = (bf16[256,512]{1,0:T(8,128)(2,1)}, bf16[256,512]{1,0:T(8,128)(2,1)}, bf16[2,256,512]{2,1,0:T(8,128)(2,1)}, f32[16,128]{1,0:T(8,128)}, bf16[8,528,128]{2,1,0:T(8,128)(2,1)}) custom-call(s32[1]{0:T(128)} %bitcast.refs_0_, s32[4,16,13]{2,1,0:T(8,128)} %copy.15.refs_1_, f32[16]{0:T(128)} %refs_2_.3, bf16[256,2048]{1,0:T(8,128)(2,1)} %bitcast.75, ...), custom_call_target="tpu_custom_call" | custom-call | flops 4429185024 | bytes 6291456 | tf_op jit(solution)/shard_map/group_attention/pallas_call | solution.py:211
  60.9 0.4 collective-permute-start.2
  61.3 0.1 collective-permute-start.1
  61.4 4.3 %all-to-all-start.2 = ((bf16[8,528,128]{2,1,0:T(8,128)(2,1)}), bf16[8,528,128]{2,1,0:T(8,128)(2,1)S(1)}, u32[]{:S(2)}, u32[]{:S(2)}) async-start(bf16[8,528,128]{2,1,0:T(8,128)(2,1)} %get-tuple-element.28), calls=%async_computation.2 | async-start | bytes 2162688 | tf_op jit(solution)/shard_map/all_to_all | solution.py:294
  65.7 0.1 bitcast_select_fusion.3
  65.8 0.8 copy-done.6
  66.6 1.0 bitcast_select_fusion.1
  67.6 1.1 maximum_bitcast_fusion.1
  68.7 12.7 %all-to-all-done.2 = bf16[8,528,128]{2,1,0:T(8,128)(2,1)S(1)} async-done(((bf16[8,528,128]{2,1,0:T(8,128)(2,1)}), bf16[8,528,128]{2,1,0:T(8,128)(2,1)S(1)}, u32[]{:S(2)}, u32[]{:S(2)}) %all-to-all-start.2) | async-done | bytes 1081376 | tf_op jit(solution)/shard_map/all_to_all | solution.py:294
  81.4 3.6 %all-to-all-start.3 = ((bf16[8,528,128]{2,1,0:T(8,128)(2,1)}), bf16[8,528,128]{2,1,0:T(8,128)(2,1)S(1)}, u32[]{:S(2)}, u32[]{:S(2)}) async-start(bf16[8,528,128]{2,1,0:T(8,128)(2,1)} %get-tuple-element.30), calls=%async_computation.3 | async-start | bytes 2162688 | tf_op jit(solution)/shard_map/all_to_all | solution.py:294
  85.0 1.1 maximum_bitcast_fusion
  86.1 0.1 fusion
  86.2 0.1 add_convert_fusion.3
  86.3 14.3 %all-to-all-done.3 = bf16[8,528,128]{2,1,0:T(8,128)(2,1)S(1)} async-done(((bf16[8,528,128]{2,1,0:T(8,128)(2,1)}), bf16[8,528,128]{2,1,0:T(8,128)(2,1)S(1)}, u32[]{:S(2)}, u32[]{:S(2)}) %all-to-all-start.3) | async-done | bytes 1081376 | tf_op jit(solution)/shard_map/all_to_all | solution.py:294
  100.7 0.6 broadcast_in_dim.23
  101.3 4.9 %all-to-all-start.4 = ((f32[4,1,128]{2,1,0:T(1,128)}), f32[4,1,128]{2,1,0:T(1,128)S(1)}, u32[]{:S(2)}, u32[]{:S(2)}) async-start(f32[4,1,128]{2,1,0:T(1,128)} %broadcast_in_dim.23), calls=%async_computation.4 | async-start | bytes 4096 | tf_op jit(solution)/shard_map/all_to_all | solution.py:323
  106.2 0.1 fusion.1
  106.4 0.7 maximum_bitcast_fusion.3
  107.2 0.7 maximum_bitcast_fusion.2
  107.9 3.8 %all-to-all-done.4 = f32[4,1,128]{2,1,0:T(1,128)S(1)} async-done(((f32[4,1,128]{2,1,0:T(1,128)}), f32[4,1,128]{2,1,0:T(1,128)S(1)}, u32[]{:S(2)}, u32[]{:S(2)}) %all-to-all-start.4) | async-done | bytes 2080 | tf_op jit(solution)/shard_map/all_to_all | solution.py:323
  111.7 0.5 slice_multiply_fusion
  (23 shorter events, 0.3 us)
Async XLA Ops:
  3.3 5.3 %copy-start.2 = (bf16[1,256,2048]{2,1,0:T(8,128)(2,1)S(1)}, bf16[1,256,2048]{2,1,0:T(8,128)(2,1)}, u32[]{:S(2)}) copy-start(bf16[1,256,2048]{2,1,0:T(8,128)(2,1)} %param.6) | copy-start | bytes 3145732
  3.3 5.3 %copy-start.3 = (bf16[1,256,2048]{2,1,0:T(8,128)(2,1)S(1)}, bf16[1,256,2048]{2,1,0:T(8,128)(2,1)}, u32[]{:S(2)}) copy-start(bf16[1,256,2048]{2,1,0:T(8,128)(2,1)} %param.10) | copy-start | bytes 3145732
  3.3 20.7 %all-to-all-start = ((bf16[8,2,2,128,128]{4,3,2,1,0:T(8,128)(2,1)}), bf16[8,2,2,128,128]{4,3,2,1,0:T(8,128)(2,1)S(1)}, u32[]{:S(2)}, u32[]{:S(2)}) async-start(bf16[8,2,2,128,128]{4,3,2,1,0:T(8,128)(2,1)} %spread_keys_values.2), calls=%async_computation | async-start | bytes 2097152 | tf_op jit(solution)/shard_map/all_to_all | solution.py:275
  8.8 19.5 %collective-permute-start = (bf16[2,256,1024]{2,1,0:T(8,128)(2,1)S(1)}, bf16[2,256,1024]{2,1,0:T(8,128)(2,1)}, u32[]{:S(2)}, u32[]{:S(2)}) collective-permute-start(bf16[2,256,1024]{2,1,0:T(8,128)(2,1)S(1)} %pad_maximum_fusion), channel_id=1, source_target_pairs={{0,4},{4,0},{8,12},{12,8},{16,20},{20,16},{24,28},{28,24},{1,5},{5... | collective-permute-start | bytes 3145736 | tf_op jit(solution)/shard_map/ppermute | solution.py:282
  12.0 15.6 %copy-start.7 = (s32[4,16,13]{1,0,2:T(4,128)S(1)}, s32[4,16,13]{1,0,2:T(4,128)}, u32[]{:S(2)}) copy-start(s32[4,16,13]{1,0,2:T(4,128)} %param.11) | copy-start | bytes 9988
  24.0 4.3 %copy-start = (bf16[8,2,2,128,128]{4,3,2,1,0:T(8,128)(2,1)}, bf16[8,2,2,128,128]{4,3,2,1,0:T(8,128)(2,1)S(1)}, u32[]{:S(2)}) copy-start(bf16[8,2,2,128,128]{4,3,2,1,0:T(8,128)(2,1)S(1)} %all-to-all-done) | copy-start | bytes 3145732
  24.0 20.2 %all-to-all-start.1 = ((bf16[8,2,2,128,128]{4,3,2,1,0:T(8,128)(2,1)}), bf16[8,2,2,128,128]{4,3,2,1,0:T(8,128)(2,1)S(1)}, u32[]{:S(2)}, u32[]{:S(2)}) async-start(bf16[8,2,2,128,128]{4,3,2,1,0:T(8,128)(2,1)} %spread_keys_values.3), calls=%async_computation.1 | async-start | bytes 2097152 | tf_op jit(solution)/shard_map/all_to_all | solution.py:275
  44.2 1.0 copy-start.1
  60.9 4.8 %collective-permute-start.2 = (bf16[2,256,512]{2,1,0:T(8,128)(2,1)}, bf16[2,256,512]{2,1,0:T(8,128)(2,1)S(1)}, u32[]{:S(2)}, u32[]{:S(2)}) collective-permute-start(bf16[2,256,512]{2,1,0:T(8,128)(2,1)} %get-tuple-element.21), channel_id=1, source_target_pairs={{0,4},{4,0},{8,12},{12,8},{16,20},{20,16},{24,28},{28,24},{1,5},{5... | collective-permute-start | bytes 1572872 | tf_op jit(solution)/shard_map/ppermute | solution.py:293
  61.3 4.4 %collective-permute-start.1 = (bf16[2,256,512]{2,1,0:T(8,128)(2,1)}, bf16[2,256,512]{2,1,0:T(8,128)(2,1)S(1)}, u32[]{:S(2)}, u32[]{:S(2)}) collective-permute-start(bf16[2,256,512]{2,1,0:T(8,128)(2,1)} %get-tuple-element.19), channel_id=1, source_target_pairs={{0,4},{4,0},{8,12},{12,8},{16,20},{20,16},{24,28},{28,24},{1,5},{5... | collective-permute-start | bytes 1572872 | tf_op jit(solution)/shard_map/ppermute | solution.py:293
  61.4 4.3 %copy-start.4 = (bf16[256,512]{1,0:T(8,128)(2,1)S(1)}, bf16[256,512]{1,0:T(8,128)(2,1)}, u32[]{:S(2)}) copy-start(bf16[256,512]{1,0:T(8,128)(2,1)} %get-tuple-element.18) | copy-start | bytes 786436
  61.4 4.3 %copy-start.5 = (bf16[256,512]{1,0:T(8,128)(2,1)S(1)}, bf16[256,512]{1,0:T(8,128)(2,1)}, u32[]{:S(2)}) copy-start(bf16[256,512]{1,0:T(8,128)(2,1)} %get-tuple-element.25) | copy-start | bytes 786436
  61.4 20.0 %all-to-all-start.2 = ((bf16[8,528,128]{2,1,0:T(8,128)(2,1)}), bf16[8,528,128]{2,1,0:T(8,128)(2,1)S(1)}, u32[]{:S(2)}, u32[]{:S(2)}) async-start(bf16[8,528,128]{2,1,0:T(8,128)(2,1)} %get-tuple-element.28), calls=%async_computation.2 | async-start | bytes 2162688 | tf_op jit(solution)/shard_map/all_to_all | solution.py:294
  65.7 0.9 copy-start.6
  81.4 19.3 %all-to-all-start.3 = ((bf16[8,528,128]{2,1,0:T(8,128)(2,1)}), bf16[8,528,128]{2,1,0:T(8,128)(2,1)S(1)}, u32[]{:S(2)}, u32[]{:S(2)}) async-start(bf16[8,528,128]{2,1,0:T(8,128)(2,1)} %get-tuple-element.30), calls=%async_computation.3 | async-start | bytes 2162688 | tf_op jit(solution)/shard_map/all_to_all | solution.py:294
  101.3 10.4 %all-to-all-start.4 = ((f32[4,1,128]{2,1,0:T(1,128)}), f32[4,1,128]{2,1,0:T(1,128)S(1)}, u32[]{:S(2)}, u32[]{:S(2)}) async-start(f32[4,1,128]{2,1,0:T(1,128)} %broadcast_in_dim.23), calls=%async_computation.4 | async-start | bytes 4096 | tf_op jit(solution)/shard_map/all_to_all | solution.py:323

commit v7 on v6

--- a/solution.py
+++ b/solution.py
@@ -15,7 +15,8 @@
 QPG = HEADS // KV_HEADS
 CHUNK = 4
 ROWS = QPG * BLOCK
-TAIL = 16
+TAIL = 8
+VMEM_BYTES = 63 * 2**20
 STRIDES = (2, 3)
 LOG2E = math.log2(math.e)
 NEVER = -1e30
@@ -39,7 +40,7 @@
 
 
 def group_kernel(gi, devices, local_blocks, listed, offsets, *refs):
-    place, key_blocks, taus = refs[:3]
+    place, strides, taus = refs[:3]
     inputs, rest = refs[3 : 8 + gi], refs[8 + gi :]
     q_own, q_sib, g_own, g_sib, kv_in = inputs[:5]
     att_own, dq_own, sib_out, tau_out, kv_out = rest[:5]
@@ -71,7 +72,7 @@
         side, at = n // local_blocks, n % local_blocks
         here = slice(at * BLOCK, (at + 1) * BLOCK)
         query_block = (me ^ side) * local_blocks + at
-        wide = (key_blocks[group, query_block, 3] - query_block) % blocks == STRIDES[1]
+        wide = strides[group * blocks + query_block] == STRIDES[1]
         ids, bias = [], []
         for (narrow_off, narrow_times), (wide_off, wide_times) in zip(*offsets):
             ids.append((query_block + jnp.where(wide, wide_off, narrow_off)) % blocks)
@@ -163,7 +164,6 @@
                 next(share, None)
 
     lane = lax.broadcasted_iota(jnp.int32, (TAIL, HD), 1)
-    row = lax.broadcasted_iota(jnp.int32, (TAIL, HD), 0)
     sums = inputs[5][...] if gi else jnp.zeros((TAIL, HD), jnp.float32)
     tau_rows = functools.reduce(jnp.add, tau_totals)
     for h in range(QPG):
@@ -171,17 +171,12 @@
         total = jnp.sum(tau_rows[:, h * BLOCK : (h + 1) * BLOCK])
         sums = sums + jnp.where(lane == head, total / taus[head], 0.0)
     tau_out[...] = sums
-    high = sums.astype(jnp.bfloat16).astype(jnp.float32)
-    mid = (sums - high).astype(jnp.bfloat16).astype(jnp.float32)
-    low = sums - high - mid
-    tail = jnp.where(row == 0, high, jnp.where(row == 1, mid, jnp.where(row == 2, low, 0.0)))
 
     def drain(d, carry):
         for half in range(local_blocks):
             for which, ref in enumerate((dk_s, dv_s)):
                 at = (2 * half + which) * BLOCK
                 kv_out[d, at : at + BLOCK, :] = ref[d * local_blocks + half].astype(jnp.bfloat16)
-        kv_out[d, 2 * local_blocks * BLOCK :, :] = tail.astype(jnp.bfloat16)
         return carry
 
     lax.fori_loop(0, devices, drain, 0, unroll=2)
@@ -191,7 +186,7 @@
     return math.log2(times) if times else NEVER
 
 
-def run_group(gi, devices, place, key_blocks, tau, queries, out_grad, qg_sib, kv_in, tau_in, offsets):
+def run_group(gi, devices, place, strides, tau, queries, out_grad, qg_sib, kv_in, tau_in, offsets):
     listed = len(offsets[0])
     tokens = queries.shape[0]
     local_blocks = tokens // BLOCK
@@ -203,7 +198,7 @@
     out_own = pl.BlockSpec((tokens, width), lambda u, p, s, t: (0, 0))
     out_sib = pl.BlockSpec((2, tokens, width), lambda u, p, s, t: (0, 0, 0))
     kv_all = pl.BlockSpec((blocks, 2, BLOCK, HD), lambda u, p, s, t: (0, 0, 0, 0))
-    kv_back = pl.BlockSpec((devices, 2 * tokens + TAIL, HD), lambda u, p, s, t: (0, 0, 0))
+    kv_back = pl.BlockSpec((devices, 2 * tokens, HD), lambda u, p, s, t: (0, 0, 0))
     small = pl.BlockSpec((TAIL, HD), lambda u, p, s, t: (0, 0))
     bf = lambda *shape: jax.ShapeDtypeStruct(shape, jnp.bfloat16)
     keys_wide = listed * BLOCK
@@ -220,15 +215,34 @@
             + [pltpu.VMEM((2 * local_blocks, keys_wide, ROWS), jnp.float32)] * 2,
         ),
         out_shape=[bf(tokens, width), bf(tokens, width), bf(2, tokens, width)]
-        + [jax.ShapeDtypeStruct((TAIL, HD), jnp.float32), bf(devices, 2 * tokens + TAIL, HD)],
+        + [jax.ShapeDtypeStruct((TAIL, HD), jnp.float32), bf(devices, 2 * tokens, HD)],
         compiler_params=pltpu.CompilerParams(
-            dimension_semantics=("arbitrary",), vmem_limit_bytes=60 * 2**20
+            dimension_semantics=("arbitrary",), vmem_limit_bytes=VMEM_BYTES
         ),
         cost_estimate=pl.CostEstimate(
             flops=12 * HD * cells, bytes_accessed=6 * 2**20, transcendentals=cells
         ),
         name="group_attention",
-    )(place, key_blocks, tau, queries, qg_sib, out_grad, qg_sib, kv_in, *tau_in[:gi])
+    )(place, strides, tau, queries, qg_sib, out_grad, qg_sib, kv_in, *tau_in[:gi])
+
+
+def total_over(x, axis):
+    size = lax.axis_size(axis)
+    if size & (size - 1):
+        return lax.psum(x, axis)
+
+    def partner(distance):
+        return lax.ppermute(x, axis, [(i, i ^ distance) for i in range(size)])
+
+    step = 1
+    while step < size:
+        if size // step % 4 == 0 and size // step != 8:
+            x = (x + partner(step)) + (partner(2 * step) + partner(3 * step))
+            step *= 4
+        else:
+            x = x + partner(step)
+            step *= 2
+    return x
 
 
 def spread(gi, devices, keys, values):
@@ -251,7 +265,7 @@
         in_specs=[taken, taken],
         out_specs=pl.BlockSpec(block, lambda d: (d, 0, 0, 0, 0)),
         out_shape=jax.ShapeDtypeStruct((devices, *block[1:]), jnp.bfloat16),
-        compiler_params=pltpu.CompilerParams(vmem_limit_bytes=60 * 2**20),
+        compiler_params=pltpu.CompilerParams(vmem_limit_bytes=VMEM_BYTES),
         name="spread_keys_values",
     )(keys, values)
 
@@ -279,20 +293,24 @@
         return lax.dynamic_slice_in_dim(x, (1 - core) * wide, wide, 1)
 
     kv_in = [kv_for(gi) for gi in range(2)]
-    qg_sib = lax.ppermute(jnp.stack([theirs(q0), theirs(g0)]), "ctx", swap)
+    strides = (key_blocks[:, :, 3] - jnp.arange(block_count, dtype=jnp.int32)) % block_count
+    rows, strides = lax.optimization_barrier((jnp.stack([theirs(q0), theirs(g0)]), strides.reshape(-1)))
+    qg_sib = lax.ppermute(rows, "ctx", swap)
 
     sibs, owns, grads, tau_rows = [], [], [], []
     for gi in range(2):
         att_own, dq_own, sib, tau_here, kv_grads = run_group(
-            gi, ctx, place, key_blocks, tau, q0, g0, qg_sib, kv_in[gi], tau_rows, offsets
+            gi, ctx, place, strides, tau, q0, g0, qg_sib, kv_in[gi], tau_rows, offsets
         )
         tau_rows.append(tau_here)
-        if gi:
-            kv_grads, grads[0] = lax.optimization_barrier((kv_grads, grads[0]))
         owns.append((att_own, dq_own))
-        sibs.append(lax.ppermute(sib, "ctx", swap))
-        grads.append(lax.all_to_all(kv_grads, "ctx", 0, 0))
-    sibs = lax.optimization_barrier(sibs)
+        sibs.append(sib)
+        grads.append(kv_grads)
+        if gi == 0:
+            grads[0] = lax.all_to_all(kv_grads, "ctx", 0, 0)
+    grads, sibs, tau_last = lax.optimization_barrier((grads, sibs, tau_rows[1]))
+    grads[1] = lax.all_to_all(grads[1], "ctx", 0, 0)
+    sibs = lax.optimization_barrier([lax.ppermute(sib, "ctx", swap) for sib in sibs])
     att_parts, dq_parts = (
         [(own[which], sib[which]) for own, sib in zip(owns, sibs)] for which in range(2)
     )
@@ -310,18 +328,14 @@
         for c in range(4):
             total = None
             for src in range(c // 2, ctx, 2):
-                term = grads[c % 2][src, : 2 * tokens].reshape(local_blocks, 2, BLOCK, HD)[:, which]
+                term = grads[c % 2][src].reshape(local_blocks, 2, BLOCK, HD)[:, which]
                 term = term.astype(jnp.float32)
                 total = term if total is None else total + term
             cols.append(total.reshape(tokens, HD).astype(jnp.bfloat16))
         return jnp.concatenate(cols, axis=1)[None]
 
     key_grad, value_grad = summed(0), summed(1)
-    tails = grads[1][:, 2 * tokens : 2 * tokens + 3].astype(jnp.float32)
-    here = jnp.sum(tails, axis=(0, 1))
-    batch = lax.axis_size("batch")
-    over_batch = lax.all_to_all(jnp.broadcast_to(here, (batch, 1, HD)), "batch", 0, 0)
-    scale_total = jnp.sum(over_batch, axis=(0, 1))[:HEADS]
+    scale_total = total_over(total_over(tau_last[:1], "ctx"), "batch")[0, :HEADS]
     tau_grad = scale_total / math.sqrt(lax.axis_size("batch") * ctx * tokens)
     return (attended, query_grad, key_grad, value_grad, tau_grad)
 

time: 113 us -> 101 us (0.89)
  waiting for transfers between devices: 42.8 us -> 26 us
  starting transfers between devices: 22.6 us -> 27.4 us
  Pallas kernels: 36.9 us -> 35.6 us
  other arithmetic: 5.75 us -> 6.89 us
    all_to_all x3 -> x2, waiting for transfers between devices: 30.8 us -> 0.04 us  [the longest x1 0.04 us: body(): grads[0] = lax.all_to_all(kv_grads, 'ctx', 0, 0)]
    ppermute x3 -> x10, waiting for transfers between devices: 0.01 us -> 15.8 us  [the longest x7 15.8 us: partner(): return lax.ppermute(x, axis, [(i, i ^ distance) for i in range(size)])]
    ppermute x3 -> x10, starting transfers between devices: 1.07 us -> 9.38 us  [the longest x7 8.24 us: partner(): return lax.ppermute(x, axis, [(i, i ^ distance) for i in range(size)])]
    all_to_all x3 -> x2, starting transfers between devices: 12.7 us -> 8.45 us  [the longest x1 4.42 us: body(): grads[0] = lax.all_to_all(kv_grads, 'ctx', 0, 0)]
    slice x2 -> x5, local copies, waits for them, and re-layouts: 0.16 us -> 2.67 us  [the longest x2 1.42 us: summed(): term = grads[c % 2][src].reshape(local_blocks, 2, BLOCK, HD)[:, which]]
    all_to_all x2, waiting for transfers between devices: 12 us -> 10.2 us  [kv_for(): arrived = lax.all_to_all(spread(gi, ctx, k0, v0), 'ctx', 0, 0)]
    unnamed x17 -> x16, local copies, waits for them, and re-layouts: 2.51 us -> 0.96 us
    pallas_call x2, Pallas kernels: 31.6 us -> 30.4 us  [run_group(): pl.pallas_call(functools.partial(group_kernel, gi, devices, local_blocks,...]
  transfers between devices with their start and end apart: 8 -> 14, of which waited for: 4 -> 6; matrix products, arithmetic and copies ran while one was open for 5% -> 7% of each run, Pallas kernels for 17% -> 33%
where the time goes in v7:
time: 101 us
  Pallas kernels  35.6 us (35%)
  starting transfers between devices  27.4 us (27%)
  waiting for transfers between devices  26 us (26%)
  other arithmetic  6.89 us (7%)
  local copies, waits for them, and re-layouts  3.9 us (4%)
    pallas_call x2, Pallas kernels, run_group(): pl.pallas_call(functools.partial(group_kernel, gi, devices, local_blocks,...  30.4 us
    ppermute x7, waiting for transfers between devices, partner(): return lax.ppermute(x, axis, [(i, i ^ distance) for i in range(size)])  15.8 us
    all_to_all x2, waiting for transfers between devices, kv_for(): arrived = lax.all_to_all(spread(gi, ctx, k0, v0), 'ctx', 0, 0)  10.2 us
    all_to_all x2, starting transfers between devices, kv_for(): arrived = lax.all_to_all(spread(gi, ctx, k0, v0), 'ctx', 0, 0)  9.55 us
    ppermute x7, starting transfers between devices, partner(): return lax.ppermute(x, axis, [(i, i ^ distance) for i in range(size)])  8.24 us
    pallas_call x2, Pallas kernels, spread(): pl.pallas_call(kernel, grid=(devices // 2,), in_specs=[taken, taken], out...  5.27 us
    all_to_all x1, starting transfers between devices, body(): grads[0] = lax.all_to_all(kv_grads, 'ctx', 0, 0)  4.42 us
    all_to_all x1, starting transfers between devices, body(): grads[1] = lax.all_to_all(grads[1], 'ctx', 0, 0)  4.03 us
  transfers between devices with their start and end apart: 14, of which 6 were waited for; matrix products, arithmetic and copies ran while one was open for 7% of the time, Pallas kernels for 33%

profile of v7, /device:TPU:0, one launch (start us, length us, event | category | flops | bytes accessed | tf_op | source)
XLA Modules:
  0.0 100.7 jit_solution(1335407497076820230)
XLA Ops:
  0.6 2.7 %spread_keys_values.2 = bf16[8,2,2,128,128]{4,3,2,1,0:T(8,128)(2,1)} custom-call(bf16[256,512]{1,0:T(8,128)(2,1)} %bitcast.55, bf16[256,512]{1,0:T(8,128)(2,1)} %bitcast.57), custom_call_target="tpu_custom_call" | custom-call | tf_op jit(solution)/shard_map/spread_keys_values/pallas_call | solution.py:262
  3.3 5.3 %all-to-all-start = ((bf16[8,2,2,128,128]{4,3,2,1,0:T(8,128)(2,1)}), bf16[8,2,2,128,128]{4,3,2,1,0:T(8,128)(2,1)}, u32[]{:S(2)}, u32[]{:S(2)}) async-start(bf16[8,2,2,128,128]{4,3,2,1,0:T(8,128)(2,1)} %spread_keys_values.2), calls=%async_computation | async-start | bytes 2097152 | tf_op jit(solution)/shard_map/all_to_all | solution.py:289
  8.7 0.6 slice-done
  9.5 1.1 %pad_maximum_fusion = bf16[2,256,1024]{2,1,0:T(8,128)(2,1)} fusion(bf16[1,256,1024]{2,1,0:T(8,128)(2,1)S(1)} %get-tuple-element.79, bf16[1,256,1024]{2,1,0:T(8,128)(2,1)S(1)} %get-tuple-element.80), kind=kLoop, calls=%fused_computation | loop fusion | flops 524288 | bytes 2097152 | tf_op jit(solution)/shard_map/stack | solution.py:297
  10.5 0.5 and_select_fusion.refs_1_
  11.1 0.5 collective-permute-start
  11.6 2.6 %spread_keys_values.3 = bf16[8,2,2,128,128]{4,3,2,1,0:T(8,128)(2,1)} custom-call(bf16[256,512]{1,0:T(8,128)(2,1)} %bitcast.56, bf16[256,512]{1,0:T(8,128)(2,1)} %bitcast.58), custom_call_target="tpu_custom_call" | custom-call | tf_op jit(solution)/shard_map/spread_keys_values/pallas_call | solution.py:262
  14.2 9.9 %all-to-all-done = bf16[8,2,2,128,128]{4,3,2,1,0:T(8,128)(2,1)} async-done(((bf16[8,2,2,128,128]{4,3,2,1,0:T(8,128)(2,1)}), bf16[8,2,2,128,128]{4,3,2,1,0:T(8,128)(2,1)}, u32[]{:S(2)}, u32[]{:S(2)}) %all-to-all-start) | async-done | bytes 1048608 | tf_op jit(solution)/shard_map/all_to_all | solution.py:289
  24.1 4.3 %all-to-all-start.2 = ((bf16[8,2,2,128,128]{4,3,2,1,0:T(8,128)(2,1)}), bf16[8,2,2,128,128]{4,3,2,1,0:T(8,128)(2,1)}, u32[]{:S(2)}, u32[]{:S(2)}) async-start(bf16[8,2,2,128,128]{4,3,2,1,0:T(8,128)(2,1)} %spread_keys_values.3), calls=%async_computation.2 | async-start | bytes 2097152 | tf_op jit(solution)/shard_map/all_to_all | solution.py:289
  28.4 15.2 %group_attention.2 = (bf16[256,512]{1,0:T(8,128)(2,1)}, bf16[256,512]{1,0:T(8,128)(2,1)}, bf16[2,256,512]{2,1,0:T(8,128)(2,1)}, f32[8,128]{1,0:T(8,128)}, bf16[8,512,128]{2,1,0:T(8,128)(2,1)}) custom-call(s32[1]{0:T(128)} %bitcast.refs_0_, s32[64]{0:T(128)} %and_select_fusion.refs_1_, f32[16]{0:T(128)} %refs_2_.3, bf16[256,2048]{1,0:T(8,128)(2,1)} %bitcast.75, ...), custom_call_target="tpu_custom_call" | custom-call | flops 4429185024 | bytes 6291456 | tf_op jit(solution)/shard_map/group_attention/pallas_call | solution.py:206
  43.6 0.2 all-to-all-done.2
  43.8 4.4 %all-to-all-start.1 = ((bf16[8,512,128]{2,1,0:T(8,128)(2,1)}), bf16[8,512,128]{2,1,0:T(8,128)(2,1)}, u32[]{:S(2)}, u32[]{:S(2)}) async-start(bf16[8,512,128]{2,1,0:T(8,128)(2,1)} %get-tuple-element.27), calls=%async_computation.1 | async-start | bytes 2097152 | tf_op jit(solution)/shard_map/all_to_all | solution.py:310
  48.2 15.2 %group_attention.3 = (bf16[256,512]{1,0:T(8,128)(2,1)}, bf16[256,512]{1,0:T(8,128)(2,1)}, bf16[2,256,512]{2,1,0:T(8,128)(2,1)}, f32[8,128]{1,0:T(8,128)}, bf16[8,512,128]{2,1,0:T(8,128)(2,1)}) custom-call(s32[1]{0:T(128)} %bitcast.refs_0_, s32[64]{0:T(128)} %and_select_fusion.refs_1_, f32[16]{0:T(128)} %refs_2_.3, bf16[256,2048]{1,0:T(8,128)(2,1)} %bitcast.76, ...), custom_call_target="tpu_custom_call" | custom-call | flops 4429185024 | bytes 6291456 | tf_op jit(solution)/shard_map/group_attention/pallas_call | solution.py:206
  63.5 0.7 slice.234
  64.3 1.4 %fusion.1 = (bf16[1,512,128]{2,1,0:T(8,128)(2,1)S(1)}, bf16[1,512,128]{2,1,0:T(8,128)(2,1)S(1)}, bf16[1,512,128]{2,1,0:T(8,128)(2,1)S(1)}, bf16[1,512,128]{2,1,0...) fusion(bf16[8,512,128]{2,1,0:T(8,128)(2,1)} %all-to-all-done.1), kind=kLoop, calls=%fused_computation.31 | loop fusion | bytes 2097152 | tf_op jit(solution)/shard_map/slice | solution.py:331
  65.7 4.0 %all-to-all-start.3 = ((bf16[8,512,128]{2,1,0:T(8,128)(2,1)}), bf16[8,512,128]{2,1,0:T(8,128)(2,1)S(1)}, u32[]{:S(2)}, u32[]{:S(2)}) async-start(bf16[8,512,128]{2,1,0:T(8,128)(2,1)} %get-tuple-element.41), calls=%async_computation.3 | async-start | bytes 2097152 | tf_op jit(solution)/shard_map/all_to_all | solution.py:312
  69.7 0.6 collective-permute-start.1
  70.4 0.7 slice_add_fusion
  71.0 1.9 %collective-permute-start.4 = (f32[1,128]{1,0:T(1,128)S(1)}, f32[1,128]{1,0:T(1,128)S(1)}, u32[]{:S(2)}, u32[]{:S(2)}) collective-permute-start(f32[1,128]{1,0:T(1,128)S(1)} %slice_add_fusion), channel_id=1, source_target_pairs={{0,8},{4,12},{8,0},{12,4},{16,24},{20,28},{24,16},{28,20},{1,9},{5... | collective-permute-start | bytes 1544 | tf_op jit(solution)/shard_map/ppermute | solution.py:235
  73.0 1.5 %collective-permute-start.5 = (f32[1,128]{1,0:T(1,128)S(1)}, f32[1,128]{1,0:T(1,128)S(1)}, u32[]{:S(2)}, u32[]{:S(2)}) collective-permute-start(f32[1,128]{1,0:T(1,128)S(1)} %slice_add_fusion), channel_id=1, source_target_pairs={{0,16},{4,20},{8,24},{12,28},{16,0},{20,4},{24,8},{28,12},{1,17},{... | collective-permute-start | bytes 1544 | tf_op jit(solution)/shard_map/ppermute | solution.py:235
  74.6 9.6 %collective-permute-done.4 = f32[1,128]{1,0:T(1,128)S(1)} collective-permute-done((f32[1,128]{1,0:T(1,128)S(1)}, f32[1,128]{1,0:T(1,128)S(1)}, u32[]{:S(2)}, u32[]{:S(2)}) %collective-permute-start.4) | collective-permute-done | bytes 544 | tf_op jit(solution)/shard_map/ppermute | solution.py:235
  84.2 1.0 collective-permute-done.6
  85.2 2.0 %collective-permute-start.7 = (f32[1,128]{1,0:T(1,128)S(1)}, f32[1,128]{1,0:T(1,128)S(1)}, u32[]{:S(2)}, u32[]{:S(2)}) collective-permute-start(f32[1,128]{1,0:T(1,128)S(1)} %add_add_fusion.1), channel_id=1, source_target_pairs={{0,1},{1,0},{2,3},{3,2},{4,5},{5,4},{6,7},{7,6},{8,9},{9,8},{10,11... | collective-permute-start | bytes 1544 | tf_op jit(solution)/shard_map/ppermute | solution.py:235
  87.2 2.6 %collective-permute-start.8 = (f32[1,128]{1,0:T(1,128)S(1)}, f32[1,128]{1,0:T(1,128)S(1)}, u32[]{:S(2)}, u32[]{:S(2)}) collective-permute-start(f32[1,128]{1,0:T(1,128)S(1)} %add_add_fusion.1), channel_id=1, source_target_pairs={{0,2},{1,3},{2,0},{3,1},{4,6},{5,7},{6,4},{7,5},{8,10},{9,11},{10,... | collective-permute-start | bytes 1544 | tf_op jit(solution)/shard_map/ppermute | solution.py:235
  89.9 1.8 %collective-permute-done.8 = f32[1,128]{1,0:T(1,128)S(1)} collective-permute-done((f32[1,128]{1,0:T(1,128)S(1)}, f32[1,128]{1,0:T(1,128)S(1)}, u32[]{:S(2)}, u32[]{:S(2)}) %collective-permute-start.8) | collective-permute-done | bytes 544 | tf_op jit(solution)/shard_map/ppermute | solution.py:235
  91.6 3.5 %collective-permute-done.9 = f32[1,128]{1,0:T(1,128)S(1)} collective-permute-done((f32[1,128]{1,0:T(1,128)S(1)}, f32[1,128]{1,0:T(1,128)S(1)}, u32[]{:S(2)}, u32[]{:S(2)}) %collective-permute-start.9) | collective-permute-done | bytes 544 | tf_op jit(solution)/shard_map/ppermute | solution.py:235
  95.1 0.5 multiply_bitcast_fusion
  95.8 0.8 copy-done.4
  96.8 1.1 %maximum_bitcast_fusion.1 = bf16[1,256,2048]{2,1,0:T(8,128)(2,1)} fusion(bf16[256,512]{1,0:T(8,128)(2,1)S(1)} %get-tuple-element.62, bf16[256,512]{1,0:T(8,128)(2,1)S(1)} %get-tuple-element.60, bf16[256,512]{1,0:T(8,128)(2,1)S(1)} %get-tuple-element.61, bf16[256,512]{1,0:T(8,128)(2,1)S(1)} %get-tuple-element.59), kind=kLoop, calls=%fused_computation.2 | loop fusion | flops 4194304 | bytes 2097152 | tf_op jit(solution)/shard_map/broadcast_in_dim | solution.py:324
  97.9 1.1 %maximum_bitcast_fusion = bf16[1,256,2048]{2,1,0:T(8,128)(2,1)} fusion(bf16[256,512]{1,0:T(8,128)(2,1)S(1)} %get-tuple-element.77, bf16[256,512]{1,0:T(8,128)(2,1)S(1)} %get-tuple-element.75, bf16[256,512]{1,0:T(8,128)(2,1)S(1)} %get-tuple-element.78, bf16[256,512]{1,0:T(8,128)(2,1)S(1)} %get-tuple-element.76), kind=kLoop, calls=%fused_computation.1 | loop fusion | flops 4194304 | bytes 2097152 | tf_op jit(solution)/shard_map/broadcast_in_dim | solution.py:323
  99.2 0.7 maximum_bitcast_fusion.3
  99.9 0.7 maximum_bitcast_fusion.2
  (41 shorter events, 1.3 us)
Async XLA Ops:
  3.3 5.3 %copy-start = (bf16[1,256,2048]{2,1,0:T(8,128)(2,1)S(1)}, bf16[1,256,2048]{2,1,0:T(8,128)(2,1)}, u32[]{:S(2)}) copy-start(bf16[1,256,2048]{2,1,0:T(8,128)(2,1)} %param.6) | copy-start | bytes 3145732
  3.3 5.3 %copy-start.1 = (bf16[1,256,2048]{2,1,0:T(8,128)(2,1)S(1)}, bf16[1,256,2048]{2,1,0:T(8,128)(2,1)}, u32[]{:S(2)}) copy-start(bf16[1,256,2048]{2,1,0:T(8,128)(2,1)} %param.10) | copy-start | bytes 3145732
  3.3 20.8 %all-to-all-start = ((bf16[8,2,2,128,128]{4,3,2,1,0:T(8,128)(2,1)}), bf16[8,2,2,128,128]{4,3,2,1,0:T(8,128)(2,1)}, u32[]{:S(2)}, u32[]{:S(2)}) async-start(bf16[8,2,2,128,128]{4,3,2,1,0:T(8,128)(2,1)} %spread_keys_values.2), calls=%async_computation | async-start | bytes 2097152 | tf_op jit(solution)/shard_map/all_to_all | solution.py:289
  8.6 0.7 slice-start
  11.1 17.3 %collective-permute-start = (bf16[2,256,1024]{2,1,0:T(8,128)(2,1)}, bf16[2,256,1024]{2,1,0:T(8,128)(2,1)}, u32[]{:S(2)}, u32[]{:S(2)}) collective-permute-start(bf16[2,256,1024]{2,1,0:T(8,128)(2,1)} %pad_maximum_fusion), channel_id=1, source_target_pairs={{0,4},{4,0},{8,12},{12,8},{16,20},{20,16},{24,28},{28,24},{1,5},{5... | collective-permute-start | bytes 3145736 | tf_op jit(solution)/shard_map/ppermute | solution.py:298
  24.1 19.7 %all-to-all-start.2 = ((bf16[8,2,2,128,128]{4,3,2,1,0:T(8,128)(2,1)}), bf16[8,2,2,128,128]{4,3,2,1,0:T(8,128)(2,1)}, u32[]{:S(2)}, u32[]{:S(2)}) async-start(bf16[8,2,2,128,128]{4,3,2,1,0:T(8,128)(2,1)} %spread_keys_values.3), calls=%async_computation.2 | async-start | bytes 2097152 | tf_op jit(solution)/shard_map/all_to_all | solution.py:289
  43.8 19.7 %all-to-all-start.1 = ((bf16[8,512,128]{2,1,0:T(8,128)(2,1)}), bf16[8,512,128]{2,1,0:T(8,128)(2,1)}, u32[]{:S(2)}, u32[]{:S(2)}) async-start(bf16[8,512,128]{2,1,0:T(8,128)(2,1)} %get-tuple-element.27), calls=%async_computation.1 | async-start | bytes 2097152 | tf_op jit(solution)/shard_map/all_to_all | solution.py:310
  64.1 6.2 %collective-permute-start.3 = (f32[1,128]{1,0:T(1,128)S(1)}, f32[1,128]{1,0:T(1,128)S(1)}, u32[]{:S(2)}, u32[]{:S(2)}) collective-permute-start(f32[1,128]{1,0:T(1,128)S(1)} %slice.234), channel_id=1, source_target_pairs={{0,4},{4,0},{8,12},{12,8},{16,20},{20,16},{24,28},{28,24},{1,5},{5... | collective-permute-start | bytes 1544 | tf_op jit(solution)/shard_map/ppermute | solution.py:235
  65.6 4.1 %copy-start.6 = (bf16[2,256,512]{2,1,0:T(8,128)(2,1)S(1)}, bf16[2,256,512]{2,1,0:T(8,128)(2,1)}, u32[]{:S(2)}) copy-start(bf16[2,256,512]{2,1,0:T(8,128)(2,1)} %get-tuple-element.33) | copy-start | bytes 1572868
  65.6 4.6 %copy-start.7 = (bf16[2,256,512]{2,1,0:T(8,128)(2,1)S(1)}, bf16[2,256,512]{2,1,0:T(8,128)(2,1)}, u32[]{:S(2)}) copy-start(bf16[2,256,512]{2,1,0:T(8,128)(2,1)} %get-tuple-element.34) | copy-start | bytes 1572868
  65.7 33.3 %all-to-all-start.3 = ((bf16[8,512,128]{2,1,0:T(8,128)(2,1)}), bf16[8,512,128]{2,1,0:T(8,128)(2,1)S(1)}, u32[]{:S(2)}, u32[]{:S(2)}) async-start(bf16[8,512,128]{2,1,0:T(8,128)(2,1)} %get-tuple-element.41), calls=%async_computation.3 | async-start | bytes 2097152 | tf_op jit(solution)/shard_map/all_to_all | solution.py:312
  69.7 26.0 %copy-start.2 = (bf16[256,512]{1,0:T(8,128)(2,1)S(1)}, bf16[256,512]{1,0:T(8,128)(2,1)}, u32[]{:S(2)}) copy-start(bf16[256,512]{1,0:T(8,128)(2,1)} %get-tuple-element.26) | copy-start | bytes 786436
  69.7 26.0 %copy-start.3 = (bf16[256,512]{1,0:T(8,128)(2,1)S(1)}, bf16[256,512]{1,0:T(8,128)(2,1)}, u32[]{:S(2)}) copy-start(bf16[256,512]{1,0:T(8,128)(2,1)} %get-tuple-element.38) | copy-start | bytes 786436
  69.7 25.9 %collective-permute-start.1 = (bf16[2,256,512]{2,1,0:T(8,128)(2,1)S(1)}, bf16[2,256,512]{2,1,0:T(8,128)(2,1)S(1)}, u32[]{:S(2)}, u32[]{:S(2)}) collective-permute-start(bf16[2,256,512]{2,1,0:T(8,128)(2,1)S(1)} %copy-done.6), channel_id=1, source_target_pairs={{0,4},{4,0},{8,12},{12,8},{16,20},{20,16},{24,28},{28,24},{1,5},{5... | collective-permute-start | bytes 1572872 | tf_op jit(solution)/shard_map/ppermute | solution.py:313
  70.3 25.4 %collective-permute-start.2 = (bf16[2,256,512]{2,1,0:T(8,128)(2,1)S(1)}, bf16[2,256,512]{2,1,0:T(8,128)(2,1)S(1)}, u32[]{:S(2)}, u32[]{:S(2)}) collective-permute-start(bf16[2,256,512]{2,1,0:T(8,128)(2,1)S(1)} %copy-done.7), channel_id=1, source_target_pairs={{0,4},{4,0},{8,12},{12,8},{16,20},{20,16},{24,28},{28,24},{1,5},{5... | collective-permute-start | bytes 1572872 | tf_op jit(solution)/shard_map/ppermute | solution.py:313
  71.0 13.1 %collective-permute-start.4 = (f32[1,128]{1,0:T(1,128)S(1)}, f32[1,128]{1,0:T(1,128)S(1)}, u32[]{:S(2)}, u32[]{:S(2)}) collective-permute-start(f32[1,128]{1,0:T(1,128)S(1)} %slice_add_fusion), channel_id=1, source_target_pairs={{0,8},{4,12},{8,0},{12,4},{16,24},{20,28},{24,16},{28,20},{1,9},{5... | collective-permute-start | bytes 1544 | tf_op jit(solution)/shard_map/ppermute | solution.py:235
  73.0 11.2 %collective-permute-start.5 = (f32[1,128]{1,0:T(1,128)S(1)}, f32[1,128]{1,0:T(1,128)S(1)}, u32[]{:S(2)}, u32[]{:S(2)}) collective-permute-start(f32[1,128]{1,0:T(1,128)S(1)} %slice_add_fusion), channel_id=1, source_target_pairs={{0,16},{4,20},{8,24},{12,28},{16,0},{20,4},{24,8},{28,12},{1,17},{... | collective-permute-start | bytes 1544 | tf_op jit(solution)/shard_map/ppermute | solution.py:235
  74.4 10.7 %collective-permute-start.6 = (f32[1,128]{1,0:T(1,128)S(1)}, f32[1,128]{1,0:T(1,128)S(1)}, u32[]{:S(2)}, u32[]{:S(2)}) collective-permute-start(f32[1,128]{1,0:T(1,128)S(1)} %slice_add_fusion), channel_id=1, source_target_pairs={{0,24},{4,28},{8,16},{12,20},{16,8},{20,12},{24,0},{28,4},{1,25},{... | collective-permute-start | bytes 1544 | tf_op jit(solution)/shard_map/ppermute | solution.py:235
  85.2 4.7 %collective-permute-start.7 = (f32[1,128]{1,0:T(1,128)S(1)}, f32[1,128]{1,0:T(1,128)S(1)}, u32[]{:S(2)}, u32[]{:S(2)}) collective-permute-start(f32[1,128]{1,0:T(1,128)S(1)} %add_add_fusion.1), channel_id=1, source_target_pairs={{0,1},{1,0},{2,3},{3,2},{4,5},{5,4},{6,7},{7,6},{8,9},{9,8},{10,11... | collective-permute-start | bytes 1544 | tf_op jit(solution)/shard_map/ppermute | solution.py:235
  87.2 4.4 %collective-permute-start.8 = (f32[1,128]{1,0:T(1,128)S(1)}, f32[1,128]{1,0:T(1,128)S(1)}, u32[]{:S(2)}, u32[]{:S(2)}) collective-permute-start(f32[1,128]{1,0:T(1,128)S(1)} %add_add_fusion.1), channel_id=1, source_target_pairs={{0,2},{1,3},{2,0},{3,1},{4,6},{5,7},{6,4},{7,5},{8,10},{9,11},{10,... | collective-permute-start | bytes 1544 | tf_op jit(solution)/shard_map/ppermute | solution.py:235
  89.8 5.3 %collective-permute-start.9 = (f32[1,128]{1,0:T(1,128)S(1)}, f32[1,128]{1,0:T(1,128)S(1)}, u32[]{:S(2)}, u32[]{:S(2)}) collective-permute-start(f32[1,128]{1,0:T(1,128)S(1)} %add_add_fusion.1), channel_id=1, source_target_pairs={{0,3},{1,2},{2,1},{3,0},{4,7},{5,6},{6,5},{7,4},{8,11},{9,10},{10,... | collective-permute-start | bytes 1544 | tf_op jit(solution)/shard_map/ppermute | solution.py:235
  95.7 1.0 copy-start.4
  95.7 1.0 %copy-start.5 = (bf16[256,512]{1,0:T(8,128)(2,1)S(1)}, bf16[256,512]{1,0:T(8,128)(2,1)}, u32[]{:S(2)}) copy-start(bf16[256,512]{1,0:T(8,128)(2,1)} %get-tuple-element.39) | copy-start | bytes 786436

commit v8 on v7

v8 whole, which is shorter than its diff:
```python
import functools
import math

import jax
import jax.numpy as jnp
from jax import lax
from jax.experimental import pallas as pl
from jax.experimental.pallas import tpu as pltpu
from jax.sharding import PartitionSpec as P

HEADS = 16
KV_HEADS = 4
HD = 128
BLOCK = 128
QPG = HEADS // KV_HEADS
CHUNK = 4
ROWS = QPG * BLOCK
TAIL = 8
VMEM_BYTES = 63 * 2**20
STRIDES = (2, 3)
LOG2E = math.log2(math.e)
NEVER = -1e30


def distinct_offsets(block_count, listed_count):
    tables = []
    for stride in STRIDES:
        steps = range(1, (listed_count - 3) // 2 + 1)
        listed = [-1, 0, 1] + [stride * m for m in steps] + [-stride * m for m in steps]
        times = {}
        for o in listed:
            times[o % block_count] = times.get(o % block_count, 0) + 1
        tables.append(sorted(times.items()))
    most = max(len(t) for t in tables)
    return [t + [(0, 0)] * (most - len(t)) for t in tables]


def nt(a, b):
    return jnp.dot(a, b, preferred_element_type=jnp.float32)


def group_kernel(gi, devices, local_blocks, listed, offsets, *refs):
    place, strides, taus = refs[:3]
    inputs, rest = refs[3 : 6 + gi], refs[6 + gi :]
    rows_in, turned_in, kv_in = inputs[:3]
    tau_out, kv_out, o_out, ds_out = rest[:4]
    vt_s, dk_s, dv_s, s_s, e_s, ds_s, sems = rest[4:]
    blocks = devices * local_blocks
    me = place[0]
    group = 2 * (me % 2) + gi
    units = 2 * local_blocks

    chunks = [range(c, min(c + CHUNK, listed)) for c in range(0, listed, CHUNK)]
    scale = jnp.concatenate(
        [jnp.full((1, BLOCK), taus[group * QPG + h], jnp.float32) for h in range(QPG)], axis=1
    ) / math.sqrt(HD)
    factor = scale * LOG2E

    def rows_of(c):
        return slice(c[0] * BLOCK, (c[-1] + 1) * BLOCK)

    def in_rows(x):
        return x.reshape(-1, 8, ROWS)

    tau_totals = []

    def part(n):
        s_n, e_n = s_s.at[n], e_s.at[n]
        query_block, ids, bias = listing(offsets, strides, me, group, n, local_blocks, blocks)

        def taken(which, c):
            return jnp.concatenate([kv_in[ids[j], which] for j in c], axis=0)

        def picked(ref, c, axis):
            return jnp.concatenate([ref[ids[j]] for j in c], axis=axis)

        def add_blocks(ref, c, x):
            for n, j in enumerate(c):
                ref[ids[j]] += x[n * BLOCK : (n + 1) * BLOCK, :]

        most = None
        for c in chunks:
            raw = nt(taken(0, c), turned_in[0, n, 0])
            s_n[rows_of(c), :] = raw
            top = jnp.max(in_rows(raw), axis=0)
            most = top if most is None else jnp.maximum(most, top)
            yield
        top_row = jnp.max(most, axis=0, keepdims=True) * factor
        total = jnp.zeros((8, ROWS), jnp.float32)
        for c in chunks:
            for j in c:
                rows = slice(j * BLOCK, (j + 1) * BLOCK)
                e = jnp.exp2(s_n[rows, :] * factor - (top_row - bias[j]))
                e_n[rows, :] = e
                total = total + jnp.sum(in_rows(e), axis=0)
            yield
        inverse = 1.0 / jnp.sum(total, axis=0, keepdims=True)
        o_t = jnp.zeros((HD, ROWS), jnp.float32)
        for c in chunks:
            probs = (e_n[rows_of(c), :] * inverse).astype(jnp.bfloat16)
            o_t = o_t + nt(picked(vt_s, c, 1), probs)
            add_blocks(dv_s, c, nt(probs, rows_in[0, n, 1]))
            yield
        row_dot = jnp.sum(turned_in[0, n, 1].astype(jnp.float32) * o_t, axis=0, keepdims=True)
        o_out[n] = o_t.astype(jnp.bfloat16)
        weight_scale = inverse * scale
        tau_rows = jnp.zeros((8, ROWS), jnp.float32)
        for c in chunks:
            dweights = nt(taken(1, c), turned_in[0, n, 1])
            scaled = e_n[rows_of(c), :] * weight_scale * (dweights - row_dot)
            tau_rows = tau_rows + jnp.sum(in_rows(scaled * s_n[rows_of(c), :]), axis=0)
            low = scaled.astype(jnp.bfloat16)
            ds_s[n, rows_of(c), :] = low
            add_blocks(dk_s, c, nt(low, rows_in[0, n, 0]))
            yield
        tau_totals.append(tau_rows)
        pltpu.make_async_copy(ds_s.at[n], ds_out.at[n], sems.at[n]).start()

    def turned(which, ref):
        turns = 2 * len(chunks)
        for turn in range(turns):
            for b in range(blocks * turn // turns, blocks * (turn + 1) // turns):
                ref[b] = kv_in[b, which].T
            yield

    dk_s[...] = jnp.zeros_like(dk_s)
    dv_s[...] = jnp.zeros_like(dv_s)
    shares = [(0, turned(1, vt_s))]
    shares += [(n * len(chunks), part(n)) for n in range(units)]
    for turn in range((4 + units) * len(chunks)):
        for begin, share in shares:
            if turn >= begin:
                next(share, None)

    lane = lax.broadcasted_iota(jnp.int32, (TAIL, HD), 1)
    sums = inputs[3][...] if gi else jnp.zeros((TAIL, HD), jnp.float32)
    tau_rows = functools.reduce(jnp.add, tau_totals)
    for h in range(QPG):
        head = group * QPG + h
        total = jnp.sum(tau_rows[:, h * BLOCK : (h + 1) * BLOCK])
        sums = sums + jnp.where(lane == head, total / taus[head], 0.0)
    tau_out[...] = sums

    def drain(d, carry):
        for half in range(local_blocks):
            for which, ref in enumerate((dk_s, dv_s)):
                at = (2 * half + which) * BLOCK
                kv_out[d, at : at + BLOCK, :] = ref[d * local_blocks + half].astype(jnp.bfloat16)
        return carry

    lax.fori_loop(0, devices, drain, 0, unroll=2)
    for n in range(units):
        pltpu.make_async_copy(ds_s.at[n], ds_out.at[n], sems.at[n]).wait()


def times_bias(times):
    return math.log2(times) if times else NEVER


def listing(offsets, strides, me, group, n, local_blocks, blocks):
    query_block = (me ^ (n // local_blocks)) * local_blocks + n % local_blocks
    wide = strides[group * blocks + query_block] == STRIDES[1]
    ids, bias = [], []
    for (narrow_off, narrow_times), (wide_off, wide_times) in zip(*offsets):
        ids.append((query_block + jnp.where(wide, wide_off, narrow_off)) % blocks)
        bias.append(
            times_bias(narrow_times)
            if narrow_times == wide_times
            else jnp.where(wide, times_bias(wide_times), times_bias(narrow_times))
        )
    return query_block, ids, bias


def per_head(x):
    return [x[:, h * HD : (h + 1) * HD] for h in range(QPG)]


def once(shape, index=None):
    at = index or (lambda *_: (0,) * len(shape))
    return pl.BlockSpec(shape, at, pipeline_mode=pl.Buffered(1))


def run_group(gi, devices, place, strides, tau, rows, turned, kv_in, tau_in, offsets):
    listed = len(offsets[0])
    units = rows.shape[1]
    local_blocks = units // 2
    blocks = devices * local_blocks
    bf = lambda *shape: jax.ShapeDtypeStruct(shape, jnp.bfloat16)
    keys_wide = listed * BLOCK
    cells = units * ROWS * keys_wide
    small = once((TAIL, HD))
    kv_back = (devices, 2 * local_blocks * BLOCK, HD)
    return pl.pallas_call(
        functools.partial(group_kernel, gi, devices, local_blocks, listed, offsets),
        grid_spec=pltpu.PrefetchScalarGridSpec(
            num_scalar_prefetch=3,
            grid=(1,),
            in_specs=[
                once((1, units, 2, ROWS, HD), lambda *_: (gi, 0, 0, 0, 0)),
                once((1, units, 2, HD, ROWS), lambda *_: (gi, 0, 0, 0, 0)),
                once((blocks, 2, BLOCK, HD)),
            ]
            + [small] * gi,
            out_specs=[small, once(kv_back), once((units, HD, ROWS)), pl.BlockSpec(memory_space=pl.ANY)],
            scratch_shapes=[pltpu.VMEM((blocks, HD, BLOCK), jnp.bfloat16)]
            + [pltpu.VMEM((blocks, BLOCK, HD), jnp.float32)] * 2
            + [pltpu.VMEM((units, keys_wide, ROWS), jnp.float32)] * 2
            + [pltpu.VMEM((units, keys_wide, ROWS), jnp.bfloat16), pltpu.SemaphoreType.DMA((units,))],
        ),
        out_shape=[jax.ShapeDtypeStruct((TAIL, HD), jnp.float32), bf(*kv_back), bf(units, HD, ROWS)]
        + [bf(units, keys_wide, ROWS)],
        compiler_params=pltpu.CompilerParams(
            dimension_semantics=("arbitrary",), vmem_limit_bytes=VMEM_BYTES
        ),
        cost_estimate=pl.CostEstimate(
            flops=10 * HD * cells, bytes_accessed=6 * 2**20, transcendentals=cells
        ),
        name="group_attention",
    )(place, strides, tau, rows, turned, kv_in, *tau_in[:gi])


def turn(place, queries, out_grad, qg_sib):
    tokens = queries.shape[0]
    local_blocks = tokens // BLOCK
    units = 2 * local_blocks
    width = QPG * HD

    def kernel(place, q_own, g_own, q_sib, g_sib, rows, turned):
        own = pl.program_id(1) < local_blocks
        for which, (a, b) in enumerate(((q_own, q_sib), (g_own, g_sib))):
            heads = per_head(jnp.where(own, a[...], b[0]))
            rows[0, 0, which] = jnp.concatenate(heads, axis=0)
            turned[0, 0, which] = jnp.concatenate([x.T for x in heads], axis=1)

    mine = pl.BlockSpec(
        (BLOCK, width), lambda gi, u, p: (jnp.minimum(u, local_blocks - 1), 2 * (p[0] % 2) + gi)
    )

    def theirs(which):
        return pl.BlockSpec(
            (1, BLOCK, width), lambda gi, u, p: (which, jnp.maximum(u - local_blocks, 0), gi)
        )

    shapes = [(2, units, 2, ROWS, HD), (2, units, 2, HD, ROWS)]
    return pl.pallas_call(
        kernel,
        grid_spec=pltpu.PrefetchScalarGridSpec(
            num_scalar_prefetch=1,
            grid=(2, units),
            in_specs=[mine, mine, theirs(0), theirs(1)],
            out_specs=[pl.BlockSpec((1, 1, *x[2:]), lambda gi, u, p: (gi, u, 0, 0, 0)) for x in shapes],
        ),
        out_shape=[jax.ShapeDtypeStruct(x, jnp.bfloat16) for x in shapes],
        compiler_params=pltpu.CompilerParams(vmem_limit_bytes=VMEM_BYTES),
        name="turn_queries",
    )(place, queries, out_grad, qg_sib, qg_sib)


def finish(devices, place, strides, parts, offsets):
    units, keys_wide, _ = parts[0][0].shape
    local_blocks = units // 2
    blocks = devices * local_blocks
    tokens = local_blocks * BLOCK
    last = local_blocks - 1
    wide = 2 * QPG * HD

    def kernel(place, strides, *refs):
        ins, (own_out, sib_out, kt_s) = (refs[:3], refs[3:6]), refs[6:]
        n = pl.program_id(0)
        me = place[0]

        @pl.when(n == 0)
        def _():
            for gi in range(2):
                for b in range(blocks):
                    kt_s[gi, b] = ins[gi][1][b, 0].T

        results = [[], []]
        for gi, (ds, _, o_t) in enumerate(ins):
            _, ids, _ = listing(offsets, strides, me, 2 * (me % 2) + gi, n, local_blocks, blocks)
            dq_t = nt(jnp.concatenate([kt_s[gi, b] for b in ids], axis=1), ds[0])
            results[0] += [x.T for x in per_head(o_t[0])]
            results[1] += [x.T for x in per_head(dq_t.astype(jnp.bfloat16))]
        results = [jnp.concatenate(x, axis=1) for x in results]

        @pl.when(n < local_blocks)
        def _():
            for which in range(2):
                own_out[which] = results[which]

        @pl.when(n >= local_blocks)
        def _():
            for which in range(2):
                sib_out[which] = results[which]

    each = [
        pl.BlockSpec((1, keys_wide, ROWS), lambda n, p, s: (n, 0, 0)),
        pl.BlockSpec((blocks, 1, BLOCK, HD), lambda n, p, s: (0, 0, 0, 0)),
        pl.BlockSpec((1, HD, ROWS), lambda n, p, s: (n, 0, 0)),
    ]
    return pl.pallas_call(
        kernel,
        grid_spec=pltpu.PrefetchScalarGridSpec(
            num_scalar_prefetch=2,
            grid=(units,),
            in_specs=each * 2,
            out_specs=[
                pl.BlockSpec((2, BLOCK, wide), lambda n, p, s: (0, jnp.minimum(n, last), 0)),
                pl.BlockSpec((2, BLOCK, wide), lambda n, p, s: (0, jnp.maximum(n - local_blocks, 0), 0)),
            ],
            scratch_shapes=[pltpu.VMEM((2, blocks, HD, BLOCK), jnp.bfloat16)],
        ),
        out_shape=[jax.ShapeDtypeStruct((2, tokens, wide), jnp.bfloat16)] * 2,
        compiler_params=pltpu.CompilerParams(vmem_limit_bytes=VMEM_BYTES),
        cost_estimate=pl.CostEstimate(flops=2**20, bytes_accessed=2**20, transcendentals=0),
        name="finish_rows",
    )(place, strides, *parts[0], *parts[1])


def partners(x, axis, distances):
    size = lax.axis_size(axis)
    a, b, c = (lax.ppermute(x, axis, [(i, i ^ d) for i in range(size)]) for d in distances)
    return (x + a) + (b + c)


def total_everywhere(x):
    ctx, batch = lax.axis_size("ctx"), lax.axis_size("batch")
    if batch != 4 or ctx not in (8, 32):
        return x, lambda y: lax.psum(y, ("ctx", "batch"))

    def rest(y):
        y = partners(y, "batch", (1, 2, 3))
        step = 2
        while step < ctx:
            y = partners(y, "ctx", (step, 2 * step, 3 * step))
            step *= 4
        return y

    return x + lax.ppermute(x, "ctx", [(i, i ^ 1) for i in range(ctx)]), rest


def spread(gi, devices, keys, values):
    tokens, width = keys.shape
    local_blocks = tokens // BLOCK

    def kernel(k_ref, v_ref, out):
        for parity in range(2):
            cols = slice((2 * parity + gi) * HD, (2 * parity + gi + 1) * HD)
            for half in range(local_blocks):
                rows = slice(half * BLOCK, (half + 1) * BLOCK)
                out[parity, half, 0] = k_ref[rows, cols]
                out[parity, half, 1] = v_ref[rows, cols]

    taken = pl.BlockSpec((tokens, width), lambda d: (0, 0))
    block = (2, local_blocks, 2, BLOCK, HD)
    return pl.pallas_call(
        kernel,
        grid=(devices // 2,),
        in_specs=[taken, taken],
        out_specs=pl.BlockSpec(block, lambda d: (d, 0, 0, 0, 0)),
        out_shape=jax.ShapeDtypeStruct((devices, *block[1:]), jnp.bfloat16),
        compiler_params=pltpu.CompilerParams(vmem_limit_bytes=VMEM_BYTES),
        name="spread_keys_values",
    )(keys, values)


def body(queries, keys, values, tau, out_grad, key_blocks):
    ctx = lax.axis_size("ctx")
    me = lax.axis_index("ctx").astype(jnp.int32)
    core = me % 2
    tokens = queries.shape[1]
    local_blocks = tokens // BLOCK
    block_count = ctx * local_blocks
    listed_count = key_blocks.shape[2]
    offsets = distinct_offsets(block_count, listed_count)
    swap = [(d, d ^ 1) for d in range(ctx)]
    wide = 2 * QPG * HD

    q0, k0, v0, g0 = queries[0], keys[0], values[0], out_grad[0]
    place = me[None]

    def kv_for(gi):
        arrived = lax.all_to_all(spread(gi, ctx, k0, v0), "ctx", 0, 0)
        return arrived.reshape(block_count, 2, BLOCK, HD)

    def theirs(x):
        return lax.dynamic_slice_in_dim(x, (1 - core) * wide, wide, 1)

    kv_in = [kv_for(gi) for gi in range(2)]
    strides = (key_blocks[:, :, 3] - jnp.arange(block_count, dtype=jnp.int32)) % block_count
    rows, strides = lax.optimization_barrier((jnp.stack([theirs(q0), theirs(g0)]), strides.reshape(-1)))
    qg_sib = lax.ppermute(rows, "ctx", swap)

    rows, turned = turn(place, q0, g0, qg_sib)
    grads, tau_rows, parts = [], [], []
    for gi in range(2):
        tau_here, kv_grads, o_t, ds = run_group(
            gi, ctx, place, strides, tau, rows, turned, kv_in[gi], tau_rows, offsets
        )
        tau_rows.append(tau_here)
        parts.append((ds, kv_in[gi], o_t))
        grads.append(kv_grads)
        if gi == 0:
            grads[0] = lax.all_to_all(kv_grads, "ctx", 0, 0)
    grads, parts, tau_last = lax.optimization_barrier((grads, parts, tau_rows[1]))
    grads[1] = lax.all_to_all(grads[1], "ctx", 0, 0)
    tau_pair, over_rest = total_everywhere(tau_last)
    tau_pair, parts, grads[0] = lax.optimization_barrier((tau_pair, parts, grads[0]))
    own, sib = finish(ctx, place, strides, parts, offsets)
    sib = lax.ppermute(sib, "ctx", swap)

    def both(which):
        a = jnp.where(core == 0, own[which], sib[which])
        b = jnp.where(core == 0, sib[which], own[which])
        return jnp.concatenate([a, b], axis=1)[None]

    attended, query_grad = both(0), both(1)

    def summed(which):
        cols = []
        for c in range(4):
            total = None
            for src in range(c // 2, ctx, 2):
                term = grads[c % 2][src].reshape(local_blocks, 2, BLOCK, HD)[:, which]
                term = term.astype(jnp.float32)
                total = term if total is None else total + term
            cols.append(total.reshape(tokens, HD).astype(jnp.bfloat16))
        return jnp.concatenate(cols, axis=1)[None]

    key_grad, value_grad = summed(0), summed(1)
    scale_total = over_rest(tau_pair)[0, :HEADS]
    tau_grad = scale_total / math.sqrt(lax.axis_size("batch") * ctx * tokens)
    return (attended, query_grad, key_grad, value_grad, tau_grad)


def solution(mesh):
    rows = P("batch", "ctx", None)
    return jax.shard_map(
        body,
        mesh=mesh,
        in_specs=(rows, rows, rows, P(), rows, P()),
        out_specs=(rows, rows, rows, rows, P()),
        check_vma=False,
    )
```

time: 101 us -> 104 us (1.030)
  Pallas kernels: 35.6 us -> 50 us
  waiting for transfers between devices: 26 us -> 14.2 us
    pallas_call x0 -> x2, Pallas kernels: none -> 15.3 us  [the longest x1 8.7 us: finish(): pl.pallas_call(kernel, grid_spec=pltpu.PrefetchScalarGridSpec(num_scalar_...]
    ppermute x9 -> x8, waiting for transfers between devices: 15.8 us -> 3.18 us  [the longest x6 3.17 us: partners(): lax.ppermute(x, axis, [(i, i ^ d) for i in range(size)])]
    slice x2, local copies, waits for them, and re-layouts: 1.42 us -> 3.45 us  [summed(): term = grads[c % 2][src].reshape(local_blocks, 2, BLOCK, HD)[:, which]]
    ppermute x9 -> x8, starting transfers between devices: 8.88 us -> 8.31 us  [the longest x6 8.31 us: partners(): lax.ppermute(x, axis, [(i, i ^ d) for i in range(size)])]
  transfers between devices with their start and end apart: 14 -> 13, of which waited for: 6 -> 5; matrix products, arithmetic and copies ran while one was open for 7% -> 8% of each run, Pallas kernels for 33% -> 46%
where the time goes in v8:
time: 104 us; the launch traced here: 103 us
  Pallas kernels  50 us (48%)
  starting transfers between devices  27.3 us (26%)
  waiting for transfers between devices  14.2 us (14%)
  other arithmetic  7.09 us (7%)
  local copies, waits for them, and re-layouts  3.73 us (4%)
    pallas_call x2, Pallas kernels, run_group(): pl.pallas_call(functools.partial(group_kernel, gi, devices, local_blocks,...  29.4 us
    all_to_all x2, waiting for transfers between devices, kv_for(): arrived = lax.all_to_all(spread(gi, ctx, k0, v0), 'ctx', 0, 0)  10.4 us
    all_to_all x2, starting transfers between devices, kv_for(): arrived = lax.all_to_all(spread(gi, ctx, k0, v0), 'ctx', 0, 0)  9.54 us
    pallas_call x1, Pallas kernels, finish(): pl.pallas_call(kernel, grid_spec=pltpu.PrefetchScalarGridSpec(num_scalar_...  8.7 us
    ppermute x6, starting transfers between devices, partners(): lax.ppermute(x, axis, [(i, i ^ d) for i in range(size)])  8.31 us
    pallas_call x1, Pallas kernels, turn(): pl.pallas_call(kernel, grid_spec=pltpu.PrefetchScalarGridSpec(num_scalar_...  6.58 us
    pallas_call x2, Pallas kernels, spread(): pl.pallas_call(kernel, grid=(devices // 2,), in_specs=[taken, taken], out...  5.28 us
    all_to_all x1, starting transfers between devices, body(): grads[1] = lax.all_to_all(grads[1], 'ctx', 0, 0)  4.47 us
  transfers between devices with their start and end apart: 13, of which 5 were waited for; matrix products, arithmetic and copies ran while one was open for 8% of the time, Pallas kernels for 46%

profile of v8, /device:TPU:0, one launch (start us, length us, event | category | flops | bytes accessed | tf_op | source)
XLA Modules:
  0.0 103.1 jit_solution(11795599050173946835)
XLA Ops:
  0.6 2.6 %spread_keys_values.2 = bf16[8,2,2,128,128]{4,3,2,1,0:T(8,128)(2,1)} custom-call(bf16[256,512]{1,0:T(8,128)(2,1)} %bitcast.53, bf16[256,512]{1,0:T(8,128)(2,1)} %bitcast.55), custom_call_target="tpu_custom_call" | custom-call | tf_op jit(solution)/shard_map/spread_keys_values/pallas_call | solution.py:356
  3.3 5.3 %all-to-all-start = ((bf16[8,2,2,128,128]{4,3,2,1,0:T(8,128)(2,1)}), bf16[8,2,2,128,128]{4,3,2,1,0:T(8,128)(2,1)}, u32[]{:S(2)}, u32[]{:S(2)}) async-start(bf16[8,2,2,128,128]{4,3,2,1,0:T(8,128)(2,1)} %spread_keys_values.2), calls=%async_computation | async-start | bytes 2097152 | tf_op jit(solution)/shard_map/all_to_all | solution.py:383
  8.9 1.1 %pad_maximum_fusion = bf16[2,256,1024]{2,1,0:T(8,128)(2,1)} fusion(bf16[1,256,1024]{2,1,0:T(8,128)(2,1)S(1)} %get-tuple-element.95, bf16[1,256,1024]{2,1,0:T(8,128)(2,1)S(1)} %get-tuple-element.96), kind=kLoop, calls=%fused_computation | loop fusion | flops 524288 | bytes 2097152 | tf_op jit(solution)/shard_map/stack | solution.py:391
  9.9 0.6 and_select_fusion.refs_1_.strides
  10.5 0.5 collective-permute-start
  11.0 2.6 %spread_keys_values.3 = bf16[8,2,2,128,128]{4,3,2,1,0:T(8,128)(2,1)} custom-call(bf16[256,512]{1,0:T(8,128)(2,1)} %bitcast.54, bf16[256,512]{1,0:T(8,128)(2,1)} %bitcast.56), custom_call_target="tpu_custom_call" | custom-call | tf_op jit(solution)/shard_map/spread_keys_values/pallas_call | solution.py:356
  13.7 10.4 %all-to-all-done = bf16[8,2,2,128,128]{4,3,2,1,0:T(8,128)(2,1)} async-done(((bf16[8,2,2,128,128]{4,3,2,1,0:T(8,128)(2,1)}), bf16[8,2,2,128,128]{4,3,2,1,0:T(8,128)(2,1)}, u32[]{:S(2)}, u32[]{:S(2)}) %all-to-all-start) | async-done | bytes 1048608 | tf_op jit(solution)/shard_map/all_to_all | solution.py:383
  24.1 4.2 %all-to-all-start.2 = ((bf16[8,2,2,128,128]{4,3,2,1,0:T(8,128)(2,1)}), bf16[8,2,2,128,128]{4,3,2,1,0:T(8,128)(2,1)}, u32[]{:S(2)}, u32[]{:S(2)}) async-start(bf16[8,2,2,128,128]{4,3,2,1,0:T(8,128)(2,1)} %spread_keys_values.3), calls=%async_computation.2 | async-start | bytes 2097152 | tf_op jit(solution)/shard_map/all_to_all | solution.py:383
  28.4 6.6 %turn_queries.1 = (bf16[2,4,2,512,128]{4,3,2,1,0:T(8,128)(2,1)}, bf16[2,4,2,128,512]{4,3,2,1,0:T(8,128)(2,1)}) custom-call(s32[1]{0:T(128)} %bitcast.place.refs_0_, bf16[256,2048]{1,0:T(8,128)(2,1)} %bitcast.51, bf16[256,2048]{1,0:T(8,128)(2,1)} %bitcast.52, bf16[2,256,1024]{2,1,0:T(8,128)(2,1)} %collective-permute-done.q_sib.g_sib, ...), custom_call_target="tpu_custom_call" | custom-call | tf_op jit(solution)/shard_map/turn_queries/pallas_call | solution.py:245
  34.9 14.7 %group_attention.2 = (f32[8,128]{1,0:T(8,128)}, bf16[8,512,128]{2,1,0:T(8,128)(2,1)}, bf16[4,128,512]{2,1,0:T(8,128)(2,1)}, bf16[4,1408,512]{2,1,0:T(8,128)(2,1)}) custom-call(s32[1]{0:T(128)} %bitcast.place.refs_0_, s32[64]{0:T(128)} %and_select_fusion.refs_1_.strides, f32[16]{0:T(128)} %refs_2_.3, bf16[2,4,2,512,128]{4,3,2,1,0:T(8,128)(2,1)} %get-tuple-element.38.refs_3_, ...), custom_call_target="tpu_custom_call" | custom-call | flops 3690987520 | bytes 6291456 | tf_op jit(solution)/shard_map/group_attention/pallas_call | solution.py:193
  49.7 4.4 %all-to-all-start.1 = ((bf16[8,512,128]{2,1,0:T(8,128)(2,1)}), bf16[8,512,128]{2,1,0:T(8,128)(2,1)}, u32[]{:S(2)}, u32[]{:S(2)}) async-start(bf16[8,512,128]{2,1,0:T(8,128)(2,1)} %get-tuple-element.40), calls=%async_computation.1 | async-start | bytes 2097152 | tf_op jit(solution)/shard_map/all_to_all | solution.py:404
  54.1 14.7 %group_attention.3 = (f32[8,128]{1,0:T(8,128)}, bf16[8,512,128]{2,1,0:T(8,128)(2,1)}, bf16[4,128,512]{2,1,0:T(8,128)(2,1)}, bf16[4,1408,512]{2,1,0:T(8,128)(2,1)}) custom-call(s32[1]{0:T(128)} %bitcast.place.refs_0_, s32[64]{0:T(128)} %and_select_fusion.refs_1_.strides, f32[16]{0:T(128)} %refs_2_.3, bf16[2,4,2,512,128]{4,3,2,1,0:T(8,128)(2,1)} %get-tuple-element.38.refs_3_, ...), custom_call_target="tpu_custom_call" | custom-call | flops 3690987520 | bytes 6291456 | tf_op jit(solution)/shard_map/group_attention/pallas_call | solution.py:193
  68.8 0.6 all-to-all-done.1
  69.4 4.5 %all-to-all-start.3 = ((bf16[8,512,128]{2,1,0:T(8,128)(2,1)}), bf16[8,512,128]{2,1,0:T(8,128)(2,1)}, u32[]{:S(2)}, u32[]{:S(2)}) async-start(bf16[8,512,128]{2,1,0:T(8,128)(2,1)} %get-tuple-element.65), calls=%async_computation.3 | async-start | bytes 2097152 | tf_op jit(solution)/shard_map/all_to_all | solution.py:406
  73.9 4.1 %collective-permute-start.5 = (f32[8,128]{1,0:T(8,128)S(1)}, f32[8,128]{1,0:T(8,128)S(1)}, u32[]{:S(2)}, u32[]{:S(2)}) collective-permute-start(f32[8,128]{1,0:T(8,128)S(1)} %add.175), channel_id=1, source_target_pairs={{0,3},{1,2},{2,1},{3,0},{4,7},{5,6},{6,5},{7,4},{8,11},{9,10},{10,... | collective-permute-start | bytes 12296 | tf_op jit(solution)/shard_map/ppermute | solution.py:322
  78.0 0.6 collective-permute-start.3
  78.7 2.0 %fusion.1 = (bf16[1,512,128]{2,1,0:T(8,128)(2,1)S(1)}, bf16[1,512,128]{2,1,0:T(8,128)(2,1)S(1)}, bf16[1,512,128]{2,1,0:T(8,128)(2,1)S(1)}, bf16[1,512,128]{2,1,0...) fusion(bf16[8,512,128]{2,1,0:T(8,128)(2,1)} %all-to-all-done.1), kind=kLoop, calls=%fused_computation.26 | loop fusion | bytes 2097152 | tf_op jit(solution)/shard_map/slice | solution.py:424
  80.7 8.7 %finish_rows.1 = (bf16[2,256,1024]{2,1,0:T(8,128)(2,1)}, bf16[2,256,1024]{2,1,0:T(8,128)(2,1)}) custom-call(s32[1]{0:T(128)} %bitcast.place.refs_0_, s32[64]{0:T(128)} %and_select_fusion.refs_1_.strides, bf16[4,1408,512]{2,1,0:T(8,128)(2,1)} %get-tuple-element.56.refs_0_, bf16[16,2,128,128]{3,2,1,0:T(8,128)(2,1)} %bitcast.5.refs_5_.refs_1_, ...), custom_call_target="tpu_custom_call" | custom-call | flops 1048576 | bytes 1048576 | tf_op jit(solution)/shard_map/finish_rows/pallas_call | solution.py:301
  89.4 1.0 add_convert_fusion.3
  90.4 2.7 %collective-permute-start.8 = (f32[8,128]{1,0:T(8,128)S(1)}, f32[8,128]{1,0:T(8,128)S(1)}, u32[]{:S(2)}, u32[]{:S(2)}) collective-permute-start(f32[8,128]{1,0:T(8,128)S(1)} %add_add_fusion.1), channel_id=1, source_target_pairs={{0,24},{4,28},{8,16},{12,20},{16,8},{20,12},{24,0},{28,4},{1,25},{... | collective-permute-start | bytes 12296 | tf_op jit(solution)/shard_map/ppermute | solution.py:322
  93.1 0.5 collective-permute-start.7
  93.6 0.4 collective-permute-start.6
  94.0 0.9 collective-permute-done.8
  95.0 1.7 %collective-permute-done.7 = f32[8,128]{1,0:T(8,128)S(1)} collective-permute-done((f32[8,128]{1,0:T(8,128)S(1)}, f32[8,128]{1,0:T(8,128)S(1)}, u32[]{:S(2)}, u32[]{:S(2)}) %collective-permute-start.7) | collective-permute-done | bytes 4128 | tf_op jit(solution)/shard_map/ppermute | solution.py:322
  96.7 0.5 collective-permute-done.6
  97.2 0.5 multiply_bitcast_fusion
  97.7 1.4 %fusion.2 = (bf16[1,512,128]{2,1,0:T(8,128)(2,1)S(1)}, bf16[1,512,128]{2,1,0:T(8,128)(2,1)S(1)}, bf16[1,512,128]{2,1,0:T(8,128)(2,1)S(1)}, bf16[1,512,128]{2,1,0...) fusion(bf16[8,512,128]{2,1,0:T(8,128)(2,1)} %all-to-all-done.3), kind=kLoop, calls=%fused_computation.27 | loop fusion | bytes 2097152 | tf_op jit(solution)/shard_map/slice | solution.py:424
  99.3 0.7 maximum_bitcast_fusion.3
  100.1 0.7 maximum_bitcast_fusion.2
  100.8 0.1 select_bitcast_fusion.1
  101.0 1.1 %maximum_bitcast_fusion.1 = bf16[1,256,2048]{2,1,0:T(8,128)(2,1)} fusion(bf16[256,1024]{1,0:T(8,128)(2,1)S(1)} %get-tuple-element.69, bf16[256,1024]{1,0:T(8,128)(2,1)S(1)} %get-tuple-element.67), kind=kLoop, calls=%fused_computation.2 | loop fusion | flops 2097152 | bytes 2097152 | tf_op jit(solution)/shard_map/broadcast_in_dim | solution.py:415
  102.0 1.1 %maximum_bitcast_fusion = bf16[1,256,2048]{2,1,0:T(8,128)(2,1)} fusion(bf16[256,1024]{1,0:T(8,128)(2,1)S(1)} %get-tuple-element.68, bf16[256,1024]{1,0:T(8,128)(2,1)S(1)} %get-tuple-element.70), kind=kLoop, calls=%fused_computation.1 | loop fusion | flops 2097152 | bytes 2097152 | tf_op jit(solution)/shard_map/broadcast_in_dim | solution.py:415
  (31 shorter events, 0.6 us)
Async XLA Ops:
  0.6 8.0 %slice-start = ((s32[4,16,13]{1,0,2:T(4,128)}), s32[4,16,1]{1,0,2:T(4,128)S(1)}, s32[]{:S(2)}) async-start(s32[4,16,13]{1,0,2:T(4,128)} %param.11), calls=%async_computation.4 | async-start | bytes 4096 | tf_op jit(solution)/shard_map/slice | solution.py:390
  3.3 5.5 %copy-start = (bf16[1,256,2048]{2,1,0:T(8,128)(2,1)S(1)}, bf16[1,256,2048]{2,1,0:T(8,128)(2,1)}, u32[]{:S(2)}) copy-start(bf16[1,256,2048]{2,1,0:T(8,128)(2,1)} %param.6) | copy-start | bytes 3145732
  3.3 5.5 %copy-start.1 = (bf16[1,256,2048]{2,1,0:T(8,128)(2,1)S(1)}, bf16[1,256,2048]{2,1,0:T(8,128)(2,1)}, u32[]{:S(2)}) copy-start(bf16[1,256,2048]{2,1,0:T(8,128)(2,1)} %param.10) | copy-start | bytes 3145732
  3.3 20.8 %all-to-all-start = ((bf16[8,2,2,128,128]{4,3,2,1,0:T(8,128)(2,1)}), bf16[8,2,2,128,128]{4,3,2,1,0:T(8,128)(2,1)}, u32[]{:S(2)}, u32[]{:S(2)}) async-start(bf16[8,2,2,128,128]{4,3,2,1,0:T(8,128)(2,1)} %spread_keys_values.2), calls=%async_computation | async-start | bytes 2097152 | tf_op jit(solution)/shard_map/all_to_all | solution.py:383
  10.5 17.8 %collective-permute-start = (bf16[2,256,1024]{2,1,0:T(8,128)(2,1)}, bf16[2,256,1024]{2,1,0:T(8,128)(2,1)}, u32[]{:S(2)}, u32[]{:S(2)}) collective-permute-start(bf16[2,256,1024]{2,1,0:T(8,128)(2,1)} %pad_maximum_fusion), channel_id=1, source_target_pairs={{0,4},{4,0},{8,12},{12,8},{16,20},{20,16},{24,28},{28,24},{1,5},{5... | collective-permute-start | bytes 3145736 | tf_op jit(solution)/shard_map/ppermute | solution.py:392
  24.1 25.6 %all-to-all-start.2 = ((bf16[8,2,2,128,128]{4,3,2,1,0:T(8,128)(2,1)}), bf16[8,2,2,128,128]{4,3,2,1,0:T(8,128)(2,1)}, u32[]{:S(2)}, u32[]{:S(2)}) async-start(bf16[8,2,2,128,128]{4,3,2,1,0:T(8,128)(2,1)} %spread_keys_values.3), calls=%async_computation.2 | async-start | bytes 2097152 | tf_op jit(solution)/shard_map/all_to_all | solution.py:383
  49.7 19.7 %all-to-all-start.1 = ((bf16[8,512,128]{2,1,0:T(8,128)(2,1)}), bf16[8,512,128]{2,1,0:T(8,128)(2,1)}, u32[]{:S(2)}, u32[]{:S(2)}) async-start(bf16[8,512,128]{2,1,0:T(8,128)(2,1)} %get-tuple-element.40), calls=%async_computation.1 | async-start | bytes 2097152 | tf_op jit(solution)/shard_map/all_to_all | solution.py:404
  68.8 5.1 %copy-start.3 = (f32[8,128]{1,0:T(8,128)S(1)}, f32[8,128]{1,0:T(8,128)}, u32[]{:S(2)}) copy-start(f32[8,128]{1,0:T(8,128)} %get-tuple-element.48) | copy-start | bytes 12292
  69.4 4.5 %collective-permute-start.1 = (f32[8,128]{1,0:T(8,128)}, f32[8,128]{1,0:T(8,128)S(1)}, u32[]{:S(2)}, u32[]{:S(2)}) collective-permute-start(f32[8,128]{1,0:T(8,128)} %get-tuple-element.48), channel_id=1, source_target_pairs={{0,4},{4,0},{8,12},{12,8},{16,20},{20,16},{24,28},{28,24},{1,5},{5... | collective-permute-start | bytes 12296 | tf_op jit(solution)/shard_map/ppermute | solution.py:339
  69.4 28.3 %all-to-all-start.3 = ((bf16[8,512,128]{2,1,0:T(8,128)(2,1)}), bf16[8,512,128]{2,1,0:T(8,128)(2,1)}, u32[]{:S(2)}, u32[]{:S(2)}) async-start(bf16[8,512,128]{2,1,0:T(8,128)(2,1)} %get-tuple-element.65), calls=%async_computation.3 | async-start | bytes 2097152 | tf_op jit(solution)/shard_map/all_to_all | solution.py:406
  73.9 16.4 %collective-permute-start.5 = (f32[8,128]{1,0:T(8,128)S(1)}, f32[8,128]{1,0:T(8,128)S(1)}, u32[]{:S(2)}, u32[]{:S(2)}) collective-permute-start(f32[8,128]{1,0:T(8,128)S(1)} %add.175), channel_id=1, source_target_pairs={{0,3},{1,2},{2,1},{3,0},{4,7},{5,6},{6,5},{7,4},{8,11},{9,10},{10,... | collective-permute-start | bytes 12296 | tf_op jit(solution)/shard_map/ppermute | solution.py:322
  78.0 12.3 %collective-permute-start.4 = (f32[8,128]{1,0:T(8,128)S(1)}, f32[8,128]{1,0:T(8,128)S(1)}, u32[]{:S(2)}, u32[]{:S(2)}) collective-permute-start(f32[8,128]{1,0:T(8,128)S(1)} %add.175), channel_id=1, source_target_pairs={{0,2},{1,3},{2,0},{3,1},{4,6},{5,7},{6,4},{7,5},{8,10},{9,11},{10,... | collective-permute-start | bytes 12296 | tf_op jit(solution)/shard_map/ppermute | solution.py:322
  78.0 12.3 %collective-permute-start.3 = (f32[8,128]{1,0:T(8,128)S(1)}, f32[8,128]{1,0:T(8,128)S(1)}, u32[]{:S(2)}, u32[]{:S(2)}) collective-permute-start(f32[8,128]{1,0:T(8,128)S(1)} %add.175), channel_id=1, source_target_pairs={{0,1},{1,0},{2,3},{3,2},{4,5},{5,4},{6,7},{7,6},{8,9},{9,8},{10,11... | collective-permute-start | bytes 12296 | tf_op jit(solution)/shard_map/ppermute | solution.py:322
  89.4 11.4 %collective-permute-start.2 = (bf16[2,256,1024]{2,1,0:T(8,128)(2,1)}, bf16[2,256,1024]{2,1,0:T(8,128)(2,1)S(1)}, u32[]{:S(2)}, u32[]{:S(2)}) collective-permute-start(bf16[2,256,1024]{2,1,0:T(8,128)(2,1)} %get-tuple-element.63), channel_id=1, source_target_pairs={{0,4},{4,0},{8,12},{12,8},{16,20},{20,16},{24,28},{28,24},{1,5},{5... | collective-permute-start | bytes 3145736 | tf_op jit(solution)/shard_map/ppermute | solution.py:410
  90.4 4.6 %collective-permute-start.8 = (f32[8,128]{1,0:T(8,128)S(1)}, f32[8,128]{1,0:T(8,128)S(1)}, u32[]{:S(2)}, u32[]{:S(2)}) collective-permute-start(f32[8,128]{1,0:T(8,128)S(1)} %add_add_fusion.1), channel_id=1, source_target_pairs={{0,24},{4,28},{8,16},{12,20},{16,8},{20,12},{24,0},{28,4},{1,25},{... | collective-permute-start | bytes 12296 | tf_op jit(solution)/shard_map/ppermute | solution.py:322
  93.1 3.6 %collective-permute-start.7 = (f32[8,128]{1,0:T(8,128)S(1)}, f32[8,128]{1,0:T(8,128)S(1)}, u32[]{:S(2)}, u32[]{:S(2)}) collective-permute-start(f32[8,128]{1,0:T(8,128)S(1)} %add_add_fusion.1), channel_id=1, source_target_pairs={{0,16},{4,20},{8,24},{12,28},{16,0},{20,4},{24,8},{28,12},{1,17},{... | collective-permute-start | bytes 12296 | tf_op jit(solution)/shard_map/ppermute | solution.py:322
  93.6 3.6 %collective-permute-start.6 = (f32[8,128]{1,0:T(8,128)S(1)}, f32[8,128]{1,0:T(8,128)S(1)}, u32[]{:S(2)}, u32[]{:S(2)}) collective-permute-start(f32[8,128]{1,0:T(8,128)S(1)} %add_add_fusion.1), channel_id=1, source_target_pairs={{0,8},{4,12},{8,0},{12,4},{16,24},{20,28},{24,16},{28,20},{1,9},{5... | collective-permute-start | bytes 12296 | tf_op jit(solution)/shard_map/ppermute | solution.py:322
  97.7 3.1 %copy-start.2 = (bf16[2,256,1024]{2,1,0:T(8,128)(2,1)S(1)}, bf16[2,256,1024]{2,1,0:T(8,128)(2,1)}, u32[]{:S(2)}) copy-start(bf16[2,256,1024]{2,1,0:T(8,128)(2,1)} %get-tuple-element.62) | copy-start | bytes 3145732

commit v9 on v7

--- a/solution.py
+++ b/solution.py
@@ -13,7 +13,7 @@
 HD = 128
 BLOCK = 128
 QPG = HEADS // KV_HEADS
-CHUNK = 4
+CHUNK = 2
 ROWS = QPG * BLOCK
 TAIL = 8
 VMEM_BYTES = 63 * 2**20
@@ -44,7 +44,7 @@
     inputs, rest = refs[3 : 8 + gi], refs[8 + gi :]
     q_own, q_sib, g_own, g_sib, kv_in = inputs[:5]
     att_own, dq_own, sib_out, tau_out, kv_out = rest[:5]
-    kt_s, vt_s, dk_s, dv_s, s_s, e_s = rest[5:]
+    kt_s, vt_s, dk_s, dv_s, s_s, e_s, qt_s, gt_s = rest[5:]
     blocks = devices * local_blocks
     me = place[0]
     group = 2 * (me % 2) + gi
@@ -92,15 +92,17 @@
             for n, j in enumerate(c):
                 ref[ids[j]] += x[n * BLOCK : (n + 1) * BLOCK, :]
 
-        q_here = q_sib[0, here, :] if side else q_own[here, :]
-        g_here = g_sib[0, here, :] if side else g_own[here, :]
-        q_rows = jnp.concatenate(per_head(q_here), axis=0)
-        g_rows = jnp.concatenate(per_head(g_here), axis=0)
-        q_t = jnp.concatenate([x.T for x in per_head(q_here)], axis=1)
-        g_t = jnp.concatenate([x.T for x in per_head(g_here)], axis=1)
+
+        def rows_of_heads(own, sib):
+            return jnp.concatenate(per_head(sib[0, here, :] if side else own[here, :]), axis=0)
+
+        for own, sib, ref in ((q_own, q_sib, qt_s), (g_own, g_sib, gt_s)):
+            heads = per_head(sib[0, here, :] if side else own[here, :])
+            for h, x in enumerate(heads):
+                ref[n, :, h * BLOCK : (h + 1) * BLOCK] = x.T
         most = None
         for c in chunks:
-            raw = nt(taken(0, c), q_t)
+            raw = nt(taken(0, c), qt_s[n])
             s_n[rows_of(c), :] = raw
             top = jnp.max(in_rows(raw), axis=0)
             most = top if most is None else jnp.maximum(most, top)
@@ -119,20 +121,20 @@
         for c in chunks:
             probs = (e_n[rows_of(c), :] * inverse).astype(jnp.bfloat16)
             o_t = o_t + nt(picked(vt_s, c, 1), probs)
-            add_blocks(dv_s, c, nt(probs, g_rows))
-            yield
-        row_dot = jnp.sum(g_t.astype(jnp.float32) * o_t, axis=0, keepdims=True)
+            add_blocks(dv_s, c, nt(probs, rows_of_heads(g_own, g_sib)))
+            yield
+        row_dot = jnp.sum(gt_s[n].astype(jnp.float32) * o_t, axis=0, keepdims=True)
         write(side, here, 0, o_t)
         weight_scale = inverse * scale
         tau_rows = jnp.zeros((8, ROWS), jnp.float32)
         dq_t = jnp.zeros((HD, ROWS), jnp.float32)
         for c in chunks:
-            dweights = nt(taken(1, c), g_t)
+            dweights = nt(taken(1, c), gt_s[n])
             scaled = e_n[rows_of(c), :] * weight_scale * (dweights - row_dot)
             tau_rows = tau_rows + jnp.sum(in_rows(scaled * s_n[rows_of(c), :]), axis=0)
             low = scaled.astype(jnp.bfloat16)
             dq_t = dq_t + nt(picked(kt_s, c, 1), low)
-            add_blocks(dk_s, c, nt(low, q_rows))
+            add_blocks(dk_s, c, nt(low, rows_of_heads(q_own, q_sib)))
             yield
         tau_totals.append(tau_rows)
         write(side, here, 1, dq_t)
@@ -192,14 +194,14 @@
     local_blocks = tokens // BLOCK
     blocks = devices * local_blocks
     width = QPG * HD
-    block_own = pl.BlockSpec((tokens, width), lambda u, p, s, t: (0, 2 * (p[0] % 2) + gi))
-    qs = pl.BlockSpec((1, tokens, width), lambda u, p, s, t: (0, 0, gi))
-    gs = pl.BlockSpec((1, tokens, width), lambda u, p, s, t: (1, 0, gi))
-    out_own = pl.BlockSpec((tokens, width), lambda u, p, s, t: (0, 0))
-    out_sib = pl.BlockSpec((2, tokens, width), lambda u, p, s, t: (0, 0, 0))
-    kv_all = pl.BlockSpec((blocks, 2, BLOCK, HD), lambda u, p, s, t: (0, 0, 0, 0))
-    kv_back = pl.BlockSpec((devices, 2 * tokens, HD), lambda u, p, s, t: (0, 0, 0))
-    small = pl.BlockSpec((TAIL, HD), lambda u, p, s, t: (0, 0))
+    block_own = pl.BlockSpec((tokens, width), lambda u, p, s, t: (0, 2 * (p[0] % 2) + gi), pipeline_mode=pl.Buffered(1))
+    qs = pl.BlockSpec((1, tokens, width), lambda u, p, s, t: (0, 0, gi), pipeline_mode=pl.Buffered(1))
+    gs = pl.BlockSpec((1, tokens, width), lambda u, p, s, t: (1, 0, gi), pipeline_mode=pl.Buffered(1))
+    out_own = pl.BlockSpec((tokens, width), lambda u, p, s, t: (0, 0), pipeline_mode=pl.Buffered(1))
+    out_sib = pl.BlockSpec((2, tokens, width), lambda u, p, s, t: (0, 0, 0), pipeline_mode=pl.Buffered(1))
+    kv_all = pl.BlockSpec((blocks, 2, BLOCK, HD), lambda u, p, s, t: (0, 0, 0, 0), pipeline_mode=pl.Buffered(1))
+    kv_back = pl.BlockSpec((devices, 2 * tokens, HD), lambda u, p, s, t: (0, 0, 0), pipeline_mode=pl.Buffered(1))
+    small = pl.BlockSpec((TAIL, HD), lambda u, p, s, t: (0, 0), pipeline_mode=pl.Buffered(1))
     bf = lambda *shape: jax.ShapeDtypeStruct(shape, jnp.bfloat16)
     keys_wide = listed * BLOCK
     cells = 2 * local_blocks * ROWS * keys_wide
@@ -212,7 +214,8 @@
             out_specs=[out_own, out_own, out_sib, small, kv_back],
             scratch_shapes=[pltpu.VMEM((blocks, HD, BLOCK), jnp.bfloat16)] * 2
             + [pltpu.VMEM((blocks, BLOCK, HD), jnp.float32)] * 2
-            + [pltpu.VMEM((2 * local_blocks, keys_wide, ROWS), jnp.float32)] * 2,
+            + [pltpu.VMEM((2 * local_blocks, keys_wide, ROWS), jnp.float32)] * 2
+            + [pltpu.VMEM((2 * local_blocks, HD, ROWS), jnp.bfloat16)] * 2,
         ),
         out_shape=[bf(tokens, width), bf(tokens, width), bf(2, tokens, width)]
         + [jax.ShapeDtypeStruct((TAIL, HD), jnp.float32), bf(devices, 2 * tokens, HD)],
@@ -226,22 +229,22 @@
     )(place, strides, tau, queries, qg_sib, out_grad, qg_sib, kv_in, *tau_in[:gi])
 
 
-def total_over(x, axis):
+def partners(x, axis, distances):
     size = lax.axis_size(axis)
-    if size & (size - 1):
-        return lax.psum(x, axis)
-
-    def partner(distance):
-        return lax.ppermute(x, axis, [(i, i ^ distance) for i in range(size)])
-
-    step = 1
-    while step < size:
-        if size // step % 4 == 0 and size // step != 8:
-            x = (x + partner(step)) + (partner(2 * step) + partner(3 * step))
-            step *= 4
-        else:
-            x = x + partner(step)
-            step *= 2
+    a, b, c = (lax.ppermute(x, axis, [(i, i ^ d) for i in range(size)]) for d in distances)
+    return (x + a) + (b + c)
+
+
+def total_everywhere(x):
+    ctx, batch = lax.axis_size("ctx"), lax.axis_size("batch")
+    if batch != 4 or ctx not in (8, 32):
+        return lax.psum(x, ("ctx", "batch"))
+    x = x + lax.ppermute(x, "ctx", [(i, i ^ 1) for i in range(ctx)])
+    x = partners(x, "batch", (1, 2, 3))
+    step = 2
+    while step < ctx:
+        x = partners(x, "ctx", (step, 2 * step, 3 * step))
+        step *= 4
     return x
 
 
@@ -310,7 +313,9 @@
             grads[0] = lax.all_to_all(kv_grads, "ctx", 0, 0)
     grads, sibs, tau_last = lax.optimization_barrier((grads, sibs, tau_rows[1]))
     grads[1] = lax.all_to_all(grads[1], "ctx", 0, 0)
-    sibs = lax.optimization_barrier([lax.ppermute(sib, "ctx", swap) for sib in sibs])
+    sibs, grads[0] = lax.optimization_barrier(
+        ([lax.ppermute(sib, "ctx", swap) for sib in sibs], grads[0])
+    )
     att_parts, dq_parts = (
         [(own[which], sib[which]) for own, sib in zip(owns, sibs)] for which in range(2)
     )
@@ -335,7 +340,7 @@
         return jnp.concatenate(cols, axis=1)[None]
 
     key_grad, value_grad = summed(0), summed(1)
-    scale_total = total_over(total_over(tau_last[:1], "ctx"), "batch")[0, :HEADS]
+    scale_total = total_everywhere(tau_last)[0, :HEADS]
     tau_grad = scale_total / math.sqrt(lax.axis_size("batch") * ctx * tokens)
     return (attended, query_grad, key_grad, value_grad, tau_grad)
 

time: 101 us -> 104 us (1.030)
  Pallas kernels: 35.6 us -> 38.9 us
    all_to_all x1, waiting for transfers between devices: 0.01 us -> 9.76 us  [body(): grads[1] = lax.all_to_all(grads[1], 'ctx', 0, 0)]
    ppermute x7, waiting for transfers between devices: 15.8 us -> 6.21 us  [the longest x6 5.18 us: partners(): lax.ppermute(x, axis, [(i, i ^ d) for i in range(size)])]
    pallas_call x2, Pallas kernels: 30.4 us -> 33.6 us  [run_group(): pl.pallas_call(functools.partial(group_kernel, gi, devices, local_blocks,...]
  transfers between devices with their start and end apart: 14 -> 14, of which waited for: 6 -> 6; matrix products, arithmetic and copies ran while one was open for 7% -> 6% of each run, Pallas kernels for 33% -> 35%
where the time goes in v9:
time: 104 us; the launch traced here: 103 us
  Pallas kernels  38.9 us (37%)
  starting transfers between devices  27.3 us (26%)
  waiting for transfers between devices  25.9 us (25%)
  other arithmetic  6.97 us (7%)
  local copies, waits for them, and re-layouts  3.18 us (3%)
    pallas_call x2, Pallas kernels, run_group(): pl.pallas_call(functools.partial(group_kernel, gi, devices, local_blocks,...  33.6 us
    all_to_all x2, waiting for transfers between devices, kv_for(): arrived = lax.all_to_all(spread(gi, ctx, k0, v0), 'ctx', 0, 0)  9.87 us
    all_to_all x1, waiting for transfers between devices, body(): grads[1] = lax.all_to_all(grads[1], 'ctx', 0, 0)  9.76 us
    all_to_all x2, starting transfers between devices, kv_for(): arrived = lax.all_to_all(spread(gi, ctx, k0, v0), 'ctx', 0, 0)  9.55 us
    ppermute x6, starting transfers between devices, partners(): lax.ppermute(x, axis, [(i, i ^ d) for i in range(size)])  8.09 us
    pallas_call x2, Pallas kernels, spread(): pl.pallas_call(kernel, grid=(devices // 2,), in_specs=[taken, taken], out...  5.25 us
    ppermute x6, waiting for transfers between devices, partners(): lax.ppermute(x, axis, [(i, i ^ d) for i in range(size)])  5.18 us
    all_to_all x1, starting transfers between devices, body(): grads[0] = lax.all_to_all(kv_grads, 'ctx', 0, 0)  4.24 us
  transfers between devices with their start and end apart: 14, of which 6 were waited for; matrix products, arithmetic and copies ran while one was open for 6% of the time, Pallas kernels for 35%

profile of v9, /device:TPU:0, one launch (start us, length us, event | category | flops | bytes accessed | tf_op | source)
XLA Modules:
  0.0 103.0 jit_solution(13018353853830255677)
XLA Ops:
  0.6 2.6 %spread_keys_values.2 = bf16[8,2,2,128,128]{4,3,2,1,0:T(8,128)(2,1)} custom-call(bf16[256,512]{1,0:T(8,128)(2,1)} %bitcast.55, bf16[256,512]{1,0:T(8,128)(2,1)} %bitcast.57), custom_call_target="tpu_custom_call" | custom-call | tf_op jit(solution)/shard_map/spread_keys_values/pallas_call | solution.py:265
  3.3 5.3 %all-to-all-start = ((bf16[8,2,2,128,128]{4,3,2,1,0:T(8,128)(2,1)}), bf16[8,2,2,128,128]{4,3,2,1,0:T(8,128)(2,1)}, u32[]{:S(2)}, u32[]{:S(2)}) async-start(bf16[8,2,2,128,128]{4,3,2,1,0:T(8,128)(2,1)} %spread_keys_values.2), calls=%async_computation | async-start | bytes 2097152 | tf_op jit(solution)/shard_map/all_to_all | solution.py:292
  8.7 0.6 slice-done
  9.5 1.1 %pad_maximum_fusion = bf16[2,256,1024]{2,1,0:T(8,128)(2,1)} fusion(bf16[1,256,1024]{2,1,0:T(8,128)(2,1)S(1)} %get-tuple-element.81, bf16[1,256,1024]{2,1,0:T(8,128)(2,1)S(1)} %get-tuple-element.82), kind=kLoop, calls=%fused_computation | loop fusion | flops 524288 | bytes 2097152 | tf_op jit(solution)/shard_map/stack | solution.py:300
  10.5 0.6 and_select_fusion.refs_1_
  11.1 0.5 collective-permute-start
  11.6 2.6 %spread_keys_values.3 = bf16[8,2,2,128,128]{4,3,2,1,0:T(8,128)(2,1)} custom-call(bf16[256,512]{1,0:T(8,128)(2,1)} %bitcast.56, bf16[256,512]{1,0:T(8,128)(2,1)} %bitcast.58), custom_call_target="tpu_custom_call" | custom-call | tf_op jit(solution)/shard_map/spread_keys_values/pallas_call | solution.py:265
  14.2 9.9 %all-to-all-done = bf16[8,2,2,128,128]{4,3,2,1,0:T(8,128)(2,1)} async-done(((bf16[8,2,2,128,128]{4,3,2,1,0:T(8,128)(2,1)}), bf16[8,2,2,128,128]{4,3,2,1,0:T(8,128)(2,1)}, u32[]{:S(2)}, u32[]{:S(2)}) %all-to-all-start) | async-done | bytes 1048608 | tf_op jit(solution)/shard_map/all_to_all | solution.py:292
  24.1 4.2 %all-to-all-start.2 = ((bf16[8,2,2,128,128]{4,3,2,1,0:T(8,128)(2,1)}), bf16[8,2,2,128,128]{4,3,2,1,0:T(8,128)(2,1)}, u32[]{:S(2)}, u32[]{:S(2)}) async-start(bf16[8,2,2,128,128]{4,3,2,1,0:T(8,128)(2,1)} %spread_keys_values.3), calls=%async_computation.2 | async-start | bytes 2097152 | tf_op jit(solution)/shard_map/all_to_all | solution.py:292
  28.4 16.8 %group_attention.2 = (bf16[256,512]{1,0:T(8,128)(2,1)}, bf16[256,512]{1,0:T(8,128)(2,1)}, bf16[2,256,512]{2,1,0:T(8,128)(2,1)}, f32[8,128]{1,0:T(8,128)}, bf16[8,512,128]{2,1,0:T(8,128)(2,1)}) custom-call(s32[1]{0:T(128)} %bitcast.refs_0_, s32[64]{0:T(128)} %and_select_fusion.refs_1_, f32[16]{0:T(128)} %refs_2_.3, bf16[256,2048]{1,0:T(8,128)(2,1)} %bitcast.75, ...), custom_call_target="tpu_custom_call" | custom-call | flops 4429185024 | bytes 6291456 | tf_op jit(solution)/shard_map/group_attention/pallas_call | solution.py:208
  45.2 4.2 %all-to-all-start.1 = ((bf16[8,512,128]{2,1,0:T(8,128)(2,1)}), bf16[8,512,128]{2,1,0:T(8,128)(2,1)}, u32[]{:S(2)}, u32[]{:S(2)}) async-start(bf16[8,512,128]{2,1,0:T(8,128)(2,1)} %get-tuple-element.28), calls=%async_computation.1 | async-start | bytes 2097152 | tf_op jit(solution)/shard_map/all_to_all | solution.py:313
  49.4 16.8 %group_attention.3 = (bf16[256,512]{1,0:T(8,128)(2,1)}, bf16[256,512]{1,0:T(8,128)(2,1)}, bf16[2,256,512]{2,1,0:T(8,128)(2,1)}, f32[8,128]{1,0:T(8,128)}, bf16[8,512,128]{2,1,0:T(8,128)(2,1)}) custom-call(s32[1]{0:T(128)} %bitcast.refs_0_, s32[64]{0:T(128)} %and_select_fusion.refs_1_, f32[16]{0:T(128)} %refs_2_.3, bf16[256,2048]{1,0:T(8,128)(2,1)} %bitcast.76, ...), custom_call_target="tpu_custom_call" | custom-call | flops 4429185024 | bytes 6291456 | tf_op jit(solution)/shard_map/group_attention/pallas_call | solution.py:208
  66.2 0.4 collective-permute-start.3
  66.6 1.0 %collective-permute-done.3 = f32[8,128]{1,0:T(8,128)S(1)} collective-permute-done((f32[8,128]{1,0:T(8,128)}, f32[8,128]{1,0:T(8,128)S(1)}, u32[]{:S(2)}, u32[]{:S(2)}) %collective-permute-start.3) | collective-permute-done | bytes 4128 | tf_op jit(solution)/shard_map/ppermute | solution.py:242
  67.6 0.7 add.207
  68.3 2.0 %collective-permute-start.4 = (f32[8,128]{1,0:T(8,128)S(1)}, f32[8,128]{1,0:T(8,128)S(1)}, u32[]{:S(2)}, u32[]{:S(2)}) collective-permute-start(f32[8,128]{1,0:T(8,128)S(1)} %add.207), channel_id=1, source_target_pairs={{0,1},{1,0},{2,3},{3,2},{4,5},{5,4},{6,7},{7,6},{8,9},{9,8},{10,11... | collective-permute-start | bytes 12296 | tf_op jit(solution)/shard_map/ppermute | solution.py:234
  70.3 2.6 %collective-permute-start.5 = (f32[8,128]{1,0:T(8,128)S(1)}, f32[8,128]{1,0:T(8,128)S(1)}, u32[]{:S(2)}, u32[]{:S(2)}) collective-permute-start(f32[8,128]{1,0:T(8,128)S(1)} %add.207), channel_id=1, source_target_pairs={{0,2},{1,3},{2,0},{3,1},{4,6},{5,7},{6,4},{7,5},{8,10},{9,11},{10,... | collective-permute-start | bytes 12296 | tf_op jit(solution)/shard_map/ppermute | solution.py:234
  72.9 0.5 collective-permute-start.2
  73.4 1.4 %collective-permute-done.5 = f32[8,128]{1,0:T(8,128)S(1)} collective-permute-done((f32[8,128]{1,0:T(8,128)S(1)}, f32[8,128]{1,0:T(8,128)S(1)}, u32[]{:S(2)}, u32[]{:S(2)}) %collective-permute-start.5) | collective-permute-done | bytes 4128 | tf_op jit(solution)/shard_map/ppermute | solution.py:234
  74.8 3.5 %collective-permute-done.6 = f32[8,128]{1,0:T(8,128)S(1)} collective-permute-done((f32[8,128]{1,0:T(8,128)S(1)}, f32[8,128]{1,0:T(8,128)S(1)}, u32[]{:S(2)}, u32[]{:S(2)}) %collective-permute-start.6) | collective-permute-done | bytes 4128 | tf_op jit(solution)/shard_map/ppermute | solution.py:234
  78.3 1.9 %collective-permute-start.7 = (f32[8,128]{1,0:T(8,128)S(1)}, f32[8,128]{1,0:T(8,128)S(1)}, u32[]{:S(2)}, u32[]{:S(2)}) collective-permute-start(f32[8,128]{1,0:T(8,128)S(1)} %add_add_fusion.1), channel_id=1, source_target_pairs={{0,8},{4,12},{8,0},{12,4},{16,24},{20,28},{24,16},{28,20},{1,9},{5... | collective-permute-start | bytes 12296 | tf_op jit(solution)/shard_map/ppermute | solution.py:234
  80.2 1.5 %collective-permute-start.8 = (f32[8,128]{1,0:T(8,128)S(1)}, f32[8,128]{1,0:T(8,128)S(1)}, u32[]{:S(2)}, u32[]{:S(2)}) collective-permute-start(f32[8,128]{1,0:T(8,128)S(1)} %add_add_fusion.1), channel_id=1, source_target_pairs={{0,16},{4,20},{8,24},{12,28},{16,0},{20,4},{24,8},{28,12},{1,17},{... | collective-permute-start | bytes 12296 | tf_op jit(solution)/shard_map/ppermute | solution.py:234
  81.8 4.1 %all-to-all-start.3 = ((bf16[8,512,128]{2,1,0:T(8,128)(2,1)}), bf16[8,512,128]{2,1,0:T(8,128)(2,1)S(1)}, u32[]{:S(2)}, u32[]{:S(2)}) async-start(bf16[8,512,128]{2,1,0:T(8,128)(2,1)} %get-tuple-element.43), calls=%async_computation.3 | async-start | bytes 2097152 | tf_op jit(solution)/shard_map/all_to_all | solution.py:315
  85.9 0.3 collective-permute-done.9
  86.2 0.5 multiply_bitcast_fusion
  86.7 1.4 %fusion.1 = (bf16[1,512,128]{2,1,0:T(8,128)(2,1)S(1)}, bf16[1,512,128]{2,1,0:T(8,128)(2,1)S(1)}, bf16[1,512,128]{2,1,0:T(8,128)(2,1)S(1)}, bf16[1,512,128]{2,1,0...) fusion(bf16[8,512,128]{2,1,0:T(8,128)(2,1)} %all-to-all-done.1), kind=kLoop, calls=%fused_computation.30 | loop fusion | bytes 2097152 | tf_op jit(solution)/shard_map/slice | solution.py:336
  88.4 0.8 copy-done.2
  89.3 1.1 %maximum_bitcast_fusion.1 = bf16[1,256,2048]{2,1,0:T(8,128)(2,1)} fusion(bf16[256,512]{1,0:T(8,128)(2,1)S(1)} %get-tuple-element.64, bf16[256,512]{1,0:T(8,128)(2,1)S(1)} %get-tuple-element.62, bf16[256,512]{1,0:T(8,128)(2,1)S(1)} %get-tuple-element.63, bf16[256,512]{1,0:T(8,128)(2,1)S(1)} %get-tuple-element.61), kind=kLoop, calls=%fused_computation.2 | loop fusion | flops 4194304 | bytes 2097152 | tf_op jit(solution)/shard_map/broadcast_in_dim | solution.py:329
  90.4 1.1 %maximum_bitcast_fusion = bf16[1,256,2048]{2,1,0:T(8,128)(2,1)} fusion(bf16[256,512]{1,0:T(8,128)(2,1)S(1)} %get-tuple-element.79, bf16[256,512]{1,0:T(8,128)(2,1)S(1)} %get-tuple-element.77, bf16[256,512]{1,0:T(8,128)(2,1)S(1)} %get-tuple-element.80, bf16[256,512]{1,0:T(8,128)(2,1)S(1)} %get-tuple-element.78), kind=kLoop, calls=%fused_computation.1 | loop fusion | flops 4194304 | bytes 2097152 | tf_op jit(solution)/shard_map/broadcast_in_dim | solution.py:328
  91.5 9.8 %all-to-all-done.3 = bf16[8,512,128]{2,1,0:T(8,128)(2,1)S(1)} async-done(((bf16[8,512,128]{2,1,0:T(8,128)(2,1)}), bf16[8,512,128]{2,1,0:T(8,128)(2,1)S(1)}, u32[]{:S(2)}, u32[]{:S(2)}) %all-to-all-start.3) | async-done | bytes 1048608 | tf_op jit(solution)/shard_map/all_to_all | solution.py:315
  101.5 0.7 maximum_bitcast_fusion.3
  102.3 0.7 maximum_bitcast_fusion.2
  (38 shorter events, 1.1 us)
Async XLA Ops:
  3.3 5.3 %copy-start = (bf16[1,256,2048]{2,1,0:T(8,128)(2,1)S(1)}, bf16[1,256,2048]{2,1,0:T(8,128)(2,1)}, u32[]{:S(2)}) copy-start(bf16[1,256,2048]{2,1,0:T(8,128)(2,1)} %param.6) | copy-start | bytes 3145732
  3.3 5.3 %copy-start.1 = (bf16[1,256,2048]{2,1,0:T(8,128)(2,1)S(1)}, bf16[1,256,2048]{2,1,0:T(8,128)(2,1)}, u32[]{:S(2)}) copy-start(bf16[1,256,2048]{2,1,0:T(8,128)(2,1)} %param.10) | copy-start | bytes 3145732
  3.3 20.8 %all-to-all-start = ((bf16[8,2,2,128,128]{4,3,2,1,0:T(8,128)(2,1)}), bf16[8,2,2,128,128]{4,3,2,1,0:T(8,128)(2,1)}, u32[]{:S(2)}, u32[]{:S(2)}) async-start(bf16[8,2,2,128,128]{4,3,2,1,0:T(8,128)(2,1)} %spread_keys_values.2), calls=%async_computation | async-start | bytes 2097152 | tf_op jit(solution)/shard_map/all_to_all | solution.py:292
  8.6 0.7 slice-start
  11.1 17.2 %collective-permute-start = (bf16[2,256,1024]{2,1,0:T(8,128)(2,1)}, bf16[2,256,1024]{2,1,0:T(8,128)(2,1)}, u32[]{:S(2)}, u32[]{:S(2)}) collective-permute-start(bf16[2,256,1024]{2,1,0:T(8,128)(2,1)} %pad_maximum_fusion), channel_id=1, source_target_pairs={{0,4},{4,0},{8,12},{12,8},{16,20},{20,16},{24,28},{28,24},{1,5},{5... | collective-permute-start | bytes 3145736 | tf_op jit(solution)/shard_map/ppermute | solution.py:301
  24.1 21.1 %all-to-all-start.2 = ((bf16[8,2,2,128,128]{4,3,2,1,0:T(8,128)(2,1)}), bf16[8,2,2,128,128]{4,3,2,1,0:T(8,128)(2,1)}, u32[]{:S(2)}, u32[]{:S(2)}) async-start(bf16[8,2,2,128,128]{4,3,2,1,0:T(8,128)(2,1)} %spread_keys_values.3), calls=%async_computation.2 | async-start | bytes 2097152 | tf_op jit(solution)/shard_map/all_to_all | solution.py:292
  45.2 21.1 %all-to-all-start.1 = ((bf16[8,512,128]{2,1,0:T(8,128)(2,1)}), bf16[8,512,128]{2,1,0:T(8,128)(2,1)}, u32[]{:S(2)}, u32[]{:S(2)}) async-start(bf16[8,512,128]{2,1,0:T(8,128)(2,1)} %get-tuple-element.28), calls=%async_computation.1 | async-start | bytes 2097152 | tf_op jit(solution)/shard_map/all_to_all | solution.py:313
  49.4 23.5 %copy-start.6 = (bf16[2,256,512]{2,1,0:T(8,128)(2,1)S(1)}, bf16[2,256,512]{2,1,0:T(8,128)(2,1)}, u32[]{:S(2)}) copy-start(bf16[2,256,512]{2,1,0:T(8,128)(2,1)} %get-tuple-element.34) | copy-start | bytes 1572868
  66.2 1.4 %collective-permute-start.3 = (f32[8,128]{1,0:T(8,128)}, f32[8,128]{1,0:T(8,128)S(1)}, u32[]{:S(2)}, u32[]{:S(2)}) collective-permute-start(f32[8,128]{1,0:T(8,128)} %get-tuple-element.44), channel_id=1, source_target_pairs={{0,4},{4,0},{8,12},{12,8},{16,20},{20,16},{24,28},{28,24},{1,5},{5... | collective-permute-start | bytes 12296 | tf_op jit(solution)/shard_map/ppermute | solution.py:242
  68.3 5.1 %collective-permute-start.4 = (f32[8,128]{1,0:T(8,128)S(1)}, f32[8,128]{1,0:T(8,128)S(1)}, u32[]{:S(2)}, u32[]{:S(2)}) collective-permute-start(f32[8,128]{1,0:T(8,128)S(1)} %add.207), channel_id=1, source_target_pairs={{0,1},{1,0},{2,3},{3,2},{4,5},{5,4},{6,7},{7,6},{8,9},{9,8},{10,11... | collective-permute-start | bytes 12296 | tf_op jit(solution)/shard_map/ppermute | solution.py:234
  70.3 4.5 %collective-permute-start.5 = (f32[8,128]{1,0:T(8,128)S(1)}, f32[8,128]{1,0:T(8,128)S(1)}, u32[]{:S(2)}, u32[]{:S(2)}) collective-permute-start(f32[8,128]{1,0:T(8,128)S(1)} %add.207), channel_id=1, source_target_pairs={{0,2},{1,3},{2,0},{3,1},{4,6},{5,7},{6,4},{7,5},{8,10},{9,11},{10,... | collective-permute-start | bytes 12296 | tf_op jit(solution)/shard_map/ppermute | solution.py:234
  72.9 5.4 %collective-permute-start.6 = (f32[8,128]{1,0:T(8,128)S(1)}, f32[8,128]{1,0:T(8,128)S(1)}, u32[]{:S(2)}, u32[]{:S(2)}) collective-permute-start(f32[8,128]{1,0:T(8,128)S(1)} %add.207), channel_id=1, source_target_pairs={{0,3},{1,2},{2,1},{3,0},{4,7},{5,6},{6,5},{7,4},{8,11},{9,10},{10,... | collective-permute-start | bytes 12296 | tf_op jit(solution)/shard_map/ppermute | solution.py:234
  72.9 13.8 %collective-permute-start.1 = (bf16[2,256,512]{2,1,0:T(8,128)(2,1)S(1)}, bf16[2,256,512]{2,1,0:T(8,128)(2,1)S(1)}, u32[]{:S(2)}, u32[]{:S(2)}) collective-permute-start(bf16[2,256,512]{2,1,0:T(8,128)(2,1)S(1)} %copy-done.6), channel_id=1, source_target_pairs={{0,4},{4,0},{8,12},{12,8},{16,20},{20,16},{24,28},{28,24},{1,5},{5... | collective-permute-start | bytes 1572872 | tf_op jit(solution)/shard_map/ppermute | solution.py:317
  72.9 13.8 %collective-permute-start.2 = (bf16[2,256,512]{2,1,0:T(8,128)(2,1)}, bf16[2,256,512]{2,1,0:T(8,128)(2,1)S(1)}, u32[]{:S(2)}, u32[]{:S(2)}) collective-permute-start(bf16[2,256,512]{2,1,0:T(8,128)(2,1)} %get-tuple-element.35), channel_id=1, source_target_pairs={{0,4},{4,0},{8,12},{12,8},{16,20},{20,16},{24,28},{28,24},{1,5},{5... | collective-permute-start | bytes 1572872 | tf_op jit(solution)/shard_map/ppermute | solution.py:317
  78.3 7.6 %collective-permute-start.7 = (f32[8,128]{1,0:T(8,128)S(1)}, f32[8,128]{1,0:T(8,128)S(1)}, u32[]{:S(2)}, u32[]{:S(2)}) collective-permute-start(f32[8,128]{1,0:T(8,128)S(1)} %add_add_fusion.1), channel_id=1, source_target_pairs={{0,8},{4,12},{8,0},{12,4},{16,24},{20,28},{24,16},{28,20},{1,9},{5... | collective-permute-start | bytes 12296 | tf_op jit(solution)/shard_map/ppermute | solution.py:234
  80.2 5.7 %collective-permute-start.8 = (f32[8,128]{1,0:T(8,128)S(1)}, f32[8,128]{1,0:T(8,128)S(1)}, u32[]{:S(2)}, u32[]{:S(2)}) collective-permute-start(f32[8,128]{1,0:T(8,128)S(1)} %add_add_fusion.1), channel_id=1, source_target_pairs={{0,16},{4,20},{8,24},{12,28},{16,0},{20,4},{24,8},{28,12},{1,17},{... | collective-permute-start | bytes 12296 | tf_op jit(solution)/shard_map/ppermute | solution.py:234
  81.7 4.5 %collective-permute-start.9 = (f32[8,128]{1,0:T(8,128)S(1)}, f32[8,128]{1,0:T(8,128)S(1)}, u32[]{:S(2)}, u32[]{:S(2)}) collective-permute-start(f32[8,128]{1,0:T(8,128)S(1)} %add_add_fusion.1), channel_id=1, source_target_pairs={{0,24},{4,28},{8,16},{12,20},{16,8},{20,12},{24,0},{28,4},{1,25},{... | collective-permute-start | bytes 12296 | tf_op jit(solution)/shard_map/ppermute | solution.py:234
  81.8 19.5 %all-to-all-start.3 = ((bf16[8,512,128]{2,1,0:T(8,128)(2,1)}), bf16[8,512,128]{2,1,0:T(8,128)(2,1)S(1)}, u32[]{:S(2)}, u32[]{:S(2)}) async-start(bf16[8,512,128]{2,1,0:T(8,128)(2,1)} %get-tuple-element.43), calls=%async_computation.3 | async-start | bytes 2097152 | tf_op jit(solution)/shard_map/all_to_all | solution.py:315
  86.7 1.5 %copy-start.4 = (bf16[256,512]{1,0:T(8,128)(2,1)S(1)}, bf16[256,512]{1,0:T(8,128)(2,1)}, u32[]{:S(2)}) copy-start(bf16[256,512]{1,0:T(8,128)(2,1)} %get-tuple-element.27) | copy-start | bytes 786436
  86.7 1.5 %copy-start.5 = (bf16[256,512]{1,0:T(8,128)(2,1)S(1)}, bf16[256,512]{1,0:T(8,128)(2,1)}, u32[]{:S(2)}) copy-start(bf16[256,512]{1,0:T(8,128)(2,1)} %get-tuple-element.40) | copy-start | bytes 786436
  88.2 1.0 copy-start.2
  88.2 1.0 copy-start.3

commit v10 on v9

--- a/solution.py
+++ b/solution.py
@@ -13,7 +13,7 @@
 HD = 128
 BLOCK = 128
 QPG = HEADS // KV_HEADS
-CHUNK = 2
+CHUNK = 6
 ROWS = QPG * BLOCK
 TAIL = 8
 VMEM_BYTES = 63 * 2**20
@@ -249,28 +249,36 @@
 
 
 def spread(gi, devices, keys, values):
-    tokens, width = keys.shape
+    tokens = keys.shape[0]
     local_blocks = tokens // BLOCK
 
-    def kernel(k_ref, v_ref, out):
-        for parity in range(2):
-            cols = slice((2 * parity + gi) * HD, (2 * parity + gi + 1) * HD)
+    def kernel(*refs):
+        columns, out, piece, sems = refs[:4], refs[4], refs[5], refs[6]
+        for n, ref in enumerate(columns):
             for half in range(local_blocks):
-                rows = slice(half * BLOCK, (half + 1) * BLOCK)
-                out[parity, half, 0] = k_ref[rows, cols]
-                out[parity, half, 1] = v_ref[rows, cols]
-
-    taken = pl.BlockSpec((tokens, width), lambda d: (0, 0))
+                piece[n % 2, half, n // 2] = ref[half * BLOCK : (half + 1) * BLOCK, :]
+        copies = [
+            pltpu.make_async_copy(piece, out.at[pl.ds(2 * d, 2)], sems.at[d]) for d in range(devices // 2)
+        ]
+        for copy in copies:
+            copy.start()
+        for copy in copies:
+            copy.wait()
+
+    def column(group):
+        return pl.BlockSpec((tokens, HD), lambda n: (0, group), pipeline_mode=pl.Buffered(1))
+
     block = (2, local_blocks, 2, BLOCK, HD)
     return pl.pallas_call(
         kernel,
-        grid=(devices // 2,),
-        in_specs=[taken, taken],
-        out_specs=pl.BlockSpec(block, lambda d: (d, 0, 0, 0, 0)),
+        grid=(1,),
+        in_specs=[column(gi), column(2 + gi)] * 2,
+        out_specs=pl.BlockSpec(memory_space=pl.ANY),
         out_shape=jax.ShapeDtypeStruct((devices, *block[1:]), jnp.bfloat16),
+        scratch_shapes=[pltpu.VMEM(block, jnp.bfloat16), pltpu.SemaphoreType.DMA((devices // 2,))],
         compiler_params=pltpu.CompilerParams(vmem_limit_bytes=VMEM_BYTES),
         name="spread_keys_values",
-    )(keys, values)
+    )(keys, keys, values, values)
 
 
 def body(queries, keys, values, tau, out_grad, key_blocks):
@@ -313,9 +321,7 @@
             grads[0] = lax.all_to_all(kv_grads, "ctx", 0, 0)
     grads, sibs, tau_last = lax.optimization_barrier((grads, sibs, tau_rows[1]))
     grads[1] = lax.all_to_all(grads[1], "ctx", 0, 0)
-    sibs, grads[0] = lax.optimization_barrier(
-        ([lax.ppermute(sib, "ctx", swap) for sib in sibs], grads[0])
-    )
+    sibs = lax.optimization_barrier([lax.ppermute(sib, "ctx", swap) for sib in sibs])
     att_parts, dq_parts = (
         [(own[which], sib[which]) for own, sib in zip(owns, sibs)] for which in range(2)
     )

time: 104 us -> 92.7 us (0.89)
  Pallas kernels: 38.9 us -> 32.8 us
  waiting for transfers between devices: 25.9 us -> 22 us
    all_to_all x1, waiting for transfers between devices: 9.76 us -> 0.01 us  [body(): grads[1] = lax.all_to_all(grads[1], 'ctx', 0, 0)]
    pallas_call x2, Pallas kernels: 33.6 us -> 28.9 us  [run_group(): pl.pallas_call(functools.partial(group_kernel, gi, devices, local_blocks,...]
    ppermute x6, waiting for transfers between devices: 5.18 us -> 9.62 us  [partners(): lax.ppermute(x, axis, [(i, i ^ d) for i in range(size)])]
    all_to_all x2, waiting for transfers between devices: 9.87 us -> 11.6 us  [kv_for(): arrived = lax.all_to_all(spread(gi, ctx, k0, v0), 'ctx', 0, 0)]
    pallas_call x2, Pallas kernels: 5.25 us -> 3.93 us  [spread(): pl.pallas_call(kernel, grid=(1,), in_specs=[column(gi), column(2 + gi)] *...]
  transfers between devices with their start and end apart: 14 -> 14, of which waited for: 6 -> 8; matrix products, arithmetic and copies ran while one was open for 6% -> 7% of each run, Pallas kernels for 35% -> 33%
where the time goes in v10:
time: 92.7 us; the launch traced here: 92.1 us
  Pallas kernels  32.8 us (35%)
  starting transfers between devices  26.9 us (29%)
  waiting for transfers between devices  22 us (24%)
  other arithmetic  6.22 us (7%)
  local copies, waits for them, and re-layouts  3.23 us (3%)
    pallas_call x2, Pallas kernels, run_group(): pl.pallas_call(functools.partial(group_kernel, gi, devices, local_blocks,...  28.9 us
    all_to_all x2, waiting for transfers between devices, kv_for(): arrived = lax.all_to_all(spread(gi, ctx, k0, v0), 'ctx', 0, 0)  11.6 us
    ppermute x6, waiting for transfers between devices, partners(): lax.ppermute(x, axis, [(i, i ^ d) for i in range(size)])  9.62 us
    all_to_all x2, starting transfers between devices, kv_for(): arrived = lax.all_to_all(spread(gi, ctx, k0, v0), 'ctx', 0, 0)  9.56 us
    ppermute x6, starting transfers between devices, partners(): lax.ppermute(x, axis, [(i, i ^ d) for i in range(size)])  8.15 us
    all_to_all x1, starting transfers between devices, body(): grads[0] = lax.all_to_all(kv_grads, 'ctx', 0, 0)  4.42 us
    pallas_call x2, Pallas kernels, spread(): pl.pallas_call(kernel, grid=(1,), in_specs=[column(gi), column(2 + gi)] *...  3.93 us
    all_to_all x1, starting transfers between devices, body(): grads[1] = lax.all_to_all(grads[1], 'ctx', 0, 0)  3.7 us
  transfers between devices with their start and end apart: 14, of which 8 were waited for; matrix products, arithmetic and copies ran while one was open for 7% of the time, Pallas kernels for 33%

profile of v10, /device:TPU:0, one launch (start us, length us, event | category | flops | bytes accessed | tf_op | source)
XLA Modules:
  0.0 92.1 jit_solution(8199431473110473035)
XLA Ops:
  0.6 2.0 %spread_keys_values.2 = bf16[8,2,2,128,128]{4,3,2,1,0:T(8,128)(2,1)} custom-call(bf16[256,512]{1,0:T(8,128)(2,1)} %bitcast.55, bf16[256,512]{1,0:T(8,128)(2,1)} %bitcast.56, bf16[256,512]{1,0:T(8,128)(2,1)} %bitcast.59, bf16[256,512]{1,0:T(8,128)(2,1)} %bitcast.60), custom_call_target="tpu_custom_call" | custom-call | tf_op jit(solution)/shard_map/spread_keys_values/pallas_call | solution.py:272
  2.6 5.3 %all-to-all-start = ((bf16[8,2,2,128,128]{4,3,2,1,0:T(8,128)(2,1)}), bf16[8,2,2,128,128]{4,3,2,1,0:T(8,128)(2,1)}, u32[]{:S(2)}, u32[]{:S(2)}) async-start(bf16[8,2,2,128,128]{4,3,2,1,0:T(8,128)(2,1)} %spread_keys_values.2), calls=%async_computation | async-start | bytes 2097152 | tf_op jit(solution)/shard_map/all_to_all | solution.py:300
  8.1 0.6 slice-done
  8.8 1.1 %pad_maximum_fusion = bf16[2,256,1024]{2,1,0:T(8,128)(2,1)} fusion(bf16[1,256,1024]{2,1,0:T(8,128)(2,1)S(1)} %get-tuple-element.79, bf16[1,256,1024]{2,1,0:T(8,128)(2,1)S(1)} %get-tuple-element.80), kind=kLoop, calls=%fused_computation | loop fusion | flops 524288 | bytes 2097152 | tf_op jit(solution)/shard_map/stack | solution.py:308
  9.9 0.5 and_select_fusion.refs_1_
  10.4 0.5 collective-permute-start
  10.9 2.0 %spread_keys_values.3 = bf16[8,2,2,128,128]{4,3,2,1,0:T(8,128)(2,1)} custom-call(bf16[256,512]{1,0:T(8,128)(2,1)} %bitcast.57, bf16[256,512]{1,0:T(8,128)(2,1)} %bitcast.58, bf16[256,512]{1,0:T(8,128)(2,1)} %bitcast.61, bf16[256,512]{1,0:T(8,128)(2,1)} %bitcast.62), custom_call_target="tpu_custom_call" | custom-call | tf_op jit(solution)/shard_map/spread_keys_values/pallas_call | solution.py:272
  12.9 10.6 %all-to-all-done = bf16[8,2,2,128,128]{4,3,2,1,0:T(8,128)(2,1)} async-done(((bf16[8,2,2,128,128]{4,3,2,1,0:T(8,128)(2,1)}), bf16[8,2,2,128,128]{4,3,2,1,0:T(8,128)(2,1)}, u32[]{:S(2)}, u32[]{:S(2)}) %all-to-all-start) | async-done | bytes 1048608 | tf_op jit(solution)/shard_map/all_to_all | solution.py:300
  23.5 4.2 %all-to-all-start.2 = ((bf16[8,2,2,128,128]{4,3,2,1,0:T(8,128)(2,1)}), bf16[8,2,2,128,128]{4,3,2,1,0:T(8,128)(2,1)}, u32[]{:S(2)}, u32[]{:S(2)}) async-start(bf16[8,2,2,128,128]{4,3,2,1,0:T(8,128)(2,1)} %spread_keys_values.3), calls=%async_computation.2 | async-start | bytes 2097152 | tf_op jit(solution)/shard_map/all_to_all | solution.py:300
  27.7 14.4 %group_attention.2 = (bf16[256,512]{1,0:T(8,128)(2,1)}, bf16[256,512]{1,0:T(8,128)(2,1)}, bf16[2,256,512]{2,1,0:T(8,128)(2,1)}, f32[8,128]{1,0:T(8,128)}, bf16[8,512,128]{2,1,0:T(8,128)(2,1)}) custom-call(s32[1]{0:T(128)} %bitcast.refs_0_, s32[64]{0:T(128)} %and_select_fusion.refs_1_, f32[16]{0:T(128)} %refs_2_.3, bf16[256,2048]{1,0:T(8,128)(2,1)} %bitcast.79, ...), custom_call_target="tpu_custom_call" | custom-call | flops 4429185024 | bytes 6291456 | tf_op jit(solution)/shard_map/group_attention/pallas_call | solution.py:208
  42.2 1.0 %all-to-all-done.2 = bf16[8,2,2,128,128]{4,3,2,1,0:T(8,128)(2,1)} async-done(((bf16[8,2,2,128,128]{4,3,2,1,0:T(8,128)(2,1)}), bf16[8,2,2,128,128]{4,3,2,1,0:T(8,128)(2,1)}, u32[]{:S(2)}, u32[]{:S(2)}) %all-to-all-start.2) | async-done | bytes 1048608 | tf_op jit(solution)/shard_map/all_to_all | solution.py:300
  43.1 4.4 %all-to-all-start.1 = ((bf16[8,512,128]{2,1,0:T(8,128)(2,1)}), bf16[8,512,128]{2,1,0:T(8,128)(2,1)}, u32[]{:S(2)}, u32[]{:S(2)}) async-start(bf16[8,512,128]{2,1,0:T(8,128)(2,1)} %get-tuple-element.27), calls=%async_computation.1 | async-start | bytes 2097152 | tf_op jit(solution)/shard_map/all_to_all | solution.py:321
  47.6 14.5 %group_attention.3 = (bf16[256,512]{1,0:T(8,128)(2,1)}, bf16[256,512]{1,0:T(8,128)(2,1)}, bf16[2,256,512]{2,1,0:T(8,128)(2,1)}, f32[8,128]{1,0:T(8,128)}, bf16[8,512,128]{2,1,0:T(8,128)(2,1)}) custom-call(s32[1]{0:T(128)} %bitcast.refs_0_, s32[64]{0:T(128)} %and_select_fusion.refs_1_, f32[16]{0:T(128)} %refs_2_.3, bf16[256,2048]{1,0:T(8,128)(2,1)} %bitcast.80, ...), custom_call_target="tpu_custom_call" | custom-call | flops 4429185024 | bytes 6291456 | tf_op jit(solution)/shard_map/group_attention/pallas_call | solution.py:208
  62.0 0.8 all-to-all-done.1
  62.8 1.4 %fusion.1 = (bf16[1,512,128]{2,1,0:T(8,128)(2,1)S(1)}, bf16[1,512,128]{2,1,0:T(8,128)(2,1)S(1)}, bf16[1,512,128]{2,1,0:T(8,128)(2,1)S(1)}, bf16[1,512,128]{2,1,0...) fusion(bf16[8,512,128]{2,1,0:T(8,128)(2,1)} %all-to-all-done.1), kind=kLoop, calls=%fused_computation.30 | loop fusion | bytes 2097152 | tf_op jit(solution)/shard_map/slice | solution.py:342
  64.2 3.7 %all-to-all-start.3 = ((bf16[8,512,128]{2,1,0:T(8,128)(2,1)}), bf16[8,512,128]{2,1,0:T(8,128)(2,1)S(1)}, u32[]{:S(2)}, u32[]{:S(2)}) async-start(bf16[8,512,128]{2,1,0:T(8,128)(2,1)} %get-tuple-element.41), calls=%async_computation.3 | async-start | bytes 2097152 | tf_op jit(solution)/shard_map/all_to_all | solution.py:323
  67.9 0.5 collective-permute-start.1
  68.6 2.1 %collective-permute-start.4 = (f32[8,128]{1,0:T(8,128)S(1)}, f32[8,128]{1,0:T(8,128)S(1)}, u32[]{:S(2)}, u32[]{:S(2)}) collective-permute-start(f32[8,128]{1,0:T(8,128)S(1)} %add.207), channel_id=1, source_target_pairs={{0,1},{1,0},{2,3},{3,2},{4,5},{5,4},{6,7},{7,6},{8,9},{9,8},{10,11... | collective-permute-start | bytes 12296 | tf_op jit(solution)/shard_map/ppermute | solution.py:234
  70.6 2.6 %collective-permute-start.5 = (f32[8,128]{1,0:T(8,128)S(1)}, f32[8,128]{1,0:T(8,128)S(1)}, u32[]{:S(2)}, u32[]{:S(2)}) collective-permute-start(f32[8,128]{1,0:T(8,128)S(1)} %add.207), channel_id=1, source_target_pairs={{0,2},{1,3},{2,0},{3,1},{4,6},{5,7},{6,4},{7,5},{8,10},{9,11},{10,... | collective-permute-start | bytes 12296 | tf_op jit(solution)/shard_map/ppermute | solution.py:234
  73.3 1.8 %collective-permute-done.5 = f32[8,128]{1,0:T(8,128)S(1)} collective-permute-done((f32[8,128]{1,0:T(8,128)S(1)}, f32[8,128]{1,0:T(8,128)S(1)}, u32[]{:S(2)}, u32[]{:S(2)}) %collective-permute-start.5) | collective-permute-done | bytes 4128 | tf_op jit(solution)/shard_map/ppermute | solution.py:234
  75.1 3.5 %collective-permute-done.6 = f32[8,128]{1,0:T(8,128)S(1)} collective-permute-done((f32[8,128]{1,0:T(8,128)S(1)}, f32[8,128]{1,0:T(8,128)S(1)}, u32[]{:S(2)}, u32[]{:S(2)}) %collective-permute-start.6) | collective-permute-done | bytes 4128 | tf_op jit(solution)/shard_map/ppermute | solution.py:234
  78.6 1.9 %collective-permute-start.7 = (f32[8,128]{1,0:T(8,128)S(1)}, f32[8,128]{1,0:T(8,128)S(1)}, u32[]{:S(2)}, u32[]{:S(2)}) collective-permute-start(f32[8,128]{1,0:T(8,128)S(1)} %add_add_fusion.1), channel_id=1, source_target_pairs={{0,8},{4,12},{8,0},{12,4},{16,24},{20,28},{24,16},{28,20},{1,9},{5... | collective-permute-start | bytes 12296 | tf_op jit(solution)/shard_map/ppermute | solution.py:234
  80.5 1.5 %collective-permute-start.8 = (f32[8,128]{1,0:T(8,128)S(1)}, f32[8,128]{1,0:T(8,128)S(1)}, u32[]{:S(2)}, u32[]{:S(2)}) collective-permute-start(f32[8,128]{1,0:T(8,128)S(1)} %add_add_fusion.1), channel_id=1, source_target_pairs={{0,16},{4,20},{8,24},{12,28},{16,0},{20,4},{24,8},{28,12},{1,17},{... | collective-permute-start | bytes 12296 | tf_op jit(solution)/shard_map/ppermute | solution.py:234
  82.2 0.2 collective-permute-done.7
  82.4 1.7 %collective-permute-done.8 = f32[8,128]{1,0:T(8,128)S(1)} collective-permute-done((f32[8,128]{1,0:T(8,128)S(1)}, f32[8,128]{1,0:T(8,128)S(1)}, u32[]{:S(2)}, u32[]{:S(2)}) %collective-permute-start.8) | collective-permute-done | bytes 4128 | tf_op jit(solution)/shard_map/ppermute | solution.py:234
  84.1 2.4 %collective-permute-done.9 = f32[8,128]{1,0:T(8,128)S(1)} collective-permute-done((f32[8,128]{1,0:T(8,128)S(1)}, f32[8,128]{1,0:T(8,128)S(1)}, u32[]{:S(2)}, u32[]{:S(2)}) %collective-permute-start.9) | collective-permute-done | bytes 4128 | tf_op jit(solution)/shard_map/ppermute | solution.py:234
  86.5 0.5 multiply_bitcast_fusion
  87.2 0.8 copy-done.4
  88.2 1.1 %maximum_bitcast_fusion.1 = bf16[1,256,2048]{2,1,0:T(8,128)(2,1)} fusion(bf16[256,512]{1,0:T(8,128)(2,1)S(1)} %get-tuple-element.62, bf16[256,512]{1,0:T(8,128)(2,1)S(1)} %get-tuple-element.60, bf16[256,512]{1,0:T(8,128)(2,1)S(1)} %get-tuple-element.61, bf16[256,512]{1,0:T(8,128)(2,1)S(1)} %get-tuple-element.59), kind=kLoop, calls=%fused_computation.2 | loop fusion | flops 4194304 | bytes 2097152 | tf_op jit(solution)/shard_map/broadcast_in_dim | solution.py:335
  89.3 1.1 %maximum_bitcast_fusion = bf16[1,256,2048]{2,1,0:T(8,128)(2,1)} fusion(bf16[256,512]{1,0:T(8,128)(2,1)S(1)} %get-tuple-element.77, bf16[256,512]{1,0:T(8,128)(2,1)S(1)} %get-tuple-element.75, bf16[256,512]{1,0:T(8,128)(2,1)S(1)} %get-tuple-element.78, bf16[256,512]{1,0:T(8,128)(2,1)S(1)} %get-tuple-element.76), kind=kLoop, calls=%fused_computation.1 | loop fusion | flops 4194304 | bytes 2097152 | tf_op jit(solution)/shard_map/broadcast_in_dim | solution.py:334
  90.6 0.7 maximum_bitcast_fusion.3
  91.3 0.7 maximum_bitcast_fusion.2
  (42 shorter events, 1.2 us)
Async XLA Ops:
  2.6 5.3 %copy-start = (bf16[1,256,2048]{2,1,0:T(8,128)(2,1)S(1)}, bf16[1,256,2048]{2,1,0:T(8,128)(2,1)}, u32[]{:S(2)}) copy-start(bf16[1,256,2048]{2,1,0:T(8,128)(2,1)} %param.6) | copy-start | bytes 3145732
  2.6 5.3 %copy-start.1 = (bf16[1,256,2048]{2,1,0:T(8,128)(2,1)S(1)}, bf16[1,256,2048]{2,1,0:T(8,128)(2,1)}, u32[]{:S(2)}) copy-start(bf16[1,256,2048]{2,1,0:T(8,128)(2,1)} %param.10) | copy-start | bytes 3145732
  2.6 20.8 %all-to-all-start = ((bf16[8,2,2,128,128]{4,3,2,1,0:T(8,128)(2,1)}), bf16[8,2,2,128,128]{4,3,2,1,0:T(8,128)(2,1)}, u32[]{:S(2)}, u32[]{:S(2)}) async-start(bf16[8,2,2,128,128]{4,3,2,1,0:T(8,128)(2,1)} %spread_keys_values.2), calls=%async_computation | async-start | bytes 2097152 | tf_op jit(solution)/shard_map/all_to_all | solution.py:300
  8.0 0.7 slice-start
  10.4 17.3 %collective-permute-start = (bf16[2,256,1024]{2,1,0:T(8,128)(2,1)}, bf16[2,256,1024]{2,1,0:T(8,128)(2,1)}, u32[]{:S(2)}, u32[]{:S(2)}) collective-permute-start(bf16[2,256,1024]{2,1,0:T(8,128)(2,1)} %pad_maximum_fusion), channel_id=1, source_target_pairs={{0,4},{4,0},{8,12},{12,8},{16,20},{20,16},{24,28},{28,24},{1,5},{5... | collective-permute-start | bytes 3145736 | tf_op jit(solution)/shard_map/ppermute | solution.py:309
  23.5 19.7 %all-to-all-start.2 = ((bf16[8,2,2,128,128]{4,3,2,1,0:T(8,128)(2,1)}), bf16[8,2,2,128,128]{4,3,2,1,0:T(8,128)(2,1)}, u32[]{:S(2)}, u32[]{:S(2)}) async-start(bf16[8,2,2,128,128]{4,3,2,1,0:T(8,128)(2,1)} %spread_keys_values.3), calls=%async_computation.2 | async-start | bytes 2097152 | tf_op jit(solution)/shard_map/all_to_all | solution.py:300
  43.1 19.7 %all-to-all-start.1 = ((bf16[8,512,128]{2,1,0:T(8,128)(2,1)}), bf16[8,512,128]{2,1,0:T(8,128)(2,1)}, u32[]{:S(2)}, u32[]{:S(2)}) async-start(bf16[8,512,128]{2,1,0:T(8,128)(2,1)} %get-tuple-element.27), calls=%async_computation.1 | async-start | bytes 2097152 | tf_op jit(solution)/shard_map/all_to_all | solution.py:321
  62.8 5.8 %collective-permute-start.3 = (f32[8,128]{1,0:T(8,128)}, f32[8,128]{1,0:T(8,128)S(1)}, u32[]{:S(2)}, u32[]{:S(2)}) collective-permute-start(f32[8,128]{1,0:T(8,128)} %get-tuple-element.42), channel_id=1, source_target_pairs={{0,4},{4,0},{8,12},{12,8},{16,20},{20,16},{24,28},{28,24},{1,5},{5... | collective-permute-start | bytes 12296 | tf_op jit(solution)/shard_map/ppermute | solution.py:242
  64.2 3.7 %copy-start.7 = (bf16[2,256,512]{2,1,0:T(8,128)(2,1)S(1)}, bf16[2,256,512]{2,1,0:T(8,128)(2,1)}, u32[]{:S(2)}) copy-start(bf16[2,256,512]{2,1,0:T(8,128)(2,1)} %get-tuple-element.33) | copy-start | bytes 1572868
  64.2 4.3 %copy-start.8 = (bf16[2,256,512]{2,1,0:T(8,128)(2,1)S(1)}, bf16[2,256,512]{2,1,0:T(8,128)(2,1)}, u32[]{:S(2)}) copy-start(bf16[2,256,512]{2,1,0:T(8,128)(2,1)} %get-tuple-element.34) | copy-start | bytes 1572868
  64.2 4.4 %copy-start.6 = (f32[8,128]{1,0:T(8,128)S(1)}, f32[8,128]{1,0:T(8,128)}, u32[]{:S(2)}) copy-start(f32[8,128]{1,0:T(8,128)} %get-tuple-element.42) | copy-start | bytes 12292
  64.2 26.2 %all-to-all-start.3 = ((bf16[8,512,128]{2,1,0:T(8,128)(2,1)}), bf16[8,512,128]{2,1,0:T(8,128)(2,1)S(1)}, u32[]{:S(2)}, u32[]{:S(2)}) async-start(bf16[8,512,128]{2,1,0:T(8,128)(2,1)} %get-tuple-element.41), calls=%async_computation.3 | async-start | bytes 2097152 | tf_op jit(solution)/shard_map/all_to_all | solution.py:323
  67.9 19.1 %copy-start.2 = (bf16[256,512]{1,0:T(8,128)(2,1)S(1)}, bf16[256,512]{1,0:T(8,128)(2,1)}, u32[]{:S(2)}) copy-start(bf16[256,512]{1,0:T(8,128)(2,1)} %get-tuple-element.26) | copy-start | bytes 786436
  67.9 19.1 %copy-start.3 = (bf16[256,512]{1,0:T(8,128)(2,1)S(1)}, bf16[256,512]{1,0:T(8,128)(2,1)}, u32[]{:S(2)}) copy-start(bf16[256,512]{1,0:T(8,128)(2,1)} %get-tuple-element.38) | copy-start | bytes 786436
  67.9 19.1 %collective-permute-start.1 = (bf16[2,256,512]{2,1,0:T(8,128)(2,1)S(1)}, bf16[2,256,512]{2,1,0:T(8,128)(2,1)S(1)}, u32[]{:S(2)}, u32[]{:S(2)}) collective-permute-start(bf16[2,256,512]{2,1,0:T(8,128)(2,1)S(1)} %copy-done.7), channel_id=1, source_target_pairs={{0,4},{4,0},{8,12},{12,8},{16,20},{20,16},{24,28},{28,24},{1,5},{5... | collective-permute-start | bytes 1572872 | tf_op jit(solution)/shard_map/ppermute | solution.py:324
  68.5 18.6 %collective-permute-start.2 = (bf16[2,256,512]{2,1,0:T(8,128)(2,1)S(1)}, bf16[2,256,512]{2,1,0:T(8,128)(2,1)S(1)}, u32[]{:S(2)}, u32[]{:S(2)}) collective-permute-start(bf16[2,256,512]{2,1,0:T(8,128)(2,1)S(1)} %copy-done.8), channel_id=1, source_target_pairs={{0,4},{4,0},{8,12},{12,8},{16,20},{20,16},{24,28},{28,24},{1,5},{5... | collective-permute-start | bytes 1572872 | tf_op jit(solution)/shard_map/ppermute | solution.py:324
  68.6 4.7 %collective-permute-start.4 = (f32[8,128]{1,0:T(8,128)S(1)}, f32[8,128]{1,0:T(8,128)S(1)}, u32[]{:S(2)}, u32[]{:S(2)}) collective-permute-start(f32[8,128]{1,0:T(8,128)S(1)} %add.207), channel_id=1, source_target_pairs={{0,1},{1,0},{2,3},{3,2},{4,5},{5,4},{6,7},{7,6},{8,9},{9,8},{10,11... | collective-permute-start | bytes 12296 | tf_op jit(solution)/shard_map/ppermute | solution.py:234
  70.6 4.5 %collective-permute-start.5 = (f32[8,128]{1,0:T(8,128)S(1)}, f32[8,128]{1,0:T(8,128)S(1)}, u32[]{:S(2)}, u32[]{:S(2)}) collective-permute-start(f32[8,128]{1,0:T(8,128)S(1)} %add.207), channel_id=1, source_target_pairs={{0,2},{1,3},{2,0},{3,1},{4,6},{5,7},{6,4},{7,5},{8,10},{9,11},{10,... | collective-permute-start | bytes 12296 | tf_op jit(solution)/shard_map/ppermute | solution.py:234
  73.2 5.4 %collective-permute-start.6 = (f32[8,128]{1,0:T(8,128)S(1)}, f32[8,128]{1,0:T(8,128)S(1)}, u32[]{:S(2)}, u32[]{:S(2)}) collective-permute-start(f32[8,128]{1,0:T(8,128)S(1)} %add.207), channel_id=1, source_target_pairs={{0,3},{1,2},{2,1},{3,0},{4,7},{5,6},{6,5},{7,4},{8,11},{9,10},{10,... | collective-permute-start | bytes 12296 | tf_op jit(solution)/shard_map/ppermute | solution.py:234
  78.6 3.8 %collective-permute-start.7 = (f32[8,128]{1,0:T(8,128)S(1)}, f32[8,128]{1,0:T(8,128)S(1)}, u32[]{:S(2)}, u32[]{:S(2)}) collective-permute-start(f32[8,128]{1,0:T(8,128)S(1)} %add_add_fusion.1), channel_id=1, source_target_pairs={{0,8},{4,12},{8,0},{12,4},{16,24},{20,28},{24,16},{28,20},{1,9},{5... | collective-permute-start | bytes 12296 | tf_op jit(solution)/shard_map/ppermute | solution.py:234
  80.5 3.6 %collective-permute-start.8 = (f32[8,128]{1,0:T(8,128)S(1)}, f32[8,128]{1,0:T(8,128)S(1)}, u32[]{:S(2)}, u32[]{:S(2)}) collective-permute-start(f32[8,128]{1,0:T(8,128)S(1)} %add_add_fusion.1), channel_id=1, source_target_pairs={{0,16},{4,20},{8,24},{12,28},{16,0},{20,4},{24,8},{28,12},{1,17},{... | collective-permute-start | bytes 12296 | tf_op jit(solution)/shard_map/ppermute | solution.py:234
  82.0 4.5 %collective-permute-start.9 = (f32[8,128]{1,0:T(8,128)S(1)}, f32[8,128]{1,0:T(8,128)S(1)}, u32[]{:S(2)}, u32[]{:S(2)}) collective-permute-start(f32[8,128]{1,0:T(8,128)S(1)} %add_add_fusion.1), channel_id=1, source_target_pairs={{0,24},{4,28},{8,16},{12,20},{16,8},{20,12},{24,0},{28,4},{1,25},{... | collective-permute-start | bytes 12296 | tf_op jit(solution)/shard_map/ppermute | solution.py:234
  87.1 1.0 %copy-start.4 = (bf16[256,512]{1,0:T(8,128)(2,1)S(1)}, bf16[256,512]{1,0:T(8,128)(2,1)}, u32[]{:S(2)}) copy-start(bf16[256,512]{1,0:T(8,128)(2,1)} %get-tuple-element.36) | copy-start | bytes 786436
  87.1 1.0 %copy-start.5 = (bf16[256,512]{1,0:T(8,128)(2,1)S(1)}, bf16[256,512]{1,0:T(8,128)(2,1)}, u32[]{:S(2)}) copy-start(bf16[256,512]{1,0:T(8,128)(2,1)} %get-tuple-element.39) | copy-start | bytes 786436

commit v11 on v10

--- a/solution.py
+++ b/solution.py
@@ -13,7 +13,7 @@
 HD = 128
 BLOCK = 128
 QPG = HEADS // KV_HEADS
-CHUNK = 6
+CHUNK = 11
 ROWS = QPG * BLOCK
 TAIL = 8
 VMEM_BYTES = 63 * 2**20
@@ -235,17 +235,18 @@
     return (x + a) + (b + c)
 
 
-def total_everywhere(x):
+def total_everywhere(x, ready):
     ctx, batch = lax.axis_size("ctx"), lax.axis_size("batch")
     if batch != 4 or ctx not in (8, 32):
-        return lax.psum(x, ("ctx", "batch"))
+        return lax.psum(x, ("ctx", "batch")), ready
     x = x + lax.ppermute(x, "ctx", [(i, i ^ 1) for i in range(ctx)])
     x = partners(x, "batch", (1, 2, 3))
+    x, ready = lax.optimization_barrier((x, ready))
     step = 2
     while step < ctx:
         x = partners(x, "ctx", (step, 2 * step, 3 * step))
         step *= 4
-    return x
+    return x, ready
 
 
 def spread(gi, devices, keys, values):
@@ -321,7 +322,9 @@
             grads[0] = lax.all_to_all(kv_grads, "ctx", 0, 0)
     grads, sibs, tau_last = lax.optimization_barrier((grads, sibs, tau_rows[1]))
     grads[1] = lax.all_to_all(grads[1], "ctx", 0, 0)
-    sibs = lax.optimization_barrier([lax.ppermute(sib, "ctx", swap) for sib in sibs])
+    sibs, grads[0] = lax.optimization_barrier(
+        ([lax.ppermute(sib, "ctx", swap) for sib in sibs], grads[0])
+    )
     att_parts, dq_parts = (
         [(own[which], sib[which]) for own, sib in zip(owns, sibs)] for which in range(2)
     )
@@ -334,19 +337,27 @@
     attended = by_group(att_parts)[None]
     query_grad = by_group(dq_parts)[None]
 
-    def summed(which):
-        cols = []
-        for c in range(4):
-            total = None
-            for src in range(c // 2, ctx, 2):
-                term = grads[c % 2][src].reshape(local_blocks, 2, BLOCK, HD)[:, which]
-                term = term.astype(jnp.float32)
-                total = term if total is None else total + term
-            cols.append(total.reshape(tokens, HD).astype(jnp.bfloat16))
-        return jnp.concatenate(cols, axis=1)[None]
-
-    key_grad, value_grad = summed(0), summed(1)
-    scale_total = total_everywhere(tau_last)[0, :HEADS]
+    def summed(gi):
+        columns = []
+        for which in range(2):
+            for parity in range(2):
+                total = None
+                for src in range(parity, ctx, 2):
+                    term = grads[gi][src].reshape(local_blocks, 2, BLOCK, HD)[:, which]
+                    term = term.astype(jnp.float32)
+                    total = term if total is None else total + term
+                columns.append(total.reshape(tokens, HD).astype(jnp.bfloat16))
+        return columns
+
+    scale_total, (attended, query_grad, first) = total_everywhere(
+        tau_last, (attended, query_grad, summed(0))
+    )
+    second = summed(1)
+    key_grad, value_grad = (
+        jnp.concatenate([first[i], second[i], first[i + 1], second[i + 1]], axis=1)[None]
+        for i in (0, 2)
+    )
+    scale_total = scale_total[0, :HEADS]
     tau_grad = scale_total / math.sqrt(lax.axis_size("batch") * ctx * tokens)
     return (attended, query_grad, key_grad, value_grad, tau_grad)
 

time: 92.7 us -> 93.1 us (level)
  waiting for transfers between devices: 22 us -> 21 us
    ppermute x6, waiting for transfers between devices: 9.62 us -> 7.16 us  [partners(): lax.ppermute(x, axis, [(i, i ^ d) for i in range(size)])]
    ppermute x1, waiting for transfers between devices: 0.01 us -> 2.36 us  [total_everywhere(): x = x + lax.ppermute(x, 'ctx', [(i, i ^ 1) for i in range(ctx)])]
  transfers between devices with their start and end apart: 14 -> 14, of which waited for: 8 -> 7; matrix products, arithmetic and copies ran while one was open for 7% -> 8% of each run, Pallas kernels for 33% -> 34%
where the time goes in v11:
time: 93.1 us; the launch traced here: 92.5 us
  Pallas kernels  33.6 us (36%)
  starting transfers between devices  26.7 us (29%)
  waiting for transfers between devices  21 us (23%)
  other arithmetic  6.98 us (7%)
  local copies, waits for them, and re-layouts  3.27 us (4%)
    pallas_call x2, Pallas kernels, run_group(): pl.pallas_call(functools.partial(group_kernel, gi, devices, local_blocks,...  29.7 us
    all_to_all x2, waiting for transfers between devices, kv_for(): arrived = lax.all_to_all(spread(gi, ctx, k0, v0), 'ctx', 0, 0)  11.2 us
    all_to_all x2, starting transfers between devices, kv_for(): arrived = lax.all_to_all(spread(gi, ctx, k0, v0), 'ctx', 0, 0)  9.56 us
    ppermute x6, starting transfers between devices, partners(): lax.ppermute(x, axis, [(i, i ^ d) for i in range(size)])  8.08 us
    ppermute x6, waiting for transfers between devices, partners(): lax.ppermute(x, axis, [(i, i ^ d) for i in range(size)])  7.16 us
    all_to_all x1, starting transfers between devices, body(): grads[0] = lax.all_to_all(kv_grads, 'ctx', 0, 0)  4.42 us
    pallas_call x2, Pallas kernels, spread(): pl.pallas_call(kernel, grid=(1,), in_specs=[column(gi), column(2 + gi)] *...  3.95 us
    all_to_all x1, starting transfers between devices, body(): grads[1] = lax.all_to_all(grads[1], 'ctx', 0, 0)  3.65 us
  transfers between devices with their start and end apart: 14, of which 7 were waited for; matrix products, arithmetic and copies ran while one was open for 8% of the time, Pallas kernels for 34%

profile of v11, /device:TPU:0, one launch (start us, length us, event | category | flops | bytes accessed | tf_op | source)
XLA Modules:
  0.0 92.5 jit_solution(13651219279641414675)
XLA Ops:
  0.6 2.0 %spread_keys_values.2 = bf16[8,2,2,128,128]{4,3,2,1,0:T(8,128)(2,1)} custom-call(bf16[256,512]{1,0:T(8,128)(2,1)} %bitcast.55, bf16[256,512]{1,0:T(8,128)(2,1)} %bitcast.56, bf16[256,512]{1,0:T(8,128)(2,1)} %bitcast.59, bf16[256,512]{1,0:T(8,128)(2,1)} %bitcast.60), custom_call_target="tpu_custom_call" | custom-call | tf_op jit(solution)/shard_map/spread_keys_values/pallas_call | solution.py:273
  2.7 5.3 %all-to-all-start = ((bf16[8,2,2,128,128]{4,3,2,1,0:T(8,128)(2,1)}), bf16[8,2,2,128,128]{4,3,2,1,0:T(8,128)(2,1)}, u32[]{:S(2)}, u32[]{:S(2)}) async-start(bf16[8,2,2,128,128]{4,3,2,1,0:T(8,128)(2,1)} %spread_keys_values.2), calls=%async_computation | async-start | bytes 2097152 | tf_op jit(solution)/shard_map/all_to_all | solution.py:301
  8.1 0.6 slice-done
  8.8 1.1 %pad_maximum_fusion = bf16[2,256,1024]{2,1,0:T(8,128)(2,1)} fusion(bf16[1,256,1024]{2,1,0:T(8,128)(2,1)S(1)} %get-tuple-element.95, bf16[1,256,1024]{2,1,0:T(8,128)(2,1)S(1)} %get-tuple-element.96), kind=kLoop, calls=%fused_computation | loop fusion | flops 524288 | bytes 2097152 | tf_op jit(solution)/shard_map/stack | solution.py:309
  9.9 0.6 and_select_fusion.refs_1_
  10.5 0.5 collective-permute-start
  11.0 2.0 %spread_keys_values.3 = bf16[8,2,2,128,128]{4,3,2,1,0:T(8,128)(2,1)} custom-call(bf16[256,512]{1,0:T(8,128)(2,1)} %bitcast.57, bf16[256,512]{1,0:T(8,128)(2,1)} %bitcast.58, bf16[256,512]{1,0:T(8,128)(2,1)} %bitcast.61, bf16[256,512]{1,0:T(8,128)(2,1)} %bitcast.62), custom_call_target="tpu_custom_call" | custom-call | tf_op jit(solution)/shard_map/spread_keys_values/pallas_call | solution.py:273
  13.0 10.5 %all-to-all-done = bf16[8,2,2,128,128]{4,3,2,1,0:T(8,128)(2,1)} async-done(((bf16[8,2,2,128,128]{4,3,2,1,0:T(8,128)(2,1)}), bf16[8,2,2,128,128]{4,3,2,1,0:T(8,128)(2,1)}, u32[]{:S(2)}, u32[]{:S(2)}) %all-to-all-start) | async-done | bytes 1048608 | tf_op jit(solution)/shard_map/all_to_all | solution.py:301
  23.5 4.2 %all-to-all-start.2 = ((bf16[8,2,2,128,128]{4,3,2,1,0:T(8,128)(2,1)}), bf16[8,2,2,128,128]{4,3,2,1,0:T(8,128)(2,1)}, u32[]{:S(2)}, u32[]{:S(2)}) async-start(bf16[8,2,2,128,128]{4,3,2,1,0:T(8,128)(2,1)} %spread_keys_values.3), calls=%async_computation.2 | async-start | bytes 2097152 | tf_op jit(solution)/shard_map/all_to_all | solution.py:301
  27.8 14.8 %group_attention.2 = (bf16[256,512]{1,0:T(8,128)(2,1)}, bf16[256,512]{1,0:T(8,128)(2,1)}, bf16[2,256,512]{2,1,0:T(8,128)(2,1)}, f32[8,128]{1,0:T(8,128)}, bf16[8,512,128]{2,1,0:T(8,128)(2,1)}) custom-call(s32[1]{0:T(128)} %bitcast.refs_0_, s32[64]{0:T(128)} %and_select_fusion.refs_1_, f32[16]{0:T(128)} %refs_2_.3, bf16[256,2048]{1,0:T(8,128)(2,1)} %bitcast.79, ...), custom_call_target="tpu_custom_call" | custom-call | flops 4429185024 | bytes 6291456 | tf_op jit(solution)/shard_map/group_attention/pallas_call | solution.py:208
  42.5 0.7 all-to-all-done.2
  43.2 4.4 %all-to-all-start.1 = ((bf16[8,512,128]{2,1,0:T(8,128)(2,1)}), bf16[8,512,128]{2,1,0:T(8,128)(2,1)}, u32[]{:S(2)}, u32[]{:S(2)}) async-start(bf16[8,512,128]{2,1,0:T(8,128)(2,1)} %get-tuple-element.34), calls=%async_computation.1 | async-start | bytes 2097152 | tf_op jit(solution)/shard_map/all_to_all | solution.py:322
  47.6 14.9 %group_attention.3 = (bf16[256,512]{1,0:T(8,128)(2,1)}, bf16[256,512]{1,0:T(8,128)(2,1)}, bf16[2,256,512]{2,1,0:T(8,128)(2,1)}, f32[8,128]{1,0:T(8,128)}, bf16[8,512,128]{2,1,0:T(8,128)(2,1)}) custom-call(s32[1]{0:T(128)} %bitcast.refs_0_, s32[64]{0:T(128)} %and_select_fusion.refs_1_, f32[16]{0:T(128)} %refs_2_.3, bf16[256,2048]{1,0:T(8,128)(2,1)} %bitcast.80, ...), custom_call_target="tpu_custom_call" | custom-call | flops 4429185024 | bytes 6291456 | tf_op jit(solution)/shard_map/group_attention/pallas_call | solution.py:208
  62.8 0.5 collective-permute-start.6
  63.3 2.4 %collective-permute-done.1 = f32[8,128]{1,0:T(8,128)S(1)} collective-permute-done((f32[8,128]{1,0:T(8,128)}, f32[8,128]{1,0:T(8,128)S(1)}, u32[]{:S(2)}, u32[]{:S(2)}) %collective-permute-start.1) | collective-permute-done | bytes 4128 | tf_op jit(solution)/shard_map/ppermute | solution.py:242
  65.7 0.7 add.175
  66.4 2.0 %collective-permute-start.2 = (f32[8,128]{1,0:T(8,128)S(1)}, f32[8,128]{1,0:T(8,128)S(1)}, u32[]{:S(2)}, u32[]{:S(2)}) collective-permute-start(f32[8,128]{1,0:T(8,128)S(1)} %add.175), channel_id=1, source_target_pairs={{0,1},{1,0},{2,3},{3,2},{4,5},{5,4},{6,7},{7,6},{8,9},{9,8},{10,11... | collective-permute-start | bytes 12296 | tf_op jit(solution)/shard_map/ppermute | solution.py:234
  68.4 2.6 %collective-permute-start.3 = (f32[8,128]{1,0:T(8,128)S(1)}, f32[8,128]{1,0:T(8,128)S(1)}, u32[]{:S(2)}, u32[]{:S(2)}) collective-permute-start(f32[8,128]{1,0:T(8,128)S(1)} %add.175), channel_id=1, source_target_pairs={{0,2},{1,3},{2,0},{3,1},{4,6},{5,7},{6,4},{7,5},{8,10},{9,11},{10,... | collective-permute-start | bytes 12296 | tf_op jit(solution)/shard_map/ppermute | solution.py:234
  71.0 3.7 %all-to-all-start.3 = ((bf16[8,512,128]{2,1,0:T(8,128)(2,1)}), bf16[8,512,128]{2,1,0:T(8,128)(2,1)S(1)}, u32[]{:S(2)}, u32[]{:S(2)}) async-start(bf16[8,512,128]{2,1,0:T(8,128)(2,1)} %get-tuple-element.54), calls=%async_computation.3 | async-start | bytes 2097152 | tf_op jit(solution)/shard_map/all_to_all | solution.py:324
  74.6 1.7 %collective-permute-done.4 = f32[8,128]{1,0:T(8,128)S(1)} collective-permute-done((f32[8,128]{1,0:T(8,128)S(1)}, f32[8,128]{1,0:T(8,128)S(1)}, u32[]{:S(2)}, u32[]{:S(2)}) %collective-permute-start.4) | collective-permute-done | bytes 4128 | tf_op jit(solution)/shard_map/ppermute | solution.py:234
  76.4 1.4 %fusion.2 = (bf16[1,512,128]{2,1,0:T(8,128)(2,1)S(1)}, bf16[1,512,128]{2,1,0:T(8,128)(2,1)S(1)}, bf16[1,512,128]{2,1,0:T(8,128)(2,1)S(1)}, bf16[1,512,128]{2,1,0...) fusion(bf16[8,512,128]{2,1,0:T(8,128)(2,1)} %all-to-all-done.1), kind=kLoop, calls=%fused_computation.31 | loop fusion | bytes 2097152 | tf_op jit(solution)/shard_map/slice | solution.py:346
  77.9 0.8 copy-done.4
  79.0 1.1 %maximum_bitcast_fusion.1 = bf16[1,256,2048]{2,1,0:T(8,128)(2,1)} fusion(bf16[256,512]{1,0:T(8,128)(2,1)S(1)} %get-tuple-element.78, bf16[256,512]{1,0:T(8,128)(2,1)S(1)} %get-tuple-element.76, bf16[256,512]{1,0:T(8,128)(2,1)S(1)} %get-tuple-element.77, bf16[256,512]{1,0:T(8,128)(2,1)S(1)} %get-tuple-element.75), kind=kLoop, calls=%fused_computation.2 | loop fusion | flops 4194304 | bytes 2097152 | tf_op jit(solution)/shard_map/broadcast_in_dim | solution.py:338
  80.2 1.1 %maximum_bitcast_fusion = bf16[1,256,2048]{2,1,0:T(8,128)(2,1)} fusion(bf16[256,512]{1,0:T(8,128)(2,1)S(1)} %get-tuple-element.93, bf16[256,512]{1,0:T(8,128)(2,1)S(1)} %get-tuple-element.91, bf16[256,512]{1,0:T(8,128)(2,1)S(1)} %get-tuple-element.94, bf16[256,512]{1,0:T(8,128)(2,1)S(1)} %get-tuple-element.92), kind=kLoop, calls=%fused_computation.1 | loop fusion | flops 4194304 | bytes 2097152 | tf_op jit(solution)/shard_map/broadcast_in_dim | solution.py:337
  81.3 1.4 %collective-permute-start.7 = (f32[8,128]{1,0:T(8,128)S(1)}, f32[8,128]{1,0:T(8,128)S(1)}, u32[]{:S(2)}, u32[]{:S(2)}) collective-permute-start(f32[8,128]{1,0:T(8,128)S(1)} %add_add_fusion.1), channel_id=1, source_target_pairs={{0,8},{4,12},{8,0},{12,4},{16,24},{20,28},{24,16},{28,20},{1,9},{5... | collective-permute-start | bytes 12296 | tf_op jit(solution)/shard_map/ppermute | solution.py:234
  82.7 1.5 %collective-permute-start.8 = (f32[8,128]{1,0:T(8,128)S(1)}, f32[8,128]{1,0:T(8,128)S(1)}, u32[]{:S(2)}, u32[]{:S(2)}) collective-permute-start(f32[8,128]{1,0:T(8,128)S(1)} %add_add_fusion.1), channel_id=1, source_target_pairs={{0,16},{4,20},{8,24},{12,28},{16,0},{20,4},{24,8},{28,12},{1,17},{... | collective-permute-start | bytes 12296 | tf_op jit(solution)/shard_map/ppermute | solution.py:234
  84.2 0.5 collective-permute-start.9
  84.8 4.5 %collective-permute-done.7 = f32[8,128]{1,0:T(8,128)S(1)} collective-permute-done((f32[8,128]{1,0:T(8,128)S(1)}, f32[8,128]{1,0:T(8,128)S(1)}, u32[]{:S(2)}, u32[]{:S(2)}) %collective-permute-start.7) | collective-permute-done | bytes 4128 | tf_op jit(solution)/shard_map/ppermute | solution.py:234
  89.3 0.9 %collective-permute-done.9 = f32[8,128]{1,0:T(8,128)S(1)} collective-permute-done((f32[8,128]{1,0:T(8,128)S(1)}, f32[8,128]{1,0:T(8,128)S(1)}, u32[]{:S(2)}, u32[]{:S(2)}) %collective-permute-start.9) | collective-permute-done | bytes 4128 | tf_op jit(solution)/shard_map/ppermute | solution.py:234
  90.2 0.5 multiply_bitcast_fusion
  91.0 0.7 maximum_bitcast_fusion.3
  91.7 0.7 maximum_bitcast_fusion.2
  (38 shorter events, 1.3 us)
Async XLA Ops:
  2.6 5.3 %copy-start = (bf16[1,256,2048]{2,1,0:T(8,128)(2,1)S(1)}, bf16[1,256,2048]{2,1,0:T(8,128)(2,1)}, u32[]{:S(2)}) copy-start(bf16[1,256,2048]{2,1,0:T(8,128)(2,1)} %param.6) | copy-start | bytes 3145732
  2.6 5.3 %copy-start.1 = (bf16[1,256,2048]{2,1,0:T(8,128)(2,1)S(1)}, bf16[1,256,2048]{2,1,0:T(8,128)(2,1)}, u32[]{:S(2)}) copy-start(bf16[1,256,2048]{2,1,0:T(8,128)(2,1)} %param.10) | copy-start | bytes 3145732
  2.7 20.8 %all-to-all-start = ((bf16[8,2,2,128,128]{4,3,2,1,0:T(8,128)(2,1)}), bf16[8,2,2,128,128]{4,3,2,1,0:T(8,128)(2,1)}, u32[]{:S(2)}, u32[]{:S(2)}) async-start(bf16[8,2,2,128,128]{4,3,2,1,0:T(8,128)(2,1)} %spread_keys_values.2), calls=%async_computation | async-start | bytes 2097152 | tf_op jit(solution)/shard_map/all_to_all | solution.py:301
  8.0 0.7 slice-start
  10.5 17.2 %collective-permute-start = (bf16[2,256,1024]{2,1,0:T(8,128)(2,1)}, bf16[2,256,1024]{2,1,0:T(8,128)(2,1)}, u32[]{:S(2)}, u32[]{:S(2)}) collective-permute-start(bf16[2,256,1024]{2,1,0:T(8,128)(2,1)} %pad_maximum_fusion), channel_id=1, source_target_pairs={{0,4},{4,0},{8,12},{12,8},{16,20},{20,16},{24,28},{28,24},{1,5},{5... | collective-permute-start | bytes 3145736 | tf_op jit(solution)/shard_map/ppermute | solution.py:310
  23.5 19.7 %all-to-all-start.2 = ((bf16[8,2,2,128,128]{4,3,2,1,0:T(8,128)(2,1)}), bf16[8,2,2,128,128]{4,3,2,1,0:T(8,128)(2,1)}, u32[]{:S(2)}, u32[]{:S(2)}) async-start(bf16[8,2,2,128,128]{4,3,2,1,0:T(8,128)(2,1)} %spread_keys_values.3), calls=%async_computation.2 | async-start | bytes 2097152 | tf_op jit(solution)/shard_map/all_to_all | solution.py:301
  43.2 19.7 %all-to-all-start.1 = ((bf16[8,512,128]{2,1,0:T(8,128)(2,1)}), bf16[8,512,128]{2,1,0:T(8,128)(2,1)}, u32[]{:S(2)}, u32[]{:S(2)}) async-start(bf16[8,512,128]{2,1,0:T(8,128)(2,1)} %get-tuple-element.34), calls=%async_computation.1 | async-start | bytes 2097152 | tf_op jit(solution)/shard_map/all_to_all | solution.py:322
  47.6 15.2 %copy-start.6 = (bf16[2,256,512]{2,1,0:T(8,128)(2,1)S(1)}, bf16[2,256,512]{2,1,0:T(8,128)(2,1)}, u32[]{:S(2)}) copy-start(bf16[2,256,512]{2,1,0:T(8,128)(2,1)} %get-tuple-element.42) | copy-start | bytes 1572868
  62.8 13.6 %collective-permute-start.5 = (bf16[2,256,512]{2,1,0:T(8,128)(2,1)S(1)}, bf16[2,256,512]{2,1,0:T(8,128)(2,1)S(1)}, u32[]{:S(2)}, u32[]{:S(2)}) collective-permute-start(bf16[2,256,512]{2,1,0:T(8,128)(2,1)S(1)} %copy-done.6), channel_id=1, source_target_pairs={{0,4},{4,0},{8,12},{12,8},{16,20},{20,16},{24,28},{28,24},{1,5},{5... | collective-permute-start | bytes 1572872 | tf_op jit(solution)/shard_map/ppermute | solution.py:326
  62.8 13.6 %collective-permute-start.6 = (bf16[2,256,512]{2,1,0:T(8,128)(2,1)}, bf16[2,256,512]{2,1,0:T(8,128)(2,1)S(1)}, u32[]{:S(2)}, u32[]{:S(2)}) collective-permute-start(bf16[2,256,512]{2,1,0:T(8,128)(2,1)} %get-tuple-element.43), channel_id=1, source_target_pairs={{0,4},{4,0},{8,12},{12,8},{16,20},{20,16},{24,28},{28,24},{1,5},{5... | collective-permute-start | bytes 1572872 | tf_op jit(solution)/shard_map/ppermute | solution.py:326
  63.3 2.4 %collective-permute-start.1 = (f32[8,128]{1,0:T(8,128)}, f32[8,128]{1,0:T(8,128)S(1)}, u32[]{:S(2)}, u32[]{:S(2)}) collective-permute-start(f32[8,128]{1,0:T(8,128)} %get-tuple-element.40), channel_id=1, source_target_pairs={{0,4},{4,0},{8,12},{12,8},{16,20},{20,16},{24,28},{28,24},{1,5},{5... | collective-permute-start | bytes 12296 | tf_op jit(solution)/shard_map/ppermute | solution.py:242
  66.4 8.3 %collective-permute-start.2 = (f32[8,128]{1,0:T(8,128)S(1)}, f32[8,128]{1,0:T(8,128)S(1)}, u32[]{:S(2)}, u32[]{:S(2)}) collective-permute-start(f32[8,128]{1,0:T(8,128)S(1)} %add.175), channel_id=1, source_target_pairs={{0,1},{1,0},{2,3},{3,2},{4,5},{5,4},{6,7},{7,6},{8,9},{9,8},{10,11... | collective-permute-start | bytes 12296 | tf_op jit(solution)/shard_map/ppermute | solution.py:234
  68.4 6.3 %collective-permute-start.3 = (f32[8,128]{1,0:T(8,128)S(1)}, f32[8,128]{1,0:T(8,128)S(1)}, u32[]{:S(2)}, u32[]{:S(2)}) collective-permute-start(f32[8,128]{1,0:T(8,128)S(1)} %add.175), channel_id=1, source_target_pairs={{0,2},{1,3},{2,0},{3,1},{4,6},{5,7},{6,4},{7,5},{8,10},{9,11},{10,... | collective-permute-start | bytes 12296 | tf_op jit(solution)/shard_map/ppermute | solution.py:234
  71.0 5.4 %collective-permute-start.4 = (f32[8,128]{1,0:T(8,128)S(1)}, f32[8,128]{1,0:T(8,128)S(1)}, u32[]{:S(2)}, u32[]{:S(2)}) collective-permute-start(f32[8,128]{1,0:T(8,128)S(1)} %add.175), channel_id=1, source_target_pairs={{0,3},{1,2},{2,1},{3,0},{4,7},{5,6},{6,5},{7,4},{8,11},{9,10},{10,... | collective-permute-start | bytes 12296 | tf_op jit(solution)/shard_map/ppermute | solution.py:234
  71.0 19.8 %all-to-all-start.3 = ((bf16[8,512,128]{2,1,0:T(8,128)(2,1)}), bf16[8,512,128]{2,1,0:T(8,128)(2,1)S(1)}, u32[]{:S(2)}, u32[]{:S(2)}) async-start(bf16[8,512,128]{2,1,0:T(8,128)(2,1)} %get-tuple-element.54), calls=%async_computation.3 | async-start | bytes 2097152 | tf_op jit(solution)/shard_map/all_to_all | solution.py:324
  76.4 1.4 %copy-start.2 = (bf16[256,512]{1,0:T(8,128)(2,1)S(1)}, bf16[256,512]{1,0:T(8,128)(2,1)}, u32[]{:S(2)}) copy-start(bf16[256,512]{1,0:T(8,128)(2,1)} %get-tuple-element.41) | copy-start | bytes 786436
  76.4 1.4 %copy-start.3 = (bf16[256,512]{1,0:T(8,128)(2,1)S(1)}, bf16[256,512]{1,0:T(8,128)(2,1)}, u32[]{:S(2)}) copy-start(bf16[256,512]{1,0:T(8,128)(2,1)} %get-tuple-element.48) | copy-start | bytes 786436
  77.8 1.0 %copy-start.4 = (bf16[256,512]{1,0:T(8,128)(2,1)S(1)}, bf16[256,512]{1,0:T(8,128)(2,1)}, u32[]{:S(2)}) copy-start(bf16[256,512]{1,0:T(8,128)(2,1)} %get-tuple-element.46) | copy-start | bytes 786436
  77.9 1.0 %copy-start.5 = (bf16[256,512]{1,0:T(8,128)(2,1)S(1)}, bf16[256,512]{1,0:T(8,128)(2,1)}, u32[]{:S(2)}) copy-start(bf16[256,512]{1,0:T(8,128)(2,1)} %get-tuple-element.49) | copy-start | bytes 786436
  81.3 8.0 %collective-permute-start.7 = (f32[8,128]{1,0:T(8,128)S(1)}, f32[8,128]{1,0:T(8,128)S(1)}, u32[]{:S(2)}, u32[]{:S(2)}) collective-permute-start(f32[8,128]{1,0:T(8,128)S(1)} %add_add_fusion.1), channel_id=1, source_target_pairs={{0,8},{4,12},{8,0},{12,4},{16,24},{20,28},{24,16},{28,20},{1,9},{5... | collective-permute-start | bytes 12296 | tf_op jit(solution)/shard_map/ppermute | solution.py:234
  82.7 6.5 %collective-permute-start.8 = (f32[8,128]{1,0:T(8,128)S(1)}, f32[8,128]{1,0:T(8,128)S(1)}, u32[]{:S(2)}, u32[]{:S(2)}) collective-permute-start(f32[8,128]{1,0:T(8,128)S(1)} %add_add_fusion.1), channel_id=1, source_target_pairs={{0,16},{4,20},{8,24},{12,28},{16,0},{20,4},{24,8},{28,12},{1,17},{... | collective-permute-start | bytes 12296 | tf_op jit(solution)/shard_map/ppermute | solution.py:234
  84.2 6.0 %collective-permute-start.9 = (f32[8,128]{1,0:T(8,128)S(1)}, f32[8,128]{1,0:T(8,128)S(1)}, u32[]{:S(2)}, u32[]{:S(2)}) collective-permute-start(f32[8,128]{1,0:T(8,128)S(1)} %add_add_fusion.1), channel_id=1, source_target_pairs={{0,24},{4,28},{8,16},{12,20},{16,8},{20,12},{24,0},{28,4},{1,25},{... | collective-permute-start | bytes 12296 | tf_op jit(solution)/shard_map/ppermute | solution.py:234

commit v12 on v11

--- a/solution.py
+++ b/solution.py
@@ -13,7 +13,7 @@
 HD = 128
 BLOCK = 128
 QPG = HEADS // KV_HEADS
-CHUNK = 11
+CHUNK = 6
 ROWS = QPG * BLOCK
 TAIL = 8
 VMEM_BYTES = 63 * 2**20
@@ -322,9 +322,7 @@
             grads[0] = lax.all_to_all(kv_grads, "ctx", 0, 0)
     grads, sibs, tau_last = lax.optimization_barrier((grads, sibs, tau_rows[1]))
     grads[1] = lax.all_to_all(grads[1], "ctx", 0, 0)
-    sibs, grads[0] = lax.optimization_barrier(
-        ([lax.ppermute(sib, "ctx", swap) for sib in sibs], grads[0])
-    )
+    sibs = lax.optimization_barrier([lax.ppermute(sib, "ctx", swap) for sib in sibs])
     att_parts, dq_parts = (
         [(own[which], sib[which]) for own, sib in zip(owns, sibs)] for which in range(2)
     )
@@ -349,10 +347,8 @@
                 columns.append(total.reshape(tokens, HD).astype(jnp.bfloat16))
         return columns
 
-    scale_total, (attended, query_grad, first) = total_everywhere(
-        tau_last, (attended, query_grad, summed(0))
-    )
-    second = summed(1)
+    scale_total, (attended, query_grad) = total_everywhere(tau_last, (attended, query_grad))
+    first, second = summed(0), summed(1)
     key_grad, value_grad = (
         jnp.concatenate([first[i], second[i], first[i + 1], second[i + 1]], axis=1)[None]
         for i in (0, 2)

time: 93.1 us -> 92.7 us (level)
  waiting for transfers between devices: 21 us -> 22 us
  local copies, waits for them, and re-layouts: 3.27 us -> 2.29 us
    ppermute x6, waiting for transfers between devices: 7.16 us -> 9.66 us  [partners(): lax.ppermute(x, axis, [(i, i ^ d) for i in range(size)])]
    ppermute x1, waiting for transfers between devices: 2.36 us -> 0.01 us  [total_everywhere(): x = x + lax.ppermute(x, 'ctx', [(i, i ^ 1) for i in range(ctx)])]
    select_n x2, other arithmetic: 0.15 us -> 1.16 us  [by_group(): jnp.where(core == c // 2, parts[c % 2][0], parts[c % 2][1])]
  transfers between devices with their start and end apart: 14 -> 14, of which waited for: 7 -> 7; matrix products, arithmetic and copies ran while one was open for 8% -> 8% of each run, Pallas kernels for 34% -> 33%
where the time goes in v12:
time: 92.7 us; the launch traced here: 92.1 us
  Pallas kernels  32.8 us (35%)
  starting transfers between devices  26.9 us (29%)
  waiting for transfers between devices  22 us (24%)
  other arithmetic  7.21 us (8%)
  local copies, waits for them, and re-layouts  2.29 us (2%)
    pallas_call x2, Pallas kernels, run_group(): pl.pallas_call(functools.partial(group_kernel, gi, devices, local_blocks,...  28.9 us
    all_to_all x2, waiting for transfers between devices, kv_for(): arrived = lax.all_to_all(spread(gi, ctx, k0, v0), 'ctx', 0, 0)  11.6 us
    ppermute x6, waiting for transfers between devices, partners(): lax.ppermute(x, axis, [(i, i ^ d) for i in range(size)])  9.66 us
    all_to_all x2, starting transfers between devices, kv_for(): arrived = lax.all_to_all(spread(gi, ctx, k0, v0), 'ctx', 0, 0)  9.56 us
    ppermute x6, starting transfers between devices, partners(): lax.ppermute(x, axis, [(i, i ^ d) for i in range(size)])  8.16 us
    all_to_all x1, starting transfers between devices, body(): grads[0] = lax.all_to_all(kv_grads, 'ctx', 0, 0)  4.43 us
    pallas_call x2, Pallas kernels, spread(): pl.pallas_call(kernel, grid=(1,), in_specs=[column(gi), column(2 + gi)] *...  3.9 us
    all_to_all x1, starting transfers between devices, body(): grads[1] = lax.all_to_all(grads[1], 'ctx', 0, 0)  3.7 us
  transfers between devices with their start and end apart: 14, of which 7 were waited for; matrix products, arithmetic and copies ran while one was open for 8% of the time, Pallas kernels for 33%

profile of v12, /device:TPU:0, one launch (start us, length us, event | category | flops | bytes accessed | tf_op | source)
XLA Modules:
  0.0 92.1 jit_solution(10599802872441397267)
XLA Ops:
  0.6 2.0 %spread_keys_values.2 = bf16[8,2,2,128,128]{4,3,2,1,0:T(8,128)(2,1)} custom-call(bf16[256,512]{1,0:T(8,128)(2,1)} %bitcast.55, bf16[256,512]{1,0:T(8,128)(2,1)} %bitcast.56, bf16[256,512]{1,0:T(8,128)(2,1)} %bitcast.59, bf16[256,512]{1,0:T(8,128)(2,1)} %bitcast.60), custom_call_target="tpu_custom_call" | custom-call | tf_op jit(solution)/shard_map/spread_keys_values/pallas_call | solution.py:273
  2.6 5.3 %all-to-all-start = ((bf16[8,2,2,128,128]{4,3,2,1,0:T(8,128)(2,1)}), bf16[8,2,2,128,128]{4,3,2,1,0:T(8,128)(2,1)}, u32[]{:S(2)}, u32[]{:S(2)}) async-start(bf16[8,2,2,128,128]{4,3,2,1,0:T(8,128)(2,1)} %spread_keys_values.2), calls=%async_computation | async-start | bytes 2097152 | tf_op jit(solution)/shard_map/all_to_all | solution.py:301
  8.0 0.1 constant_dynamic-slice_fusion
  8.1 0.6 slice-done
  8.8 1.1 %pad_maximum_fusion = bf16[2,256,1024]{2,1,0:T(8,128)(2,1)} fusion(bf16[1,256,1024]{2,1,0:T(8,128)(2,1)S(1)} %get-tuple-element.85, bf16[1,256,1024]{2,1,0:T(8,128)(2,1)S(1)} %get-tuple-element.86), kind=kLoop, calls=%fused_computation | loop fusion | flops 524288 | bytes 2097152 | tf_op jit(solution)/shard_map/stack | solution.py:309
  9.9 0.5 and_select_fusion.refs_1_
  10.4 0.5 collective-permute-start
  10.9 2.0 %spread_keys_values.3 = bf16[8,2,2,128,128]{4,3,2,1,0:T(8,128)(2,1)} custom-call(bf16[256,512]{1,0:T(8,128)(2,1)} %bitcast.57, bf16[256,512]{1,0:T(8,128)(2,1)} %bitcast.58, bf16[256,512]{1,0:T(8,128)(2,1)} %bitcast.61, bf16[256,512]{1,0:T(8,128)(2,1)} %bitcast.62), custom_call_target="tpu_custom_call" | custom-call | tf_op jit(solution)/shard_map/spread_keys_values/pallas_call | solution.py:273
  12.8 10.6 %all-to-all-done = bf16[8,2,2,128,128]{4,3,2,1,0:T(8,128)(2,1)} async-done(((bf16[8,2,2,128,128]{4,3,2,1,0:T(8,128)(2,1)}), bf16[8,2,2,128,128]{4,3,2,1,0:T(8,128)(2,1)}, u32[]{:S(2)}, u32[]{:S(2)}) %all-to-all-start) | async-done | bytes 1048608 | tf_op jit(solution)/shard_map/all_to_all | solution.py:301
  23.4 4.2 %all-to-all-start.2 = ((bf16[8,2,2,128,128]{4,3,2,1,0:T(8,128)(2,1)}), bf16[8,2,2,128,128]{4,3,2,1,0:T(8,128)(2,1)}, u32[]{:S(2)}, u32[]{:S(2)}) async-start(bf16[8,2,2,128,128]{4,3,2,1,0:T(8,128)(2,1)} %spread_keys_values.3), calls=%async_computation.2 | async-start | bytes 2097152 | tf_op jit(solution)/shard_map/all_to_all | solution.py:301
  27.7 14.4 %group_attention.2 = (bf16[256,512]{1,0:T(8,128)(2,1)}, bf16[256,512]{1,0:T(8,128)(2,1)}, bf16[2,256,512]{2,1,0:T(8,128)(2,1)}, f32[8,128]{1,0:T(8,128)}, bf16[8,512,128]{2,1,0:T(8,128)(2,1)}) custom-call(s32[1]{0:T(128)} %bitcast.refs_0_, s32[64]{0:T(128)} %and_select_fusion.refs_1_, f32[16]{0:T(128)} %refs_2_.3, bf16[256,2048]{1,0:T(8,128)(2,1)} %bitcast.79, ...), custom_call_target="tpu_custom_call" | custom-call | flops 4429185024 | bytes 6291456 | tf_op jit(solution)/shard_map/group_attention/pallas_call | solution.py:208
  42.1 1.0 %all-to-all-done.2 = bf16[8,2,2,128,128]{4,3,2,1,0:T(8,128)(2,1)} async-done(((bf16[8,2,2,128,128]{4,3,2,1,0:T(8,128)(2,1)}), bf16[8,2,2,128,128]{4,3,2,1,0:T(8,128)(2,1)}, u32[]{:S(2)}, u32[]{:S(2)}) %all-to-all-start.2) | async-done | bytes 1048608 | tf_op jit(solution)/shard_map/all_to_all | solution.py:301
  43.1 4.4 %all-to-all-start.1 = ((bf16[8,512,128]{2,1,0:T(8,128)(2,1)}), bf16[8,512,128]{2,1,0:T(8,128)(2,1)}, u32[]{:S(2)}, u32[]{:S(2)}) async-start(bf16[8,512,128]{2,1,0:T(8,128)(2,1)} %get-tuple-element.29), calls=%async_computation.1 | async-start | bytes 2097152 | tf_op jit(solution)/shard_map/all_to_all | solution.py:322
  47.6 14.5 %group_attention.3 = (bf16[256,512]{1,0:T(8,128)(2,1)}, bf16[256,512]{1,0:T(8,128)(2,1)}, bf16[2,256,512]{2,1,0:T(8,128)(2,1)}, f32[8,128]{1,0:T(8,128)}, bf16[8,512,128]{2,1,0:T(8,128)(2,1)}) custom-call(s32[1]{0:T(128)} %bitcast.refs_0_, s32[64]{0:T(128)} %and_select_fusion.refs_1_, f32[16]{0:T(128)} %refs_2_.3, bf16[256,2048]{1,0:T(8,128)(2,1)} %bitcast.80, ...), custom_call_target="tpu_custom_call" | custom-call | flops 4429185024 | bytes 6291456 | tf_op jit(solution)/shard_map/group_attention/pallas_call | solution.py:208
  62.0 0.8 all-to-all-done.1
  62.8 0.5 collective-permute-start.6
  63.3 1.4 %fusion.1 = (bf16[1,512,128]{2,1,0:T(8,128)(2,1)S(1)}, bf16[1,512,128]{2,1,0:T(8,128)(2,1)S(1)}, bf16[1,512,128]{2,1,0:T(8,128)(2,1)S(1)}, bf16[1,512,128]{2,1,0...) fusion(bf16[8,512,128]{2,1,0:T(8,128)(2,1)} %all-to-all-done.1), kind=kLoop, calls=%fused_computation.30 | loop fusion | bytes 2097152 | tf_op jit(solution)/shard_map/slice | solution.py:344
  64.7 3.7 %all-to-all-start.3 = ((bf16[8,512,128]{2,1,0:T(8,128)(2,1)}), bf16[8,512,128]{2,1,0:T(8,128)(2,1)S(1)}, u32[]{:S(2)}, u32[]{:S(2)}) async-start(bf16[8,512,128]{2,1,0:T(8,128)(2,1)} %get-tuple-element.47), calls=%async_computation.3 | async-start | bytes 2097152 | tf_op jit(solution)/shard_map/all_to_all | solution.py:324
  68.4 2.1 %collective-permute-start.2 = (f32[8,128]{1,0:T(8,128)S(1)}, f32[8,128]{1,0:T(8,128)S(1)}, u32[]{:S(2)}, u32[]{:S(2)}) collective-permute-start(f32[8,128]{1,0:T(8,128)S(1)} %add.175), channel_id=1, source_target_pairs={{0,1},{1,0},{2,3},{3,2},{4,5},{5,4},{6,7},{7,6},{8,9},{9,8},{10,11... | collective-permute-start | bytes 12296 | tf_op jit(solution)/shard_map/ppermute | solution.py:234
  70.5 2.6 %collective-permute-start.3 = (f32[8,128]{1,0:T(8,128)S(1)}, f32[8,128]{1,0:T(8,128)S(1)}, u32[]{:S(2)}, u32[]{:S(2)}) collective-permute-start(f32[8,128]{1,0:T(8,128)S(1)} %add.175), channel_id=1, source_target_pairs={{0,2},{1,3},{2,0},{3,1},{4,6},{5,7},{6,4},{7,5},{8,10},{9,11},{10,... | collective-permute-start | bytes 12296 | tf_op jit(solution)/shard_map/ppermute | solution.py:234
  73.2 1.8 %collective-permute-done.3 = f32[8,128]{1,0:T(8,128)S(1)} collective-permute-done((f32[8,128]{1,0:T(8,128)S(1)}, f32[8,128]{1,0:T(8,128)S(1)}, u32[]{:S(2)}, u32[]{:S(2)}) %collective-permute-start.3) | collective-permute-done | bytes 4128 | tf_op jit(solution)/shard_map/ppermute | solution.py:234
  75.0 3.5 %collective-permute-done.4 = f32[8,128]{1,0:T(8,128)S(1)} collective-permute-done((f32[8,128]{1,0:T(8,128)S(1)}, f32[8,128]{1,0:T(8,128)S(1)}, u32[]{:S(2)}, u32[]{:S(2)}) %collective-permute-start.4) | collective-permute-done | bytes 4128 | tf_op jit(solution)/shard_map/ppermute | solution.py:234
  78.6 1.1 %bitcast_select_fusion.3 = (bf16[256,512]{1,0:T(8,128)(2,1)S(1)}, bf16[256,512]{1,0:T(8,128)(2,1)S(1)}, bf16[256,512]{1,0:T(8,128)(2,1)S(1)}, bf16[256,512]{1,0:T(8,128)(2,1)S(1)}) fusion(bf16[256,512]{1,0:T(8,128)(2,1)} %get-tuple-element.42, pred[]{:T(512)S(6)} %eq.8, bf16[2,256,512]{2,1,0:T(8,128)(2,1)S(1)} %collective-permute-done.5, pred[]{:T(512)S(6)} %eq.9, ...), kind=kLoop, calls=%fused_computation.8 | loop fusion | flops 524288 | bytes 2097154 | tf_op jit(solution)/shard_map/jit(_where)/select_n | solution.py:332
  79.7 1.1 %maximum_bitcast_fusion.1 = bf16[1,256,2048]{2,1,0:T(8,128)(2,1)} fusion(bf16[256,512]{1,0:T(8,128)(2,1)S(1)} %get-tuple-element.68, bf16[256,512]{1,0:T(8,128)(2,1)S(1)} %get-tuple-element.66, bf16[256,512]{1,0:T(8,128)(2,1)S(1)} %get-tuple-element.67, bf16[256,512]{1,0:T(8,128)(2,1)S(1)} %get-tuple-element.65), kind=kLoop, calls=%fused_computation.2 | loop fusion | flops 4194304 | bytes 2097152 | tf_op jit(solution)/shard_map/broadcast_in_dim | solution.py:336
  80.8 1.1 %maximum_bitcast_fusion = bf16[1,256,2048]{2,1,0:T(8,128)(2,1)} fusion(bf16[256,512]{1,0:T(8,128)(2,1)S(1)} %get-tuple-element.83, bf16[256,512]{1,0:T(8,128)(2,1)S(1)} %get-tuple-element.81, bf16[256,512]{1,0:T(8,128)(2,1)S(1)} %get-tuple-element.84, bf16[256,512]{1,0:T(8,128)(2,1)S(1)} %get-tuple-element.82), kind=kLoop, calls=%fused_computation.1 | loop fusion | flops 4194304 | bytes 2097152 | tf_op jit(solution)/shard_map/broadcast_in_dim | solution.py:335
  81.9 1.9 %collective-permute-start.7 = (f32[8,128]{1,0:T(8,128)S(1)}, f32[8,128]{1,0:T(8,128)S(1)}, u32[]{:S(2)}, u32[]{:S(2)}) collective-permute-start(f32[8,128]{1,0:T(8,128)S(1)} %add_add_fusion.1), channel_id=1, source_target_pairs={{0,8},{4,12},{8,0},{12,4},{16,24},{20,28},{24,16},{28,20},{1,9},{5... | collective-permute-start | bytes 12296 | tf_op jit(solution)/shard_map/ppermute | solution.py:234
  83.8 1.5 %collective-permute-start.8 = (f32[8,128]{1,0:T(8,128)S(1)}, f32[8,128]{1,0:T(8,128)S(1)}, u32[]{:S(2)}, u32[]{:S(2)}) collective-permute-start(f32[8,128]{1,0:T(8,128)S(1)} %add_add_fusion.1), channel_id=1, source_target_pairs={{0,16},{4,20},{8,24},{12,28},{16,0},{20,4},{24,8},{28,12},{1,17},{... | collective-permute-start | bytes 12296 | tf_op jit(solution)/shard_map/ppermute | solution.py:234
  85.5 1.9 %collective-permute-done.8 = f32[8,128]{1,0:T(8,128)S(1)} collective-permute-done((f32[8,128]{1,0:T(8,128)S(1)}, f32[8,128]{1,0:T(8,128)S(1)}, u32[]{:S(2)}, u32[]{:S(2)}) %collective-permute-start.8) | collective-permute-done | bytes 4128 | tf_op jit(solution)/shard_map/ppermute | solution.py:234
  87.5 2.4 %collective-permute-done.9 = f32[8,128]{1,0:T(8,128)S(1)} collective-permute-done((f32[8,128]{1,0:T(8,128)S(1)}, f32[8,128]{1,0:T(8,128)S(1)}, u32[]{:S(2)}, u32[]{:S(2)}) %collective-permute-start.9) | collective-permute-done | bytes 4128 | tf_op jit(solution)/shard_map/ppermute | solution.py:234
  89.8 0.5 multiply_bitcast_fusion
  90.6 0.7 maximum_bitcast_fusion.3
  91.3 0.7 maximum_bitcast_fusion.2
  (36 shorter events, 0.8 us)
Async XLA Ops:
  2.6 5.3 %copy-start = (bf16[1,256,2048]{2,1,0:T(8,128)(2,1)S(1)}, bf16[1,256,2048]{2,1,0:T(8,128)(2,1)}, u32[]{:S(2)}) copy-start(bf16[1,256,2048]{2,1,0:T(8,128)(2,1)} %param.6) | copy-start | bytes 3145732
  2.6 5.3 %copy-start.1 = (bf16[1,256,2048]{2,1,0:T(8,128)(2,1)S(1)}, bf16[1,256,2048]{2,1,0:T(8,128)(2,1)}, u32[]{:S(2)}) copy-start(bf16[1,256,2048]{2,1,0:T(8,128)(2,1)} %param.10) | copy-start | bytes 3145732
  2.6 20.8 %all-to-all-start = ((bf16[8,2,2,128,128]{4,3,2,1,0:T(8,128)(2,1)}), bf16[8,2,2,128,128]{4,3,2,1,0:T(8,128)(2,1)}, u32[]{:S(2)}, u32[]{:S(2)}) async-start(bf16[8,2,2,128,128]{4,3,2,1,0:T(8,128)(2,1)} %spread_keys_values.2), calls=%async_computation | async-start | bytes 2097152 | tf_op jit(solution)/shard_map/all_to_all | solution.py:301
  7.9 0.7 slice-start
  10.4 17.3 %collective-permute-start = (bf16[2,256,1024]{2,1,0:T(8,128)(2,1)}, bf16[2,256,1024]{2,1,0:T(8,128)(2,1)}, u32[]{:S(2)}, u32[]{:S(2)}) collective-permute-start(bf16[2,256,1024]{2,1,0:T(8,128)(2,1)} %pad_maximum_fusion), channel_id=1, source_target_pairs={{0,4},{4,0},{8,12},{12,8},{16,20},{20,16},{24,28},{28,24},{1,5},{5... | collective-permute-start | bytes 3145736 | tf_op jit(solution)/shard_map/ppermute | solution.py:310
  23.4 19.7 %all-to-all-start.2 = ((bf16[8,2,2,128,128]{4,3,2,1,0:T(8,128)(2,1)}), bf16[8,2,2,128,128]{4,3,2,1,0:T(8,128)(2,1)}, u32[]{:S(2)}, u32[]{:S(2)}) async-start(bf16[8,2,2,128,128]{4,3,2,1,0:T(8,128)(2,1)} %spread_keys_values.3), calls=%async_computation.2 | async-start | bytes 2097152 | tf_op jit(solution)/shard_map/all_to_all | solution.py:301
  43.1 19.7 %all-to-all-start.1 = ((bf16[8,512,128]{2,1,0:T(8,128)(2,1)}), bf16[8,512,128]{2,1,0:T(8,128)(2,1)}, u32[]{:S(2)}, u32[]{:S(2)}) async-start(bf16[8,512,128]{2,1,0:T(8,128)(2,1)} %get-tuple-element.29), calls=%async_computation.1 | async-start | bytes 2097152 | tf_op jit(solution)/shard_map/all_to_all | solution.py:322
  62.8 15.7 %collective-permute-start.5 = (bf16[2,256,512]{2,1,0:T(8,128)(2,1)}, bf16[2,256,512]{2,1,0:T(8,128)(2,1)S(1)}, u32[]{:S(2)}, u32[]{:S(2)}) collective-permute-start(bf16[2,256,512]{2,1,0:T(8,128)(2,1)} %get-tuple-element.37), channel_id=1, source_target_pairs={{0,4},{4,0},{8,12},{12,8},{16,20},{20,16},{24,28},{28,24},{1,5},{5... | collective-permute-start | bytes 1572872 | tf_op jit(solution)/shard_map/ppermute | solution.py:325
  62.8 15.7 %collective-permute-start.6 = (bf16[2,256,512]{2,1,0:T(8,128)(2,1)}, bf16[2,256,512]{2,1,0:T(8,128)(2,1)S(1)}, u32[]{:S(2)}, u32[]{:S(2)}) collective-permute-start(bf16[2,256,512]{2,1,0:T(8,128)(2,1)} %get-tuple-element.38), channel_id=1, source_target_pairs={{0,4},{4,0},{8,12},{12,8},{16,20},{20,16},{24,28},{28,24},{1,5},{5... | collective-permute-start | bytes 1572872 | tf_op jit(solution)/shard_map/ppermute | solution.py:325
  63.3 5.1 %collective-permute-start.1 = (f32[8,128]{1,0:T(8,128)}, f32[8,128]{1,0:T(8,128)S(1)}, u32[]{:S(2)}, u32[]{:S(2)}) collective-permute-start(f32[8,128]{1,0:T(8,128)} %get-tuple-element.35), channel_id=1, source_target_pairs={{0,4},{4,0},{8,12},{12,8},{16,20},{20,16},{24,28},{28,24},{1,5},{5... | collective-permute-start | bytes 12296 | tf_op jit(solution)/shard_map/ppermute | solution.py:242
  64.7 3.7 %copy-start.5 = (f32[8,128]{1,0:T(8,128)S(1)}, f32[8,128]{1,0:T(8,128)}, u32[]{:S(2)}) copy-start(f32[8,128]{1,0:T(8,128)} %get-tuple-element.35) | copy-start | bytes 12292
  64.7 13.8 %copy-start.2 = (bf16[256,512]{1,0:T(8,128)(2,1)S(1)}, bf16[256,512]{1,0:T(8,128)(2,1)}, u32[]{:S(2)}) copy-start(bf16[256,512]{1,0:T(8,128)(2,1)} %get-tuple-element.36) | copy-start | bytes 786436
  64.7 25.7 %all-to-all-start.3 = ((bf16[8,512,128]{2,1,0:T(8,128)(2,1)}), bf16[8,512,128]{2,1,0:T(8,128)(2,1)S(1)}, u32[]{:S(2)}, u32[]{:S(2)}) async-start(bf16[8,512,128]{2,1,0:T(8,128)(2,1)} %get-tuple-element.47), calls=%async_computation.3 | async-start | bytes 2097152 | tf_op jit(solution)/shard_map/all_to_all | solution.py:324
  68.4 4.7 %collective-permute-start.2 = (f32[8,128]{1,0:T(8,128)S(1)}, f32[8,128]{1,0:T(8,128)S(1)}, u32[]{:S(2)}, u32[]{:S(2)}) collective-permute-start(f32[8,128]{1,0:T(8,128)S(1)} %add.175), channel_id=1, source_target_pairs={{0,1},{1,0},{2,3},{3,2},{4,5},{5,4},{6,7},{7,6},{8,9},{9,8},{10,11... | collective-permute-start | bytes 12296 | tf_op jit(solution)/shard_map/ppermute | solution.py:234
  70.5 4.5 %collective-permute-start.3 = (f32[8,128]{1,0:T(8,128)S(1)}, f32[8,128]{1,0:T(8,128)S(1)}, u32[]{:S(2)}, u32[]{:S(2)}) collective-permute-start(f32[8,128]{1,0:T(8,128)S(1)} %add.175), channel_id=1, source_target_pairs={{0,2},{1,3},{2,0},{3,1},{4,6},{5,7},{6,4},{7,5},{8,10},{9,11},{10,... | collective-permute-start | bytes 12296 | tf_op jit(solution)/shard_map/ppermute | solution.py:234
  73.1 5.4 %collective-permute-start.4 = (f32[8,128]{1,0:T(8,128)S(1)}, f32[8,128]{1,0:T(8,128)S(1)}, u32[]{:S(2)}, u32[]{:S(2)}) collective-permute-start(f32[8,128]{1,0:T(8,128)S(1)} %add.175), channel_id=1, source_target_pairs={{0,3},{1,2},{2,1},{3,0},{4,7},{5,6},{6,5},{7,4},{8,11},{9,10},{10,... | collective-permute-start | bytes 12296 | tf_op jit(solution)/shard_map/ppermute | solution.py:234
  78.5 1.1 %copy-start.3 = (bf16[256,512]{1,0:T(8,128)(2,1)S(1)}, bf16[256,512]{1,0:T(8,128)(2,1)}, u32[]{:S(2)}) copy-start(bf16[256,512]{1,0:T(8,128)(2,1)} %get-tuple-element.40) | copy-start | bytes 786436
  78.5 1.1 %copy-start.4 = (bf16[256,512]{1,0:T(8,128)(2,1)S(1)}, bf16[256,512]{1,0:T(8,128)(2,1)}, u32[]{:S(2)}) copy-start(bf16[256,512]{1,0:T(8,128)(2,1)} %get-tuple-element.43) | copy-start | bytes 786436
  81.9 3.6 %collective-permute-start.7 = (f32[8,128]{1,0:T(8,128)S(1)}, f32[8,128]{1,0:T(8,128)S(1)}, u32[]{:S(2)}, u32[]{:S(2)}) collective-permute-start(f32[8,128]{1,0:T(8,128)S(1)} %add_add_fusion.1), channel_id=1, source_target_pairs={{0,8},{4,12},{8,0},{12,4},{16,24},{20,28},{24,16},{28,20},{1,9},{5... | collective-permute-start | bytes 12296 | tf_op jit(solution)/shard_map/ppermute | solution.py:234
  83.8 3.6 %collective-permute-start.8 = (f32[8,128]{1,0:T(8,128)S(1)}, f32[8,128]{1,0:T(8,128)S(1)}, u32[]{:S(2)}, u32[]{:S(2)}) collective-permute-start(f32[8,128]{1,0:T(8,128)S(1)} %add_add_fusion.1), channel_id=1, source_target_pairs={{0,16},{4,20},{8,24},{12,28},{16,0},{20,4},{24,8},{28,12},{1,17},{... | collective-permute-start | bytes 12296 | tf_op jit(solution)/shard_map/ppermute | solution.py:234
  85.3 4.5 %collective-permute-start.9 = (f32[8,128]{1,0:T(8,128)S(1)}, f32[8,128]{1,0:T(8,128)S(1)}, u32[]{:S(2)}, u32[]{:S(2)}) collective-permute-start(f32[8,128]{1,0:T(8,128)S(1)} %add_add_fusion.1), channel_id=1, source_target_pairs={{0,24},{4,28},{8,16},{12,20},{16,8},{20,12},{24,0},{28,4},{1,25},{... | collective-permute-start | bytes 12296 | tf_op jit(solution)/shard_map/ppermute | solution.py:234

commit v13 on v12

--- a/solution.py
+++ b/solution.py
@@ -240,8 +240,9 @@
     if batch != 4 or ctx not in (8, 32):
         return lax.psum(x, ("ctx", "batch")), ready
     x = x + lax.ppermute(x, "ctx", [(i, i ^ 1) for i in range(ctx)])
-    x = partners(x, "batch", (1, 2, 3))
-    x, ready = lax.optimization_barrier((x, ready))
+    a, b, c = (lax.ppermute(x, "batch", [(i, i ^ d) for i in range(batch)]) for d in (1, 2, 3))
+    x, ready = lax.optimization_barrier((x + a, ready))
+    x = x + (b + c)
     step = 2
     while step < ctx:
         x = partners(x, "ctx", (step, 2 * step, 3 * step))

time: 92.7 us -> 89.4 us (0.964)
  waiting for transfers between devices: 22 us -> 18.7 us
    ppermute x6 -> x3, waiting for transfers between devices: 9.66 us -> 4.35 us  [partners(): lax.ppermute(x, axis, [(i, i ^ d) for i in range(size)])]
    ppermute x0 -> x3, starting transfers between devices: none -> 4.73 us  [total_everywhere(): lax.ppermute(x, 'batch', [(i, i ^ d) for i in range(batch)])]
    ppermute x6 -> x3, starting transfers between devices: 8.16 us -> 3.49 us  [partners(): lax.ppermute(x, axis, [(i, i ^ d) for i in range(size)])]
    ppermute x0 -> x3, waiting for transfers between devices: none -> 1.97 us  [total_everywhere(): lax.ppermute(x, 'batch', [(i, i ^ d) for i in range(batch)])]
  transfers between devices with their start and end apart: 14 -> 14, of which waited for: 7 -> 7; matrix products, arithmetic and copies ran while one was open for 8% -> 8% of each run, Pallas kernels for 33% -> 35%
where the time goes in v13:
time: 89.4 us; the launch traced here: 88.8 us
  Pallas kernels  32.8 us (37%)
  starting transfers between devices  26.9 us (30%)
  waiting for transfers between devices  18.7 us (21%)
  other arithmetic  7.21 us (8%)
  local copies, waits for them, and re-layouts  2.29 us (3%)
    pallas_call x2, Pallas kernels, run_group(): pl.pallas_call(functools.partial(group_kernel, gi, devices, local_blocks,...  28.9 us
    all_to_all x2, waiting for transfers between devices, kv_for(): arrived = lax.all_to_all(spread(gi, ctx, k0, v0), 'ctx', 0, 0)  11.6 us
    all_to_all x2, starting transfers between devices, kv_for(): arrived = lax.all_to_all(spread(gi, ctx, k0, v0), 'ctx', 0, 0)  9.56 us
    ppermute x3, starting transfers between devices, total_everywhere(): lax.ppermute(x, 'batch', [(i, i ^ d) for i in range(batch)])  4.73 us
    all_to_all x1, starting transfers between devices, body(): grads[0] = lax.all_to_all(kv_grads, 'ctx', 0, 0)  4.43 us
    ppermute x3, waiting for transfers between devices, partners(): lax.ppermute(x, axis, [(i, i ^ d) for i in range(size)])  4.35 us
    pallas_call x2, Pallas kernels, spread(): pl.pallas_call(kernel, grid=(1,), in_specs=[column(gi), column(2 + gi)] *...  3.9 us
    all_to_all x1, starting transfers between devices, body(): grads[1] = lax.all_to_all(grads[1], 'ctx', 0, 0)  3.7 us
  transfers between devices with their start and end apart: 14, of which 7 were waited for; matrix products, arithmetic and copies ran while one was open for 8% of the time, Pallas kernels for 35%

profile of v13, /device:TPU:0, one launch (start us, length us, event | category | flops | bytes accessed | tf_op | source)
XLA Modules:
  0.0 88.8 jit_solution(12826460412989803722)
XLA Ops:
  0.6 2.0 %spread_keys_values.2 = bf16[8,2,2,128,128]{4,3,2,1,0:T(8,128)(2,1)} custom-call(bf16[256,512]{1,0:T(8,128)(2,1)} %bitcast.55, bf16[256,512]{1,0:T(8,128)(2,1)} %bitcast.56, bf16[256,512]{1,0:T(8,128)(2,1)} %bitcast.59, bf16[256,512]{1,0:T(8,128)(2,1)} %bitcast.60), custom_call_target="tpu_custom_call" | custom-call | tf_op jit(solution)/shard_map/spread_keys_values/pallas_call | solution.py:274
  2.6 5.3 %all-to-all-start = ((bf16[8,2,2,128,128]{4,3,2,1,0:T(8,128)(2,1)}), bf16[8,2,2,128,128]{4,3,2,1,0:T(8,128)(2,1)}, u32[]{:S(2)}, u32[]{:S(2)}) async-start(bf16[8,2,2,128,128]{4,3,2,1,0:T(8,128)(2,1)} %spread_keys_values.2), calls=%async_computation | async-start | bytes 2097152 | tf_op jit(solution)/shard_map/all_to_all | solution.py:302
  8.0 0.1 constant_dynamic-slice_fusion
  8.1 0.6 slice-done
  8.8 1.1 %pad_maximum_fusion = bf16[2,256,1024]{2,1,0:T(8,128)(2,1)} fusion(bf16[1,256,1024]{2,1,0:T(8,128)(2,1)S(1)} %get-tuple-element.85, bf16[1,256,1024]{2,1,0:T(8,128)(2,1)S(1)} %get-tuple-element.86), kind=kLoop, calls=%fused_computation | loop fusion | flops 524288 | bytes 2097152 | tf_op jit(solution)/shard_map/stack | solution.py:310
  9.9 0.5 and_select_fusion.refs_1_
  10.4 0.5 collective-permute-start
  10.9 2.0 %spread_keys_values.3 = bf16[8,2,2,128,128]{4,3,2,1,0:T(8,128)(2,1)} custom-call(bf16[256,512]{1,0:T(8,128)(2,1)} %bitcast.57, bf16[256,512]{1,0:T(8,128)(2,1)} %bitcast.58, bf16[256,512]{1,0:T(8,128)(2,1)} %bitcast.61, bf16[256,512]{1,0:T(8,128)(2,1)} %bitcast.62), custom_call_target="tpu_custom_call" | custom-call | tf_op jit(solution)/shard_map/spread_keys_values/pallas_call | solution.py:274
  12.8 10.6 %all-to-all-done = bf16[8,2,2,128,128]{4,3,2,1,0:T(8,128)(2,1)} async-done(((bf16[8,2,2,128,128]{4,3,2,1,0:T(8,128)(2,1)}), bf16[8,2,2,128,128]{4,3,2,1,0:T(8,128)(2,1)}, u32[]{:S(2)}, u32[]{:S(2)}) %all-to-all-start) | async-done | bytes 1048608 | tf_op jit(solution)/shard_map/all_to_all | solution.py:302
  23.4 4.2 %all-to-all-start.2 = ((bf16[8,2,2,128,128]{4,3,2,1,0:T(8,128)(2,1)}), bf16[8,2,2,128,128]{4,3,2,1,0:T(8,128)(2,1)}, u32[]{:S(2)}, u32[]{:S(2)}) async-start(bf16[8,2,2,128,128]{4,3,2,1,0:T(8,128)(2,1)} %spread_keys_values.3), calls=%async_computation.2 | async-start | bytes 2097152 | tf_op jit(solution)/shard_map/all_to_all | solution.py:302
  27.7 14.4 %group_attention.2 = (bf16[256,512]{1,0:T(8,128)(2,1)}, bf16[256,512]{1,0:T(8,128)(2,1)}, bf16[2,256,512]{2,1,0:T(8,128)(2,1)}, f32[8,128]{1,0:T(8,128)}, bf16[8,512,128]{2,1,0:T(8,128)(2,1)}) custom-call(s32[1]{0:T(128)} %bitcast.refs_0_, s32[64]{0:T(128)} %and_select_fusion.refs_1_, f32[16]{0:T(128)} %refs_2_.3, bf16[256,2048]{1,0:T(8,128)(2,1)} %bitcast.79, ...), custom_call_target="tpu_custom_call" | custom-call | flops 4429185024 | bytes 6291456 | tf_op jit(solution)/shard_map/group_attention/pallas_call | solution.py:208
  42.1 1.0 %all-to-all-done.2 = bf16[8,2,2,128,128]{4,3,2,1,0:T(8,128)(2,1)} async-done(((bf16[8,2,2,128,128]{4,3,2,1,0:T(8,128)(2,1)}), bf16[8,2,2,128,128]{4,3,2,1,0:T(8,128)(2,1)}, u32[]{:S(2)}, u32[]{:S(2)}) %all-to-all-start.2) | async-done | bytes 1048608 | tf_op jit(solution)/shard_map/all_to_all | solution.py:302
  43.1 4.4 %all-to-all-start.1 = ((bf16[8,512,128]{2,1,0:T(8,128)(2,1)}), bf16[8,512,128]{2,1,0:T(8,128)(2,1)}, u32[]{:S(2)}, u32[]{:S(2)}) async-start(bf16[8,512,128]{2,1,0:T(8,128)(2,1)} %get-tuple-element.29), calls=%async_computation.1 | async-start | bytes 2097152 | tf_op jit(solution)/shard_map/all_to_all | solution.py:323
  47.6 14.5 %group_attention.3 = (bf16[256,512]{1,0:T(8,128)(2,1)}, bf16[256,512]{1,0:T(8,128)(2,1)}, bf16[2,256,512]{2,1,0:T(8,128)(2,1)}, f32[8,128]{1,0:T(8,128)}, bf16[8,512,128]{2,1,0:T(8,128)(2,1)}) custom-call(s32[1]{0:T(128)} %bitcast.refs_0_, s32[64]{0:T(128)} %and_select_fusion.refs_1_, f32[16]{0:T(128)} %refs_2_.3, bf16[256,2048]{1,0:T(8,128)(2,1)} %bitcast.80, ...), custom_call_target="tpu_custom_call" | custom-call | flops 4429185024 | bytes 6291456 | tf_op jit(solution)/shard_map/group_attention/pallas_call | solution.py:208
  62.0 0.8 all-to-all-done.1
  62.8 0.5 collective-permute-start.4
  63.3 1.4 %fusion.1 = (bf16[1,512,128]{2,1,0:T(8,128)(2,1)S(1)}, bf16[1,512,128]{2,1,0:T(8,128)(2,1)S(1)}, bf16[1,512,128]{2,1,0:T(8,128)(2,1)S(1)}, bf16[1,512,128]{2,1,0...) fusion(bf16[8,512,128]{2,1,0:T(8,128)(2,1)} %all-to-all-done.1), kind=kLoop, calls=%fused_computation.30 | loop fusion | bytes 2097152 | tf_op jit(solution)/shard_map/slice | solution.py:345
  64.7 3.7 %all-to-all-start.3 = ((bf16[8,512,128]{2,1,0:T(8,128)(2,1)}), bf16[8,512,128]{2,1,0:T(8,128)(2,1)S(1)}, u32[]{:S(2)}, u32[]{:S(2)}) async-start(bf16[8,512,128]{2,1,0:T(8,128)(2,1)} %get-tuple-element.47), calls=%async_computation.3 | async-start | bytes 2097152 | tf_op jit(solution)/shard_map/all_to_all | solution.py:325
  68.4 2.1 %collective-permute-start.2 = (f32[8,128]{1,0:T(8,128)S(1)}, f32[8,128]{1,0:T(8,128)S(1)}, u32[]{:S(2)}, u32[]{:S(2)}) collective-permute-start(f32[8,128]{1,0:T(8,128)S(1)} %add.175), channel_id=1, source_target_pairs={{0,1},{1,0},{2,3},{3,2},{4,5},{5,4},{6,7},{7,6},{8,9},{9,8},{10,11... | collective-permute-start | bytes 12296 | tf_op jit(solution)/shard_map/ppermute | solution.py:243
  70.6 2.7 %collective-permute-start.5 = (f32[8,128]{1,0:T(8,128)S(1)}, f32[8,128]{1,0:T(8,128)S(1)}, u32[]{:S(2)}, u32[]{:S(2)}) collective-permute-start(f32[8,128]{1,0:T(8,128)S(1)} %add.175), channel_id=1, source_target_pairs={{0,2},{1,3},{2,0},{3,1},{4,6},{5,7},{6,4},{7,5},{8,10},{9,11},{10,... | collective-permute-start | bytes 12296 | tf_op jit(solution)/shard_map/ppermute | solution.py:243
  73.3 1.1 %bitcast_select_fusion.3 = (bf16[256,512]{1,0:T(8,128)(2,1)S(1)}, bf16[256,512]{1,0:T(8,128)(2,1)S(1)}, bf16[256,512]{1,0:T(8,128)(2,1)S(1)}, bf16[256,512]{1,0:T(8,128)(2,1)S(1)}) fusion(bf16[256,512]{1,0:T(8,128)(2,1)} %get-tuple-element.42, pred[]{:T(512)S(6)} %eq.8, bf16[2,256,512]{2,1,0:T(8,128)(2,1)S(1)} %collective-permute-done.3, pred[]{:T(512)S(6)} %eq.9, ...), kind=kLoop, calls=%fused_computation.8 | loop fusion | flops 524288 | bytes 2097154 | tf_op jit(solution)/shard_map/jit(_where)/select_n | solution.py:333
  74.5 1.1 %maximum_bitcast_fusion.1 = bf16[1,256,2048]{2,1,0:T(8,128)(2,1)} fusion(bf16[256,512]{1,0:T(8,128)(2,1)S(1)} %get-tuple-element.68, bf16[256,512]{1,0:T(8,128)(2,1)S(1)} %get-tuple-element.66, bf16[256,512]{1,0:T(8,128)(2,1)S(1)} %get-tuple-element.67, bf16[256,512]{1,0:T(8,128)(2,1)S(1)} %get-tuple-element.65), kind=kLoop, calls=%fused_computation.2 | loop fusion | flops 4194304 | bytes 2097152 | tf_op jit(solution)/shard_map/broadcast_in_dim | solution.py:337
  75.6 1.1 %maximum_bitcast_fusion = bf16[1,256,2048]{2,1,0:T(8,128)(2,1)} fusion(bf16[256,512]{1,0:T(8,128)(2,1)S(1)} %get-tuple-element.83, bf16[256,512]{1,0:T(8,128)(2,1)S(1)} %get-tuple-element.81, bf16[256,512]{1,0:T(8,128)(2,1)S(1)} %get-tuple-element.84, bf16[256,512]{1,0:T(8,128)(2,1)S(1)} %get-tuple-element.82), kind=kLoop, calls=%fused_computation.1 | loop fusion | flops 4194304 | bytes 2097152 | tf_op jit(solution)/shard_map/broadcast_in_dim | solution.py:336
  76.7 2.0 %collective-permute-done.6 = f32[8,128]{1,0:T(8,128)S(1)} collective-permute-done((f32[8,128]{1,0:T(8,128)S(1)}, f32[8,128]{1,0:T(8,128)S(1)}, u32[]{:S(2)}, u32[]{:S(2)}) %collective-permute-start.6) | collective-permute-done | bytes 4128 | tf_op jit(solution)/shard_map/ppermute | solution.py:243
  78.7 1.9 %collective-permute-start.7 = (f32[8,128]{1,0:T(8,128)S(1)}, f32[8,128]{1,0:T(8,128)S(1)}, u32[]{:S(2)}, u32[]{:S(2)}) collective-permute-start(f32[8,128]{1,0:T(8,128)S(1)} %add_add_fusion.1), channel_id=1, source_target_pairs={{0,8},{4,12},{8,0},{12,4},{16,24},{20,28},{24,16},{28,20},{1,9},{5... | collective-permute-start | bytes 12296 | tf_op jit(solution)/shard_map/ppermute | solution.py:234
  80.6 1.5 %collective-permute-start.8 = (f32[8,128]{1,0:T(8,128)S(1)}, f32[8,128]{1,0:T(8,128)S(1)}, u32[]{:S(2)}, u32[]{:S(2)}) collective-permute-start(f32[8,128]{1,0:T(8,128)S(1)} %add_add_fusion.1), channel_id=1, source_target_pairs={{0,16},{4,20},{8,24},{12,28},{16,0},{20,4},{24,8},{28,12},{1,17},{... | collective-permute-start | bytes 12296 | tf_op jit(solution)/shard_map/ppermute | solution.py:234
  82.2 0.7 collective-permute-done.7
  82.9 1.2 %collective-permute-done.8 = f32[8,128]{1,0:T(8,128)S(1)} collective-permute-done((f32[8,128]{1,0:T(8,128)S(1)}, f32[8,128]{1,0:T(8,128)S(1)}, u32[]{:S(2)}, u32[]{:S(2)}) %collective-permute-start.8) | collective-permute-done | bytes 4128 | tf_op jit(solution)/shard_map/ppermute | solution.py:234
  84.2 2.4 %collective-permute-done.9 = f32[8,128]{1,0:T(8,128)S(1)} collective-permute-done((f32[8,128]{1,0:T(8,128)S(1)}, f32[8,128]{1,0:T(8,128)S(1)}, u32[]{:S(2)}, u32[]{:S(2)}) %collective-permute-start.9) | collective-permute-done | bytes 4128 | tf_op jit(solution)/shard_map/ppermute | solution.py:234
  86.6 0.5 multiply_bitcast_fusion
  87.3 0.7 maximum_bitcast_fusion.3
  88.1 0.7 maximum_bitcast_fusion.2
  (37 shorter events, 0.8 us)
Async XLA Ops:
  2.6 5.3 %copy-start = (bf16[1,256,2048]{2,1,0:T(8,128)(2,1)S(1)}, bf16[1,256,2048]{2,1,0:T(8,128)(2,1)}, u32[]{:S(2)}) copy-start(bf16[1,256,2048]{2,1,0:T(8,128)(2,1)} %param.6) | copy-start | bytes 3145732
  2.6 5.3 %copy-start.1 = (bf16[1,256,2048]{2,1,0:T(8,128)(2,1)S(1)}, bf16[1,256,2048]{2,1,0:T(8,128)(2,1)}, u32[]{:S(2)}) copy-start(bf16[1,256,2048]{2,1,0:T(8,128)(2,1)} %param.10) | copy-start | bytes 3145732
  2.6 20.8 %all-to-all-start = ((bf16[8,2,2,128,128]{4,3,2,1,0:T(8,128)(2,1)}), bf16[8,2,2,128,128]{4,3,2,1,0:T(8,128)(2,1)}, u32[]{:S(2)}, u32[]{:S(2)}) async-start(bf16[8,2,2,128,128]{4,3,2,1,0:T(8,128)(2,1)} %spread_keys_values.2), calls=%async_computation | async-start | bytes 2097152 | tf_op jit(solution)/shard_map/all_to_all | solution.py:302
  7.9 0.7 slice-start
  10.4 17.3 %collective-permute-start = (bf16[2,256,1024]{2,1,0:T(8,128)(2,1)}, bf16[2,256,1024]{2,1,0:T(8,128)(2,1)}, u32[]{:S(2)}, u32[]{:S(2)}) collective-permute-start(bf16[2,256,1024]{2,1,0:T(8,128)(2,1)} %pad_maximum_fusion), channel_id=1, source_target_pairs={{0,4},{4,0},{8,12},{12,8},{16,20},{20,16},{24,28},{28,24},{1,5},{5... | collective-permute-start | bytes 3145736 | tf_op jit(solution)/shard_map/ppermute | solution.py:311
  23.4 19.7 %all-to-all-start.2 = ((bf16[8,2,2,128,128]{4,3,2,1,0:T(8,128)(2,1)}), bf16[8,2,2,128,128]{4,3,2,1,0:T(8,128)(2,1)}, u32[]{:S(2)}, u32[]{:S(2)}) async-start(bf16[8,2,2,128,128]{4,3,2,1,0:T(8,128)(2,1)} %spread_keys_values.3), calls=%async_computation.2 | async-start | bytes 2097152 | tf_op jit(solution)/shard_map/all_to_all | solution.py:302
  43.1 19.7 %all-to-all-start.1 = ((bf16[8,512,128]{2,1,0:T(8,128)(2,1)}), bf16[8,512,128]{2,1,0:T(8,128)(2,1)}, u32[]{:S(2)}, u32[]{:S(2)}) async-start(bf16[8,512,128]{2,1,0:T(8,128)(2,1)} %get-tuple-element.29), calls=%async_computation.1 | async-start | bytes 2097152 | tf_op jit(solution)/shard_map/all_to_all | solution.py:323
  62.8 10.5 %collective-permute-start.3 = (bf16[2,256,512]{2,1,0:T(8,128)(2,1)}, bf16[2,256,512]{2,1,0:T(8,128)(2,1)S(1)}, u32[]{:S(2)}, u32[]{:S(2)}) collective-permute-start(bf16[2,256,512]{2,1,0:T(8,128)(2,1)} %get-tuple-element.37), channel_id=1, source_target_pairs={{0,4},{4,0},{8,12},{12,8},{16,20},{20,16},{24,28},{28,24},{1,5},{5... | collective-permute-start | bytes 1572872 | tf_op jit(solution)/shard_map/ppermute | solution.py:326
  62.8 10.5 %collective-permute-start.4 = (bf16[2,256,512]{2,1,0:T(8,128)(2,1)}, bf16[2,256,512]{2,1,0:T(8,128)(2,1)S(1)}, u32[]{:S(2)}, u32[]{:S(2)}) collective-permute-start(bf16[2,256,512]{2,1,0:T(8,128)(2,1)} %get-tuple-element.38), channel_id=1, source_target_pairs={{0,4},{4,0},{8,12},{12,8},{16,20},{20,16},{24,28},{28,24},{1,5},{5... | collective-permute-start | bytes 1572872 | tf_op jit(solution)/shard_map/ppermute | solution.py:326
  63.3 5.1 %collective-permute-start.1 = (f32[8,128]{1,0:T(8,128)}, f32[8,128]{1,0:T(8,128)S(1)}, u32[]{:S(2)}, u32[]{:S(2)}) collective-permute-start(f32[8,128]{1,0:T(8,128)} %get-tuple-element.35), channel_id=1, source_target_pairs={{0,4},{4,0},{8,12},{12,8},{16,20},{20,16},{24,28},{28,24},{1,5},{5... | collective-permute-start | bytes 12296 | tf_op jit(solution)/shard_map/ppermute | solution.py:242
  64.7 3.7 %copy-start.5 = (f32[8,128]{1,0:T(8,128)S(1)}, f32[8,128]{1,0:T(8,128)}, u32[]{:S(2)}) copy-start(f32[8,128]{1,0:T(8,128)} %get-tuple-element.35) | copy-start | bytes 12292
  64.7 8.6 %copy-start.2 = (bf16[256,512]{1,0:T(8,128)(2,1)S(1)}, bf16[256,512]{1,0:T(8,128)(2,1)}, u32[]{:S(2)}) copy-start(bf16[256,512]{1,0:T(8,128)(2,1)} %get-tuple-element.36) | copy-start | bytes 786436
  64.7 22.4 %all-to-all-start.3 = ((bf16[8,512,128]{2,1,0:T(8,128)(2,1)}), bf16[8,512,128]{2,1,0:T(8,128)(2,1)S(1)}, u32[]{:S(2)}, u32[]{:S(2)}) async-start(bf16[8,512,128]{2,1,0:T(8,128)(2,1)} %get-tuple-element.47), calls=%async_computation.3 | async-start | bytes 2097152 | tf_op jit(solution)/shard_map/all_to_all | solution.py:325
  68.4 4.8 %collective-permute-start.2 = (f32[8,128]{1,0:T(8,128)S(1)}, f32[8,128]{1,0:T(8,128)S(1)}, u32[]{:S(2)}, u32[]{:S(2)}) collective-permute-start(f32[8,128]{1,0:T(8,128)S(1)} %add.175), channel_id=1, source_target_pairs={{0,1},{1,0},{2,3},{3,2},{4,5},{5,4},{6,7},{7,6},{8,9},{9,8},{10,11... | collective-permute-start | bytes 12296 | tf_op jit(solution)/shard_map/ppermute | solution.py:243
  70.6 6.1 %collective-permute-start.5 = (f32[8,128]{1,0:T(8,128)S(1)}, f32[8,128]{1,0:T(8,128)S(1)}, u32[]{:S(2)}, u32[]{:S(2)}) collective-permute-start(f32[8,128]{1,0:T(8,128)S(1)} %add.175), channel_id=1, source_target_pairs={{0,2},{1,3},{2,0},{3,1},{4,6},{5,7},{6,4},{7,5},{8,10},{9,11},{10,... | collective-permute-start | bytes 12296 | tf_op jit(solution)/shard_map/ppermute | solution.py:243
  73.2 5.4 %collective-permute-start.6 = (f32[8,128]{1,0:T(8,128)S(1)}, f32[8,128]{1,0:T(8,128)S(1)}, u32[]{:S(2)}, u32[]{:S(2)}) collective-permute-start(f32[8,128]{1,0:T(8,128)S(1)} %add.175), channel_id=1, source_target_pairs={{0,3},{1,2},{2,1},{3,0},{4,7},{5,6},{6,5},{7,4},{8,11},{9,10},{10,... | collective-permute-start | bytes 12296 | tf_op jit(solution)/shard_map/ppermute | solution.py:243
  73.3 1.1 %copy-start.3 = (bf16[256,512]{1,0:T(8,128)(2,1)S(1)}, bf16[256,512]{1,0:T(8,128)(2,1)}, u32[]{:S(2)}) copy-start(bf16[256,512]{1,0:T(8,128)(2,1)} %get-tuple-element.40) | copy-start | bytes 786436
  73.3 1.1 %copy-start.4 = (bf16[256,512]{1,0:T(8,128)(2,1)S(1)}, bf16[256,512]{1,0:T(8,128)(2,1)}, u32[]{:S(2)}) copy-start(bf16[256,512]{1,0:T(8,128)(2,1)} %get-tuple-element.43) | copy-start | bytes 786436
  78.7 4.3 %collective-permute-start.7 = (f32[8,128]{1,0:T(8,128)S(1)}, f32[8,128]{1,0:T(8,128)S(1)}, u32[]{:S(2)}, u32[]{:S(2)}) collective-permute-start(f32[8,128]{1,0:T(8,128)S(1)} %add_add_fusion.1), channel_id=1, source_target_pairs={{0,8},{4,12},{8,0},{12,4},{16,24},{20,28},{24,16},{28,20},{1,9},{5... | collective-permute-start | bytes 12296 | tf_op jit(solution)/shard_map/ppermute | solution.py:234
  80.6 3.6 %collective-permute-start.8 = (f32[8,128]{1,0:T(8,128)S(1)}, f32[8,128]{1,0:T(8,128)S(1)}, u32[]{:S(2)}, u32[]{:S(2)}) collective-permute-start(f32[8,128]{1,0:T(8,128)S(1)} %add_add_fusion.1), channel_id=1, source_target_pairs={{0,16},{4,20},{8,24},{12,28},{16,0},{20,4},{24,8},{28,12},{1,17},{... | collective-permute-start | bytes 12296 | tf_op jit(solution)/shard_map/ppermute | solution.py:234
  82.1 4.5 %collective-permute-start.9 = (f32[8,128]{1,0:T(8,128)S(1)}, f32[8,128]{1,0:T(8,128)S(1)}, u32[]{:S(2)}, u32[]{:S(2)}) collective-permute-start(f32[8,128]{1,0:T(8,128)S(1)} %add_add_fusion.1), channel_id=1, source_target_pairs={{0,24},{4,28},{8,16},{12,20},{16,8},{20,12},{24,0},{28,4},{1,25},{... | collective-permute-start | bytes 12296 | tf_op jit(solution)/shard_map/ppermute | solution.py:234
